TPU v7x, 32 devices: a whole 2x2x4 slice. The times are simulated.
32 devices in a mesh: dp: 8 (over y, x, core), ctx: 4 (over z).
Axes of the slice: x: 2, y: 2, z: 4, core: 2. Of those that a mesh axis runs over, the one named last changes fastest.
Arguments:
- keys_a: bfloat16 [8, 512, 2560], P('dp', 'ctx'), may hold values from -6 to 6
- values_a: bfloat16 [8, 512, 2560], P('dp', 'ctx'), may hold values from -6 to 6
- queries_b: bfloat16 [8, 512, 2560], P('dp', 'ctx'), may hold values from -6 to 6
- grad_out: bfloat16 [8, 512, 2560], P('dp', 'ctx'), may hold values from -1.5 to 1.5
- state_start: float32 [3, 20, 128, 128], P(None, None, 'ctx'), may hold values from -0.5 to 0.5
- state_next: float32 [8, 3, 20, 128, 128], P('dp', None, None, 'ctx'), may hold values from -0.5 to 0.5
Outputs:
- grad_keys: bfloat16 [8, 512, 2560], P('dp', 'ctx')
- grad_values: bfloat16 [8, 512, 2560], P('dp', 'ctx')
- grad_state: float32 [3, 20, 128, 128], P(None, None, 'ctx')
All inputs are finite; a program needn't handle non-finite values.
Results may differ from a plain program's by a relative error of at most 0.033.
Values may be sent and summed in bfloat16 or wider, within the bound.
No kernel may reach another device: no remote copies, remote signals or barrier semaphores. Data moves between devices by JAX's collectives and lax.ppermute only.
A program may use at most 128 MiB of HBM per device.

v0:
```python
import functools

import jax
import jax.numpy as jnp
from jax import lax
from jax.experimental import pallas as pl
from jax.experimental.pallas import tpu as pltpu
from jax.sharding import PartitionSpec as P

RATE = 4.0
CA = 3.4445
CB = -4.775
CC = 2.0315
STEPS = 2
F32 = jnp.float32
BF16 = jnp.bfloat16
VMEM_SMALL = 8 * 1024 * 1024
VMEM_LARGE = 28 * 1024 * 1024
SMEM = pl.BlockSpec(memory_space=pltpu.SMEM)
VMEM = pl.BlockSpec(memory_space=pltpu.VMEM)
ANY = pl.BlockSpec(memory_space=pl.ANY)
HBM = pl.BlockSpec(memory_space=pltpu.HBM)


def dot_nn(a, b):
    return lax.dot_general(a, b, (((1,), (0,)), ((), ())), preferred_element_type=F32)


def dot_nt(a, b):
    return lax.dot_general(a, b, (((1,), (1,)), ((), ())), preferred_element_type=F32)


def dot_tn(a, b):
    return lax.dot_general(a, b, (((0,), (0,)), ((), ())), preferred_element_type=F32)


def call(
    kernel, out_shape, args, in_specs, out_specs, name, scratch=(), flops=10**6, size=10**6, vmem=VMEM_SMALL
):
    return pl.pallas_call(
        kernel,
        out_shape=out_shape,
        in_specs=in_specs,
        out_specs=out_specs,
        scratch_shapes=list(scratch),
        compiler_params=pltpu.CompilerParams(vmem_limit_bytes=vmem),
        cost_estimate=pl.CostEstimate(flops=flops, bytes_accessed=size, transcendentals=0),
        name=name,
    )(*args)


def swish_terms(g):
    s = 1.0 / (1.0 + jnp.exp(-g))
    sw = g * s
    slope = s * (1.0 + g * (1.0 - s))
    return s, sw, slope


def newton_pullback(grads, updates):
    each = range(len(grads))
    inv = [lax.rsqrt(jnp.sum(g * g, keepdims=True) + 1e-06) for g in grads]
    xs = [[(grads[m] * inv[m]).astype(BF16) for m in each]]
    grams = []
    polys = []
    for step in range(STEPS):
        x = xs[-1]
        gram = [dot_nt(x[m], x[m]).astype(BF16) for m in each]
        poly = [(CB * gram[m].astype(F32) + CC * dot_nn(gram[m], gram[m])).astype(BF16) for m in each]
        grams.append(gram)
        polys.append(poly)
        if step + 1 < STEPS:
            xs.append([(CA * x[m].astype(F32) + dot_nn(poly[m], x[m])).astype(BF16) for m in each])
    d = updates
    for step in reversed(range(STEPS)):
        x, gram, poly = xs[step], grams[step], polys[step]
        dp = [dot_nt(d[m], x[m]) for m in each]
        sym = [dp[m] + dp[m].T for m in each]
        turned = [dot_nn(sym[m].astype(BF16), gram[m]) for m in each]
        da = [(CB * sym[m] + CC * (turned[m] + turned[m].T)).astype(BF16) for m in each]
        d = [
            (CA * d[m].astype(F32) + dot_nn(poly[m], d[m]) + dot_nn(da[m], x[m])).astype(BF16)
            for m in each
        ]
    out = []
    for m in each:
        df = d[m].astype(F32)
        along = jnp.sum(df * grads[m], keepdims=True)
        out.append(df * inv[m] - grads[m] * (along * (inv[m] * inv[m] * inv[m])))
    return out


class Plan:
    def __init__(self, n, n_dp, tokens, heads, rows, width):
        self.n, self.n_dp = n, n_dp
        self.tokens, self.heads, self.rows, self.width = tokens, heads, rows, width
        self.per = -(-heads // n)
        self.mats = 3 * self.per
        early = (self.per + 1) // 2
        self.chunks = [c for c in ((0, early), (early, self.per - early)) if c[1] > 0]
        self.group = min(4, n_dp)
        self.share = -(-self.mats // self.group)
        self.pair = min(2, n_dp)
        self.rest = n_dp // self.pair
        self.own = -(-self.mats // n_dp)
        self.block = -(-rows // 16) * 16
        self.share_rows = -(-self.share // self.per) * self.block

    def first_head(self, c):
        return min(c * self.per, self.heads - self.per)


def pack_a_kernel(head_ref, dp_ref, k_ref, v_ref, s_ref, out, state, sems, *, plan, slot):
    t, w, per = plan.tokens, plan.width, plan.per
    low = lax.rem(dp_ref[0], plan.group)
    head = head_ref[slot]
    loads = []
    for q in range(plan.share):
        mat = jnp.minimum(low * plan.share + q, plan.mats - 1)
        load = pltpu.make_async_copy(
            s_ref.at[lax.rem(mat, 3), head + lax.div(mat, 3)], state.at[q], sems.at[2 + q]
        )
        load.start()
        loads.append(load)
    cols = pl.ds(pl.multiple_of(head * w, w), per * w)
    copies = []
    for part, src in enumerate((k_ref, v_ref)):
        copy = pltpu.make_async_copy(src.at[0, :, cols], out.at[pl.ds(part * t, t), :], sems.at[part])
        copy.start()
        copies.append(copy)
    for load in loads:
        load.wait()
    for q in range(plan.share):
        top = 2 * t + (q // per) * plan.block
        left = (q % per) * w
        out[top : top + plan.rows, left : left + w] = state[q].astype(BF16)
    for copy in copies:
        copy.wait()


def pack_b_kernel(head_ref, q_ref, o_ref, s_ref, *refs, plan, chunk):
    n, t, w = plan.n, plan.tokens, plan.width
    first, count = plan.chunks[chunk]
    outs, (state, sems) = refs[:-2], refs[-2:]
    if len(outs) < n:
        outs = [outs[0].at[c] for c in range(n)]
        heads = [plan.first_head(c) + first for c in range(n)]
        offsets = [head * w for head in heads]
    else:
        heads = [head_ref[slot] + first for slot in range(n)]
        offsets = [pl.multiple_of(head * w, w) for head in heads]
    loads = []
    copies = []
    for k in range(n):
        load = pltpu.make_async_copy(
            s_ref.at[0, :, pl.ds(heads[k], count)], state.at[k], sems.at[3 * k + 2]
        )
        load.start()
        loads.append(load)
        for part, src in enumerate((q_ref, o_ref)):
            copy = pltpu.make_async_copy(
                src.at[0, :, pl.ds(offsets[k], count * w)],
                outs[k].at[pl.ds(part * t, t), :],
                sems.at[3 * k + part],
            )
            copy.start()
            copies.append(copy)
    for k in range(n):
        loads[k].wait()
        for j in range(count):
            for m in range(3):
                top = 2 * t + m * plan.block
                outs[k][top : top + plan.rows, j * w : (j + 1) * w] = state[k, m, j].astype(BF16)
    for copy in copies:
        copy.wait()


def start_kernel(from_ref, *refs, plan):
    rows, w = plan.rows, plan.width
    a_refs, (out, whole) = refs[: plan.n], refs[plan.n :]
    for slot in range(plan.n):
        at = pl.ds(pl.multiple_of(from_ref[slot] * rows, rows), rows)
        for q in range(plan.share):
            top = 2 * plan.tokens + (q // plan.per) * plan.block
            left = (q % plan.per) * w
            whole[q, at, :] = a_refs[slot][top : top + rows, left : left + w].astype(F32)
    out[...] = whole[...].astype(BF16)


def tokens_of(refs, j, plan):
    t, w = plan.tokens, plan.width
    cols = slice(j * w, (j + 1) * w)
    x = jnp.concatenate([r[0:t, cols] for r in refs], axis=0)
    y = jnp.concatenate([r[t : 2 * t, cols] for r in refs], axis=0)
    return x, y


def forward(x, y, wa, wb, wc):
    w = wa.shape[1]
    gu = dot_nn(x, jnp.concatenate([wa, wb], axis=1))
    g, u = gu[:, :w], gu[:, w:]
    p = dot_nn(y, wc)
    _, sw, slope = swish_terms(g)
    hidden = (sw * u).astype(BF16)
    dg = (p * u * slope).astype(BF16)
    du = (p * sw).astype(BF16)
    ab = dot_tn(x, jnp.concatenate([dg, du], axis=1))
    return (ab[:, :w], ab[:, w:], dot_tn(y, hidden)), (g, u, p), (dg, du, hidden)


def chunk_kernel(from_ref, dp_ref, *refs, plan, chunk):
    n, t, w = plan.n, plan.tokens, plan.width
    first, count = plan.chunks[chunk]
    last = chunk + 1 == len(plan.chunks)
    mats = 3 * count
    refs = list(refs)

    def take(k):
        got = refs[:k]
        del refs[:k]
        return got

    a_refs, shares = take(n), take(plan.group)
    joined = len(refs[0].shape) == 3
    b_refs = take(1 if joined else n)
    if joined:
        b_refs = [b_refs[0].at[c] for c in range(n)]
        sources = list(range(n))
    else:
        sources = [from_ref[slot] for slot in range(n)]
    before = take(chunk) if last else []
    (d_ref,) = take(1)
    c_refs = take(2 if last else 1)
    w0, w1, gsum, ssum, acts, fields = take(6)
    total = take(1)[0] if last else c_refs[0]
    base = 3 * first if last else 0

    low = lax.rem(dp_ref[0], plan.group)
    for k in range(plan.group):
        at = pl.ds(jnp.bitwise_xor(low, k) * plan.share, plan.share)
        w0[at] = shares[k][...]
    for slot in range(n):
        row = sources[slot] * plan.rows
        at = pl.ds(row if joined else pl.multiple_of(row, plan.rows), plan.rows)
        for j in range(count):
            for m in range(3):
                top = 2 * t + m * plan.block
                part = b_refs[slot][top : top + plan.rows, j * w : (j + 1) * w]
                w1[3 * j + m, at, :] = part.astype(F32)

    for j in range(count):
        at = 3 * (first + j)
        x, y = tokens_of(a_refs, first + j, plan)
        sums, act, field = forward(x, y, w0[at], w0[at + 1], w0[at + 2])
        for m in range(3):
            gsum[3 * j + m] = sums[m]
            acts[j, m] = act[m]
            fields[j, m] = field[m]
        x, y = tokens_of(b_refs, j, plan)
        sums, _, _ = forward(x, y, *[w1[3 * j + m].astype(BF16) for m in range(3)])
        for m in range(3):
            ssum[3 * j + m] = sums[m]

    grads = [gsum[m] for m in range(mats)]
    updates = [(RATE * ssum[m]).astype(BF16) for m in range(mats)]
    for m, val in enumerate(newton_pullback(grads, updates)):
        gsum[m] = val

    for j in range(count):
        at = 3 * (first + j)
        x, y = tokens_of(a_refs, first + j, plan)
        fab = jnp.concatenate([gsum[3 * j], gsum[3 * j + 1]], axis=1).astype(BF16)
        fc = gsum[3 * j + 2].astype(BF16)
        wab = jnp.concatenate([w0[at], w0[at + 1]], axis=1)
        wc = w0[at + 2]
        cdgu = dot_nn(x, fab)
        cdg, cdu = cdgu[:, :w], cdgu[:, w:]
        ch = dot_nn(y, fc)
        g, u, p = acts[j, 0], acts[j, 1], acts[j, 2]
        s, sw, slope = swish_terms(g)
        curve = s * (1.0 - s) * (2.0 + g * (1.0 - 2.0 * s))
        cg = ((ch * u + cdu * p) * slope + cdg * (p * u) * curve).astype(BF16)
        cu = (ch * sw + cdg * p * slope).astype(BF16)
        cp = (cdu * sw + cdg * u * slope).astype(BF16)
        dg, du, hidden = fields[j, 0], fields[j, 1], fields[j, 2]
        dx = dot_nt(jnp.concatenate([dg, du, cg, cu], axis=1), jnp.concatenate([fab, wab], axis=1))
        dy = dot_nt(jnp.concatenate([hidden, cp], axis=1), jnp.concatenate([fc, wc], axis=1))
        cols = slice(j * w, (j + 1) * w)
        for slot in range(n):
            to = from_ref[slot]
            d_ref[to, 0:t, cols] = dx[slot * t : (slot + 1) * t].astype(BF16)
            d_ref[to, t : 2 * t, cols] = dy[slot * t : (slot + 1) * t].astype(BF16)
        ab = dot_tn(x, jnp.concatenate([cg, cu], axis=1))
        grown = (ab[:, :w], ab[:, w:], dot_tn(y, cp))
        for m in range(3):
            total[base + 3 * j + m] = (ssum[3 * j + m] + grown[m]).astype(BF16)

    if last:
        for c, part in enumerate(before):
            at = 3 * plan.chunks[c][0]
            total[at : at + part.shape[0]] = part[...]
        for m in range(plan.mats, plan.n_dp * plan.own):
            total[m] = jnp.zeros((w, w), BF16)
        mine = lax.rem(dp_ref[0], plan.pair)
        for r in range(plan.rest):
            to = slice(r * plan.own, (r + 1) * plan.own)
            for ref, which in zip(c_refs, (mine, plan.pair - 1 - mine)):
                ref[to] = total[pl.ds((plan.pair * r + which) * plan.own, plan.own)]


def pair_kernel(dp_ref, keep_ref, got_ref, *refs, plan):
    outs, whole = refs[:-1], refs[-1]
    whole[...] = keep_ref[...].astype(F32) + got_ref[...].astype(F32)
    place = lax.div(dp_ref[0], plan.pair)
    for k in range(plan.rest):
        at = pl.ds(jnp.bitwise_xor(place, k) * plan.own, plan.own)
        outs[k][...] = whole[at].astype(BF16)


def sum_kernel(to_ref, *refs, plan):
    parts, outs, whole = refs[: plan.rest], refs[plan.rest : -1], refs[-1]
    added = parts[0][...].astype(F32)
    for part in parts[1:]:
        added = added + part[...].astype(F32)
    whole[...] = added / plan.n_dp
    for slot in range(plan.n):
        at = pl.ds(pl.multiple_of(to_ref[slot] * plan.rows, plan.rows), plan.rows)
        outs[slot][...] = whole[:, at, :].astype(BF16)


def order_kernel(place_ref, *refs, plan):
    parts, out = refs[:-1], refs[-1]
    for k, part in enumerate(parts):
        out[place_ref[k]] = part[...]


def state_kernel(dp_ref, *refs, plan):
    out = refs[-1]
    mine = lax.rem(dp_ref[0], plan.pair)
    for k in range(plan.pair):
        for r in range(plan.rest):
            for i in range(plan.own):
                mat = (plan.pair * r + jnp.bitwise_xor(mine, k)) * plan.own + i

                @pl.when(mat < plan.mats)
                def _(mat=mat, ref=refs[k], r=r, i=i):
                    for c in range(plan.n):
                        out[lax.rem(mat, 3), plan.first_head(c) + lax.div(mat, 3)] = ref[r, c, i].astype(F32)


def unpack_kernel(*refs, plan):
    t, w = plan.tokens, plan.width
    ins, (dk, dv, sems) = refs[:-3], refs[-3:]
    copies = []
    for c, (first, count) in enumerate(plan.chunks):
        for owner in range(plan.n):
            cols = pl.ds((plan.first_head(owner) + first) * w, count * w)
            for part, dst in enumerate((dk, dv)):
                copy = pltpu.make_async_copy(
                    ins[c].at[owner, pl.ds(part * t, t), :],
                    dst.at[0, :, cols],
                    sems.at[(c * plan.n + owner) * 2 + part],
                )
                copy.start()
                copies.append(copy)
            if plan.n * plan.per != plan.heads:
                for copy in copies:
                    copy.wait()
                copies = []
    for copy in copies:
        copy.wait()


def local(keys_a, values_a, queries_b, grad_out, state_start, state_next):
    n, n_dp = lax.axis_size("ctx"), lax.axis_size("dp")
    _, heads, rows, width = state_start.shape
    t = keys_a.shape[1]
    plan = Plan(n, n_dp, t, heads, rows, width)
    per, mats, own, chunks = plan.per, plan.mats, plan.own, plan.chunks
    bind = lambda kernel, **more: functools.partial(kernel, plan=plan, **more)

    keys_a, values_a, grad_out, state_start, state_next = (
        pltpu.with_memory_space_constraint(arg, pltpu.HBM)
        for arg in (keys_a, values_a, grad_out, state_start, state_next)
    )
    me = lax.axis_index("ctx")
    places = jnp.arange(n, dtype=jnp.int32)
    to_ids = lax.rem(me + places, n)
    from_ids = lax.rem(me + n - places, n)
    head_ids = jnp.minimum(to_ids * per, heads - per)
    dp_id = lax.axis_index("dp").reshape(1)
    rest_ids = jnp.bitwise_xor(lax.div(dp_id, plan.pair), jnp.arange(plan.rest, dtype=jnp.int32))

    def swap(value, k):
        if k == 0:
            return value
        return lax.ppermute(value, "dp", [(i, i ^ k) for i in range(n_dp)])

    def shift(values):
        return [
            lax.ppermute(v, "ctx", [(i, (i + s) % n) for i in range(n)]) if s else v
            for s, v in enumerate(values)
        ]

    def turn(value):
        return lax.all_to_all(value, "ctx", split_axis=0, concat_axis=0, tiled=True)

    def shape(*dims, dtype=BF16):
        return jax.ShapeDtypeStruct(dims, dtype)

    def pack_a(slot):
        return call(
            bind(pack_a_kernel, slot=slot),
            shape(2 * t + plan.share_rows, per * width),
            (head_ids, dp_id, keys_a, values_a, state_start),
            [SMEM] * 2 + [HBM] * 3,
            VMEM,
            f"pack_a{slot}",
            [
                pltpu.VMEM((plan.share, rows, width), F32),
                pltpu.SemaphoreType.DMA((2 + plan.share,)),
            ],
        )

    def pack_b(c, queries):
        dims = (2 * t + 3 * plan.block, chunks[c][1] * width)
        joined = c > 0
        outs = call(
            bind(pack_b_kernel, chunk=c),
            [shape(n, *dims)] if joined else [shape(*dims)] * n,
            (head_ids, pltpu.with_memory_space_constraint(queries, pltpu.HBM), grad_out, state_next),
            [SMEM] + [HBM] * 3,
            [VMEM] * (1 if joined else n),
            f"pack_b{c}",
            [
                pltpu.VMEM((n, 3, chunks[c][1], rows, width), F32),
                pltpu.SemaphoreType.DMA((3 * n,)),
            ],
        )
        return list(outs)

    a_sent = [pack_a(s) for s in [*range(1, n), 0]]
    a_sent = [a_sent[-1]] + a_sent[:-1]
    queries, a_sent[-1] = lax.optimization_barrier((queries_b, a_sent[-1]))
    a_in = shift(a_sent)
    b_in = [shift(pack_b(0, queries))]
    queries, a_in = lax.optimization_barrier((queries_b, a_in))
    b_in.append([turn(pack_b(1, queries)[0])])
    start_own = call(
        bind(start_kernel),
        shape(plan.share, width, width),
        (from_ids, *a_in),
        [SMEM] + [VMEM] * n,
        VMEM,
        "start_share",
        [pltpu.VMEM((plan.share, width, width), F32)],
    )
    shares = [swap(start_own, k) for k in range(plan.group)]
    d_sent = []
    sums = []
    for c, (_, count) in enumerate(chunks):
        last = c + 1 == len(chunks)
        if last:
            c_shapes = [shape(plan.rest * own, width, width)] * 2
        else:
            c_shapes = [shape(3 * count, width, width)]
        scratch = [
            pltpu.VMEM((plan.group * plan.share, width, width), BF16),
            pltpu.VMEM((3 * count, width, width), F32),
            pltpu.VMEM((3 * count, width, width), F32),
            pltpu.VMEM((3 * count, width, width), F32),
            pltpu.VMEM((count, 3, n * t, width), F32),
            pltpu.VMEM((count, 3, n * t, width), BF16),
        ]
        if last:
            scratch.append(pltpu.VMEM((n_dp * own, width, width), BF16))
        before = sums if last else []
        outs = call(
            bind(chunk_kernel, chunk=c),
            [shape(n, 2 * t, count * width)] + c_shapes,
            (from_ids, dp_id, *a_in, *shares, *b_in[c], *before),
            [SMEM] * 2 + [VMEM] * (n + plan.group + len(b_in[c]) + len(before)),
            [VMEM] * (1 + len(c_shapes)),
            f"chunk{c}",
            scratch,
            flops=count * 640 * 10**6,
            size=count * 10**6,
            vmem=VMEM_LARGE,
        )
        d_sent.append(outs[0])
        sums = outs[1:]
    c_keep, c_send = sums

    halves = call(
        bind(pair_kernel),
        [shape(own, width, width)] * plan.rest,
        (dp_id, c_keep, swap(c_send, plan.pair - 1)),
        [SMEM] + [VMEM] * 2,
        [VMEM] * plan.rest,
        "state_pair",
        [pltpu.VMEM((plan.rest * own, width, width), F32)],
    )
    halves = [swap(halves[k], plan.pair * k) for k in range(plan.rest)]
    by_rows = call(
        bind(sum_kernel),
        [shape(own, rows, width)] * n,
        (to_ids, *halves),
        [SMEM] + [VMEM] * plan.rest,
        [VMEM] * n,
        "state_sum",
        [pltpu.VMEM((own, width, width), F32)],
    )
    back = [turn(d_sent[0])]
    by_rows = shift(by_rows)
    by_rows[0], back[0] = lax.optimization_barrier((by_rows[0], back[0]))
    mine = call(
        bind(order_kernel),
        shape(n, own, rows, width),
        (from_ids, *by_rows),
        [SMEM] + [VMEM] * n,
        VMEM,
        "state_rows",
    )
    mine, late = lax.optimization_barrier((mine, d_sent[1]))
    back.append(turn(late))
    rest = [swap(mine, plan.pair * k) for k in range(plan.rest)]
    half = call(
        bind(order_kernel),
        shape(plan.rest, n, own, rows, width),
        (rest_ids, *rest),
        [SMEM] + [VMEM] * plan.rest,
        VMEM,
        "state_rest",
    )
    both = [swap(half, k) for k in range(plan.pair)]
    grad_state = call(
        bind(state_kernel),
        shape(*state_start.shape, dtype=F32),
        (dp_id, *both),
        [SMEM] + [VMEM] * plan.pair,
        VMEM,
        "state_out",
    )
    grad_keys, grad_values = call(
        bind(unpack_kernel),
        [shape(*keys_a.shape), shape(*values_a.shape)],
        back,
        [VMEM] * len(back),
        [ANY] * 2,
        "unpack",
        [pltpu.SemaphoreType.DMA((2 * n * len(chunks),))],
    )
    return grad_keys, grad_values, grad_state


def solution(mesh):
    placed = (
        P("dp", "ctx", None),
        P("dp", "ctx", None),
        P("dp", "ctx", None),
        P("dp", "ctx", None),
        P(None, None, "ctx", None),
        P("dp", None, None, "ctx", None),
    )
    return jax.shard_map(
        local,
        mesh=mesh,
        in_specs=placed,
        out_specs=(P("dp", "ctx", None), P("dp", "ctx", None), P(None, None, "ctx", None)),
        check_vma=False,
    )
```

profile of v0, /device:TPU:0, one launch (start us, length us, event | category | flops | bytes accessed | tf_op | source)
XLA Modules:
  0.0 143.9 jit_solution(6252388724517894763)
XLA Ops:
  0.7 1.7 %pack_a3.1 = bf16[288,640]{1,0:T(8,128)(2,1)S(1)} custom-call(s32[4]{0:T(128)S(1)} %multiply_minimum_fusion.head_ref, s32[1]{0:T(128)} %bitcast.dp_ref, bf16[1,128,2560]{2,1,0:T(8,128)(2,1)} %k_ref.7, bf16[1,128,2560]{2,1,0:T(8,128)(2,1)} %v_ref.7, f32[3,20,32,128]{3,2,1,0:T(8,128)} %s_ref.9), custom_call_target="tpu_custom_call" | custom-call | flops 1000000 | bytes 1000000 | tf_op jit(solution)/shard_map/pack_a3/pallas_call | solution.py:40
  2.3 5.1 %collective-permute-start.2 = (bf16[288,640]{1,0:T(8,128)(2,1)S(1)}, bf16[288,640]{1,0:T(8,128)(2,1)S(1)}, u32[]{:S(2)}, u32[]{:S(2)}) collective-permute-start(bf16[288,640]{1,0:T(8,128)(2,1)S(1)} %pack_a3.1), channel_id=1, source_target_pairs={{0,3},{1,0},{2,1},{3,2},{4,7},{5,4},{6,5},{7,6},{8,11},{9,8},{10,9... | collective-permute-start | bytes 1105928 | tf_op jit(solution)/shard_map/ppermute | solution.py:400
  7.4 1.7 %pack_a1.1 = bf16[288,640]{1,0:T(8,128)(2,1)S(1)} custom-call(s32[4]{0:T(128)S(1)} %multiply_minimum_fusion.head_ref, s32[1]{0:T(128)} %bitcast.dp_ref, bf16[1,128,2560]{2,1,0:T(8,128)(2,1)} %k_ref.7, bf16[1,128,2560]{2,1,0:T(8,128)(2,1)} %v_ref.7, f32[3,20,32,128]{3,2,1,0:T(8,128)} %s_ref.9), custom_call_target="tpu_custom_call" | custom-call | flops 1000000 | bytes 1000000 | tf_op jit(solution)/shard_map/pack_a1/pallas_call | solution.py:40
  9.2 1.7 %pack_a2.1 = bf16[288,640]{1,0:T(8,128)(2,1)S(1)} custom-call(s32[4]{0:T(128)S(1)} %multiply_minimum_fusion.head_ref, s32[1]{0:T(128)} %bitcast.dp_ref, bf16[1,128,2560]{2,1,0:T(8,128)(2,1)} %k_ref.7, bf16[1,128,2560]{2,1,0:T(8,128)(2,1)} %v_ref.7, f32[3,20,32,128]{3,2,1,0:T(8,128)} %s_ref.9), custom_call_target="tpu_custom_call" | custom-call | flops 1000000 | bytes 1000000 | tf_op jit(solution)/shard_map/pack_a2/pallas_call | solution.py:40
  10.9 1.1 collective-permute-start.1
  11.9 1.7 %pack_a0.1.refs_0_ = bf16[288,640]{1,0:T(8,128)(2,1)S(1)} custom-call(s32[4]{0:T(128)S(1)} %multiply_minimum_fusion.head_ref, s32[1]{0:T(128)} %bitcast.dp_ref, bf16[1,128,2560]{2,1,0:T(8,128)(2,1)} %k_ref.7, bf16[1,128,2560]{2,1,0:T(8,128)(2,1)} %v_ref.7, f32[3,20,32,128]{3,2,1,0:T(8,128)} %s_ref.9), custom_call_target="tpu_custom_call" | custom-call | flops 1000000 | bytes 1000000 | tf_op jit(solution)/shard_map/pack_a0/pallas_call | solution.py:40
  13.6 2.9 %collective-permute-done.2.refs_3_ = bf16[288,640]{1,0:T(8,128)(2,1)S(1)} collective-permute-done((bf16[288,640]{1,0:T(8,128)(2,1)S(1)}, bf16[288,640]{1,0:T(8,128)(2,1)S(1)}, u32[]{:S(2)}, u32[]{:S(2)}) %collective-permute-start.2) | collective-permute-done | bytes 368672 | tf_op jit(solution)/shard_map/ppermute | solution.py:400
  16.5 8.9 %collective-permute-done.refs_1_ = bf16[288,640]{1,0:T(8,128)(2,1)S(1)} collective-permute-done((bf16[288,640]{1,0:T(8,128)(2,1)S(1)}, bf16[288,640]{1,0:T(8,128)(2,1)S(1)}, u32[]{:S(2)}, u32[]{:S(2)}) %collective-permute-start) | collective-permute-done | bytes 368672 | tf_op jit(solution)/shard_map/ppermute | solution.py:400
  25.3 13.5 %collective-permute-done.1.refs_2_ = bf16[288,640]{1,0:T(8,128)(2,1)S(1)} collective-permute-done((bf16[288,640]{1,0:T(8,128)(2,1)S(1)}, bf16[288,640]{1,0:T(8,128)(2,1)S(1)}, u32[]{:S(2)}, u32[]{:S(2)}) %collective-permute-start.1) | collective-permute-done | bytes 368672 | tf_op jit(solution)/shard_map/ppermute | solution.py:400
  38.9 2.8 %pack_b1.1 = bf16[4,352,256]{2,1,0:T(8,128)(2,1)} custom-call(s32[4]{0:T(128)S(1)} %multiply_minimum_fusion.head_ref, bf16[1,128,2560]{2,1,0:T(8,128)(2,1)} %q_ref.1, bf16[1,128,2560]{2,1,0:T(8,128)(2,1)} %o_ref.3, f32[1,3,20,32,128]{4,3,2,1,0:T(8,128)} %s_ref.11), custom_call_target="tpu_custom_call" | custom-call | flops 1000000 | bytes 1000000 | tf_op jit(solution)/shard_map/pack_b1/pallas_call | solution.py:40
  41.6 5.7 %all-to-all-start = ((bf16[4,352,256]{2,1,0:T(8,128)(2,1)}), bf16[4,352,256]{2,1,0:T(8,128)(2,1)S(1)}, u32[]{:S(2)}, u32[]{:S(2)}) async-start(bf16[4,352,256]{2,1,0:T(8,128)(2,1)} %pack_b1.1), calls=%async_computation | async-start | bytes 1441792 | tf_op jit(solution)/shard_map/all_to_all | solution.py:405
  47.3 2.9 %pack_b0.1 = (bf16[352,384]{1,0:T(8,128)(2,1)S(1)}, bf16[352,384]{1,0:T(8,128)(2,1)}, bf16[352,384]{1,0:T(8,128)(2,1)}, bf16[352,384]{1,0:T(8,128)(2,1)}) custom-call(s32[4]{0:T(128)S(1)} %multiply_minimum_fusion.head_ref, bf16[1,128,2560]{2,1,0:T(8,128)(2,1)} %q_ref.1, bf16[1,128,2560]{2,1,0:T(8,128)(2,1)} %o_ref.3, f32[1,3,20,32,128]{4,3,2,1,0:T(8,128)} %s_ref.11), custom_call_target="tpu_custom_call" | custom-call | flops 1000000 | bytes 1000000 | tf_op jit(solution)/shard_map/pack_b0/pallas_call | solution.py:40
  50.2 2.1 %collective-permute-start.6 = (bf16[352,384]{1,0:T(8,128)(2,1)}, bf16[352,384]{1,0:T(8,128)(2,1)S(1)}, u32[]{:S(2)}, u32[]{:S(2)}) collective-permute-start(bf16[352,384]{1,0:T(8,128)(2,1)} %get-tuple-element.41), channel_id=1, source_target_pairs={{0,1},{1,2},{2,3},{3,0},{4,5},{5,6},{6,7},{7,4},{8,9},{9,10},{10,1... | collective-permute-start | bytes 811016 | tf_op jit(solution)/shard_map/ppermute | solution.py:400
  52.3 2.4 %collective-permute-start.7 = (bf16[352,384]{1,0:T(8,128)(2,1)}, bf16[352,384]{1,0:T(8,128)(2,1)S(1)}, u32[]{:S(2)}, u32[]{:S(2)}) collective-permute-start(bf16[352,384]{1,0:T(8,128)(2,1)} %get-tuple-element.42), channel_id=1, source_target_pairs={{0,2},{1,3},{2,0},{3,1},{4,6},{5,7},{6,4},{7,5},{8,10},{9,11},{10,... | collective-permute-start | bytes 811016 | tf_op jit(solution)/shard_map/ppermute | solution.py:400
  54.7 1.5 %collective-permute-start.8 = (bf16[352,384]{1,0:T(8,128)(2,1)}, bf16[352,384]{1,0:T(8,128)(2,1)}, u32[]{:S(2)}, u32[]{:S(2)}) collective-permute-start(bf16[352,384]{1,0:T(8,128)(2,1)} %get-tuple-element.43), channel_id=1, source_target_pairs={{0,3},{1,0},{2,1},{3,2},{4,7},{5,4},{6,5},{7,6},{8,11},{9,8},{10,9... | collective-permute-start | bytes 811016 | tf_op jit(solution)/shard_map/ppermute | solution.py:400
  56.1 0.6 start_share.1.refs_4_
  56.8 1.6 %collective-permute-start.4 = (bf16[4,128,128]{2,1,0:T(8,128)(2,1)S(1)}, bf16[4,128,128]{2,1,0:T(8,128)(2,1)S(1)}, u32[]{:S(2)}, u32[]{:S(2)}) collective-permute-start(bf16[4,128,128]{2,1,0:T(8,128)(2,1)S(1)} %start_share.1.refs_4_), channel_id=1, source_target_pairs={{0,8},{4,12},{8,0},{12,4},{16,24},{20,28},{24,16},{28,20},{1,9},{5... | collective-permute-start | bytes 393224 | tf_op jit(solution)/shard_map/ppermute | solution.py:396
  58.4 12.1 %collective-permute-done.6.refs_9_ = bf16[352,384]{1,0:T(8,128)(2,1)S(1)} collective-permute-done((bf16[352,384]{1,0:T(8,128)(2,1)}, bf16[352,384]{1,0:T(8,128)(2,1)S(1)}, u32[]{:S(2)}, u32[]{:S(2)}) %collective-permute-start.6) | collective-permute-done | bytes 270368 | tf_op jit(solution)/shard_map/ppermute | solution.py:400
  70.4 14.1 %collective-permute-done.7.refs_10_ = bf16[352,384]{1,0:T(8,128)(2,1)S(1)} collective-permute-done((bf16[352,384]{1,0:T(8,128)(2,1)}, bf16[352,384]{1,0:T(8,128)(2,1)S(1)}, u32[]{:S(2)}, u32[]{:S(2)}) %collective-permute-start.7) | collective-permute-done | bytes 270368 | tf_op jit(solution)/shard_map/ppermute | solution.py:400
  84.6 7.5 %chunk0.1 = (bf16[4,256,384]{2,1,0:T(8,128)(2,1)}, bf16[9,128,128]{2,1,0:T(8,128)(2,1)S(1)}) custom-call(s32[4]{0:T(128)S(1)} %compare_select_fusion.from_ref.place_ref, s32[1]{0:T(128)} %bitcast.dp_ref, bf16[288,640]{1,0:T(8,128)(2,1)S(1)} %pack_a0.1.refs_0_, bf16[288,640]{1,0:T(8,128)(2,1)S(1)} %collective-permute-done.refs_1_, ...), custom_call_target="tpu_custom_call" | custom-call | flops 1920000000 | bytes 3000000 | tf_op jit(solution)/shard_map/chunk0/pallas_call | solution.py:40
  92.1 0.7 copy-done.2
  92.7 0.7 copy-done.4
  93.5 7.9 %all-to-all-start.1 = ((bf16[4,256,384]{2,1,0:T(8,128)(2,1)}), bf16[4,256,384]{2,1,0:T(8,128)(2,1)S(1)}, u32[]{:S(2)}, u32[]{:S(2)}) async-start(bf16[4,256,384]{2,1,0:T(8,128)(2,1)} %get-tuple-element.52), calls=%async_computation.1 | async-start | bytes 1572864 | tf_op jit(solution)/shard_map/all_to_all | solution.py:405
  101.4 1.0 copy-done.5
  102.4 5.6 %chunk1.1 = (bf16[4,256,256]{2,1,0:T(8,128)(2,1)}, bf16[8,128,128]{2,1,0:T(8,128)(2,1)S(1)}, bf16[8,128,128]{2,1,0:T(8,128)(2,1)S(1)}) custom-call(s32[4]{0:T(128)S(1)} %compare_select_fusion.from_ref.place_ref, s32[1]{0:T(128)} %bitcast.dp_ref, bf16[288,640]{1,0:T(8,128)(2,1)S(1)} %pack_a0.1.refs_0_, bf16[288,640]{1,0:T(8,128)(2,1)S(1)} %collective-permute-done.refs_1_, ...), custom_call_target="tpu_custom_call" | custom-call | flops 1280000000 | bytes 2000000 | tf_op jit(solution)/shard_map/chunk1/pallas_call | solution.py:40
  107.9 1.5 %collective-permute-done.9.got_ref = bf16[8,128,128]{2,1,0:T(8,128)(2,1)S(1)} collective-permute-done((bf16[8,128,128]{2,1,0:T(8,128)(2,1)S(1)}, bf16[8,128,128]{2,1,0:T(8,128)(2,1)S(1)}, u32[]{:S(2)}, u32[]{:S(2)}) %collective-permute-start.9) | collective-permute-done | bytes 262176 | tf_op jit(solution)/shard_map/ppermute | solution.py:396
  109.6 1.2 collective-permute-start.10
  110.8 1.5 %collective-permute-start.11 = (bf16[2,128,128]{2,1,0:T(8,128)(2,1)S(1)}, bf16[2,128,128]{2,1,0:T(8,128)(2,1)S(1)}, u32[]{:S(2)}, u32[]{:S(2)}) collective-permute-start(bf16[2,128,128]{2,1,0:T(8,128)(2,1)S(1)} %get-tuple-element.49), channel_id=1, source_target_pairs={{0,16},{4,20},{8,24},{12,28},{16,0},{20,4},{24,8},{28,12},{1,17},{... | collective-permute-start | bytes 196616 | tf_op jit(solution)/shard_map/ppermute | solution.py:396
  112.4 0.8 collective-permute-start.12
  113.1 0.8 collective-permute-done.10.refs_1_
  113.9 1.2 collective-permute-done.11.refs_2_
  115.1 2.4 %collective-permute-done.12.refs_3_ = bf16[2,128,128]{2,1,0:T(8,128)(2,1)S(1)} collective-permute-done((bf16[2,128,128]{2,1,0:T(8,128)(2,1)S(1)}, bf16[2,128,128]{2,1,0:T(8,128)(2,1)S(1)}, u32[]{:S(2)}, u32[]{:S(2)}) %collective-permute-start.12) | collective-permute-done | bytes 65568 | tf_op jit(solution)/shard_map/ppermute | solution.py:396
  117.5 0.6 state_sum.1
  118.1 2.1 %collective-permute-start.13 = (bf16[2,32,128]{2,1,0:T(8,128)(2,1)S(1)}, bf16[2,32,128]{2,1,0:T(8,128)(2,1)S(1)}, u32[]{:S(2)}, u32[]{:S(2)}) collective-permute-start(bf16[2,32,128]{2,1,0:T(8,128)(2,1)S(1)} %get-tuple-element.55), channel_id=1, source_target_pairs={{0,1},{1,2},{2,3},{3,0},{4,5},{5,6},{6,7},{7,4},{8,9},{9,10},{10,1... | collective-permute-start | bytes 49160 | tf_op jit(solution)/shard_map/ppermute | solution.py:400
  120.2 2.4 %collective-permute-start.14 = (bf16[2,32,128]{2,1,0:T(8,128)(2,1)S(1)}, bf16[2,32,128]{2,1,0:T(8,128)(2,1)S(1)}, u32[]{:S(2)}, u32[]{:S(2)}) collective-permute-start(bf16[2,32,128]{2,1,0:T(8,128)(2,1)S(1)} %get-tuple-element.56), channel_id=1, source_target_pairs={{0,2},{1,3},{2,0},{3,1},{4,6},{5,7},{6,4},{7,5},{8,10},{9,11},{10,... | collective-permute-start | bytes 49160 | tf_op jit(solution)/shard_map/ppermute | solution.py:400
  122.6 1.5 %collective-permute-start.15 = (bf16[2,32,128]{2,1,0:T(8,128)(2,1)S(1)}, bf16[2,32,128]{2,1,0:T(8,128)(2,1)S(1)}, u32[]{:S(2)}, u32[]{:S(2)}) collective-permute-start(bf16[2,32,128]{2,1,0:T(8,128)(2,1)S(1)} %get-tuple-element.57), channel_id=1, source_target_pairs={{0,3},{1,0},{2,1},{3,2},{4,7},{5,4},{6,5},{7,6},{8,11},{9,8},{10,9... | collective-permute-start | bytes 49160 | tf_op jit(solution)/shard_map/ppermute | solution.py:400
  124.0 0.8 collective-permute-done.14.refs_2_
  124.8 1.5 %collective-permute-done.15.refs_3_ = bf16[2,32,128]{2,1,0:T(8,128)(2,1)S(1)} collective-permute-done((bf16[2,32,128]{2,1,0:T(8,128)(2,1)S(1)}, bf16[2,32,128]{2,1,0:T(8,128)(2,1)S(1)}, u32[]{:S(2)}, u32[]{:S(2)}) %collective-permute-start.15) | collective-permute-done | bytes 16416 | tf_op jit(solution)/shard_map/ppermute | solution.py:400
  126.9 4.5 %all-to-all-start.2 = ((bf16[4,256,256]{2,1,0:T(8,128)(2,1)}), bf16[4,256,256]{2,1,0:T(8,128)(2,1)S(1)}, u32[]{:S(2)}, u32[]{:S(2)}) async-start(bf16[4,256,256]{2,1,0:T(8,128)(2,1)} %get-tuple-element.59), calls=%async_computation.2 | async-start | bytes 1048576 | tf_op jit(solution)/shard_map/all_to_all | solution.py:405
  131.4 0.8 collective-permute-start.16
  132.7 2.1 %collective-permute-start.18 = (bf16[4,2,32,128]{3,2,1,0:T(8,128)(2,1)S(1)}, bf16[4,2,32,128]{3,2,1,0:T(8,128)(2,1)S(1)}, u32[]{:S(2)}, u32[]{:S(2)}) collective-permute-start(bf16[4,2,32,128]{3,2,1,0:T(8,128)(2,1)S(1)} %state_rows.1.refs_0_), channel_id=1, source_target_pairs={{0,24},{4,28},{8,16},{12,20},{16,8},{20,12},{24,0},{28,4},{1,25},{... | collective-permute-start | bytes 196616 | tf_op jit(solution)/shard_map/ppermute | solution.py:396
  134.9 0.8 collective-permute-done.16.refs_1_
  135.7 0.8 collective-permute-done.17.refs_2_
  136.5 1.4 collective-permute-done.18.refs_3_
  138.6 1.5 %collective-permute-done.19.refs_1_ = bf16[4,4,2,32,128]{4,3,2,1,0:T(8,128)(2,1)S(1)} collective-permute-done((bf16[4,4,2,32,128]{4,3,2,1,0:T(8,128)(2,1)S(1)}, bf16[4,4,2,32,128]{4,3,2,1,0:T(8,128)(2,1)S(1)}, u32[]{:S(2)}, u32[]{:S(2)}) %collective-permute-start.19) | collective-permute-done | bytes 262176 | tf_op jit(solution)/shard_map/ppermute | solution.py:396
  140.1 1.1 state_out.1
  141.2 1.6 %all-to-all-done.2.refs_1_ = bf16[4,256,256]{2,1,0:T(8,128)(2,1)S(1)} async-done(((bf16[4,256,256]{2,1,0:T(8,128)(2,1)}), bf16[4,256,256]{2,1,0:T(8,128)(2,1)S(1)}, u32[]{:S(2)}, u32[]{:S(2)}) %all-to-all-start.2) | async-done | bytes 524320 | tf_op jit(solution)/shard_map/all_to_all | solution.py:405
  142.8 1.2 unpack.1
  (29 shorter events, 2.0 us)
Async XLA Ops:
  2.3 14.1 %collective-permute-start.2 = (bf16[288,640]{1,0:T(8,128)(2,1)S(1)}, bf16[288,640]{1,0:T(8,128)(2,1)S(1)}, u32[]{:S(2)}, u32[]{:S(2)}) collective-permute-start(bf16[288,640]{1,0:T(8,128)(2,1)S(1)} %pack_a3.1), channel_id=1, source_target_pairs={{0,3},{1,0},{2,1},{3,2},{4,7},{5,4},{6,5},{7,6},{8,11},{9,8},{10,9... | collective-permute-start | bytes 1105928 | tf_op jit(solution)/shard_map/ppermute | solution.py:400
  9.1 16.2 %collective-permute-start = (bf16[288,640]{1,0:T(8,128)(2,1)S(1)}, bf16[288,640]{1,0:T(8,128)(2,1)S(1)}, u32[]{:S(2)}, u32[]{:S(2)}) collective-permute-start(bf16[288,640]{1,0:T(8,128)(2,1)S(1)} %pack_a1.1), channel_id=1, source_target_pairs={{0,1},{1,2},{2,3},{3,0},{4,5},{5,6},{6,7},{7,4},{8,9},{9,10},{10,1... | collective-permute-start | bytes 1105928 | tf_op jit(solution)/shard_map/ppermute | solution.py:400
  10.9 28.0 %collective-permute-start.1 = (bf16[288,640]{1,0:T(8,128)(2,1)S(1)}, bf16[288,640]{1,0:T(8,128)(2,1)S(1)}, u32[]{:S(2)}, u32[]{:S(2)}) collective-permute-start(bf16[288,640]{1,0:T(8,128)(2,1)S(1)} %pack_a2.1), channel_id=1, source_target_pairs={{0,2},{1,3},{2,0},{3,1},{4,6},{5,7},{6,4},{7,5},{8,10},{9,11},{10,... | collective-permute-start | bytes 1105928 | tf_op jit(solution)/shard_map/ppermute | solution.py:400
  41.6 51.8 %all-to-all-start = ((bf16[4,352,256]{2,1,0:T(8,128)(2,1)}), bf16[4,352,256]{2,1,0:T(8,128)(2,1)S(1)}, u32[]{:S(2)}, u32[]{:S(2)}) async-start(bf16[4,352,256]{2,1,0:T(8,128)(2,1)} %pack_b1.1), calls=%async_computation | async-start | bytes 1441792 | tf_op jit(solution)/shard_map/all_to_all | solution.py:405
  50.2 20.2 %collective-permute-start.6 = (bf16[352,384]{1,0:T(8,128)(2,1)}, bf16[352,384]{1,0:T(8,128)(2,1)S(1)}, u32[]{:S(2)}, u32[]{:S(2)}) collective-permute-start(bf16[352,384]{1,0:T(8,128)(2,1)} %get-tuple-element.41), channel_id=1, source_target_pairs={{0,1},{1,2},{2,3},{3,0},{4,5},{5,6},{6,7},{7,4},{8,9},{9,10},{10,1... | collective-permute-start | bytes 811016 | tf_op jit(solution)/shard_map/ppermute | solution.py:400
  52.3 32.3 %collective-permute-start.7 = (bf16[352,384]{1,0:T(8,128)(2,1)}, bf16[352,384]{1,0:T(8,128)(2,1)S(1)}, u32[]{:S(2)}, u32[]{:S(2)}) collective-permute-start(bf16[352,384]{1,0:T(8,128)(2,1)} %get-tuple-element.42), channel_id=1, source_target_pairs={{0,2},{1,3},{2,0},{3,1},{4,6},{5,7},{6,4},{7,5},{8,10},{9,11},{10,... | collective-permute-start | bytes 811016 | tf_op jit(solution)/shard_map/ppermute | solution.py:400
  54.7 29.9 %collective-permute-start.8 = (bf16[352,384]{1,0:T(8,128)(2,1)}, bf16[352,384]{1,0:T(8,128)(2,1)}, u32[]{:S(2)}, u32[]{:S(2)}) collective-permute-start(bf16[352,384]{1,0:T(8,128)(2,1)} %get-tuple-element.43), channel_id=1, source_target_pairs={{0,3},{1,0},{2,1},{3,2},{4,7},{5,4},{6,5},{7,6},{8,11},{9,8},{10,9... | collective-permute-start | bytes 811016 | tf_op jit(solution)/shard_map/ppermute | solution.py:400
  56.7 27.8 %collective-permute-start.3 = (bf16[4,128,128]{2,1,0:T(8,128)(2,1)S(1)}, bf16[4,128,128]{2,1,0:T(8,128)(2,1)S(1)}, u32[]{:S(2)}, u32[]{:S(2)}) collective-permute-start(bf16[4,128,128]{2,1,0:T(8,128)(2,1)S(1)} %start_share.1.refs_4_), channel_id=1, source_target_pairs={{0,4},{4,0},{8,12},{12,8},{16,20},{20,16},{24,28},{28,24},{1,5},{5... | collective-permute-start | bytes 393224 | tf_op jit(solution)/shard_map/ppermute | solution.py:396
  56.8 27.8 %collective-permute-start.4 = (bf16[4,128,128]{2,1,0:T(8,128)(2,1)S(1)}, bf16[4,128,128]{2,1,0:T(8,128)(2,1)S(1)}, u32[]{:S(2)}, u32[]{:S(2)}) collective-permute-start(bf16[4,128,128]{2,1,0:T(8,128)(2,1)S(1)} %start_share.1.refs_4_), channel_id=1, source_target_pairs={{0,8},{4,12},{8,0},{12,4},{16,24},{20,28},{24,16},{28,20},{1,9},{5... | collective-permute-start | bytes 393224 | tf_op jit(solution)/shard_map/ppermute | solution.py:396
  70.4 14.2 %collective-permute-start.5 = (bf16[4,128,128]{2,1,0:T(8,128)(2,1)S(1)}, bf16[4,128,128]{2,1,0:T(8,128)(2,1)S(1)}, u32[]{:S(2)}, u32[]{:S(2)}) collective-permute-start(bf16[4,128,128]{2,1,0:T(8,128)(2,1)S(1)} %start_share.1.refs_4_), channel_id=1, source_target_pairs={{0,12},{4,8},{8,4},{12,0},{16,28},{20,24},{24,20},{28,16},{1,13},{... | collective-permute-start | bytes 393224 | tf_op jit(solution)/shard_map/ppermute | solution.py:396
  84.6 7.5 %copy-start = (bf16[4,128,128]{2,1,0:T(8,128)(2,1)}, bf16[4,128,128]{2,1,0:T(8,128)(2,1)S(1)}, u32[]{:S(2)}) copy-start(bf16[4,128,128]{2,1,0:T(8,128)(2,1)S(1)} %collective-permute-done.4.refs_6_) | copy-start | bytes 393220
  92.1 0.7 copy-start.2
  92.7 0.7 copy-start.4
  93.5 7.9 %copy-start.1 = (bf16[4,128,128]{2,1,0:T(8,128)(2,1)S(1)}, bf16[4,128,128]{2,1,0:T(8,128)(2,1)}, u32[]{:S(2)}) copy-start(bf16[4,128,128]{2,1,0:T(8,128)(2,1)} %copy-done) | copy-start | bytes 393220
  93.5 7.9 %copy-start.3 = (bf16[4,128,128]{2,1,0:T(8,128)(2,1)S(1)}, bf16[4,128,128]{2,1,0:T(8,128)(2,1)}, u32[]{:S(2)}) copy-start(bf16[4,128,128]{2,1,0:T(8,128)(2,1)} %copy-done.2) | copy-start | bytes 393220
  93.5 30.6 %all-to-all-start.1 = ((bf16[4,256,384]{2,1,0:T(8,128)(2,1)}), bf16[4,256,384]{2,1,0:T(8,128)(2,1)S(1)}, u32[]{:S(2)}, u32[]{:S(2)}) async-start(bf16[4,256,384]{2,1,0:T(8,128)(2,1)} %get-tuple-element.52), calls=%async_computation.1 | async-start | bytes 1572864 | tf_op jit(solution)/shard_map/all_to_all | solution.py:405
  101.4 1.0 copy-start.5
  107.9 1.5 %collective-permute-start.9 = (bf16[8,128,128]{2,1,0:T(8,128)(2,1)S(1)}, bf16[8,128,128]{2,1,0:T(8,128)(2,1)S(1)}, u32[]{:S(2)}, u32[]{:S(2)}) collective-permute-start(bf16[8,128,128]{2,1,0:T(8,128)(2,1)S(1)} %get-tuple-element.46), channel_id=1, source_target_pairs={{0,4},{4,0},{8,12},{12,8},{16,20},{20,16},{24,28},{28,24},{1,5},{5... | collective-permute-start | bytes 786440 | tf_op jit(solution)/shard_map/ppermute | solution.py:396
  109.6 4.3 %collective-permute-start.10 = (bf16[2,128,128]{2,1,0:T(8,128)(2,1)S(1)}, bf16[2,128,128]{2,1,0:T(8,128)(2,1)S(1)}, u32[]{:S(2)}, u32[]{:S(2)}) collective-permute-start(bf16[2,128,128]{2,1,0:T(8,128)(2,1)S(1)} %get-tuple-element.48), channel_id=1, source_target_pairs={{0,8},{4,12},{8,0},{12,4},{16,24},{20,28},{24,16},{28,20},{1,9},{5... | collective-permute-start | bytes 196616 | tf_op jit(solution)/shard_map/ppermute | solution.py:396
  110.8 4.3 %collective-permute-start.11 = (bf16[2,128,128]{2,1,0:T(8,128)(2,1)S(1)}, bf16[2,128,128]{2,1,0:T(8,128)(2,1)S(1)}, u32[]{:S(2)}, u32[]{:S(2)}) collective-permute-start(bf16[2,128,128]{2,1,0:T(8,128)(2,1)S(1)} %get-tuple-element.49), channel_id=1, source_target_pairs={{0,16},{4,20},{8,24},{12,28},{16,0},{20,4},{24,8},{28,12},{1,17},{... | collective-permute-start | bytes 196616 | tf_op jit(solution)/shard_map/ppermute | solution.py:396
  112.4 5.2 %collective-permute-start.12 = (bf16[2,128,128]{2,1,0:T(8,128)(2,1)S(1)}, bf16[2,128,128]{2,1,0:T(8,128)(2,1)S(1)}, u32[]{:S(2)}, u32[]{:S(2)}) collective-permute-start(bf16[2,128,128]{2,1,0:T(8,128)(2,1)S(1)} %get-tuple-element.50), channel_id=1, source_target_pairs={{0,24},{4,28},{8,16},{12,20},{16,8},{20,12},{24,0},{28,4},{1,25},{... | collective-permute-start | bytes 196616 | tf_op jit(solution)/shard_map/ppermute | solution.py:396
  118.1 5.9 %collective-permute-start.13 = (bf16[2,32,128]{2,1,0:T(8,128)(2,1)S(1)}, bf16[2,32,128]{2,1,0:T(8,128)(2,1)S(1)}, u32[]{:S(2)}, u32[]{:S(2)}) collective-permute-start(bf16[2,32,128]{2,1,0:T(8,128)(2,1)S(1)} %get-tuple-element.55), channel_id=1, source_target_pairs={{0,1},{1,2},{2,3},{3,0},{4,5},{5,6},{6,7},{7,4},{8,9},{9,10},{10,1... | collective-permute-start | bytes 49160 | tf_op jit(solution)/shard_map/ppermute | solution.py:400
  120.2 4.6 %collective-permute-start.14 = (bf16[2,32,128]{2,1,0:T(8,128)(2,1)S(1)}, bf16[2,32,128]{2,1,0:T(8,128)(2,1)S(1)}, u32[]{:S(2)}, u32[]{:S(2)}) collective-permute-start(bf16[2,32,128]{2,1,0:T(8,128)(2,1)S(1)} %get-tuple-element.56), channel_id=1, source_target_pairs={{0,2},{1,3},{2,0},{3,1},{4,6},{5,7},{6,4},{7,5},{8,10},{9,11},{10,... | collective-permute-start | bytes 49160 | tf_op jit(solution)/shard_map/ppermute | solution.py:400
  122.6 3.7 %collective-permute-start.15 = (bf16[2,32,128]{2,1,0:T(8,128)(2,1)S(1)}, bf16[2,32,128]{2,1,0:T(8,128)(2,1)S(1)}, u32[]{:S(2)}, u32[]{:S(2)}) collective-permute-start(bf16[2,32,128]{2,1,0:T(8,128)(2,1)S(1)} %get-tuple-element.57), channel_id=1, source_target_pairs={{0,3},{1,0},{2,1},{3,2},{4,7},{5,4},{6,5},{7,6},{8,11},{9,8},{10,9... | collective-permute-start | bytes 49160 | tf_op jit(solution)/shard_map/ppermute | solution.py:400
  126.9 15.9 %all-to-all-start.2 = ((bf16[4,256,256]{2,1,0:T(8,128)(2,1)}), bf16[4,256,256]{2,1,0:T(8,128)(2,1)S(1)}, u32[]{:S(2)}, u32[]{:S(2)}) async-start(bf16[4,256,256]{2,1,0:T(8,128)(2,1)} %get-tuple-element.59), calls=%async_computation.2 | async-start | bytes 1048576 | tf_op jit(solution)/shard_map/all_to_all | solution.py:405
  131.4 4.3 %collective-permute-start.16 = (bf16[4,2,32,128]{3,2,1,0:T(8,128)(2,1)S(1)}, bf16[4,2,32,128]{3,2,1,0:T(8,128)(2,1)S(1)}, u32[]{:S(2)}, u32[]{:S(2)}) collective-permute-start(bf16[4,2,32,128]{3,2,1,0:T(8,128)(2,1)S(1)} %state_rows.1.refs_0_), channel_id=1, source_target_pairs={{0,8},{4,12},{8,0},{12,4},{16,24},{20,28},{24,16},{28,20},{1,9},{5... | collective-permute-start | bytes 196616 | tf_op jit(solution)/shard_map/ppermute | solution.py:396
  132.2 4.3 %collective-permute-start.17 = (bf16[4,2,32,128]{3,2,1,0:T(8,128)(2,1)S(1)}, bf16[4,2,32,128]{3,2,1,0:T(8,128)(2,1)S(1)}, u32[]{:S(2)}, u32[]{:S(2)}) collective-permute-start(bf16[4,2,32,128]{3,2,1,0:T(8,128)(2,1)S(1)} %state_rows.1.refs_0_), channel_id=1, source_target_pairs={{0,16},{4,20},{8,24},{12,28},{16,0},{20,4},{24,8},{28,12},{1,17},{... | collective-permute-start | bytes 196616 | tf_op jit(solution)/shard_map/ppermute | solution.py:396
  132.7 5.2 %collective-permute-start.18 = (bf16[4,2,32,128]{3,2,1,0:T(8,128)(2,1)S(1)}, bf16[4,2,32,128]{3,2,1,0:T(8,128)(2,1)S(1)}, u32[]{:S(2)}, u32[]{:S(2)}) collective-permute-start(bf16[4,2,32,128]{3,2,1,0:T(8,128)(2,1)S(1)} %state_rows.1.refs_0_), channel_id=1, source_target_pairs={{0,24},{4,28},{8,16},{12,20},{16,8},{20,12},{24,0},{28,4},{1,25},{... | collective-permute-start | bytes 196616 | tf_op jit(solution)/shard_map/ppermute | solution.py:396
  138.5 1.6 %collective-permute-start.19 = (bf16[4,4,2,32,128]{4,3,2,1,0:T(8,128)(2,1)S(1)}, bf16[4,4,2,32,128]{4,3,2,1,0:T(8,128)(2,1)S(1)}, u32[]{:S(2)}, u32[]{:S(2)}) collective-permute-start(bf16[4,4,2,32,128]{4,3,2,1,0:T(8,128)(2,1)S(1)} %state_rest.1.refs_0_), channel_id=1, source_target_pairs={{0,4},{4,0},{8,12},{12,8},{16,20},{20,16},{24,28},{28,24},{1,5},{5... | collective-permute-start | bytes 786440 | tf_op jit(solution)/shard_map/ppermute | solution.py:396
where the time goes:
time: 145 us; the launch traced here: 144 us
  waiting for transfers between devices  65.8 us (45%)
  starting transfers between devices  44.9 us (31%)
  Pallas kernels  30.1 us (21%)
  local copies, waits for them, and re-layouts  2.33 us (2%)
    ppermute x9, waiting for transfers between devices, shift(): lax.ppermute(v, 'ctx', [(i, (i + s) % n) for i in range(n)])  53.8 us
    pallas_call x15, Pallas kernels, call(): pl.pallas_call(kernel, out_shape=out_shape, in_specs=in_specs, out_specs=...  30.1 us
    all_to_all x3, starting transfers between devices, turn(): return lax.all_to_all(value, 'ctx', split_axis=0, concat_axis=0, tiled=True)  18.1 us
    ppermute x9, starting transfers between devices, shift(): lax.ppermute(v, 'ctx', [(i, (i + s) % n) for i in range(n)])  18 us
    ppermute x11, waiting for transfers between devices, swap(): return lax.ppermute(value, 'dp', [(i, i ^ k) for i in range(n_dp)])  10.5 us
    ppermute x11, starting transfers between devices, swap(): return lax.ppermute(value, 'dp', [(i, i ^ k) for i in range(n_dp)])  8.74 us
  transfers between devices with their start and end apart: 23, of which 16 were waited for; matrix products, arithmetic and copies ran while one was open for 0% of the time, Pallas kernels for 17%

commit v1 on v0

--- a/solution.py
+++ b/solution.py
@@ -95,7 +95,7 @@
         self.tokens, self.heads, self.rows, self.width = tokens, heads, rows, width
         self.per = -(-heads // n)
         self.mats = 3 * self.per
-        early = (self.per + 1) // 2
+        early = max(1, self.per - 1)
         self.chunks = [c for c in ((0, early), (early, self.per - early)) if c[1] > 0]
         self.group = min(4, n_dp)
         self.share = -(-self.mats // self.group)
@@ -109,30 +109,35 @@
         return min(c * self.per, self.heads - self.per)
 
 
-def pack_a_kernel(head_ref, dp_ref, k_ref, v_ref, s_ref, out, state, sems, *, plan, slot):
-    t, w, per = plan.tokens, plan.width, plan.per
+def pack_a_kernel(dp_ref, k_ref, v_ref, s_ref, out, state, sems, *, plan):
+    n, t, w, per = plan.n, plan.tokens, plan.width, plan.per
     low = lax.rem(dp_ref[0], plan.group)
-    head = head_ref[slot]
     loads = []
-    for q in range(plan.share):
-        mat = jnp.minimum(low * plan.share + q, plan.mats - 1)
-        load = pltpu.make_async_copy(
-            s_ref.at[lax.rem(mat, 3), head + lax.div(mat, 3)], state.at[q], sems.at[2 + q]
-        )
-        load.start()
-        loads.append(load)
-    cols = pl.ds(pl.multiple_of(head * w, w), per * w)
     copies = []
-    for part, src in enumerate((k_ref, v_ref)):
-        copy = pltpu.make_async_copy(src.at[0, :, cols], out.at[pl.ds(part * t, t), :], sems.at[part])
-        copy.start()
-        copies.append(copy)
+    for c in range(n):
+        for q in range(plan.share):
+            mat = jnp.minimum(low * plan.share + q, plan.mats - 1)
+            load = pltpu.make_async_copy(
+                s_ref.at[lax.rem(mat, 3), plan.first_head(c) + lax.div(mat, 3)],
+                state.at[c, q],
+                sems.at[c, 2 + q],
+            )
+            load.start()
+            loads.append(load)
+        cols = pl.ds(plan.first_head(c) * w, per * w)
+        for part, src in enumerate((k_ref, v_ref)):
+            copy = pltpu.make_async_copy(
+                src.at[0, :, cols], out.at[c, pl.ds(part * t, t), :], sems.at[c, part]
+            )
+            copy.start()
+            copies.append(copy)
     for load in loads:
         load.wait()
-    for q in range(plan.share):
-        top = 2 * t + (q // per) * plan.block
-        left = (q % per) * w
-        out[top : top + plan.rows, left : left + w] = state[q].astype(BF16)
+    for c in range(n):
+        for q in range(plan.share):
+            top = 2 * t + (q // per) * plan.block
+            left = (q % per) * w
+            out[c, top : top + plan.rows, left : left + w] = state[c, q].astype(BF16)
     for copy in copies:
         copy.wait()
 
@@ -174,15 +179,14 @@
         copy.wait()
 
 
-def start_kernel(from_ref, *refs, plan):
+def start_kernel(a_ref, out, whole, *, plan):
     rows, w = plan.rows, plan.width
-    a_refs, (out, whole) = refs[: plan.n], refs[plan.n :]
-    for slot in range(plan.n):
-        at = pl.ds(pl.multiple_of(from_ref[slot] * rows, rows), rows)
+    for c in range(plan.n):
         for q in range(plan.share):
             top = 2 * plan.tokens + (q // plan.per) * plan.block
             left = (q % plan.per) * w
-            whole[q, at, :] = a_refs[slot][top : top + rows, left : left + w].astype(F32)
+            part = a_ref[c, top : top + rows, left : left + w]
+            whole[q, c * rows : (c + 1) * rows, :] = part.astype(F32)
     out[...] = whole[...].astype(BF16)
 
 
@@ -219,7 +223,8 @@
         del refs[:k]
         return got
 
-    a_refs, shares = take(n), take(plan.group)
+    (a_ref,), shares = take(1), take(plan.group)
+    a_refs = [a_ref.at[c] for c in range(n)]
     joined = len(refs[0].shape) == 3
     b_refs = take(1 if joined else n)
     if joined:
@@ -285,10 +290,9 @@
         dx = dot_nt(jnp.concatenate([dg, du, cg, cu], axis=1), jnp.concatenate([fab, wab], axis=1))
         dy = dot_nt(jnp.concatenate([hidden, cp], axis=1), jnp.concatenate([fc, wc], axis=1))
         cols = slice(j * w, (j + 1) * w)
-        for slot in range(n):
-            to = from_ref[slot]
-            d_ref[to, 0:t, cols] = dx[slot * t : (slot + 1) * t].astype(BF16)
-            d_ref[to, t : 2 * t, cols] = dy[slot * t : (slot + 1) * t].astype(BF16)
+        for c in range(n):
+            d_ref[c, 0:t, cols] = dx[c * t : (c + 1) * t].astype(BF16)
+            d_ref[c, t : 2 * t, cols] = dy[c * t : (c + 1) * t].astype(BF16)
         ab = dot_tn(x, jnp.concatenate([cg, cu], axis=1))
         grown = (ab[:, :w], ab[:, w:], dot_tn(y, cp))
         for m in range(3):
@@ -407,20 +411,6 @@
     def shape(*dims, dtype=BF16):
         return jax.ShapeDtypeStruct(dims, dtype)
 
-    def pack_a(slot):
-        return call(
-            bind(pack_a_kernel, slot=slot),
-            shape(2 * t + plan.share_rows, per * width),
-            (head_ids, dp_id, keys_a, values_a, state_start),
-            [SMEM] * 2 + [HBM] * 3,
-            VMEM,
-            f"pack_a{slot}",
-            [
-                pltpu.VMEM((plan.share, rows, width), F32),
-                pltpu.SemaphoreType.DMA((2 + plan.share,)),
-            ],
-        )
-
     def pack_b(c, queries):
         dims = (2 * t + 3 * plan.block, chunks[c][1] * width)
         joined = c > 0
@@ -438,18 +428,28 @@
         )
         return list(outs)
 
-    a_sent = [pack_a(s) for s in [*range(1, n), 0]]
-    a_sent = [a_sent[-1]] + a_sent[:-1]
-    queries, a_sent[-1] = lax.optimization_barrier((queries_b, a_sent[-1]))
-    a_in = shift(a_sent)
+    a_sent = call(
+        bind(pack_a_kernel),
+        shape(n, 2 * t + plan.share_rows, per * width),
+        (dp_id, keys_a, values_a, state_start),
+        [SMEM] + [HBM] * 3,
+        VMEM,
+        "pack_a",
+        [
+            pltpu.VMEM((n, plan.share, rows, width), F32),
+            pltpu.SemaphoreType.DMA((n, 2 + plan.share)),
+        ],
+    )
+    queries, a_sent = lax.optimization_barrier((queries_b, a_sent))
+    a_in = turn(a_sent)
     b_in = [shift(pack_b(0, queries))]
     queries, a_in = lax.optimization_barrier((queries_b, a_in))
     b_in.append([turn(pack_b(1, queries)[0])])
     start_own = call(
         bind(start_kernel),
         shape(plan.share, width, width),
-        (from_ids, *a_in),
-        [SMEM] + [VMEM] * n,
+        (a_in,),
+        [VMEM],
         VMEM,
         "start_share",
         [pltpu.VMEM((plan.share, width, width), F32)],
@@ -477,8 +477,8 @@
         outs = call(
             bind(chunk_kernel, chunk=c),
             [shape(n, 2 * t, count * width)] + c_shapes,
-            (from_ids, dp_id, *a_in, *shares, *b_in[c], *before),
-            [SMEM] * 2 + [VMEM] * (n + plan.group + len(b_in[c]) + len(before)),
+            (from_ids, dp_id, a_in, *shares, *b_in[c], *before),
+            [SMEM] * 2 + [VMEM] * (1 + plan.group + len(b_in[c]) + len(before)),
             [VMEM] * (1 + len(c_shapes)),
             f"chunk{c}",
             scratch,

time: 145 us -> 140 us (0.966)
  local copies, waits for them, and re-layouts: 2.33 us -> 9.35 us
  Pallas kernels: 30.1 us -> 24 us
  waiting for transfers between devices: 65.8 us -> 60.6 us
    ppermute x9 -> x6, waiting for transfers between devices: 53.8 us -> 0.35 us  [shift(): lax.ppermute(v, 'ctx', [(i, (i + s) % n) for i in range(n)])]
    all_to_all x3 -> x4, waiting for transfers between devices: 1.58 us -> 43.8 us  [turn(): return lax.all_to_all(value, 'ctx', split_axis=0, concat_axis=0, tiled=True)]
    unnamed x12 -> x24, local copies, waits for them, and re-layouts: 2.33 us -> 9.35 us
    ppermute x9 -> x6, starting transfers between devices: 18 us -> 11.8 us  [shift(): lax.ppermute(v, 'ctx', [(i, (i + s) % n) for i in range(n)])]
    pallas_call x15 -> x12, Pallas kernels: 30.1 us -> 24 us  [call(): pl.pallas_call(kernel, out_shape=out_shape, in_specs=in_specs, out_specs=...]
    ppermute x11, waiting for transfers between devices: 10.5 us -> 16.5 us  [swap(): return lax.ppermute(value, 'dp', [(i, i ^ k) for i in range(n_dp)])]
    all_to_all x3 -> x4, starting transfers between devices: 18.1 us -> 23.2 us  [turn(): return lax.all_to_all(value, 'ctx', split_axis=0, concat_axis=0, tiled=True)]
  transfers between devices with their start and end apart: 23 -> 21, of which waited for: 16 -> 14; matrix products, arithmetic and copies ran while one was open for 0% -> 0% of each run, Pallas kernels for 17% -> 14%
where the time goes in v1:
time: 140 us; the launch traced here: 139 us
  waiting for transfers between devices  60.6 us (43%)
  starting transfers between devices  44 us (31%)
  Pallas kernels  24 us (17%)
  local copies, waits for them, and re-layouts  9.35 us (7%)
    all_to_all x4, waiting for transfers between devices, turn(): return lax.all_to_all(value, 'ctx', split_axis=0, concat_axis=0, tiled=True)  43.8 us
    pallas_call x12, Pallas kernels, call(): pl.pallas_call(kernel, out_shape=out_shape, in_specs=in_specs, out_specs=...  24 us
    all_to_all x4, starting transfers between devices, turn(): return lax.all_to_all(value, 'ctx', split_axis=0, concat_axis=0, tiled=True)  23.2 us
    ppermute x11, waiting for transfers between devices, swap(): return lax.ppermute(value, 'dp', [(i, i ^ k) for i in range(n_dp)])  16.5 us
    ppermute x6, starting transfers between devices, shift(): lax.ppermute(v, 'ctx', [(i, (i + s) % n) for i in range(n)])  11.8 us
    unnamed x24, local copies, waits for them, and re-layouts  9.35 us
    ppermute x11, starting transfers between devices, swap(): return lax.ppermute(value, 'dp', [(i, i ^ k) for i in range(n_dp)])  9.12 us
  transfers between devices with their start and end apart: 21, of which 14 were waited for; matrix products, arithmetic and copies ran while one was open for 0% of the time, Pallas kernels for 14%

profile of v1, /device:TPU:0, one launch (start us, length us, event | category | flops | bytes accessed | tf_op | source)
XLA Modules:
  0.0 138.8 jit_solution(16484469434088652636)
XLA Ops:
  0.6 2.9 %pack_a.1 = bf16[4,288,640]{2,1,0:T(8,128)(2,1)} custom-call(s32[1]{0:T(128)} %bitcast.dp_ref, bf16[1,128,2560]{2,1,0:T(8,128)(2,1)} %k_ref.1, bf16[1,128,2560]{2,1,0:T(8,128)(2,1)} %v_ref.1, f32[3,20,32,128]{3,2,1,0:T(8,128)} %s_ref.3), custom_call_target="tpu_custom_call" | custom-call | flops 1000000 | bytes 1000000 | tf_op jit(solution)/shard_map/pack_a/pallas_call | solution.py:40
  3.5 6.3 %all-to-all-start = ((bf16[4,288,640]{2,1,0:T(8,128)(2,1)}), bf16[4,288,640]{2,1,0:T(8,128)(2,1)S(1)}, u32[]{:S(2)}, u32[]{:S(2)}) async-start(bf16[4,288,640]{2,1,0:T(8,128)(2,1)} %pack_a.1), calls=%async_computation | async-start | bytes 2949120 | tf_op jit(solution)/shard_map/all_to_all | solution.py:409
  9.9 3.2 %pack_b0.1 = (bf16[352,512]{1,0:T(8,128)(2,1)S(1)}, bf16[352,512]{1,0:T(8,128)(2,1)}, bf16[352,512]{1,0:T(8,128)(2,1)}, bf16[352,512]{1,0:T(8,128)(2,1)}) custom-call(s32[4]{0:T(128)S(1)} %multiply_minimum_fusion.head_ref, bf16[1,128,2560]{2,1,0:T(8,128)(2,1)} %q_ref.1, bf16[1,128,2560]{2,1,0:T(8,128)(2,1)} %o_ref.3, f32[1,3,20,32,128]{4,3,2,1,0:T(8,128)} %s_ref.5), custom_call_target="tpu_custom_call" | custom-call | flops 1000000 | bytes 1000000 | tf_op jit(solution)/shard_map/pack_b0/pallas_call | solution.py:40
  13.1 0.7 copy-done.8
  13.8 2.0 %collective-permute-start.3 = (bf16[352,512]{1,0:T(8,128)(2,1)}, bf16[352,512]{1,0:T(8,128)(2,1)S(1)}, u32[]{:S(2)}, u32[]{:S(2)}) collective-permute-start(bf16[352,512]{1,0:T(8,128)(2,1)} %get-tuple-element.35), channel_id=1, source_target_pairs={{0,1},{1,2},{2,3},{3,0},{4,5},{5,6},{6,7},{7,4},{8,9},{9,10},{10,1... | collective-permute-start | bytes 1081352 | tf_op jit(solution)/shard_map/ppermute | solution.py:404
  15.8 2.4 %collective-permute-start.4 = (bf16[352,512]{1,0:T(8,128)(2,1)}, bf16[352,512]{1,0:T(8,128)(2,1)}, u32[]{:S(2)}, u32[]{:S(2)}) collective-permute-start(bf16[352,512]{1,0:T(8,128)(2,1)} %get-tuple-element.36), channel_id=1, source_target_pairs={{0,2},{1,3},{2,0},{3,1},{4,6},{5,7},{6,4},{7,5},{8,10},{9,11},{10,... | collective-permute-start | bytes 1081352 | tf_op jit(solution)/shard_map/ppermute | solution.py:404
  18.2 1.5 %collective-permute-start.5 = (bf16[352,512]{1,0:T(8,128)(2,1)}, bf16[352,512]{1,0:T(8,128)(2,1)}, u32[]{:S(2)}, u32[]{:S(2)}) collective-permute-start(bf16[352,512]{1,0:T(8,128)(2,1)} %get-tuple-element.37), channel_id=1, source_target_pairs={{0,3},{1,0},{2,1},{3,2},{4,7},{5,4},{6,5},{7,6},{8,11},{9,8},{10,9... | collective-permute-start | bytes 1081352 | tf_op jit(solution)/shard_map/ppermute | solution.py:404
  19.6 41.6 %all-to-all-done.a_ref.refs_0_ = bf16[4,288,640]{2,1,0:T(8,128)(2,1)S(1)} async-done(((bf16[4,288,640]{2,1,0:T(8,128)(2,1)}), bf16[4,288,640]{2,1,0:T(8,128)(2,1)S(1)}, u32[]{:S(2)}, u32[]{:S(2)}) %all-to-all-start) | async-done | bytes 1474592 | tf_op jit(solution)/shard_map/all_to_all | solution.py:409
  61.2 2.4 %pack_b1.1 = bf16[4,352,128]{2,1,0:T(8,128)(2,1)} custom-call(s32[4]{0:T(128)S(1)} %multiply_minimum_fusion.head_ref, bf16[1,128,2560]{2,1,0:T(8,128)(2,1)} %q_ref.1, bf16[1,128,2560]{2,1,0:T(8,128)(2,1)} %o_ref.3, f32[1,3,20,32,128]{4,3,2,1,0:T(8,128)} %s_ref.5), custom_call_target="tpu_custom_call" | custom-call | flops 1000000 | bytes 1000000 | tf_op jit(solution)/shard_map/pack_b1/pallas_call | solution.py:40
  63.6 3.5 %all-to-all-start.1 = ((bf16[4,352,128]{2,1,0:T(8,128)(2,1)}), bf16[4,352,128]{2,1,0:T(8,128)(2,1)S(1)}, u32[]{:S(2)}, u32[]{:S(2)}) async-start(bf16[4,352,128]{2,1,0:T(8,128)(2,1)} %pack_b1.1), calls=%async_computation.1 | async-start | bytes 720896 | tf_op jit(solution)/shard_map/all_to_all | solution.py:409
  67.2 1.6 %collective-permute-start.1 = (bf16[4,128,128]{2,1,0:T(8,128)(2,1)S(1)}, bf16[4,128,128]{2,1,0:T(8,128)(2,1)S(1)}, u32[]{:S(2)}, u32[]{:S(2)}) collective-permute-start(bf16[4,128,128]{2,1,0:T(8,128)(2,1)S(1)} %start_share.1.refs_1_), channel_id=1, source_target_pairs={{0,8},{4,12},{8,0},{12,4},{16,24},{20,28},{24,16},{28,20},{1,9},{5... | collective-permute-start | bytes 393224 | tf_op jit(solution)/shard_map/ppermute | solution.py:400
  68.7 0.7 copy-done.10
  69.8 3.7 %collective-permute-done.1.refs_3_ = bf16[4,128,128]{2,1,0:T(8,128)(2,1)S(1)} collective-permute-done((bf16[4,128,128]{2,1,0:T(8,128)(2,1)S(1)}, bf16[4,128,128]{2,1,0:T(8,128)(2,1)S(1)}, u32[]{:S(2)}, u32[]{:S(2)}) %collective-permute-start.1) | collective-permute-done | bytes 131104 | tf_op jit(solution)/shard_map/ppermute | solution.py:400
  73.5 0.7 copy-done.2
  74.2 1.2 collective-permute-done.2.refs_4_
  75.4 0.7 copy-done.5
  76.1 0.9 copy-done.3
  77.0 0.9 copy-done.6
  77.9 1.0 copy-done.9
  78.9 1.0 copy-done.11
  79.9 7.8 %chunk0.1 = (bf16[4,256,512]{2,1,0:T(8,128)(2,1)S(1)}, bf16[12,128,128]{2,1,0:T(8,128)(2,1)S(1)}) custom-call(s32[4]{0:T(128)S(1)} %compare_select_fusion.from_ref.place_ref, s32[1]{0:T(128)} %bitcast.dp_ref, bf16[4,288,640]{2,1,0:T(8,128)(2,1)S(1)} %all-to-all-done.a_ref.refs_0_, bf16[4,128,128]{2,1,0:T(8,128)(2,1)S(1)} %start_share.1.refs_1_, ...), custom_call_target="tpu_custom_call" | custom-call | flops 2560000000 | bytes 4000000 | tf_op jit(solution)/shard_map/chunk0/pallas_call | solution.py:40
  87.7 1.0 copy-done
  88.7 9.1 %all-to-all-start.2 = ((bf16[4,256,512]{2,1,0:T(8,128)(2,1)}), bf16[4,256,512]{2,1,0:T(8,128)(2,1)S(1)}, u32[]{:S(2)}, u32[]{:S(2)}) async-start(bf16[4,256,512]{2,1,0:T(8,128)(2,1)} %copy-done), calls=%async_computation.2 | async-start | bytes 2097152 | tf_op jit(solution)/shard_map/all_to_all | solution.py:409
  97.8 0.9 copy-done.4
  98.7 0.9 copy-done.7
  99.6 3.7 %chunk1.1 = (bf16[4,256,128]{2,1,0:T(8,128)(2,1)S(1)}, bf16[8,128,128]{2,1,0:T(8,128)(2,1)S(1)}, bf16[8,128,128]{2,1,0:T(8,128)(2,1)S(1)}) custom-call(s32[4]{0:T(128)S(1)} %compare_select_fusion.from_ref.place_ref, s32[1]{0:T(128)} %bitcast.dp_ref, bf16[4,288,640]{2,1,0:T(8,128)(2,1)S(1)} %all-to-all-done.a_ref.refs_0_, ...), custom_call_target="tpu_custom_call" | custom-call | flops 640000000 | bytes 1000000 | tf_op jit(solution)/shard_map/chunk1/pallas_call | solution.py:40
  103.4 1.5 %collective-permute-done.6.got_ref = bf16[8,128,128]{2,1,0:T(8,128)(2,1)S(1)} collective-permute-done((bf16[8,128,128]{2,1,0:T(8,128)(2,1)S(1)}, bf16[8,128,128]{2,1,0:T(8,128)(2,1)S(1)}, u32[]{:S(2)}, u32[]{:S(2)}) %collective-permute-start.6) | collective-permute-done | bytes 262176 | tf_op jit(solution)/shard_map/ppermute | solution.py:400
  105.0 1.6 %collective-permute-start.7 = (bf16[2,128,128]{2,1,0:T(8,128)(2,1)S(1)}, bf16[2,128,128]{2,1,0:T(8,128)(2,1)S(1)}, u32[]{:S(2)}, u32[]{:S(2)}) collective-permute-start(bf16[2,128,128]{2,1,0:T(8,128)(2,1)S(1)} %get-tuple-element.42), channel_id=1, source_target_pairs={{0,8},{4,12},{8,0},{12,4},{16,24},{20,28},{24,16},{28,20},{1,9},{5... | collective-permute-start | bytes 196616 | tf_op jit(solution)/shard_map/ppermute | solution.py:400
  106.6 1.5 %collective-permute-start.8 = (bf16[2,128,128]{2,1,0:T(8,128)(2,1)S(1)}, bf16[2,128,128]{2,1,0:T(8,128)(2,1)S(1)}, u32[]{:S(2)}, u32[]{:S(2)}) collective-permute-start(bf16[2,128,128]{2,1,0:T(8,128)(2,1)S(1)} %get-tuple-element.43), channel_id=1, source_target_pairs={{0,16},{4,20},{8,24},{12,28},{16,0},{20,4},{24,8},{28,12},{1,17},{... | collective-permute-start | bytes 196616 | tf_op jit(solution)/shard_map/ppermute | solution.py:400
  108.6 0.8 collective-permute-done.7.refs_1_
  109.3 1.5 %collective-permute-done.8.refs_2_ = bf16[2,128,128]{2,1,0:T(8,128)(2,1)S(1)} collective-permute-done((bf16[2,128,128]{2,1,0:T(8,128)(2,1)S(1)}, bf16[2,128,128]{2,1,0:T(8,128)(2,1)S(1)}, u32[]{:S(2)}, u32[]{:S(2)}) %collective-permute-start.8) | collective-permute-done | bytes 65568 | tf_op jit(solution)/shard_map/ppermute | solution.py:400
  110.8 2.4 %collective-permute-done.9.refs_3_ = bf16[2,128,128]{2,1,0:T(8,128)(2,1)S(1)} collective-permute-done((bf16[2,128,128]{2,1,0:T(8,128)(2,1)S(1)}, bf16[2,128,128]{2,1,0:T(8,128)(2,1)S(1)}, u32[]{:S(2)}, u32[]{:S(2)}) %collective-permute-start.9) | collective-permute-done | bytes 65568 | tf_op jit(solution)/shard_map/ppermute | solution.py:400
  113.2 0.6 state_sum.1
  113.8 2.1 %collective-permute-start.10 = (bf16[2,32,128]{2,1,0:T(8,128)(2,1)S(1)}, bf16[2,32,128]{2,1,0:T(8,128)(2,1)S(1)}, u32[]{:S(2)}, u32[]{:S(2)}) collective-permute-start(bf16[2,32,128]{2,1,0:T(8,128)(2,1)S(1)} %get-tuple-element.49), channel_id=1, source_target_pairs={{0,1},{1,2},{2,3},{3,0},{4,5},{5,6},{6,7},{7,4},{8,9},{9,10},{10,1... | collective-permute-start | bytes 49160 | tf_op jit(solution)/shard_map/ppermute | solution.py:404
  115.9 2.4 %collective-permute-start.11 = (bf16[2,32,128]{2,1,0:T(8,128)(2,1)S(1)}, bf16[2,32,128]{2,1,0:T(8,128)(2,1)S(1)}, u32[]{:S(2)}, u32[]{:S(2)}) collective-permute-start(bf16[2,32,128]{2,1,0:T(8,128)(2,1)S(1)} %get-tuple-element.50), channel_id=1, source_target_pairs={{0,2},{1,3},{2,0},{3,1},{4,6},{5,7},{6,4},{7,5},{8,10},{9,11},{10,... | collective-permute-start | bytes 49160 | tf_op jit(solution)/shard_map/ppermute | solution.py:404
  118.3 1.5 %collective-permute-start.12 = (bf16[2,32,128]{2,1,0:T(8,128)(2,1)S(1)}, bf16[2,32,128]{2,1,0:T(8,128)(2,1)S(1)}, u32[]{:S(2)}, u32[]{:S(2)}) collective-permute-start(bf16[2,32,128]{2,1,0:T(8,128)(2,1)S(1)} %get-tuple-element.51), channel_id=1, source_target_pairs={{0,3},{1,0},{2,1},{3,2},{4,7},{5,4},{6,5},{7,6},{8,11},{9,8},{10,9... | collective-permute-start | bytes 49160 | tf_op jit(solution)/shard_map/ppermute | solution.py:404
  119.7 2.2 %all-to-all-done.2.refs_0_ = bf16[4,256,512]{2,1,0:T(8,128)(2,1)S(1)} async-done(((bf16[4,256,512]{2,1,0:T(8,128)(2,1)}), bf16[4,256,512]{2,1,0:T(8,128)(2,1)S(1)}, u32[]{:S(2)}, u32[]{:S(2)}) %all-to-all-start.2) | async-done | bytes 1048608 | tf_op jit(solution)/shard_map/all_to_all | solution.py:409
  122.8 4.3 %all-to-all-start.3 = ((bf16[4,256,128]{2,1,0:T(8,128)(2,1)}), bf16[4,256,128]{2,1,0:T(8,128)(2,1)S(1)}, u32[]{:S(2)}, u32[]{:S(2)}) async-start(bf16[4,256,128]{2,1,0:T(8,128)(2,1)} %copy-done.1), calls=%async_computation.3 | async-start | bytes 524288 | tf_op jit(solution)/shard_map/all_to_all | solution.py:409
  127.1 0.7 collective-permute-start.13
  127.8 1.4 %collective-permute-start.14 = (bf16[4,2,32,128]{3,2,1,0:T(8,128)(2,1)S(1)}, bf16[4,2,32,128]{3,2,1,0:T(8,128)(2,1)S(1)}, u32[]{:S(2)}, u32[]{:S(2)}) collective-permute-start(bf16[4,2,32,128]{3,2,1,0:T(8,128)(2,1)S(1)} %state_rows.1.refs_0_), channel_id=1, source_target_pairs={{0,16},{4,20},{8,24},{12,28},{16,0},{20,4},{24,8},{28,12},{1,17},{... | collective-permute-start | bytes 196616 | tf_op jit(solution)/shard_map/ppermute | solution.py:400
  129.2 1.4 %collective-permute-start.15 = (bf16[4,2,32,128]{3,2,1,0:T(8,128)(2,1)S(1)}, bf16[4,2,32,128]{3,2,1,0:T(8,128)(2,1)S(1)}, u32[]{:S(2)}, u32[]{:S(2)}) collective-permute-start(bf16[4,2,32,128]{3,2,1,0:T(8,128)(2,1)S(1)} %state_rows.1.refs_0_), channel_id=1, source_target_pairs={{0,24},{4,28},{8,16},{12,20},{16,8},{20,12},{24,0},{28,4},{1,25},{... | collective-permute-start | bytes 196616 | tf_op jit(solution)/shard_map/ppermute | solution.py:400
  130.6 0.8 collective-permute-done.13.refs_1_
  131.4 1.0 collective-permute-done.14.refs_2_
  132.4 1.9 %collective-permute-done.15.refs_3_ = bf16[4,2,32,128]{3,2,1,0:T(8,128)(2,1)S(1)} collective-permute-done((bf16[4,2,32,128]{3,2,1,0:T(8,128)(2,1)S(1)}, bf16[4,2,32,128]{3,2,1,0:T(8,128)(2,1)S(1)}, u32[]{:S(2)}, u32[]{:S(2)}) %collective-permute-start.15) | collective-permute-done | bytes 65568 | tf_op jit(solution)/shard_map/ppermute | solution.py:400
  134.4 0.6 state_rest.1.refs_0_
  135.0 1.5 %collective-permute-done.16.refs_1_ = bf16[4,4,2,32,128]{4,3,2,1,0:T(8,128)(2,1)S(1)} collective-permute-done((bf16[4,4,2,32,128]{4,3,2,1,0:T(8,128)(2,1)S(1)}, bf16[4,4,2,32,128]{4,3,2,1,0:T(8,128)(2,1)S(1)}, u32[]{:S(2)}, u32[]{:S(2)}) %collective-permute-start.16) | collective-permute-done | bytes 262176 | tf_op jit(solution)/shard_map/ppermute | solution.py:400
  136.5 1.1 state_out.1
  137.6 1.2 unpack.1
  (34 shorter events, 2.1 us)
Async XLA Ops:
  3.5 57.7 %all-to-all-start = ((bf16[4,288,640]{2,1,0:T(8,128)(2,1)}), bf16[4,288,640]{2,1,0:T(8,128)(2,1)S(1)}, u32[]{:S(2)}, u32[]{:S(2)}) async-start(bf16[4,288,640]{2,1,0:T(8,128)(2,1)} %pack_a.1), calls=%async_computation | async-start | bytes 2949120 | tf_op jit(solution)/shard_map/all_to_all | solution.py:409
  13.0 0.7 copy-start.8
  13.8 54.9 %collective-permute-start.3 = (bf16[352,512]{1,0:T(8,128)(2,1)}, bf16[352,512]{1,0:T(8,128)(2,1)S(1)}, u32[]{:S(2)}, u32[]{:S(2)}) collective-permute-start(bf16[352,512]{1,0:T(8,128)(2,1)} %get-tuple-element.35), channel_id=1, source_target_pairs={{0,1},{1,2},{2,3},{3,0},{4,5},{5,6},{6,7},{7,4},{8,9},{9,10},{10,1... | collective-permute-start | bytes 1081352 | tf_op jit(solution)/shard_map/ppermute | solution.py:404
  15.8 54.0 %collective-permute-start.4 = (bf16[352,512]{1,0:T(8,128)(2,1)}, bf16[352,512]{1,0:T(8,128)(2,1)}, u32[]{:S(2)}, u32[]{:S(2)}) collective-permute-start(bf16[352,512]{1,0:T(8,128)(2,1)} %get-tuple-element.36), channel_id=1, source_target_pairs={{0,2},{1,3},{2,0},{3,1},{4,6},{5,7},{6,4},{7,5},{8,10},{9,11},{10,... | collective-permute-start | bytes 1081352 | tf_op jit(solution)/shard_map/ppermute | solution.py:404
  18.2 51.6 %collective-permute-start.5 = (bf16[352,512]{1,0:T(8,128)(2,1)}, bf16[352,512]{1,0:T(8,128)(2,1)}, u32[]{:S(2)}, u32[]{:S(2)}) collective-permute-start(bf16[352,512]{1,0:T(8,128)(2,1)} %get-tuple-element.37), channel_id=1, source_target_pairs={{0,3},{1,0},{2,1},{3,2},{4,7},{5,4},{6,5},{7,6},{8,11},{9,8},{10,9... | collective-permute-start | bytes 1081352 | tf_op jit(solution)/shard_map/ppermute | solution.py:404
  63.6 25.1 %all-to-all-start.1 = ((bf16[4,352,128]{2,1,0:T(8,128)(2,1)}), bf16[4,352,128]{2,1,0:T(8,128)(2,1)S(1)}, u32[]{:S(2)}, u32[]{:S(2)}) async-start(bf16[4,352,128]{2,1,0:T(8,128)(2,1)} %pack_b1.1), calls=%async_computation.1 | async-start | bytes 720896 | tf_op jit(solution)/shard_map/all_to_all | solution.py:409
  67.1 2.7 %collective-permute-start = (bf16[4,128,128]{2,1,0:T(8,128)(2,1)S(1)}, bf16[4,128,128]{2,1,0:T(8,128)(2,1)S(1)}, u32[]{:S(2)}, u32[]{:S(2)}) collective-permute-start(bf16[4,128,128]{2,1,0:T(8,128)(2,1)S(1)} %start_share.1.refs_1_), channel_id=1, source_target_pairs={{0,4},{4,0},{8,12},{12,8},{16,20},{20,16},{24,28},{28,24},{1,5},{5... | collective-permute-start | bytes 393224 | tf_op jit(solution)/shard_map/ppermute | solution.py:400
  67.2 6.4 %collective-permute-start.1 = (bf16[4,128,128]{2,1,0:T(8,128)(2,1)S(1)}, bf16[4,128,128]{2,1,0:T(8,128)(2,1)S(1)}, u32[]{:S(2)}, u32[]{:S(2)}) collective-permute-start(bf16[4,128,128]{2,1,0:T(8,128)(2,1)S(1)} %start_share.1.refs_1_), channel_id=1, source_target_pairs={{0,8},{4,12},{8,0},{12,4},{16,24},{20,28},{24,16},{28,20},{1,9},{5... | collective-permute-start | bytes 393224 | tf_op jit(solution)/shard_map/ppermute | solution.py:400
  68.7 0.7 copy-start.10
  69.5 6.0 %collective-permute-start.2 = (bf16[4,128,128]{2,1,0:T(8,128)(2,1)S(1)}, bf16[4,128,128]{2,1,0:T(8,128)(2,1)S(1)}, u32[]{:S(2)}, u32[]{:S(2)}) collective-permute-start(bf16[4,128,128]{2,1,0:T(8,128)(2,1)S(1)} %start_share.1.refs_1_), channel_id=1, source_target_pairs={{0,12},{4,8},{8,4},{12,0},{16,28},{20,24},{24,20},{28,16},{1,13},{... | collective-permute-start | bytes 393224 | tf_op jit(solution)/shard_map/ppermute | solution.py:400
  73.5 0.7 copy-start.2
  75.4 0.7 copy-start.5
  76.1 0.9 copy-start.3
  77.0 0.9 copy-start.6
  77.9 1.0 copy-start.9
  78.9 1.0 copy-start.11
  87.7 1.0 copy-start
  88.7 33.2 %all-to-all-start.2 = ((bf16[4,256,512]{2,1,0:T(8,128)(2,1)}), bf16[4,256,512]{2,1,0:T(8,128)(2,1)S(1)}, u32[]{:S(2)}, u32[]{:S(2)}) async-start(bf16[4,256,512]{2,1,0:T(8,128)(2,1)} %copy-done), calls=%async_computation.2 | async-start | bytes 2097152 | tf_op jit(solution)/shard_map/all_to_all | solution.py:409
  97.8 0.9 copy-start.4
  98.7 0.9 copy-start.7
  103.3 15.0 %copy-start.1 = (bf16[4,256,128]{2,1,0:T(8,128)(2,1)}, bf16[4,256,128]{2,1,0:T(8,128)(2,1)S(1)}, u32[]{:S(2)}) copy-start(bf16[4,256,128]{2,1,0:T(8,128)(2,1)S(1)} %get-tuple-element.53) | copy-start | bytes 786436
  103.3 1.6 %collective-permute-start.6 = (bf16[8,128,128]{2,1,0:T(8,128)(2,1)S(1)}, bf16[8,128,128]{2,1,0:T(8,128)(2,1)S(1)}, u32[]{:S(2)}, u32[]{:S(2)}) collective-permute-start(bf16[8,128,128]{2,1,0:T(8,128)(2,1)S(1)} %get-tuple-element.40), channel_id=1, source_target_pairs={{0,4},{4,0},{8,12},{12,8},{16,20},{20,16},{24,28},{28,24},{1,5},{5... | collective-permute-start | bytes 786440 | tf_op jit(solution)/shard_map/ppermute | solution.py:400
  105.0 4.3 %collective-permute-start.7 = (bf16[2,128,128]{2,1,0:T(8,128)(2,1)S(1)}, bf16[2,128,128]{2,1,0:T(8,128)(2,1)S(1)}, u32[]{:S(2)}, u32[]{:S(2)}) collective-permute-start(bf16[2,128,128]{2,1,0:T(8,128)(2,1)S(1)} %get-tuple-element.42), channel_id=1, source_target_pairs={{0,8},{4,12},{8,0},{12,4},{16,24},{20,28},{24,16},{28,20},{1,9},{5... | collective-permute-start | bytes 196616 | tf_op jit(solution)/shard_map/ppermute | solution.py:400
  106.6 4.3 %collective-permute-start.8 = (bf16[2,128,128]{2,1,0:T(8,128)(2,1)S(1)}, bf16[2,128,128]{2,1,0:T(8,128)(2,1)S(1)}, u32[]{:S(2)}, u32[]{:S(2)}) collective-permute-start(bf16[2,128,128]{2,1,0:T(8,128)(2,1)S(1)} %get-tuple-element.43), channel_id=1, source_target_pairs={{0,16},{4,20},{8,24},{12,28},{16,0},{20,4},{24,8},{28,12},{1,17},{... | collective-permute-start | bytes 196616 | tf_op jit(solution)/shard_map/ppermute | solution.py:400
  108.1 5.2 %collective-permute-start.9 = (bf16[2,128,128]{2,1,0:T(8,128)(2,1)S(1)}, bf16[2,128,128]{2,1,0:T(8,128)(2,1)S(1)}, u32[]{:S(2)}, u32[]{:S(2)}) collective-permute-start(bf16[2,128,128]{2,1,0:T(8,128)(2,1)S(1)} %get-tuple-element.44), channel_id=1, source_target_pairs={{0,24},{4,28},{8,16},{12,20},{16,8},{20,12},{24,0},{28,4},{1,25},{... | collective-permute-start | bytes 196616 | tf_op jit(solution)/shard_map/ppermute | solution.py:400
  113.8 8.1 %collective-permute-start.10 = (bf16[2,32,128]{2,1,0:T(8,128)(2,1)S(1)}, bf16[2,32,128]{2,1,0:T(8,128)(2,1)S(1)}, u32[]{:S(2)}, u32[]{:S(2)}) collective-permute-start(bf16[2,32,128]{2,1,0:T(8,128)(2,1)S(1)} %get-tuple-element.49), channel_id=1, source_target_pairs={{0,1},{1,2},{2,3},{3,0},{4,5},{5,6},{6,7},{7,4},{8,9},{9,10},{10,1... | collective-permute-start | bytes 49160 | tf_op jit(solution)/shard_map/ppermute | solution.py:404
  115.9 6.2 %collective-permute-start.11 = (bf16[2,32,128]{2,1,0:T(8,128)(2,1)S(1)}, bf16[2,32,128]{2,1,0:T(8,128)(2,1)S(1)}, u32[]{:S(2)}, u32[]{:S(2)}) collective-permute-start(bf16[2,32,128]{2,1,0:T(8,128)(2,1)S(1)} %get-tuple-element.50), channel_id=1, source_target_pairs={{0,2},{1,3},{2,0},{3,1},{4,6},{5,7},{6,4},{7,5},{8,10},{9,11},{10,... | collective-permute-start | bytes 49160 | tf_op jit(solution)/shard_map/ppermute | solution.py:404
  118.3 4.0 %collective-permute-start.12 = (bf16[2,32,128]{2,1,0:T(8,128)(2,1)S(1)}, bf16[2,32,128]{2,1,0:T(8,128)(2,1)S(1)}, u32[]{:S(2)}, u32[]{:S(2)}) collective-permute-start(bf16[2,32,128]{2,1,0:T(8,128)(2,1)S(1)} %get-tuple-element.51), channel_id=1, source_target_pairs={{0,3},{1,0},{2,1},{3,2},{4,7},{5,4},{6,5},{7,6},{8,11},{9,8},{10,9... | collective-permute-start | bytes 49160 | tf_op jit(solution)/shard_map/ppermute | solution.py:404
  122.8 14.8 %all-to-all-start.3 = ((bf16[4,256,128]{2,1,0:T(8,128)(2,1)}), bf16[4,256,128]{2,1,0:T(8,128)(2,1)S(1)}, u32[]{:S(2)}, u32[]{:S(2)}) async-start(bf16[4,256,128]{2,1,0:T(8,128)(2,1)} %copy-done.1), calls=%async_computation.3 | async-start | bytes 524288 | tf_op jit(solution)/shard_map/all_to_all | solution.py:409
  127.1 4.3 %collective-permute-start.13 = (bf16[4,2,32,128]{3,2,1,0:T(8,128)(2,1)S(1)}, bf16[4,2,32,128]{3,2,1,0:T(8,128)(2,1)S(1)}, u32[]{:S(2)}, u32[]{:S(2)}) collective-permute-start(bf16[4,2,32,128]{3,2,1,0:T(8,128)(2,1)S(1)} %state_rows.1.refs_0_), channel_id=1, source_target_pairs={{0,8},{4,12},{8,0},{12,4},{16,24},{20,28},{24,16},{28,20},{1,9},{5... | collective-permute-start | bytes 196616 | tf_op jit(solution)/shard_map/ppermute | solution.py:400
  127.8 4.6 %collective-permute-start.14 = (bf16[4,2,32,128]{3,2,1,0:T(8,128)(2,1)S(1)}, bf16[4,2,32,128]{3,2,1,0:T(8,128)(2,1)S(1)}, u32[]{:S(2)}, u32[]{:S(2)}) collective-permute-start(bf16[4,2,32,128]{3,2,1,0:T(8,128)(2,1)S(1)} %state_rows.1.refs_0_), channel_id=1, source_target_pairs={{0,16},{4,20},{8,24},{12,28},{16,0},{20,4},{24,8},{28,12},{1,17},{... | collective-permute-start | bytes 196616 | tf_op jit(solution)/shard_map/ppermute | solution.py:400
  129.2 5.2 %collective-permute-start.15 = (bf16[4,2,32,128]{3,2,1,0:T(8,128)(2,1)S(1)}, bf16[4,2,32,128]{3,2,1,0:T(8,128)(2,1)S(1)}, u32[]{:S(2)}, u32[]{:S(2)}) collective-permute-start(bf16[4,2,32,128]{3,2,1,0:T(8,128)(2,1)S(1)} %state_rows.1.refs_0_), channel_id=1, source_target_pairs={{0,24},{4,28},{8,16},{12,20},{16,8},{20,12},{24,0},{28,4},{1,25},{... | collective-permute-start | bytes 196616 | tf_op jit(solution)/shard_map/ppermute | solution.py:400
  134.9 1.6 %collective-permute-start.16 = (bf16[4,4,2,32,128]{4,3,2,1,0:T(8,128)(2,1)S(1)}, bf16[4,4,2,32,128]{4,3,2,1,0:T(8,128)(2,1)S(1)}, u32[]{:S(2)}, u32[]{:S(2)}) collective-permute-start(bf16[4,4,2,32,128]{4,3,2,1,0:T(8,128)(2,1)S(1)} %state_rest.1.refs_0_), channel_id=1, source_target_pairs={{0,4},{4,0},{8,12},{12,8},{16,20},{20,16},{24,28},{28,24},{1,5},{5... | collective-permute-start | bytes 786440 | tf_op jit(solution)/shard_map/ppermute | solution.py:400

commit v2 on v0

v2 whole, which is shorter than its diff:
```python
import functools

import jax
import jax.numpy as jnp
from jax import lax
from jax.experimental import pallas as pl
from jax.experimental.pallas import tpu as pltpu
from jax.sharding import PartitionSpec as P

RATE = 4.0
CA = 3.4445
CB = -4.775
CC = 2.0315
STEPS = 2
F32 = jnp.float32
BF16 = jnp.bfloat16
VMEM_SMALL = 8 * 1024 * 1024
VMEM_LARGE = 28 * 1024 * 1024
SMEM = pl.BlockSpec(memory_space=pltpu.SMEM)
VMEM = pl.BlockSpec(memory_space=pltpu.VMEM)
ANY = pl.BlockSpec(memory_space=pl.ANY)
HBM = pl.BlockSpec(memory_space=pltpu.HBM)


def dot_nn(a, b):
    return lax.dot_general(a, b, (((1,), (0,)), ((), ())), preferred_element_type=F32)


def dot_nt(a, b):
    return lax.dot_general(a, b, (((1,), (1,)), ((), ())), preferred_element_type=F32)


def dot_tn(a, b):
    return lax.dot_general(a, b, (((0,), (0,)), ((), ())), preferred_element_type=F32)


def call(
    kernel, out_shape, args, in_specs, out_specs, name, scratch=(), flops=10**6, size=10**6, vmem=VMEM_SMALL
):
    return pl.pallas_call(
        kernel,
        out_shape=out_shape,
        in_specs=in_specs,
        out_specs=out_specs,
        scratch_shapes=list(scratch),
        compiler_params=pltpu.CompilerParams(vmem_limit_bytes=vmem),
        cost_estimate=pl.CostEstimate(flops=flops, bytes_accessed=size, transcendentals=0),
        name=name,
    )(*args)


def swish_terms(g):
    s = 1.0 / (1.0 + jnp.exp(-g))
    sw = g * s
    slope = s * (1.0 + g * (1.0 - s))
    return s, sw, slope


def newton_pullback(grads, updates):
    each = range(len(grads))
    inv = [lax.rsqrt(jnp.sum(g * g, keepdims=True) + 1e-06) for g in grads]
    xs = [[(grads[m] * inv[m]).astype(BF16) for m in each]]
    grams = []
    polys = []
    for step in range(STEPS):
        x = xs[-1]
        gram = [dot_nt(x[m], x[m]).astype(BF16) for m in each]
        poly = [(CB * gram[m].astype(F32) + CC * dot_nn(gram[m], gram[m])).astype(BF16) for m in each]
        grams.append(gram)
        polys.append(poly)
        if step + 1 < STEPS:
            xs.append([(CA * x[m].astype(F32) + dot_nn(poly[m], x[m])).astype(BF16) for m in each])
    d = updates
    for step in reversed(range(STEPS)):
        x, gram, poly = xs[step], grams[step], polys[step]
        dp = [dot_nt(d[m], x[m]) for m in each]
        sym = [dp[m] + dp[m].T for m in each]
        turned = [dot_nn(sym[m].astype(BF16), gram[m]) for m in each]
        da = [(CB * sym[m] + CC * (turned[m] + turned[m].T)).astype(BF16) for m in each]
        d = [
            (CA * d[m].astype(F32) + dot_nn(poly[m], d[m]) + dot_nn(da[m], x[m])).astype(BF16)
            for m in each
        ]
    out = []
    for m in each:
        df = d[m].astype(F32)
        along = jnp.sum(df * grads[m], keepdims=True)
        out.append(df * inv[m] - grads[m] * (along * (inv[m] * inv[m] * inv[m])))
    return out


class Plan:
    def __init__(self, n, n_dp, tokens, heads, rows, width):
        self.n, self.n_dp = n, n_dp
        self.tokens, self.heads, self.rows, self.width = tokens, heads, rows, width
        self.per = -(-heads // n)
        self.mats = 3 * self.per
        most = max(1, self.per - 1)
        self.chunks = [(0, most), (most, self.per - most)]
        self.early = (most + 2) // 2
        self.pair = min(2, n_dp)
        self.rest = n_dp // self.pair
        self.own = -(-self.mats // n_dp)
        self.block = -(-rows // 16) * 16
        self.packed_rows = 4 * tokens + 6 * self.block
        self.ids = {}
        at = 0
        for name, size in (("to", n), ("from", n), ("head", n), ("rest", self.rest), ("mine", 1), ("place", 1)):
            self.ids[name] = at
            at += size

    def first_head(self, c):
        return min(c * self.per, self.heads - self.per)


def pack_kernel(ids, k_ref, v_ref, q_ref, o_ref, s_ref, t_ref, *refs, plan, slots, chunk):
    t, w = plan.tokens, plan.width
    first, count = plan.chunks[chunk]
    outs, (state, sems) = refs[:-2], refs[-2:]
    loads = []
    copies = []
    for k, slot in enumerate(slots):
        head = ids[plan.ids["head"] + slot] + first
        for i, src in enumerate((s_ref, t_ref.at[0])):
            loads.append(
                pltpu.make_async_copy(src.at[:, pl.ds(head, count)], state.at[k, i], sems.at[k, 4 + i])
            )
            loads[-1].start()
        cols = pl.ds(pl.multiple_of(head * w, w), count * w)
        for i, src in enumerate((k_ref, v_ref, q_ref, o_ref)):
            copies.append(
                pltpu.make_async_copy(src.at[0, :, cols], outs[k].at[pl.ds(i * t, t), :], sems.at[k, i])
            )
            copies[-1].start()
    for k in range(len(slots)):
        for i in range(2):
            loads[2 * k + i].wait()
            for j in range(count):
                for m in range(3):
                    top = 4 * t + (3 * i + m) * plan.block
                    outs[k][top : top + plan.rows, j * w : (j + 1) * w] = state[k, i, m, j].astype(BF16)
    for copy in copies:
        copy.wait()


def tokens_of(refs, j, group, plan):
    t, w = plan.tokens, plan.width
    cols = slice(j * w, (j + 1) * w)
    top = 2 * group * t
    x = jnp.concatenate([r[top : top + t, cols] for r in refs], axis=0)
    y = jnp.concatenate([r[top + t : top + 2 * t, cols] for r in refs], axis=0)
    return x, y


def forward(x, y, wa, wb, wc):
    w = wa.shape[1]
    gu = dot_nn(x, jnp.concatenate([wa, wb], axis=1))
    g, u = gu[:, :w], gu[:, w:]
    p = dot_nn(y, wc)
    _, sw, slope = swish_terms(g)
    hidden = (sw * u).astype(BF16)
    dg = (p * u * slope).astype(BF16)
    du = (p * sw).astype(BF16)
    ab = dot_tn(x, jnp.concatenate([dg, du], axis=1))
    return (ab[:, :w], ab[:, w:], dot_tn(y, hidden)), (g, u, p), (dg, du, hidden)


def chunk_kernel(ids, *refs, plan, chunk):
    n, t, w = plan.n, plan.tokens, plan.width
    first, count = plan.chunks[chunk]
    last = chunk + 1 == len(plan.chunks)
    mats = 3 * count
    refs = list(refs)

    def take(k):
        got = refs[:k]
        del refs[:k]
        return got

    in_refs = take(n)
    before, held = take(2) if last else (None, None)
    d_refs = take(1 if last else 2)
    c_refs = take(2 if last else 1)
    w0, w1, gsum, ssum, acts, fields = take(6)
    total = take(1)[0] if last else c_refs[0]
    base = 3 * first if last else 0

    for slot in range(n):
        at = pl.ds(pl.multiple_of(ids[plan.ids["from"] + slot] * plan.rows, plan.rows), plan.rows)
        for j in range(count):
            for m in range(3):
                for i, dst in enumerate((w0, w1)):
                    top = 4 * t + (3 * i + m) * plan.block
                    part = in_refs[slot][top : top + plan.rows, j * w : (j + 1) * w]
                    dst[3 * j + m, at, :] = part.astype(F32)

    for j in range(count):
        x, y = tokens_of(in_refs, j, 0, plan)
        sums, act, field = forward(x, y, *[w0[3 * j + m].astype(BF16) for m in range(3)])
        for m in range(3):
            gsum[3 * j + m] = sums[m]
            acts[j, m] = act[m]
            fields[j, m] = field[m]
        x, y = tokens_of(in_refs, j, 1, plan)
        sums, _, _ = forward(x, y, *[w1[3 * j + m].astype(BF16) for m in range(3)])
        for m in range(3):
            ssum[3 * j + m] = sums[m]

    grads = [gsum[m] for m in range(mats)]
    updates = [(RATE * ssum[m]).astype(BF16) for m in range(mats)]
    for m, val in enumerate(newton_pullback(grads, updates)):
        gsum[m] = val

    for j in range(count):
        x, y = tokens_of(in_refs, j, 0, plan)
        fab = jnp.concatenate([gsum[3 * j], gsum[3 * j + 1]], axis=1).astype(BF16)
        fc = gsum[3 * j + 2].astype(BF16)
        wab = jnp.concatenate([w0[3 * j], w0[3 * j + 1]], axis=1).astype(BF16)
        wc = w0[3 * j + 2].astype(BF16)
        cdgu = dot_nn(x, fab)
        cdg, cdu = cdgu[:, :w], cdgu[:, w:]
        ch = dot_nn(y, fc)
        g, u, p = acts[j, 0], acts[j, 1], acts[j, 2]
        s, sw, slope = swish_terms(g)
        curve = s * (1.0 - s) * (2.0 + g * (1.0 - 2.0 * s))
        cg = ((ch * u + cdu * p) * slope + cdg * (p * u) * curve).astype(BF16)
        cu = (ch * sw + cdg * p * slope).astype(BF16)
        cp = (cdu * sw + cdg * u * slope).astype(BF16)
        dg, du, hidden = fields[j, 0], fields[j, 1], fields[j, 2]
        dx = dot_nt(jnp.concatenate([dg, du, cg, cu], axis=1), jnp.concatenate([fab, wab], axis=1))
        dy = dot_nt(jnp.concatenate([hidden, cp], axis=1), jnp.concatenate([fc, wc], axis=1))
        if last:
            d_ref, at = d_refs[0], first - plan.early + j
        elif j < plan.early:
            d_ref, at = d_refs[0], j
        else:
            d_ref, at = d_refs[1], j - plan.early
        cols = slice(at * w, (at + 1) * w)
        for slot in range(n):
            to = ids[plan.ids["from"] + slot]
            d_ref[to, 0:t, cols] = dx[slot * t : (slot + 1) * t].astype(BF16)
            d_ref[to, t : 2 * t, cols] = dy[slot * t : (slot + 1) * t].astype(BF16)
        ab = dot_tn(x, jnp.concatenate([cg, cu], axis=1))
        grown = (ab[:, :w], ab[:, w:], dot_tn(y, cp))
        for m in range(3):
            total[base + 3 * j + m] = (ssum[3 * j + m] + grown[m]).astype(BF16)

    if last:
        total[0 : before.shape[0]] = before[...]
        if first > plan.early:
            d_refs[0][:, :, 0 : held.shape[2]] = held[...]
        for m in range(plan.mats, plan.n_dp * plan.own):
            total[m] = jnp.zeros((w, w), BF16)
        mine = ids[plan.ids["mine"]]
        for r in range(plan.rest):
            to = slice(r * plan.own, (r + 1) * plan.own)
            for ref, which in zip(c_refs, (mine, plan.pair - 1 - mine)):
                ref[to] = total[pl.ds((plan.pair * r + which) * plan.own, plan.own)]


def pair_kernel(ids, keep_ref, got_ref, *refs, plan):
    outs, whole = refs[:-1], refs[-1]
    whole[...] = keep_ref[...].astype(F32) + got_ref[...].astype(F32)
    for k in range(plan.rest):
        outs[k][...] = whole[pl.ds(ids[plan.ids["rest"] + k] * plan.own, plan.own)].astype(BF16)


def sum_kernel(ids, *refs, plan):
    parts, outs, whole = refs[: plan.rest], refs[plan.rest : -1], refs[-1]
    added = parts[0][...].astype(F32)
    for part in parts[1:]:
        added = added + part[...].astype(F32)
    whole[...] = added / plan.n_dp
    for slot in range(plan.n):
        at = pl.ds(pl.multiple_of(ids[plan.ids["to"] + slot] * plan.rows, plan.rows), plan.rows)
        outs[slot][...] = whole[:, at, :].astype(BF16)


def order_kernel(ids, *refs, plan, name):
    parts, out = refs[:-1], refs[-1]
    for k, part in enumerate(parts):
        out[ids[plan.ids[name] + k]] = part[...]


def state_kernel(ids, *refs, plan):
    out = refs[-1]
    for k in range(plan.pair):
        for r in range(plan.rest):
            for i in range(plan.own):
                mat = (plan.pair * r + jnp.bitwise_xor(ids[plan.ids["mine"]], k)) * plan.own + i

                @pl.when(mat < plan.mats)
                def _(mat=mat, ref=refs[k], r=r, i=i):
                    for c in range(plan.n):
                        head = plan.first_head(c) + lax.div(mat, 3)
                        out[lax.rem(mat, 3), head] = ref[r, c, i].astype(F32)


def unpack_kernel(*refs, plan):
    t, w = plan.tokens, plan.width
    ins, (dk, dv, sems) = refs[:-3], refs[-3:]
    copies = []
    parts = [(0, plan.early), (plan.early, plan.per - plan.early)]
    for c, (first, count) in enumerate(parts):
        for owner in range(plan.n):
            cols = pl.ds((plan.first_head(owner) + first) * w, count * w)
            for part, dst in enumerate((dk, dv)):
                copy = pltpu.make_async_copy(
                    ins[c].at[owner, pl.ds(part * t, t), :],
                    dst.at[0, :, cols],
                    sems.at[(c * plan.n + owner) * 2 + part],
                )
                copy.start()
                copies.append(copy)
            if plan.n * plan.per != plan.heads:
                for copy in copies:
                    copy.wait()
                copies = []
    for copy in copies:
        copy.wait()


def local(keys_a, values_a, queries_b, grad_out, state_start, state_next):
    n, n_dp = lax.axis_size("ctx"), lax.axis_size("dp")
    _, heads, rows, width = state_start.shape
    t = keys_a.shape[1]
    plan = Plan(n, n_dp, t, heads, rows, width)
    per, own, chunks = plan.per, plan.own, plan.chunks
    bind = lambda kernel, **more: functools.partial(kernel, plan=plan, **more)

    me, dp = lax.axis_index("ctx"), lax.axis_index("dp")
    places = jnp.arange(n, dtype=jnp.int32)
    to_ids = lax.rem(me + places, n)
    place = lax.div(dp, plan.pair)
    ids = jnp.concatenate(
        [
            to_ids,
            lax.rem(me + n - places, n),
            jnp.minimum(to_ids * per, heads - per),
            jnp.bitwise_xor(place, jnp.arange(plan.rest, dtype=jnp.int32)),
            lax.rem(dp, plan.pair).reshape(1),
            place.reshape(1),
        ]
    )

    def swap(value, k):
        if k == 0:
            return value
        return lax.ppermute(value, "dp", [(i, i ^ k) for i in range(n_dp)])

    def shift(value, s):
        if s == 0:
            return value
        return lax.ppermute(value, "ctx", [(i, (i + s) % n) for i in range(n)])

    def turn(value):
        return lax.all_to_all(value, "ctx", split_axis=0, concat_axis=0, tiled=True)

    def shape(*dims, dtype=BF16):
        return jax.ShapeDtypeStruct(dims, dtype)

    def pack(c, slots, keys):
        args = (keys, values_a, queries_b, grad_out, state_start, state_next)
        outs = call(
            bind(pack_kernel, slots=slots, chunk=c),
            [shape(plan.packed_rows, chunks[c][1] * width)] * len(slots),
            (ids, *[pltpu.with_memory_space_constraint(arg, pltpu.HBM) for arg in args]),
            [SMEM] + [HBM] * 6,
            [VMEM] * len(slots),
            f"pack{c}_{slots[0]}",
            [
                pltpu.VMEM((len(slots), 2, 3, chunks[c][1], rows, width), F32),
                pltpu.SemaphoreType.DMA((len(slots), 6)),
            ],
        )
        return list(outs)

    keys = keys_a
    arrived = []
    for c in range(len(chunks)):
        sent = pack(c, range(1, n), keys)
        keys, sent = lax.optimization_barrier((keys_a, sent))
        arrived.append([shift(v, s + 1) for s, v in enumerate(sent)])
    for c in range(len(chunks)):
        arrived[c] = pack(c, range(1), keys) + arrived[c]

    before = []
    early = None
    for c, (_, count) in enumerate(chunks):
        last = c + 1 == len(chunks)
        if last:
            outs = [shape(n, 2 * t, (per - plan.early) * width)] + [shape(plan.rest * own, width, width)] * 2
        else:
            held = max(1, count - plan.early)
            outs = [
                shape(n, 2 * t, plan.early * width),
                shape(n, 2 * t, held * width),
                shape(3 * count, width, width),
            ]
        scratch = [pltpu.VMEM((3 * count, width, width), F32)] * 4 + [
            pltpu.VMEM((count, 3, n * t, width), F32),
            pltpu.VMEM((count, 3, n * t, width), BF16),
        ]
        if last:
            scratch.append(pltpu.VMEM((n_dp * own, width, width), BF16))
        got = call(
            bind(chunk_kernel, chunk=c),
            outs,
            (ids, *arrived[c], *before),
            [SMEM] + [VMEM] * (n + len(before)),
            [VMEM] * len(outs),
            f"chunk{c}",
            scratch,
            flops=count * 640 * 10**6,
            size=count * 10**6,
            vmem=VMEM_LARGE,
        )
        if not last:
            early = got[0]
            before = [got[2], got[1]]
    late, c_keep, c_send = got
    early, c_send = lax.optimization_barrier((early, c_send))
    early = turn(early)

    halves = call(
        bind(pair_kernel),
        [shape(own, width, width)] * plan.rest,
        (ids, c_keep, swap(c_send, plan.pair - 1)),
        [SMEM] + [VMEM] * 2,
        [VMEM] * plan.rest,
        "state_pair",
        [pltpu.VMEM((plan.rest * own, width, width), F32)],
    )
    halves = [swap(halves[k], plan.pair * k) for k in range(plan.rest)]
    by_rows = call(
        bind(sum_kernel),
        [shape(own, rows, width)] * n,
        (ids, *halves),
        [SMEM] + [VMEM] * plan.rest,
        [VMEM] * n,
        "state_sum",
        [pltpu.VMEM((own, width, width), F32)],
    )
    by_rows = [shift(by_rows[s], s) for s in range(n)]
    by_rows[0], early = lax.optimization_barrier((by_rows[0], early))
    mine = call(
        bind(order_kernel, name="from"),
        shape(n, own, rows, width),
        (ids, *by_rows),
        [SMEM] + [VMEM] * n,
        VMEM,
        "state_rows",
    )
    mine, late = lax.optimization_barrier((mine, late))
    late = turn(late)
    rest = [swap(mine, plan.pair * k) for k in range(plan.rest)]
    half = call(
        bind(order_kernel, name="rest"),
        shape(plan.rest, n, own, rows, width),
        (ids, *rest),
        [SMEM] + [VMEM] * plan.rest,
        VMEM,
        "state_rest",
    )
    both = [swap(half, k) for k in range(plan.pair)]
    grad_state = call(
        bind(state_kernel),
        shape(*state_start.shape, dtype=F32),
        (ids, *both),
        [SMEM] + [VMEM] * plan.pair,
        VMEM,
        "state_out",
    )
    grad_keys, grad_values = call(
        bind(unpack_kernel),
        [shape(*keys_a.shape), shape(*values_a.shape)],
        (early, late),
        [VMEM] * 2,
        [ANY] * 2,
        "unpack",
        [pltpu.SemaphoreType.DMA((4 * n,))],
    )
    return grad_keys, grad_values, grad_state


def solution(mesh):
    placed = (
        P("dp", "ctx", None),
        P("dp", "ctx", None),
        P("dp", "ctx", None),
        P("dp", "ctx", None),
        P(None, None, "ctx", None),
        P("dp", None, None, "ctx", None),
    )
    return jax.shard_map(
        local,
        mesh=mesh,
        in_specs=placed,
        out_specs=(P("dp", "ctx", None), P("dp", "ctx", None), P(None, None, "ctx", None)),
        check_vma=False,
    )
```

time: 145 us -> 134 us (0.924)
  starting transfers between devices: 44.9 us -> 36.1 us
  waiting for transfers between devices: 65.8 us -> 71.1 us
  Pallas kernels: 30.1 us -> 25.7 us
  local copies, waits for them, and re-layouts: 2.33 us -> 0.09 us
    all_to_all x3 -> x2, starting transfers between devices: 18.1 us -> 12.5 us  [turn(): return lax.all_to_all(value, 'ctx', split_axis=0, concat_axis=0, tiled=True)]
    pallas_call x15 -> x12, Pallas kernels: 30.1 us -> 25.7 us  [call(): pl.pallas_call(kernel, out_shape=out_shape, in_specs=in_specs, out_specs=...]
    unnamed x12 -> x0, local copies, waits for them, and re-layouts: 2.33 us -> none
    all_to_all x3 -> x2, waiting for transfers between devices: 1.58 us -> 3.67 us  [turn(): return lax.all_to_all(value, 'ctx', split_axis=0, concat_axis=0, tiled=True)]
    ppermute x9, waiting for transfers between devices: 53.8 us -> 55.7 us  [shift(): return lax.ppermute(value, 'ctx', [(i, (i + s) % n) for i in range(n)])]
    ppermute x11 -> x8, starting transfers between devices: 8.74 us -> 7.11 us  [swap(): return lax.ppermute(value, 'dp', [(i, i ^ k) for i in range(n_dp)])]
    ppermute x9, starting transfers between devices: 18 us -> 16.5 us  [shift(): return lax.ppermute(value, 'ctx', [(i, (i + s) % n) for i in range(n)])]
    ppermute x11 -> x8, waiting for transfers between devices: 10.5 us -> 11.7 us  [swap(): return lax.ppermute(value, 'dp', [(i, i ^ k) for i in range(n_dp)])]
  transfers between devices with their start and end apart: 23 -> 19, of which waited for: 16 -> 15; matrix products, arithmetic and copies ran while one was open for 0% -> 0% of each run, Pallas kernels for 17% -> 13%
where the time goes in v2:
time: 134 us
  waiting for transfers between devices  71.1 us (53%)
  starting transfers between devices  36.1 us (27%)
  Pallas kernels  25.7 us (19%)
    ppermute x9, waiting for transfers between devices, shift(): return lax.ppermute(value, 'ctx', [(i, (i + s) % n) for i in range(n)])  55.7 us
    pallas_call x12, Pallas kernels, call(): pl.pallas_call(kernel, out_shape=out_shape, in_specs=in_specs, out_specs=...  25.7 us
    ppermute x9, starting transfers between devices, shift(): return lax.ppermute(value, 'ctx', [(i, (i + s) % n) for i in range(n)])  16.5 us
    all_to_all x2, starting transfers between devices, turn(): return lax.all_to_all(value, 'ctx', split_axis=0, concat_axis=0, tiled=True)  12.5 us
    ppermute x8, waiting for transfers between devices, swap(): return lax.ppermute(value, 'dp', [(i, i ^ k) for i in range(n_dp)])  11.7 us
    ppermute x8, starting transfers between devices, swap(): return lax.ppermute(value, 'dp', [(i, i ^ k) for i in range(n_dp)])  7.11 us
    all_to_all x2, waiting for transfers between devices, turn(): return lax.all_to_all(value, 'ctx', split_axis=0, concat_axis=0, tiled=True)  3.67 us
  transfers between devices with their start and end apart: 19, of which 15 were waited for; matrix products, arithmetic and copies ran while one was open for 0% of the time, Pallas kernels for 13%

profile of v2, /device:TPU:0, one launch (start us, length us, event | category | flops | bytes accessed | tf_op | source)
XLA Modules:
  0.0 133.7 jit_solution(16030906945584006857)
XLA Ops:
  0.7 0.1 concatenate.3.ids
  0.8 2.5 %pack0_1.1 = (bf16[704,512]{1,0:T(8,128)(2,1)S(1)}, bf16[704,512]{1,0:T(8,128)(2,1)S(1)}, bf16[704,512]{1,0:T(8,128)(2,1)S(1)}) custom-call(s32[18]{0:T(128)S(1)} %concatenate.3.ids, bf16[1,128,2560]{2,1,0:T(8,128)(2,1)} %k_ref.4, bf16[1,128,2560]{2,1,0:T(8,128)(2,1)} %v_ref.7, bf16[1,128,2560]{2,1,0:T(8,128)(2,1)} %q_ref.7, bf16[1,128,2560]{2,1,0:T(8,128)(2,1)} %o_ref.7, ...), custom_call_target="tpu_custom_call" | custom-call | flops 1000000 | bytes 1000000 | tf_op jit(solution)/shard_map/pack0_1/pallas_call | solution.py:40
  3.3 3.1 %collective-permute-start.3 = (bf16[704,512]{1,0:T(8,128)(2,1)S(1)}, bf16[704,512]{1,0:T(8,128)(2,1)S(1)}, u32[]{:S(2)}, u32[]{:S(2)}) collective-permute-start(bf16[704,512]{1,0:T(8,128)(2,1)S(1)} %get-tuple-element.50), channel_id=1, source_target_pairs={{0,1},{1,2},{2,3},{3,0},{4,5},{5,6},{6,7},{7,4},{8,9},{9,10},{10,1... | collective-permute-start | bytes 2162696 | tf_op jit(solution)/shard_map/ppermute | solution.py:354
  6.3 2.6 %collective-permute-start.4 = (bf16[704,512]{1,0:T(8,128)(2,1)S(1)}, bf16[704,512]{1,0:T(8,128)(2,1)S(1)}, u32[]{:S(2)}, u32[]{:S(2)}) collective-permute-start(bf16[704,512]{1,0:T(8,128)(2,1)S(1)} %get-tuple-element.51), channel_id=1, source_target_pairs={{0,2},{1,3},{2,0},{3,1},{4,6},{5,7},{6,4},{7,5},{8,10},{9,11},{10,... | collective-permute-start | bytes 2162696 | tf_op jit(solution)/shard_map/ppermute | solution.py:354
  8.9 1.3 %collective-permute-start.5 = (bf16[704,512]{1,0:T(8,128)(2,1)S(1)}, bf16[704,512]{1,0:T(8,128)(2,1)S(1)}, u32[]{:S(2)}, u32[]{:S(2)}) collective-permute-start(bf16[704,512]{1,0:T(8,128)(2,1)S(1)} %get-tuple-element.52), channel_id=1, source_target_pairs={{0,3},{1,0},{2,1},{3,2},{4,7},{5,4},{6,5},{7,6},{8,11},{9,8},{10,9... | collective-permute-start | bytes 2162696 | tf_op jit(solution)/shard_map/ppermute | solution.py:354
  10.3 1.8 %pack1_1.1 = (bf16[704,128]{1,0:T(8,128)(2,1)S(1)}, bf16[704,128]{1,0:T(8,128)(2,1)S(1)}, bf16[704,128]{1,0:T(8,128)(2,1)S(1)}) custom-call(s32[18]{0:T(128)S(1)} %concatenate.3.ids, bf16[1,128,2560]{2,1,0:T(8,128)(2,1)} %k_ref.4, bf16[1,128,2560]{2,1,0:T(8,128)(2,1)} %v_ref.7, bf16[1,128,2560]{2,1,0:T(8,128)(2,1)} %q_ref.7, bf16[1,128,2560]{2,1,0:T(8,128)(2,1)} %o_ref.7, ...), custom_call_target="tpu_custom_call" | custom-call | flops 1000000 | bytes 1000000 | tf_op jit(solution)/shard_map/pack1_1/pallas_call | solution.py:40
  12.1 0.7 collective-permute-start
  12.8 0.3 collective-permute-start.1
  13.1 1.8 %pack0_0.1.refs_0_ = bf16[704,512]{1,0:T(8,128)(2,1)S(1)} custom-call(s32[18]{0:T(128)S(1)} %concatenate.3.ids, bf16[1,128,2560]{2,1,0:T(8,128)(2,1)} %k_ref.4, bf16[1,128,2560]{2,1,0:T(8,128)(2,1)} %v_ref.7, bf16[1,128,2560]{2,1,0:T(8,128)(2,1)} %q_ref.7, bf16[1,128,2560]{2,1,0:T(8,128)(2,1)} %o_ref.7, f32[3,20,32,128]{3,2,1,0:T(8,128)} %s_ref.7, ...), custom_call_target="tpu_custom_call" | custom-call | flops 1000000 | bytes 1000000 | tf_op jit(solution)/shard_map/pack0_0/pallas_call | solution.py:40
  15.0 1.5 %pack1_0.1.refs_0_ = bf16[704,128]{1,0:T(8,128)(2,1)S(1)} custom-call(s32[18]{0:T(128)S(1)} %concatenate.3.ids, bf16[1,128,2560]{2,1,0:T(8,128)(2,1)} %k_ref.4, bf16[1,128,2560]{2,1,0:T(8,128)(2,1)} %v_ref.7, bf16[1,128,2560]{2,1,0:T(8,128)(2,1)} %q_ref.7, bf16[1,128,2560]{2,1,0:T(8,128)(2,1)} %o_ref.7, f32[3,20,32,128]{3,2,1,0:T(8,128)} %s_ref.7, ...), custom_call_target="tpu_custom_call" | custom-call | flops 1000000 | bytes 1000000 | tf_op jit(solution)/shard_map/pack1_0/pallas_call | solution.py:40
  16.5 9.0 %collective-permute-done.3.refs_1_ = bf16[704,512]{1,0:T(8,128)(2,1)S(1)} collective-permute-done((bf16[704,512]{1,0:T(8,128)(2,1)S(1)}, bf16[704,512]{1,0:T(8,128)(2,1)S(1)}, u32[]{:S(2)}, u32[]{:S(2)}) %collective-permute-start.3) | collective-permute-done | bytes 720928 | tf_op jit(solution)/shard_map/ppermute | solution.py:354
  25.5 2.5 %collective-permute-start.2 = (bf16[704,128]{1,0:T(8,128)(2,1)S(1)}, bf16[704,128]{1,0:T(8,128)(2,1)S(1)}, u32[]{:S(2)}, u32[]{:S(2)}) collective-permute-start(bf16[704,128]{1,0:T(8,128)(2,1)S(1)} %get-tuple-element.49), channel_id=1, source_target_pairs={{0,3},{1,0},{2,1},{3,2},{4,7},{5,4},{6,5},{7,6},{8,11},{9,8},{10,9... | collective-permute-start | bytes 540680 | tf_op jit(solution)/shard_map/ppermute | solution.py:354
  28.0 28.5 %collective-permute-done.4.refs_2_ = bf16[704,512]{1,0:T(8,128)(2,1)S(1)} collective-permute-done((bf16[704,512]{1,0:T(8,128)(2,1)S(1)}, bf16[704,512]{1,0:T(8,128)(2,1)S(1)}, u32[]{:S(2)}, u32[]{:S(2)}) %collective-permute-start.4) | collective-permute-done | bytes 720928 | tf_op jit(solution)/shard_map/ppermute | solution.py:354
  56.4 0.0 collective-permute-done.5.refs_3_
  56.4 8.3 %chunk0.1 = (bf16[4,256,384]{2,1,0:T(8,128)(2,1)}, bf16[4,256,128]{2,1,0:T(8,128)(2,1)S(1)}, bf16[12,128,128]{2,1,0:T(8,128)(2,1)S(1)}) custom-call(s32[18]{0:T(128)S(1)} %concatenate.3.ids, bf16[704,512]{1,0:T(8,128)(2,1)S(1)} %pack0_0.1.refs_0_, bf16[704,512]{1,0:T(8,128)(2,1)S(1)} %collective-permute-done.3.refs_1_, ...), custom_call_target="tpu_custom_call" | custom-call | flops 2560000000 | bytes 4000000 | tf_op jit(solution)/shard_map/chunk0/pallas_call | solution.py:40
  64.7 0.0 collective-permute-done.refs_1_
  64.7 17.9 %collective-permute-done.1.refs_2_ = bf16[704,128]{1,0:T(8,128)(2,1)S(1)} collective-permute-done((bf16[704,128]{1,0:T(8,128)(2,1)S(1)}, bf16[704,128]{1,0:T(8,128)(2,1)S(1)}, u32[]{:S(2)}, u32[]{:S(2)}) %collective-permute-start.1) | collective-permute-done | bytes 180256 | tf_op jit(solution)/shard_map/ppermute | solution.py:354
  82.6 4.5 %chunk1.1 = (bf16[4,256,256]{2,1,0:T(8,128)(2,1)}, bf16[8,128,128]{2,1,0:T(8,128)(2,1)S(1)}, bf16[8,128,128]{2,1,0:T(8,128)(2,1)S(1)}) custom-call(s32[18]{0:T(128)S(1)} %concatenate.3.ids, bf16[704,128]{1,0:T(8,128)(2,1)S(1)} %pack1_0.1.refs_0_, bf16[704,128]{1,0:T(8,128)(2,1)S(1)} %collective-permute-done.refs_1_, ...), custom_call_target="tpu_custom_call" | custom-call | flops 640000000 | bytes 1000000 | tf_op jit(solution)/shard_map/chunk1/pallas_call | solution.py:40
  87.1 8.3 %all-to-all-start = ((bf16[4,256,384]{2,1,0:T(8,128)(2,1)}), bf16[4,256,384]{2,1,0:T(8,128)(2,1)S(1)}, u32[]{:S(2)}, u32[]{:S(2)}) async-start(bf16[4,256,384]{2,1,0:T(8,128)(2,1)} %get-tuple-element.64), calls=%async_computation | async-start | bytes 1572864 | tf_op jit(solution)/shard_map/all_to_all | solution.py:357
  95.4 1.5 %collective-permute-done.6.got_ref = bf16[8,128,128]{2,1,0:T(8,128)(2,1)S(1)} collective-permute-done((bf16[8,128,128]{2,1,0:T(8,128)(2,1)S(1)}, bf16[8,128,128]{2,1,0:T(8,128)(2,1)S(1)}, u32[]{:S(2)}, u32[]{:S(2)}) %collective-permute-start.6) | collective-permute-done | bytes 262176 | tf_op jit(solution)/shard_map/ppermute | solution.py:349
  97.0 0.6 state_pair.1
  97.6 1.6 %collective-permute-start.7 = (bf16[2,128,128]{2,1,0:T(8,128)(2,1)S(1)}, bf16[2,128,128]{2,1,0:T(8,128)(2,1)S(1)}, u32[]{:S(2)}, u32[]{:S(2)}) collective-permute-start(bf16[2,128,128]{2,1,0:T(8,128)(2,1)S(1)} %get-tuple-element.60), channel_id=1, source_target_pairs={{0,8},{4,12},{8,0},{12,4},{16,24},{20,28},{24,16},{28,20},{1,9},{5... | collective-permute-start | bytes 196616 | tf_op jit(solution)/shard_map/ppermute | solution.py:349
  99.2 1.5 %collective-permute-start.8 = (bf16[2,128,128]{2,1,0:T(8,128)(2,1)S(1)}, bf16[2,128,128]{2,1,0:T(8,128)(2,1)S(1)}, u32[]{:S(2)}, u32[]{:S(2)}) collective-permute-start(bf16[2,128,128]{2,1,0:T(8,128)(2,1)S(1)} %get-tuple-element.61), channel_id=1, source_target_pairs={{0,16},{4,20},{8,24},{12,28},{16,0},{20,4},{24,8},{28,12},{1,17},{... | collective-permute-start | bytes 196616 | tf_op jit(solution)/shard_map/ppermute | solution.py:349
  100.7 0.5 collective-permute-start.9
  101.2 0.8 collective-permute-done.7.refs_1_
  101.9 1.5 %collective-permute-done.8.refs_2_ = bf16[2,128,128]{2,1,0:T(8,128)(2,1)S(1)} collective-permute-done((bf16[2,128,128]{2,1,0:T(8,128)(2,1)S(1)}, bf16[2,128,128]{2,1,0:T(8,128)(2,1)S(1)}, u32[]{:S(2)}, u32[]{:S(2)}) %collective-permute-start.8) | collective-permute-done | bytes 65568 | tf_op jit(solution)/shard_map/ppermute | solution.py:349
  103.4 2.4 %collective-permute-done.9.refs_3_ = bf16[2,128,128]{2,1,0:T(8,128)(2,1)S(1)} collective-permute-done((bf16[2,128,128]{2,1,0:T(8,128)(2,1)S(1)}, bf16[2,128,128]{2,1,0:T(8,128)(2,1)S(1)}, u32[]{:S(2)}, u32[]{:S(2)}) %collective-permute-start.9) | collective-permute-done | bytes 65568 | tf_op jit(solution)/shard_map/ppermute | solution.py:349
  105.9 0.6 state_sum.1
  106.4 2.1 %collective-permute-start.10 = (bf16[2,32,128]{2,1,0:T(8,128)(2,1)S(1)}, bf16[2,32,128]{2,1,0:T(8,128)(2,1)S(1)}, u32[]{:S(2)}, u32[]{:S(2)}) collective-permute-start(bf16[2,32,128]{2,1,0:T(8,128)(2,1)S(1)} %get-tuple-element.67), channel_id=1, source_target_pairs={{0,1},{1,2},{2,3},{3,0},{4,5},{5,6},{6,7},{7,4},{8,9},{9,10},{10,1... | collective-permute-start | bytes 49160 | tf_op jit(solution)/shard_map/ppermute | solution.py:354
  108.5 2.4 %collective-permute-start.11 = (bf16[2,32,128]{2,1,0:T(8,128)(2,1)S(1)}, bf16[2,32,128]{2,1,0:T(8,128)(2,1)S(1)}, u32[]{:S(2)}, u32[]{:S(2)}) collective-permute-start(bf16[2,32,128]{2,1,0:T(8,128)(2,1)S(1)} %get-tuple-element.68), channel_id=1, source_target_pairs={{0,2},{1,3},{2,0},{3,1},{4,6},{5,7},{6,4},{7,5},{8,10},{9,11},{10,... | collective-permute-start | bytes 49160 | tf_op jit(solution)/shard_map/ppermute | solution.py:354
  110.9 1.5 %collective-permute-start.12 = (bf16[2,32,128]{2,1,0:T(8,128)(2,1)S(1)}, bf16[2,32,128]{2,1,0:T(8,128)(2,1)S(1)}, u32[]{:S(2)}, u32[]{:S(2)}) collective-permute-start(bf16[2,32,128]{2,1,0:T(8,128)(2,1)S(1)} %get-tuple-element.69), channel_id=1, source_target_pairs={{0,3},{1,0},{2,1},{3,2},{4,7},{5,4},{6,5},{7,6},{8,11},{9,8},{10,9... | collective-permute-start | bytes 49160 | tf_op jit(solution)/shard_map/ppermute | solution.py:354
  112.3 2.3 %all-to-all-done.refs_0_ = bf16[4,256,384]{2,1,0:T(8,128)(2,1)S(1)} async-done(((bf16[4,256,384]{2,1,0:T(8,128)(2,1)}), bf16[4,256,384]{2,1,0:T(8,128)(2,1)S(1)}, u32[]{:S(2)}, u32[]{:S(2)}) %all-to-all-start) | async-done | bytes 786464 | tf_op jit(solution)/shard_map/all_to_all | solution.py:357
  114.7 0.2 collective-permute-done.11.refs_2_
  114.8 0.1 collective-permute-done.12.refs_3_
  115.0 0.5 state_rows.1.refs_0_
  115.5 4.2 %all-to-all-start.1 = ((bf16[4,256,256]{2,1,0:T(8,128)(2,1)}), bf16[4,256,256]{2,1,0:T(8,128)(2,1)S(1)}, u32[]{:S(2)}, u32[]{:S(2)}) async-start(bf16[4,256,256]{2,1,0:T(8,128)(2,1)} %get-tuple-element.71), calls=%async_computation.1 | async-start | bytes 1048576 | tf_op jit(solution)/shard_map/all_to_all | solution.py:357
  119.7 0.8 collective-permute-start.13
  120.5 1.5 %collective-permute-start.14 = (bf16[4,2,32,128]{3,2,1,0:T(8,128)(2,1)S(1)}, bf16[4,2,32,128]{3,2,1,0:T(8,128)(2,1)S(1)}, u32[]{:S(2)}, u32[]{:S(2)}) collective-permute-start(bf16[4,2,32,128]{3,2,1,0:T(8,128)(2,1)S(1)} %state_rows.1.refs_0_), channel_id=1, source_target_pairs={{0,16},{4,20},{8,24},{12,28},{16,0},{20,4},{24,8},{28,12},{1,17},{... | collective-permute-start | bytes 196616 | tf_op jit(solution)/shard_map/ppermute | solution.py:349
  122.0 1.2 collective-permute-start.15
  123.2 0.8 collective-permute-done.13.refs_1_
  124.0 1.2 collective-permute-done.14.refs_2_
  125.2 2.0 %collective-permute-done.15.refs_3_ = bf16[4,2,32,128]{3,2,1,0:T(8,128)(2,1)S(1)} collective-permute-done((bf16[4,2,32,128]{3,2,1,0:T(8,128)(2,1)S(1)}, bf16[4,2,32,128]{3,2,1,0:T(8,128)(2,1)S(1)}, u32[]{:S(2)}, u32[]{:S(2)}) %collective-permute-start.15) | collective-permute-done | bytes 65568 | tf_op jit(solution)/shard_map/ppermute | solution.py:349
  127.2 0.6 state_rest.1.refs_0_
  127.8 0.1 collective-permute-start.16
  127.9 1.5 %collective-permute-done.16.refs_1_ = bf16[4,4,2,32,128]{4,3,2,1,0:T(8,128)(2,1)S(1)} collective-permute-done((bf16[4,4,2,32,128]{4,3,2,1,0:T(8,128)(2,1)S(1)}, bf16[4,4,2,32,128]{4,3,2,1,0:T(8,128)(2,1)S(1)}, u32[]{:S(2)}, u32[]{:S(2)}) %collective-permute-start.16) | collective-permute-done | bytes 262176 | tf_op jit(solution)/shard_map/ppermute | solution.py:349
  129.4 1.8 %state_out.1 = f32[3,20,32,128]{3,2,1,0:T(8,128)} custom-call(s32[18]{0:T(128)S(1)} %concatenate.3.ids, bf16[4,4,2,32,128]{4,3,2,1,0:T(8,128)(2,1)S(1)} %state_rest.1.refs_0_, bf16[4,4,2,32,128]{4,3,2,1,0:T(8,128)(2,1)S(1)} %collective-permute-done.16.refs_1_), custom_call_target="tpu_custom_call" | custom-call | flops 1000000 | bytes 1000000 | tf_op jit(solution)/shard_map/state_out/pallas_call | solution.py:40
  131.2 1.4 %all-to-all-done.1.refs_1_ = bf16[4,256,256]{2,1,0:T(8,128)(2,1)S(1)} async-done(((bf16[4,256,256]{2,1,0:T(8,128)(2,1)}), bf16[4,256,256]{2,1,0:T(8,128)(2,1)S(1)}, u32[]{:S(2)}, u32[]{:S(2)}) %all-to-all-start.1) | async-done | bytes 524320 | tf_op jit(solution)/shard_map/all_to_all | solution.py:357
  132.5 1.2 unpack.1
  (5 shorter events, 0.0 us)
Async XLA Ops:
  3.3 22.2 %collective-permute-start.3 = (bf16[704,512]{1,0:T(8,128)(2,1)S(1)}, bf16[704,512]{1,0:T(8,128)(2,1)S(1)}, u32[]{:S(2)}, u32[]{:S(2)}) collective-permute-start(bf16[704,512]{1,0:T(8,128)(2,1)S(1)} %get-tuple-element.50), channel_id=1, source_target_pairs={{0,1},{1,2},{2,3},{3,0},{4,5},{5,6},{6,7},{7,4},{8,9},{9,10},{10,1... | collective-permute-start | bytes 2162696 | tf_op jit(solution)/shard_map/ppermute | solution.py:354
  6.3 50.1 %collective-permute-start.4 = (bf16[704,512]{1,0:T(8,128)(2,1)S(1)}, bf16[704,512]{1,0:T(8,128)(2,1)S(1)}, u32[]{:S(2)}, u32[]{:S(2)}) collective-permute-start(bf16[704,512]{1,0:T(8,128)(2,1)S(1)} %get-tuple-element.51), channel_id=1, source_target_pairs={{0,2},{1,3},{2,0},{3,1},{4,6},{5,7},{6,4},{7,5},{8,10},{9,11},{10,... | collective-permute-start | bytes 2162696 | tf_op jit(solution)/shard_map/ppermute | solution.py:354
  8.9 47.5 %collective-permute-start.5 = (bf16[704,512]{1,0:T(8,128)(2,1)S(1)}, bf16[704,512]{1,0:T(8,128)(2,1)S(1)}, u32[]{:S(2)}, u32[]{:S(2)}) collective-permute-start(bf16[704,512]{1,0:T(8,128)(2,1)S(1)} %get-tuple-element.52), channel_id=1, source_target_pairs={{0,3},{1,0},{2,1},{3,2},{4,7},{5,4},{6,5},{7,6},{8,11},{9,8},{10,9... | collective-permute-start | bytes 2162696 | tf_op jit(solution)/shard_map/ppermute | solution.py:354
  12.1 52.7 %collective-permute-start = (bf16[704,128]{1,0:T(8,128)(2,1)S(1)}, bf16[704,128]{1,0:T(8,128)(2,1)S(1)}, u32[]{:S(2)}, u32[]{:S(2)}) collective-permute-start(bf16[704,128]{1,0:T(8,128)(2,1)S(1)} %get-tuple-element.47), channel_id=1, source_target_pairs={{0,1},{1,2},{2,3},{3,0},{4,5},{5,6},{6,7},{7,4},{8,9},{9,10},{10,1... | collective-permute-start | bytes 540680 | tf_op jit(solution)/shard_map/ppermute | solution.py:354
  12.8 69.8 %collective-permute-start.1 = (bf16[704,128]{1,0:T(8,128)(2,1)S(1)}, bf16[704,128]{1,0:T(8,128)(2,1)S(1)}, u32[]{:S(2)}, u32[]{:S(2)}) collective-permute-start(bf16[704,128]{1,0:T(8,128)(2,1)S(1)} %get-tuple-element.48), channel_id=1, source_target_pairs={{0,2},{1,3},{2,0},{3,1},{4,6},{5,7},{6,4},{7,5},{8,10},{9,11},{10,... | collective-permute-start | bytes 540680 | tf_op jit(solution)/shard_map/ppermute | solution.py:354
  25.5 57.1 %collective-permute-start.2 = (bf16[704,128]{1,0:T(8,128)(2,1)S(1)}, bf16[704,128]{1,0:T(8,128)(2,1)S(1)}, u32[]{:S(2)}, u32[]{:S(2)}) collective-permute-start(bf16[704,128]{1,0:T(8,128)(2,1)S(1)} %get-tuple-element.49), channel_id=1, source_target_pairs={{0,3},{1,0},{2,1},{3,2},{4,7},{5,4},{6,5},{7,6},{8,11},{9,8},{10,9... | collective-permute-start | bytes 540680 | tf_op jit(solution)/shard_map/ppermute | solution.py:354
  87.1 27.5 %all-to-all-start = ((bf16[4,256,384]{2,1,0:T(8,128)(2,1)}), bf16[4,256,384]{2,1,0:T(8,128)(2,1)S(1)}, u32[]{:S(2)}, u32[]{:S(2)}) async-start(bf16[4,256,384]{2,1,0:T(8,128)(2,1)} %get-tuple-element.64), calls=%async_computation | async-start | bytes 1572864 | tf_op jit(solution)/shard_map/all_to_all | solution.py:357
  95.4 1.5 %collective-permute-start.6 = (bf16[8,128,128]{2,1,0:T(8,128)(2,1)S(1)}, bf16[8,128,128]{2,1,0:T(8,128)(2,1)S(1)}, u32[]{:S(2)}, u32[]{:S(2)}) collective-permute-start(bf16[8,128,128]{2,1,0:T(8,128)(2,1)S(1)} %get-tuple-element.58), channel_id=1, source_target_pairs={{0,4},{4,0},{8,12},{12,8},{16,20},{20,16},{24,28},{28,24},{1,5},{5... | collective-permute-start | bytes 786440 | tf_op jit(solution)/shard_map/ppermute | solution.py:349
  97.6 4.3 %collective-permute-start.7 = (bf16[2,128,128]{2,1,0:T(8,128)(2,1)S(1)}, bf16[2,128,128]{2,1,0:T(8,128)(2,1)S(1)}, u32[]{:S(2)}, u32[]{:S(2)}) collective-permute-start(bf16[2,128,128]{2,1,0:T(8,128)(2,1)S(1)} %get-tuple-element.60), channel_id=1, source_target_pairs={{0,8},{4,12},{8,0},{12,4},{16,24},{20,28},{24,16},{28,20},{1,9},{5... | collective-permute-start | bytes 196616 | tf_op jit(solution)/shard_map/ppermute | solution.py:349
  99.2 4.3 %collective-permute-start.8 = (bf16[2,128,128]{2,1,0:T(8,128)(2,1)S(1)}, bf16[2,128,128]{2,1,0:T(8,128)(2,1)S(1)}, u32[]{:S(2)}, u32[]{:S(2)}) collective-permute-start(bf16[2,128,128]{2,1,0:T(8,128)(2,1)S(1)} %get-tuple-element.61), channel_id=1, source_target_pairs={{0,16},{4,20},{8,24},{12,28},{16,0},{20,4},{24,8},{28,12},{1,17},{... | collective-permute-start | bytes 196616 | tf_op jit(solution)/shard_map/ppermute | solution.py:349
  100.7 5.2 %collective-permute-start.9 = (bf16[2,128,128]{2,1,0:T(8,128)(2,1)S(1)}, bf16[2,128,128]{2,1,0:T(8,128)(2,1)S(1)}, u32[]{:S(2)}, u32[]{:S(2)}) collective-permute-start(bf16[2,128,128]{2,1,0:T(8,128)(2,1)S(1)} %get-tuple-element.62), channel_id=1, source_target_pairs={{0,24},{4,28},{8,16},{12,20},{16,8},{20,12},{24,0},{28,4},{1,25},{... | collective-permute-start | bytes 196616 | tf_op jit(solution)/shard_map/ppermute | solution.py:349
  106.4 8.2 %collective-permute-start.10 = (bf16[2,32,128]{2,1,0:T(8,128)(2,1)S(1)}, bf16[2,32,128]{2,1,0:T(8,128)(2,1)S(1)}, u32[]{:S(2)}, u32[]{:S(2)}) collective-permute-start(bf16[2,32,128]{2,1,0:T(8,128)(2,1)S(1)} %get-tuple-element.67), channel_id=1, source_target_pairs={{0,1},{1,2},{2,3},{3,0},{4,5},{5,6},{6,7},{7,4},{8,9},{9,10},{10,1... | collective-permute-start | bytes 49160 | tf_op jit(solution)/shard_map/ppermute | solution.py:354
  108.5 6.3 %collective-permute-start.11 = (bf16[2,32,128]{2,1,0:T(8,128)(2,1)S(1)}, bf16[2,32,128]{2,1,0:T(8,128)(2,1)S(1)}, u32[]{:S(2)}, u32[]{:S(2)}) collective-permute-start(bf16[2,32,128]{2,1,0:T(8,128)(2,1)S(1)} %get-tuple-element.68), channel_id=1, source_target_pairs={{0,2},{1,3},{2,0},{3,1},{4,6},{5,7},{6,4},{7,5},{8,10},{9,11},{10,... | collective-permute-start | bytes 49160 | tf_op jit(solution)/shard_map/ppermute | solution.py:354
  110.9 4.1 %collective-permute-start.12 = (bf16[2,32,128]{2,1,0:T(8,128)(2,1)S(1)}, bf16[2,32,128]{2,1,0:T(8,128)(2,1)S(1)}, u32[]{:S(2)}, u32[]{:S(2)}) collective-permute-start(bf16[2,32,128]{2,1,0:T(8,128)(2,1)S(1)} %get-tuple-element.69), channel_id=1, source_target_pairs={{0,3},{1,0},{2,1},{3,2},{4,7},{5,4},{6,5},{7,6},{8,11},{9,8},{10,9... | collective-permute-start | bytes 49160 | tf_op jit(solution)/shard_map/ppermute | solution.py:354
  115.5 17.0 %all-to-all-start.1 = ((bf16[4,256,256]{2,1,0:T(8,128)(2,1)}), bf16[4,256,256]{2,1,0:T(8,128)(2,1)S(1)}, u32[]{:S(2)}, u32[]{:S(2)}) async-start(bf16[4,256,256]{2,1,0:T(8,128)(2,1)} %get-tuple-element.71), calls=%async_computation.1 | async-start | bytes 1048576 | tf_op jit(solution)/shard_map/all_to_all | solution.py:357
  119.7 4.3 %collective-permute-start.13 = (bf16[4,2,32,128]{3,2,1,0:T(8,128)(2,1)S(1)}, bf16[4,2,32,128]{3,2,1,0:T(8,128)(2,1)S(1)}, u32[]{:S(2)}, u32[]{:S(2)}) collective-permute-start(bf16[4,2,32,128]{3,2,1,0:T(8,128)(2,1)S(1)} %state_rows.1.refs_0_), channel_id=1, source_target_pairs={{0,8},{4,12},{8,0},{12,4},{16,24},{20,28},{24,16},{28,20},{1,9},{5... | collective-permute-start | bytes 196616 | tf_op jit(solution)/shard_map/ppermute | solution.py:349
  120.5 4.7 %collective-permute-start.14 = (bf16[4,2,32,128]{3,2,1,0:T(8,128)(2,1)S(1)}, bf16[4,2,32,128]{3,2,1,0:T(8,128)(2,1)S(1)}, u32[]{:S(2)}, u32[]{:S(2)}) collective-permute-start(bf16[4,2,32,128]{3,2,1,0:T(8,128)(2,1)S(1)} %state_rows.1.refs_0_), channel_id=1, source_target_pairs={{0,16},{4,20},{8,24},{12,28},{16,0},{20,4},{24,8},{28,12},{1,17},{... | collective-permute-start | bytes 196616 | tf_op jit(solution)/shard_map/ppermute | solution.py:349
  122.0 5.2 %collective-permute-start.15 = (bf16[4,2,32,128]{3,2,1,0:T(8,128)(2,1)S(1)}, bf16[4,2,32,128]{3,2,1,0:T(8,128)(2,1)S(1)}, u32[]{:S(2)}, u32[]{:S(2)}) collective-permute-start(bf16[4,2,32,128]{3,2,1,0:T(8,128)(2,1)S(1)} %state_rows.1.refs_0_), channel_id=1, source_target_pairs={{0,24},{4,28},{8,16},{12,20},{16,8},{20,12},{24,0},{28,4},{1,25},{... | collective-permute-start | bytes 196616 | tf_op jit(solution)/shard_map/ppermute | solution.py:349
  127.8 1.6 %collective-permute-start.16 = (bf16[4,4,2,32,128]{4,3,2,1,0:T(8,128)(2,1)S(1)}, bf16[4,4,2,32,128]{4,3,2,1,0:T(8,128)(2,1)S(1)}, u32[]{:S(2)}, u32[]{:S(2)}) collective-permute-start(bf16[4,4,2,32,128]{4,3,2,1,0:T(8,128)(2,1)S(1)} %state_rest.1.refs_0_), channel_id=1, source_target_pairs={{0,4},{4,0},{8,12},{12,8},{16,20},{20,16},{24,28},{28,24},{1,5},{5... | collective-permute-start | bytes 786440 | tf_op jit(solution)/shard_map/ppermute | solution.py:349

commit v3 on v2

--- a/solution.py
+++ b/solution.py
@@ -102,12 +102,16 @@
         self.rest = n_dp // self.pair
         self.own = -(-self.mats // n_dp)
         self.block = -(-rows // 16) * 16
-        self.packed_rows = 4 * tokens + 6 * self.block
+        self.share = -(-3 * most // self.pair)
+        self.share_blocks = -(-self.share // most)
         self.ids = {}
         at = 0
         for name, size in (("to", n), ("from", n), ("head", n), ("rest", self.rest), ("mine", 1), ("place", 1)):
             self.ids[name] = at
             at += size
+
+    def packed_rows(self, chunk):
+        return 4 * self.tokens + (3 + (self.share_blocks if chunk == 0 else 3)) * self.block
 
     def first_head(self, c):
         return min(c * self.per, self.heads - self.per)
@@ -133,14 +137,35 @@
             )
             copies[-1].start()
     for k in range(len(slots)):
-        for i in range(2):
-            loads[2 * k + i].wait()
-            for j in range(count):
-                for m in range(3):
-                    top = 4 * t + (3 * i + m) * plan.block
-                    outs[k][top : top + plan.rows, j * w : (j + 1) * w] = state[k, i, m, j].astype(BF16)
+        loads[2 * k].wait()
+        loads[2 * k + 1].wait()
+        for j in range(count):
+            for m in range(3):
+                top = 4 * t + m * plan.block
+                outs[k][top : top + plan.rows, j * w : (j + 1) * w] = state[k, 1, m, j].astype(BF16)
+                if chunk > 0:
+                    top += 3 * plan.block
+                    outs[k][top : top + plan.rows, j * w : (j + 1) * w] = state[k, 0, m, j].astype(BF16)
+        for q in range(plan.share if chunk == 0 else 0):
+            mat = jnp.minimum(ids[plan.ids["mine"]] * plan.share + q, 3 * count - 1)
+            top = 4 * t + (3 + q // count) * plan.block
+            left = (q % count) * w
+            part = state[k, 0, lax.rem(mat, 3), lax.div(mat, 3)]
+            outs[k][top : top + plan.rows, left : left + w] = part.astype(BF16)
     for copy in copies:
         copy.wait()
+
+
+def start_kernel(ids, *refs, plan):
+    in_refs, (out, whole) = refs[: plan.n], refs[plan.n :]
+    count, w = plan.chunks[0][1], plan.width
+    for slot in range(plan.n):
+        at = pl.ds(pl.multiple_of(ids[plan.ids["from"] + slot] * plan.rows, plan.rows), plan.rows)
+        for q in range(plan.share):
+            top = 4 * plan.tokens + (3 + q // count) * plan.block
+            left = (q % count) * w
+            whole[q, at, :] = in_refs[slot][top : top + plan.rows, left : left + w].astype(F32)
+    out[...] = whole[...].astype(BF16)
 
 
 def tokens_of(refs, j, group, plan):
@@ -179,6 +204,7 @@
 
     in_refs = take(n)
     before, held = take(2) if last else (None, None)
+    shares = take(0 if last else plan.pair)
     d_refs = take(1 if last else 2)
     c_refs = take(2 if last else 1)
     w0, w1, gsum, ssum, acts, fields = take(6)
@@ -189,10 +215,13 @@
         at = pl.ds(pl.multiple_of(ids[plan.ids["from"] + slot] * plan.rows, plan.rows), plan.rows)
         for j in range(count):
             for m in range(3):
-                for i, dst in enumerate((w0, w1)):
+                for i, dst in enumerate((w1, w0) if last else (w1,)):
                     top = 4 * t + (3 * i + m) * plan.block
                     part = in_refs[slot][top : top + plan.rows, j * w : (j + 1) * w]
                     dst[3 * j + m, at, :] = part.astype(F32)
+    for k, part in enumerate(shares):
+        at = jnp.bitwise_xor(ids[plan.ids["mine"]], k) * plan.share
+        w0[pl.ds(at, plan.share)] = part[...].astype(F32)
 
     for j in range(count):
         x, y = tokens_of(in_refs, j, 0, plan)
@@ -363,7 +392,7 @@
         args = (keys, values_a, queries_b, grad_out, state_start, state_next)
         outs = call(
             bind(pack_kernel, slots=slots, chunk=c),
-            [shape(plan.packed_rows, chunks[c][1] * width)] * len(slots),
+            [shape(plan.packed_rows(c), chunks[c][1] * width)] * len(slots),
             (ids, *[pltpu.with_memory_space_constraint(arg, pltpu.HBM) for arg in args]),
             [SMEM] + [HBM] * 6,
             [VMEM] * len(slots),
@@ -375,17 +404,25 @@
         )
         return list(outs)
 
-    keys = keys_a
-    arrived = []
-    for c in range(len(chunks)):
-        sent = pack(c, range(1, n), keys)
-        keys, sent = lax.optimization_barrier((keys_a, sent))
-        arrived.append([shift(v, s + 1) for s, v in enumerate(sent)])
-    for c in range(len(chunks)):
-        arrived[c] = pack(c, range(1), keys) + arrived[c]
-
-    before = []
-    early = None
+    sent = pack(0, range(1, n), keys_a)
+    keys, sent = lax.optimization_barrier((keys_a, sent))
+    arrived = [[shift(v, s + 1) for s, v in enumerate(sent)]]
+    sent = pack(1, range(1, n), keys)
+    sent, arrived[0][0] = lax.optimization_barrier((sent, arrived[0][0]))
+    arrived.append([shift(v, s + 1) for s, v in enumerate(sent)])
+    arrived = [pack(c, range(1), keys) + arrived[c] for c in range(2)]
+    start_own = call(
+        bind(start_kernel),
+        shape(plan.share, width, width),
+        (ids, *arrived[0]),
+        [SMEM] + [VMEM] * n,
+        VMEM,
+        "start_share",
+        [pltpu.VMEM((plan.share, width, width), F32)],
+    )
+    shares = [swap(start_own, k) for k in range(plan.pair)]
+
+    before = shares
     for c, (_, count) in enumerate(chunks):
         last = c + 1 == len(chunks)
         if last:
@@ -397,7 +434,8 @@
                 shape(n, 2 * t, held * width),
                 shape(3 * count, width, width),
             ]
-        scratch = [pltpu.VMEM((3 * count, width, width), F32)] * 4 + [
+        weights = 3 * count if last else plan.pair * plan.share
+        scratch = [pltpu.VMEM((weights, width, width), F32)] + [pltpu.VMEM((3 * count, width, width), F32)] * 3 + [
             pltpu.VMEM((count, 3, n * t, width), F32),
             pltpu.VMEM((count, 3, n * t, width), BF16),
         ]

time: 134 us -> 137 us (1.022)
  starting transfers between devices: 36.1 us -> 47.7 us
  waiting for transfers between devices: 71.1 us -> 61.4 us
    ppermute x9, starting transfers between devices: 16.5 us -> 30.6 us  [shift(): return lax.ppermute(value, 'ctx', [(i, (i + s) % n) for i in range(n)])]
    ppermute x9, waiting for transfers between devices: 55.7 us -> 43 us  [shift(): return lax.ppermute(value, 'ctx', [(i, (i + s) % n) for i in range(n)])]
    all_to_all x2, waiting for transfers between devices: 3.67 us -> 6.91 us  [turn(): return lax.all_to_all(value, 'ctx', split_axis=0, concat_axis=0, tiled=True)]
    all_to_all x2, starting transfers between devices: 12.5 us -> 9.84 us  [turn(): return lax.all_to_all(value, 'ctx', split_axis=0, concat_axis=0, tiled=True)]
    pallas_call x12 -> x13, Pallas kernels: 25.7 us -> 26.3 us  [call(): pl.pallas_call(kernel, out_shape=out_shape, in_specs=in_specs, out_specs=...]
    ppermute x8 -> x9, waiting for transfers between devices: 11.7 us -> 11.5 us  [swap(): return lax.ppermute(value, 'dp', [(i, i ^ k) for i in range(n_dp)])]
    ppermute x8 -> x9, starting transfers between devices: 7.11 us -> 7.25 us  [swap(): return lax.ppermute(value, 'dp', [(i, i ^ k) for i in range(n_dp)])]
  transfers between devices with their start and end apart: 19 -> 20, of which waited for: 15 -> 14; matrix products, arithmetic and copies ran while one was open for 0% -> 0% of each run, Pallas kernels for 13% -> 12%
where the time goes in v3:
time: 137 us; the launch traced here: 136 us
  waiting for transfers between devices  61.4 us (45%)
  starting transfers between devices  47.7 us (35%)
  Pallas kernels  26.3 us (19%)
    ppermute x9, waiting for transfers between devices, shift(): return lax.ppermute(value, 'ctx', [(i, (i + s) % n) for i in range(n)])  43 us
    ppermute x9, starting transfers between devices, shift(): return lax.ppermute(value, 'ctx', [(i, (i + s) % n) for i in range(n)])  30.6 us
    pallas_call x13, Pallas kernels, call(): pl.pallas_call(kernel, out_shape=out_shape, in_specs=in_specs, out_specs=...  26.3 us
    ppermute x9, waiting for transfers between devices, swap(): return lax.ppermute(value, 'dp', [(i, i ^ k) for i in range(n_dp)])  11.5 us
    all_to_all x2, starting transfers between devices, turn(): return lax.all_to_all(value, 'ctx', split_axis=0, concat_axis=0, tiled=True)  9.84 us
    ppermute x9, starting transfers between devices, swap(): return lax.ppermute(value, 'dp', [(i, i ^ k) for i in range(n_dp)])  7.25 us
    all_to_all x2, waiting for transfers between devices, turn(): return lax.all_to_all(value, 'ctx', split_axis=0, concat_axis=0, tiled=True)  6.91 us
  transfers between devices with their start and end apart: 20, of which 14 were waited for; matrix products, arithmetic and copies ran while one was open for 0% of the time, Pallas kernels for 12%

profile of v3, /device:TPU:0, one launch (start us, length us, event | category | flops | bytes accessed | tf_op | source)
XLA Modules:
  0.0 136.2 jit_solution(10333212140229393235)
XLA Ops:
  0.7 0.1 concatenate.3.ids
  0.8 2.5 %pack0_1.1 = (bf16[672,512]{1,0:T(8,128)(2,1)S(1)}, bf16[672,512]{1,0:T(8,128)(2,1)S(1)}, bf16[672,512]{1,0:T(8,128)(2,1)S(1)}) custom-call(s32[18]{0:T(128)S(1)} %concatenate.3.ids, bf16[1,128,2560]{2,1,0:T(8,128)(2,1)} %k_ref.4, bf16[1,128,2560]{2,1,0:T(8,128)(2,1)} %v_ref.7, bf16[1,128,2560]{2,1,0:T(8,128)(2,1)} %q_ref.7, bf16[1,128,2560]{2,1,0:T(8,128)(2,1)} %o_ref.7, ...), custom_call_target="tpu_custom_call" | custom-call | flops 1000000 | bytes 1000000 | tf_op jit(solution)/shard_map/pack0_1/pallas_call | solution.py:40
  3.3 3.1 %collective-permute-start = (bf16[672,512]{1,0:T(8,128)(2,1)S(1)}, bf16[672,512]{1,0:T(8,128)(2,1)S(1)}, u32[]{:S(2)}, u32[]{:S(2)}) collective-permute-start(bf16[672,512]{1,0:T(8,128)(2,1)S(1)} %get-tuple-element.46), channel_id=1, source_target_pairs={{0,1},{1,2},{2,3},{3,0},{4,5},{5,6},{6,7},{7,4},{8,9},{9,10},{10,1... | collective-permute-start | bytes 2064392 | tf_op jit(solution)/shard_map/ppermute | solution.py:383
  6.3 2.6 %collective-permute-start.4 = (bf16[672,512]{1,0:T(8,128)(2,1)S(1)}, bf16[672,512]{1,0:T(8,128)(2,1)S(1)}, u32[]{:S(2)}, u32[]{:S(2)}) collective-permute-start(bf16[672,512]{1,0:T(8,128)(2,1)S(1)} %get-tuple-element.51), channel_id=1, source_target_pairs={{0,2},{1,3},{2,0},{3,1},{4,6},{5,7},{6,4},{7,5},{8,10},{9,11},{10,... | collective-permute-start | bytes 2064392 | tf_op jit(solution)/shard_map/ppermute | solution.py:383
  8.9 1.3 collective-permute-start.5
  10.3 1.8 %pack1_1.1 = (bf16[704,128]{1,0:T(8,128)(2,1)S(1)}, bf16[704,128]{1,0:T(8,128)(2,1)S(1)}, bf16[704,128]{1,0:T(8,128)(2,1)S(1)}) custom-call(s32[18]{0:T(128)S(1)} %concatenate.3.ids, bf16[1,128,2560]{2,1,0:T(8,128)(2,1)} %k_ref.4, bf16[1,128,2560]{2,1,0:T(8,128)(2,1)} %v_ref.7, bf16[1,128,2560]{2,1,0:T(8,128)(2,1)} %q_ref.7, bf16[1,128,2560]{2,1,0:T(8,128)(2,1)} %o_ref.7, ...), custom_call_target="tpu_custom_call" | custom-call | flops 1000000 | bytes 1000000 | tf_op jit(solution)/shard_map/pack1_1/pallas_call | solution.py:40
  12.1 1.8 %pack0_0.1.refs_0_ = bf16[672,512]{1,0:T(8,128)(2,1)S(1)} custom-call(s32[18]{0:T(128)S(1)} %concatenate.3.ids, bf16[1,128,2560]{2,1,0:T(8,128)(2,1)} %k_ref.4, bf16[1,128,2560]{2,1,0:T(8,128)(2,1)} %v_ref.7, bf16[1,128,2560]{2,1,0:T(8,128)(2,1)} %q_ref.7, bf16[1,128,2560]{2,1,0:T(8,128)(2,1)} %o_ref.7, f32[3,20,32,128]{3,2,1,0:T(8,128)} %s_ref.7, ...), custom_call_target="tpu_custom_call" | custom-call | flops 1000000 | bytes 1000000 | tf_op jit(solution)/shard_map/pack0_0/pallas_call | solution.py:40
  13.9 10.8 %collective-permute-done.refs_1_ = bf16[672,512]{1,0:T(8,128)(2,1)S(1)} collective-permute-done((bf16[672,512]{1,0:T(8,128)(2,1)S(1)}, bf16[672,512]{1,0:T(8,128)(2,1)S(1)}, u32[]{:S(2)}, u32[]{:S(2)}) %collective-permute-start) | collective-permute-done | bytes 688160 | tf_op jit(solution)/shard_map/ppermute | solution.py:383
  24.8 28.7 %collective-permute-done.4.refs_2_ = bf16[672,512]{1,0:T(8,128)(2,1)S(1)} collective-permute-done((bf16[672,512]{1,0:T(8,128)(2,1)S(1)}, bf16[672,512]{1,0:T(8,128)(2,1)S(1)}, u32[]{:S(2)}, u32[]{:S(2)}) %collective-permute-start.4) | collective-permute-done | bytes 688160 | tf_op jit(solution)/shard_map/ppermute | solution.py:383
  53.4 0.0 collective-permute-done.5.refs_3_
  53.4 0.6 start_share.1.refs_4_
  54.0 0.1 collective-permute-start.6
  54.1 1.5 %pack1_0.1.refs_0_ = bf16[704,128]{1,0:T(8,128)(2,1)S(1)} custom-call(s32[18]{0:T(128)S(1)} %concatenate.3.ids, bf16[1,128,2560]{2,1,0:T(8,128)(2,1)} %k_ref.4, bf16[1,128,2560]{2,1,0:T(8,128)(2,1)} %v_ref.7, bf16[1,128,2560]{2,1,0:T(8,128)(2,1)} %q_ref.7, bf16[1,128,2560]{2,1,0:T(8,128)(2,1)} %o_ref.7, f32[3,20,32,128]{3,2,1,0:T(8,128)} %s_ref.7, ...), custom_call_target="tpu_custom_call" | custom-call | flops 1000000 | bytes 1000000 | tf_op jit(solution)/shard_map/pack1_0/pallas_call | solution.py:40
  55.6 15.3 %collective-permute-start.1 = (bf16[704,128]{1,0:T(8,128)(2,1)S(1)}, bf16[704,128]{1,0:T(8,128)(2,1)S(1)}, u32[]{:S(2)}, u32[]{:S(2)}) collective-permute-start(bf16[704,128]{1,0:T(8,128)(2,1)S(1)} %get-tuple-element.47), channel_id=1, source_target_pairs={{0,1},{1,2},{2,3},{3,0},{4,5},{5,6},{6,7},{7,4},{8,9},{9,10},{10,1... | collective-permute-start | bytes 540680 | tf_op jit(solution)/shard_map/ppermute | solution.py:383
  70.8 1.6 %collective-permute-start.2 = (bf16[704,128]{1,0:T(8,128)(2,1)S(1)}, bf16[704,128]{1,0:T(8,128)(2,1)S(1)}, u32[]{:S(2)}, u32[]{:S(2)}) collective-permute-start(bf16[704,128]{1,0:T(8,128)(2,1)S(1)} %get-tuple-element.48), channel_id=1, source_target_pairs={{0,2},{1,3},{2,0},{3,1},{4,6},{5,7},{6,4},{7,5},{8,10},{9,11},{10,... | collective-permute-start | bytes 540680 | tf_op jit(solution)/shard_map/ppermute | solution.py:383
  72.4 0.9 collective-permute-start.3
  73.3 8.3 %chunk0.1 = (bf16[4,256,384]{2,1,0:T(8,128)(2,1)}, bf16[4,256,128]{2,1,0:T(8,128)(2,1)S(1)}, bf16[12,128,128]{2,1,0:T(8,128)(2,1)S(1)}) custom-call(s32[18]{0:T(128)S(1)} %concatenate.3.ids, bf16[672,512]{1,0:T(8,128)(2,1)S(1)} %pack0_0.1.refs_0_, bf16[672,512]{1,0:T(8,128)(2,1)S(1)} %collective-permute-done.refs_1_, ...), custom_call_target="tpu_custom_call" | custom-call | flops 2560000000 | bytes 4000000 | tf_op jit(solution)/shard_map/chunk0/pallas_call | solution.py:40
  81.6 3.3 %collective-permute-done.2.refs_2_ = bf16[704,128]{1,0:T(8,128)(2,1)S(1)} collective-permute-done((bf16[704,128]{1,0:T(8,128)(2,1)S(1)}, bf16[704,128]{1,0:T(8,128)(2,1)S(1)}, u32[]{:S(2)}, u32[]{:S(2)}) %collective-permute-start.2) | collective-permute-done | bytes 180256 | tf_op jit(solution)/shard_map/ppermute | solution.py:383
  84.9 4.5 %chunk1.1 = (bf16[4,256,256]{2,1,0:T(8,128)(2,1)}, bf16[8,128,128]{2,1,0:T(8,128)(2,1)S(1)}, bf16[8,128,128]{2,1,0:T(8,128)(2,1)S(1)}) custom-call(s32[18]{0:T(128)S(1)} %concatenate.3.ids, bf16[704,128]{1,0:T(8,128)(2,1)S(1)} %pack1_0.1.refs_0_, bf16[704,128]{1,0:T(8,128)(2,1)S(1)} %collective-permute-done.1.refs_1_, ...), custom_call_target="tpu_custom_call" | custom-call | flops 640000000 | bytes 1000000 | tf_op jit(solution)/shard_map/chunk1/pallas_call | solution.py:40
  89.4 6.4 %all-to-all-start = ((bf16[4,256,384]{2,1,0:T(8,128)(2,1)}), bf16[4,256,384]{2,1,0:T(8,128)(2,1)S(1)}, u32[]{:S(2)}, u32[]{:S(2)}) async-start(bf16[4,256,384]{2,1,0:T(8,128)(2,1)} %get-tuple-element.64), calls=%async_computation | async-start | bytes 1572864 | tf_op jit(solution)/shard_map/all_to_all | solution.py:386
  95.8 1.5 %collective-permute-done.7.got_ref = bf16[8,128,128]{2,1,0:T(8,128)(2,1)S(1)} collective-permute-done((bf16[8,128,128]{2,1,0:T(8,128)(2,1)S(1)}, bf16[8,128,128]{2,1,0:T(8,128)(2,1)S(1)}, u32[]{:S(2)}, u32[]{:S(2)}) %collective-permute-start.7) | collective-permute-done | bytes 262176 | tf_op jit(solution)/shard_map/ppermute | solution.py:378
  97.3 0.6 state_pair.1
  98.0 2.5 %collective-permute-start.10 = (bf16[2,128,128]{2,1,0:T(8,128)(2,1)S(1)}, bf16[2,128,128]{2,1,0:T(8,128)(2,1)S(1)}, u32[]{:S(2)}, u32[]{:S(2)}) collective-permute-start(bf16[2,128,128]{2,1,0:T(8,128)(2,1)S(1)} %get-tuple-element.62), channel_id=1, source_target_pairs={{0,24},{4,28},{8,16},{12,20},{16,8},{20,12},{24,0},{28,4},{1,25},{... | collective-permute-start | bytes 196616 | tf_op jit(solution)/shard_map/ppermute | solution.py:378
  100.5 0.5 collective-permute-start.8
  101.0 0.5 collective-permute-start.9
  101.5 2.1 %collective-permute-done.10.refs_3_ = bf16[2,128,128]{2,1,0:T(8,128)(2,1)S(1)} collective-permute-done((bf16[2,128,128]{2,1,0:T(8,128)(2,1)S(1)}, bf16[2,128,128]{2,1,0:T(8,128)(2,1)S(1)}, u32[]{:S(2)}, u32[]{:S(2)}) %collective-permute-start.10) | collective-permute-done | bytes 65568 | tf_op jit(solution)/shard_map/ppermute | solution.py:378
  103.6 1.1 collective-permute-done.8.refs_1_
  104.7 0.5 collective-permute-done.9.refs_2_
  105.3 0.6 state_sum.1
  105.9 2.1 %collective-permute-start.11 = (bf16[2,32,128]{2,1,0:T(8,128)(2,1)S(1)}, bf16[2,32,128]{2,1,0:T(8,128)(2,1)S(1)}, u32[]{:S(2)}, u32[]{:S(2)}) collective-permute-start(bf16[2,32,128]{2,1,0:T(8,128)(2,1)S(1)} %get-tuple-element.67), channel_id=1, source_target_pairs={{0,1},{1,2},{2,3},{3,0},{4,5},{5,6},{6,7},{7,4},{8,9},{9,10},{10,1... | collective-permute-start | bytes 49160 | tf_op jit(solution)/shard_map/ppermute | solution.py:383
  107.9 2.4 %collective-permute-start.12 = (bf16[2,32,128]{2,1,0:T(8,128)(2,1)S(1)}, bf16[2,32,128]{2,1,0:T(8,128)(2,1)S(1)}, u32[]{:S(2)}, u32[]{:S(2)}) collective-permute-start(bf16[2,32,128]{2,1,0:T(8,128)(2,1)S(1)} %get-tuple-element.68), channel_id=1, source_target_pairs={{0,2},{1,3},{2,0},{3,1},{4,6},{5,7},{6,4},{7,5},{8,10},{9,11},{10,... | collective-permute-start | bytes 49160 | tf_op jit(solution)/shard_map/ppermute | solution.py:383
  110.3 1.5 %collective-permute-start.13 = (bf16[2,32,128]{2,1,0:T(8,128)(2,1)S(1)}, bf16[2,32,128]{2,1,0:T(8,128)(2,1)S(1)}, u32[]{:S(2)}, u32[]{:S(2)}) collective-permute-start(bf16[2,32,128]{2,1,0:T(8,128)(2,1)S(1)} %get-tuple-element.69), channel_id=1, source_target_pairs={{0,3},{1,0},{2,1},{3,2},{4,7},{5,4},{6,5},{7,6},{8,11},{9,8},{10,9... | collective-permute-start | bytes 49160 | tf_op jit(solution)/shard_map/ppermute | solution.py:383
  111.8 5.3 %all-to-all-done.refs_0_ = bf16[4,256,384]{2,1,0:T(8,128)(2,1)S(1)} async-done(((bf16[4,256,384]{2,1,0:T(8,128)(2,1)}), bf16[4,256,384]{2,1,0:T(8,128)(2,1)S(1)}, u32[]{:S(2)}, u32[]{:S(2)}) %all-to-all-start) | async-done | bytes 786464 | tf_op jit(solution)/shard_map/all_to_all | solution.py:386
  117.0 0.2 collective-permute-done.12.refs_2_
  117.2 0.5 state_rows.1.refs_0_
  117.8 3.5 %all-to-all-start.1 = ((bf16[4,256,256]{2,1,0:T(8,128)(2,1)}), bf16[4,256,256]{2,1,0:T(8,128)(2,1)S(1)}, u32[]{:S(2)}, u32[]{:S(2)}) async-start(bf16[4,256,256]{2,1,0:T(8,128)(2,1)} %get-tuple-element.71), calls=%async_computation.1 | async-start | bytes 1048576 | tf_op jit(solution)/shard_map/all_to_all | solution.py:386
  121.3 1.6 %collective-permute-start.14 = (bf16[4,2,32,128]{3,2,1,0:T(8,128)(2,1)S(1)}, bf16[4,2,32,128]{3,2,1,0:T(8,128)(2,1)S(1)}, u32[]{:S(2)}, u32[]{:S(2)}) collective-permute-start(bf16[4,2,32,128]{3,2,1,0:T(8,128)(2,1)S(1)} %state_rows.1.refs_0_), channel_id=1, source_target_pairs={{0,8},{4,12},{8,0},{12,4},{16,24},{20,28},{24,16},{28,20},{1,9},{5... | collective-permute-start | bytes 196616 | tf_op jit(solution)/shard_map/ppermute | solution.py:378
  122.8 1.5 %collective-permute-start.15 = (bf16[4,2,32,128]{3,2,1,0:T(8,128)(2,1)S(1)}, bf16[4,2,32,128]{3,2,1,0:T(8,128)(2,1)S(1)}, u32[]{:S(2)}, u32[]{:S(2)}) collective-permute-start(bf16[4,2,32,128]{3,2,1,0:T(8,128)(2,1)S(1)} %state_rows.1.refs_0_), channel_id=1, source_target_pairs={{0,16},{4,20},{8,24},{12,28},{16,0},{20,4},{24,8},{28,12},{1,17},{... | collective-permute-start | bytes 196616 | tf_op jit(solution)/shard_map/ppermute | solution.py:378
  124.3 0.5 collective-permute-start.16
  124.8 1.2 collective-permute-done.14.refs_1_
  126.0 1.7 %collective-permute-done.15.refs_2_ = bf16[4,2,32,128]{3,2,1,0:T(8,128)(2,1)S(1)} collective-permute-done((bf16[4,2,32,128]{3,2,1,0:T(8,128)(2,1)S(1)}, bf16[4,2,32,128]{3,2,1,0:T(8,128)(2,1)S(1)}, u32[]{:S(2)}, u32[]{:S(2)}) %collective-permute-start.15) | collective-permute-done | bytes 65568 | tf_op jit(solution)/shard_map/ppermute | solution.py:378
  127.7 1.8 %collective-permute-done.16.refs_3_ = bf16[4,2,32,128]{3,2,1,0:T(8,128)(2,1)S(1)} collective-permute-done((bf16[4,2,32,128]{3,2,1,0:T(8,128)(2,1)S(1)}, bf16[4,2,32,128]{3,2,1,0:T(8,128)(2,1)S(1)}, u32[]{:S(2)}, u32[]{:S(2)}) %collective-permute-start.16) | collective-permute-done | bytes 65568 | tf_op jit(solution)/shard_map/ppermute | solution.py:378
  129.5 0.6 state_rest.1.refs_0_
  130.0 0.1 collective-permute-start.17
  130.1 1.5 %collective-permute-done.17.refs_1_ = bf16[4,4,2,32,128]{4,3,2,1,0:T(8,128)(2,1)S(1)} collective-permute-done((bf16[4,4,2,32,128]{4,3,2,1,0:T(8,128)(2,1)S(1)}, bf16[4,4,2,32,128]{4,3,2,1,0:T(8,128)(2,1)S(1)}, u32[]{:S(2)}, u32[]{:S(2)}) %collective-permute-start.17) | collective-permute-done | bytes 262176 | tf_op jit(solution)/shard_map/ppermute | solution.py:378
  131.6 1.8 %state_out.1 = f32[3,20,32,128]{3,2,1,0:T(8,128)} custom-call(s32[18]{0:T(128)S(1)} %concatenate.3.ids, bf16[4,4,2,32,128]{4,3,2,1,0:T(8,128)(2,1)S(1)} %state_rest.1.refs_0_, bf16[4,4,2,32,128]{4,3,2,1,0:T(8,128)(2,1)S(1)} %collective-permute-done.17.refs_1_), custom_call_target="tpu_custom_call" | custom-call | flops 1000000 | bytes 1000000 | tf_op jit(solution)/shard_map/state_out/pallas_call | solution.py:40
  133.4 1.6 %all-to-all-done.1.refs_1_ = bf16[4,256,256]{2,1,0:T(8,128)(2,1)S(1)} async-done(((bf16[4,256,256]{2,1,0:T(8,128)(2,1)}), bf16[4,256,256]{2,1,0:T(8,128)(2,1)S(1)}, u32[]{:S(2)}, u32[]{:S(2)}) %all-to-all-start.1) | async-done | bytes 524320 | tf_op jit(solution)/shard_map/all_to_all | solution.py:386
  135.1 1.2 unpack.1
  (8 shorter events, 0.0 us)
Async XLA Ops:
  3.3 21.5 %collective-permute-start = (bf16[672,512]{1,0:T(8,128)(2,1)S(1)}, bf16[672,512]{1,0:T(8,128)(2,1)S(1)}, u32[]{:S(2)}, u32[]{:S(2)}) collective-permute-start(bf16[672,512]{1,0:T(8,128)(2,1)S(1)} %get-tuple-element.46), channel_id=1, source_target_pairs={{0,1},{1,2},{2,3},{3,0},{4,5},{5,6},{6,7},{7,4},{8,9},{9,10},{10,1... | collective-permute-start | bytes 2064392 | tf_op jit(solution)/shard_map/ppermute | solution.py:383
  6.3 47.1 %collective-permute-start.4 = (bf16[672,512]{1,0:T(8,128)(2,1)S(1)}, bf16[672,512]{1,0:T(8,128)(2,1)S(1)}, u32[]{:S(2)}, u32[]{:S(2)}) collective-permute-start(bf16[672,512]{1,0:T(8,128)(2,1)S(1)} %get-tuple-element.51), channel_id=1, source_target_pairs={{0,2},{1,3},{2,0},{3,1},{4,6},{5,7},{6,4},{7,5},{8,10},{9,11},{10,... | collective-permute-start | bytes 2064392 | tf_op jit(solution)/shard_map/ppermute | solution.py:383
  8.9 44.5 %collective-permute-start.5 = (bf16[672,512]{1,0:T(8,128)(2,1)S(1)}, bf16[672,512]{1,0:T(8,128)(2,1)S(1)}, u32[]{:S(2)}, u32[]{:S(2)}) collective-permute-start(bf16[672,512]{1,0:T(8,128)(2,1)S(1)} %get-tuple-element.52), channel_id=1, source_target_pairs={{0,3},{1,0},{2,1},{3,2},{4,7},{5,4},{6,5},{7,6},{8,11},{9,8},{10,9... | collective-permute-start | bytes 2064392 | tf_op jit(solution)/shard_map/ppermute | solution.py:383
  54.0 19.3 %collective-permute-start.6 = (bf16[6,128,128]{2,1,0:T(8,128)(2,1)S(1)}, bf16[6,128,128]{2,1,0:T(8,128)(2,1)S(1)}, u32[]{:S(2)}, u32[]{:S(2)}) collective-permute-start(bf16[6,128,128]{2,1,0:T(8,128)(2,1)S(1)} %start_share.1.refs_4_), channel_id=1, source_target_pairs={{0,4},{4,0},{8,12},{12,8},{16,20},{20,16},{24,28},{28,24},{1,5},{5... | collective-permute-start | bytes 589832 | tf_op jit(solution)/shard_map/ppermute | solution.py:378
  55.6 26.0 %collective-permute-start.1 = (bf16[704,128]{1,0:T(8,128)(2,1)S(1)}, bf16[704,128]{1,0:T(8,128)(2,1)S(1)}, u32[]{:S(2)}, u32[]{:S(2)}) collective-permute-start(bf16[704,128]{1,0:T(8,128)(2,1)S(1)} %get-tuple-element.47), channel_id=1, source_target_pairs={{0,1},{1,2},{2,3},{3,0},{4,5},{5,6},{6,7},{7,4},{8,9},{9,10},{10,1... | collective-permute-start | bytes 540680 | tf_op jit(solution)/shard_map/ppermute | solution.py:383
  70.8 14.1 %collective-permute-start.2 = (bf16[704,128]{1,0:T(8,128)(2,1)S(1)}, bf16[704,128]{1,0:T(8,128)(2,1)S(1)}, u32[]{:S(2)}, u32[]{:S(2)}) collective-permute-start(bf16[704,128]{1,0:T(8,128)(2,1)S(1)} %get-tuple-element.48), channel_id=1, source_target_pairs={{0,2},{1,3},{2,0},{3,1},{4,6},{5,7},{6,4},{7,5},{8,10},{9,11},{10,... | collective-permute-start | bytes 540680 | tf_op jit(solution)/shard_map/ppermute | solution.py:383
  72.4 12.5 %collective-permute-start.3 = (bf16[704,128]{1,0:T(8,128)(2,1)S(1)}, bf16[704,128]{1,0:T(8,128)(2,1)S(1)}, u32[]{:S(2)}, u32[]{:S(2)}) collective-permute-start(bf16[704,128]{1,0:T(8,128)(2,1)S(1)} %get-tuple-element.49), channel_id=1, source_target_pairs={{0,3},{1,0},{2,1},{3,2},{4,7},{5,4},{6,5},{7,6},{8,11},{9,8},{10,9... | collective-permute-start | bytes 540680 | tf_op jit(solution)/shard_map/ppermute | solution.py:383
  89.4 27.6 %all-to-all-start = ((bf16[4,256,384]{2,1,0:T(8,128)(2,1)}), bf16[4,256,384]{2,1,0:T(8,128)(2,1)S(1)}, u32[]{:S(2)}, u32[]{:S(2)}) async-start(bf16[4,256,384]{2,1,0:T(8,128)(2,1)} %get-tuple-element.64), calls=%async_computation | async-start | bytes 1572864 | tf_op jit(solution)/shard_map/all_to_all | solution.py:386
  95.8 1.5 %collective-permute-start.7 = (bf16[8,128,128]{2,1,0:T(8,128)(2,1)S(1)}, bf16[8,128,128]{2,1,0:T(8,128)(2,1)S(1)}, u32[]{:S(2)}, u32[]{:S(2)}) collective-permute-start(bf16[8,128,128]{2,1,0:T(8,128)(2,1)S(1)} %get-tuple-element.58), channel_id=1, source_target_pairs={{0,4},{4,0},{8,12},{12,8},{16,20},{20,16},{24,28},{28,24},{1,5},{5... | collective-permute-start | bytes 786440 | tf_op jit(solution)/shard_map/ppermute | solution.py:378
  98.0 5.6 %collective-permute-start.10 = (bf16[2,128,128]{2,1,0:T(8,128)(2,1)S(1)}, bf16[2,128,128]{2,1,0:T(8,128)(2,1)S(1)}, u32[]{:S(2)}, u32[]{:S(2)}) collective-permute-start(bf16[2,128,128]{2,1,0:T(8,128)(2,1)S(1)} %get-tuple-element.62), channel_id=1, source_target_pairs={{0,24},{4,28},{8,16},{12,20},{16,8},{20,12},{24,0},{28,4},{1,25},{... | collective-permute-start | bytes 196616 | tf_op jit(solution)/shard_map/ppermute | solution.py:378
  100.5 4.3 %collective-permute-start.8 = (bf16[2,128,128]{2,1,0:T(8,128)(2,1)S(1)}, bf16[2,128,128]{2,1,0:T(8,128)(2,1)S(1)}, u32[]{:S(2)}, u32[]{:S(2)}) collective-permute-start(bf16[2,128,128]{2,1,0:T(8,128)(2,1)S(1)} %get-tuple-element.60), channel_id=1, source_target_pairs={{0,8},{4,12},{8,0},{12,4},{16,24},{20,28},{24,16},{28,20},{1,9},{5... | collective-permute-start | bytes 196616 | tf_op jit(solution)/shard_map/ppermute | solution.py:378
  101.0 4.3 %collective-permute-start.9 = (bf16[2,128,128]{2,1,0:T(8,128)(2,1)S(1)}, bf16[2,128,128]{2,1,0:T(8,128)(2,1)S(1)}, u32[]{:S(2)}, u32[]{:S(2)}) collective-permute-start(bf16[2,128,128]{2,1,0:T(8,128)(2,1)S(1)} %get-tuple-element.61), channel_id=1, source_target_pairs={{0,16},{4,20},{8,24},{12,28},{16,0},{20,4},{24,8},{28,12},{1,17},{... | collective-permute-start | bytes 196616 | tf_op jit(solution)/shard_map/ppermute | solution.py:378
  105.9 11.2 %collective-permute-start.11 = (bf16[2,32,128]{2,1,0:T(8,128)(2,1)S(1)}, bf16[2,32,128]{2,1,0:T(8,128)(2,1)S(1)}, u32[]{:S(2)}, u32[]{:S(2)}) collective-permute-start(bf16[2,32,128]{2,1,0:T(8,128)(2,1)S(1)} %get-tuple-element.67), channel_id=1, source_target_pairs={{0,1},{1,2},{2,3},{3,0},{4,5},{5,6},{6,7},{7,4},{8,9},{9,10},{10,1... | collective-permute-start | bytes 49160 | tf_op jit(solution)/shard_map/ppermute | solution.py:383
  107.9 9.3 %collective-permute-start.12 = (bf16[2,32,128]{2,1,0:T(8,128)(2,1)S(1)}, bf16[2,32,128]{2,1,0:T(8,128)(2,1)S(1)}, u32[]{:S(2)}, u32[]{:S(2)}) collective-permute-start(bf16[2,32,128]{2,1,0:T(8,128)(2,1)S(1)} %get-tuple-element.68), channel_id=1, source_target_pairs={{0,2},{1,3},{2,0},{3,1},{4,6},{5,7},{6,4},{7,5},{8,10},{9,11},{10,... | collective-permute-start | bytes 49160 | tf_op jit(solution)/shard_map/ppermute | solution.py:383
  110.3 6.9 %collective-permute-start.13 = (bf16[2,32,128]{2,1,0:T(8,128)(2,1)S(1)}, bf16[2,32,128]{2,1,0:T(8,128)(2,1)S(1)}, u32[]{:S(2)}, u32[]{:S(2)}) collective-permute-start(bf16[2,32,128]{2,1,0:T(8,128)(2,1)S(1)} %get-tuple-element.69), channel_id=1, source_target_pairs={{0,3},{1,0},{2,1},{3,2},{4,7},{5,4},{6,5},{7,6},{8,11},{9,8},{10,9... | collective-permute-start | bytes 49160 | tf_op jit(solution)/shard_map/ppermute | solution.py:383
  117.8 17.3 %all-to-all-start.1 = ((bf16[4,256,256]{2,1,0:T(8,128)(2,1)}), bf16[4,256,256]{2,1,0:T(8,128)(2,1)S(1)}, u32[]{:S(2)}, u32[]{:S(2)}) async-start(bf16[4,256,256]{2,1,0:T(8,128)(2,1)} %get-tuple-element.71), calls=%async_computation.1 | async-start | bytes 1048576 | tf_op jit(solution)/shard_map/all_to_all | solution.py:386
  121.3 4.7 %collective-permute-start.14 = (bf16[4,2,32,128]{3,2,1,0:T(8,128)(2,1)S(1)}, bf16[4,2,32,128]{3,2,1,0:T(8,128)(2,1)S(1)}, u32[]{:S(2)}, u32[]{:S(2)}) collective-permute-start(bf16[4,2,32,128]{3,2,1,0:T(8,128)(2,1)S(1)} %state_rows.1.refs_0_), channel_id=1, source_target_pairs={{0,8},{4,12},{8,0},{12,4},{16,24},{20,28},{24,16},{28,20},{1,9},{5... | collective-permute-start | bytes 196616 | tf_op jit(solution)/shard_map/ppermute | solution.py:378
  122.8 4.8 %collective-permute-start.15 = (bf16[4,2,32,128]{3,2,1,0:T(8,128)(2,1)S(1)}, bf16[4,2,32,128]{3,2,1,0:T(8,128)(2,1)S(1)}, u32[]{:S(2)}, u32[]{:S(2)}) collective-permute-start(bf16[4,2,32,128]{3,2,1,0:T(8,128)(2,1)S(1)} %state_rows.1.refs_0_), channel_id=1, source_target_pairs={{0,16},{4,20},{8,24},{12,28},{16,0},{20,4},{24,8},{28,12},{1,17},{... | collective-permute-start | bytes 196616 | tf_op jit(solution)/shard_map/ppermute | solution.py:378
  124.3 5.2 %collective-permute-start.16 = (bf16[4,2,32,128]{3,2,1,0:T(8,128)(2,1)S(1)}, bf16[4,2,32,128]{3,2,1,0:T(8,128)(2,1)S(1)}, u32[]{:S(2)}, u32[]{:S(2)}) collective-permute-start(bf16[4,2,32,128]{3,2,1,0:T(8,128)(2,1)S(1)} %state_rows.1.refs_0_), channel_id=1, source_target_pairs={{0,24},{4,28},{8,16},{12,20},{16,8},{20,12},{24,0},{28,4},{1,25},{... | collective-permute-start | bytes 196616 | tf_op jit(solution)/shard_map/ppermute | solution.py:378
  130.0 1.6 %collective-permute-start.17 = (bf16[4,4,2,32,128]{4,3,2,1,0:T(8,128)(2,1)S(1)}, bf16[4,4,2,32,128]{4,3,2,1,0:T(8,128)(2,1)S(1)}, u32[]{:S(2)}, u32[]{:S(2)}) collective-permute-start(bf16[4,4,2,32,128]{4,3,2,1,0:T(8,128)(2,1)S(1)} %state_rest.1.refs_0_), channel_id=1, source_target_pairs={{0,4},{4,0},{8,12},{12,8},{16,20},{20,16},{24,28},{28,24},{1,5},{5... | collective-permute-start | bytes 786440 | tf_op jit(solution)/shard_map/ppermute | solution.py:378

commit v4 on v3

--- a/solution.py
+++ b/solution.py
@@ -49,11 +49,11 @@
     )(*args)
 
 
-def swish_terms(g):
-    s = 1.0 / (1.0 + jnp.exp(-g))
-    sw = g * s
-    slope = s * (1.0 + g * (1.0 - s))
-    return s, sw, slope
+def swish_terms(g, s):
+    rest = 1.0 - s
+    both = s * rest
+    bent = g * both
+    return g * s, s + bent, 2.0 * both + bent * (rest - s)
 
 
 def newton_pullback(grads, updates):
@@ -95,15 +95,15 @@
         self.tokens, self.heads, self.rows, self.width = tokens, heads, rows, width
         self.per = -(-heads // n)
         self.mats = 3 * self.per
-        most = max(1, self.per - 1)
-        self.chunks = [(0, most), (most, self.per - most)]
-        self.early = (most + 2) // 2
+        least = max(1, self.per // 2)
+        self.chunks = [(0, least), (least, self.per - least)]
+        self.early = (self.per + 1) // 2
         self.pair = min(2, n_dp)
         self.rest = n_dp // self.pair
         self.own = -(-self.mats // n_dp)
         self.block = -(-rows // 16) * 16
-        self.share = -(-3 * most // self.pair)
-        self.share_blocks = -(-self.share // most)
+        self.share = -(-self.mats // self.pair)
+        self.share_blocks = -(-self.share // least)
         self.ids = {}
         at = 0
         for name, size in (("to", n), ("from", n), ("head", n), ("rest", self.rest), ("mine", 1), ("place", 1)):
@@ -111,7 +111,7 @@
             at += size
 
     def packed_rows(self, chunk):
-        return 4 * self.tokens + (3 + (self.share_blocks if chunk == 0 else 3)) * self.block
+        return 4 * self.tokens + (3 + (self.share_blocks if chunk == 0 else 0)) * self.block
 
     def first_head(self, c):
         return min(c * self.per, self.heads - self.per)
@@ -121,36 +121,35 @@
     t, w = plan.tokens, plan.width
     first, count = plan.chunks[chunk]
     outs, (state, sems) = refs[:-2], refs[-2:]
+    per = plan.per
     loads = []
     copies = []
     for k, slot in enumerate(slots):
-        head = ids[plan.ids["head"] + slot] + first
-        for i, src in enumerate((s_ref, t_ref.at[0])):
-            loads.append(
-                pltpu.make_async_copy(src.at[:, pl.ds(head, count)], state.at[k, i], sems.at[k, 4 + i])
-            )
+        head = ids[plan.ids["head"] + slot]
+        wanted = [(t_ref.at[0, :, pl.ds(head + first, count)], state.at[k, :, pl.ds(0, count)])]
+        if chunk == 0:
+            wanted.append((s_ref.at[:, pl.ds(head, per)], state.at[k, :, pl.ds(count, per)]))
+        for i, (src, dst) in enumerate(wanted):
+            loads.append(pltpu.make_async_copy(src, dst, sems.at[k, 4 + i]))
             loads[-1].start()
-        cols = pl.ds(pl.multiple_of(head * w, w), count * w)
+        cols = pl.ds(pl.multiple_of((head + first) * w, w), count * w)
         for i, src in enumerate((k_ref, v_ref, q_ref, o_ref)):
             copies.append(
                 pltpu.make_async_copy(src.at[0, :, cols], outs[k].at[pl.ds(i * t, t), :], sems.at[k, i])
             )
             copies[-1].start()
+    for load in loads:
+        load.wait()
     for k in range(len(slots)):
-        loads[2 * k].wait()
-        loads[2 * k + 1].wait()
         for j in range(count):
             for m in range(3):
                 top = 4 * t + m * plan.block
-                outs[k][top : top + plan.rows, j * w : (j + 1) * w] = state[k, 1, m, j].astype(BF16)
-                if chunk > 0:
-                    top += 3 * plan.block
-                    outs[k][top : top + plan.rows, j * w : (j + 1) * w] = state[k, 0, m, j].astype(BF16)
+                outs[k][top : top + plan.rows, j * w : (j + 1) * w] = state[k, m, j].astype(BF16)
         for q in range(plan.share if chunk == 0 else 0):
-            mat = jnp.minimum(ids[plan.ids["mine"]] * plan.share + q, 3 * count - 1)
+            mat = jnp.minimum(ids[plan.ids["mine"]] * plan.share + q, plan.mats - 1)
             top = 4 * t + (3 + q // count) * plan.block
             left = (q % count) * w
-            part = state[k, 0, lax.rem(mat, 3), lax.div(mat, 3)]
+            part = state[k, lax.rem(mat, 3), count + lax.div(mat, 3)]
             outs[k][top : top + plan.rows, left : left + w] = part.astype(BF16)
     for copy in copies:
         copy.wait()
@@ -182,12 +181,13 @@
     gu = dot_nn(x, jnp.concatenate([wa, wb], axis=1))
     g, u = gu[:, :w], gu[:, w:]
     p = dot_nn(y, wc)
-    _, sw, slope = swish_terms(g)
+    s = 0.5 + 0.5 * jnp.tanh(0.5 * g)
+    sw, slope, _ = swish_terms(g, s)
     hidden = (sw * u).astype(BF16)
     dg = (p * u * slope).astype(BF16)
     du = (p * sw).astype(BF16)
     ab = dot_tn(x, jnp.concatenate([dg, du], axis=1))
-    return (ab[:, :w], ab[:, w:], dot_tn(y, hidden)), (g, u, p), (dg, du, hidden)
+    return (ab[:, :w], ab[:, w:], dot_tn(y, hidden)), (g, u, p, s), (dg, du, hidden)
 
 
 def chunk_kernel(ids, *refs, plan, chunk):
@@ -203,9 +203,9 @@
         return got
 
     in_refs = take(n)
+    shares = take(plan.pair)
     before, held = take(2) if last else (None, None)
-    shares = take(0 if last else plan.pair)
-    d_refs = take(1 if last else 2)
+    d_refs = take(2 if last else 1)
     c_refs = take(2 if last else 1)
     w0, w1, gsum, ssum, acts, fields = take(6)
     total = take(1)[0] if last else c_refs[0]
@@ -215,21 +215,21 @@
         at = pl.ds(pl.multiple_of(ids[plan.ids["from"] + slot] * plan.rows, plan.rows), plan.rows)
         for j in range(count):
             for m in range(3):
-                for i, dst in enumerate((w1, w0) if last else (w1,)):
-                    top = 4 * t + (3 * i + m) * plan.block
-                    part = in_refs[slot][top : top + plan.rows, j * w : (j + 1) * w]
-                    dst[3 * j + m, at, :] = part.astype(F32)
+                top = 4 * t + m * plan.block
+                part = in_refs[slot][top : top + plan.rows, j * w : (j + 1) * w]
+                w1[3 * j + m, at, :] = part.astype(F32)
     for k, part in enumerate(shares):
         at = jnp.bitwise_xor(ids[plan.ids["mine"]], k) * plan.share
-        w0[pl.ds(at, plan.share)] = part[...].astype(F32)
+        w0[pl.ds(at, plan.share)] = part[...]
 
     for j in range(count):
         x, y = tokens_of(in_refs, j, 0, plan)
-        sums, act, field = forward(x, y, *[w0[3 * j + m].astype(BF16) for m in range(3)])
+        sums, act, field = forward(x, y, *[w0[3 * (first + j) + m] for m in range(3)])
         for m in range(3):
             gsum[3 * j + m] = sums[m]
-            acts[j, m] = act[m]
             fields[j, m] = field[m]
+        for i, val in enumerate(act):
+            acts[j, i] = val
         x, y = tokens_of(in_refs, j, 1, plan)
         sums, _, _ = forward(x, y, *[w1[3 * j + m].astype(BF16) for m in range(3)])
         for m in range(3):
@@ -244,26 +244,21 @@
         x, y = tokens_of(in_refs, j, 0, plan)
         fab = jnp.concatenate([gsum[3 * j], gsum[3 * j + 1]], axis=1).astype(BF16)
         fc = gsum[3 * j + 2].astype(BF16)
-        wab = jnp.concatenate([w0[3 * j], w0[3 * j + 1]], axis=1).astype(BF16)
-        wc = w0[3 * j + 2].astype(BF16)
+        at = 3 * (first + j)
+        wab = jnp.concatenate([w0[at], w0[at + 1]], axis=1)
+        wc = w0[at + 2]
         cdgu = dot_nn(x, fab)
         cdg, cdu = cdgu[:, :w], cdgu[:, w:]
         ch = dot_nn(y, fc)
-        g, u, p = acts[j, 0], acts[j, 1], acts[j, 2]
-        s, sw, slope = swish_terms(g)
-        curve = s * (1.0 - s) * (2.0 + g * (1.0 - 2.0 * s))
+        g, u, p, s = [acts[j, i] for i in range(4)]
+        sw, slope, curve = swish_terms(g, s)
         cg = ((ch * u + cdu * p) * slope + cdg * (p * u) * curve).astype(BF16)
         cu = (ch * sw + cdg * p * slope).astype(BF16)
         cp = (cdu * sw + cdg * u * slope).astype(BF16)
         dg, du, hidden = fields[j, 0], fields[j, 1], fields[j, 2]
         dx = dot_nt(jnp.concatenate([dg, du, cg, cu], axis=1), jnp.concatenate([fab, wab], axis=1))
         dy = dot_nt(jnp.concatenate([hidden, cp], axis=1), jnp.concatenate([fc, wc], axis=1))
-        if last:
-            d_ref, at = d_refs[0], first - plan.early + j
-        elif j < plan.early:
-            d_ref, at = d_refs[0], j
-        else:
-            d_ref, at = d_refs[1], j - plan.early
+        d_ref, at = (d_refs[0], first + j) if first + j < plan.early else (d_refs[1], first + j - plan.early)
         cols = slice(at * w, (at + 1) * w)
         for slot in range(n):
             to = ids[plan.ids["from"] + slot]
@@ -276,8 +271,7 @@
 
     if last:
         total[0 : before.shape[0]] = before[...]
-        if first > plan.early:
-            d_refs[0][:, :, 0 : held.shape[2]] = held[...]
+        d_refs[0][:, :, 0 : held.shape[2]] = held[...]
         for m in range(plan.mats, plan.n_dp * plan.own):
             total[m] = jnp.zeros((w, w), BF16)
         mine = ids[plan.ids["mine"]]
@@ -398,7 +392,7 @@
             [VMEM] * len(slots),
             f"pack{c}_{slots[0]}",
             [
-                pltpu.VMEM((len(slots), 2, 3, chunks[c][1], rows, width), F32),
+                pltpu.VMEM((len(slots), 3, chunks[c][1] + (0 if c else per), rows, width), F32),
                 pltpu.SemaphoreType.DMA((len(slots), 6)),
             ],
         )
@@ -408,7 +402,7 @@
     keys, sent = lax.optimization_barrier((keys_a, sent))
     arrived = [[shift(v, s + 1) for s, v in enumerate(sent)]]
     sent = pack(1, range(1, n), keys)
-    sent, arrived[0][0] = lax.optimization_barrier((sent, arrived[0][0]))
+    keys, sent = lax.optimization_barrier((keys_a, sent))
     arrived.append([shift(v, s + 1) for s, v in enumerate(sent)])
     arrived = [pack(c, range(1), keys) + arrived[c] for c in range(2)]
     start_own = call(
@@ -422,21 +416,17 @@
     )
     shares = [swap(start_own, k) for k in range(plan.pair)]
 
-    before = shares
+    before = []
     for c, (_, count) in enumerate(chunks):
         last = c + 1 == len(chunks)
         if last:
-            outs = [shape(n, 2 * t, (per - plan.early) * width)] + [shape(plan.rest * own, width, width)] * 2
+            outs = [shape(n, 2 * t, size * width) for size in (plan.early, per - plan.early)]
+            outs += [shape(plan.rest * own, width, width)] * 2
         else:
-            held = max(1, count - plan.early)
-            outs = [
-                shape(n, 2 * t, plan.early * width),
-                shape(n, 2 * t, held * width),
-                shape(3 * count, width, width),
-            ]
-        weights = 3 * count if last else plan.pair * plan.share
-        scratch = [pltpu.VMEM((weights, width, width), F32)] + [pltpu.VMEM((3 * count, width, width), F32)] * 3 + [
-            pltpu.VMEM((count, 3, n * t, width), F32),
+            outs = [shape(n, 2 * t, count * width), shape(3 * count, width, width)]
+        scratch = [pltpu.VMEM((plan.pair * plan.share, width, width), BF16)]
+        scratch += [pltpu.VMEM((3 * count, width, width), F32)] * 3 + [
+            pltpu.VMEM((count, 4, n * t, width), F32),
             pltpu.VMEM((count, 3, n * t, width), BF16),
         ]
         if last:
@@ -444,8 +434,8 @@
         got = call(
             bind(chunk_kernel, chunk=c),
             outs,
-            (ids, *arrived[c], *before),
-            [SMEM] + [VMEM] * (n + len(before)),
+            (ids, *arrived[c], *shares, *before),
+            [SMEM] + [VMEM] * (n + plan.pair + len(before)),
             [VMEM] * len(outs),
             f"chunk{c}",
             scratch,
@@ -453,10 +443,8 @@
             size=count * 10**6,
             vmem=VMEM_LARGE,
         )
-        if not last:
-            early = got[0]
-            before = [got[2], got[1]]
-    late, c_keep, c_send = got
+        before = [got[1], got[0]]
+    early, late, c_keep, c_send = got
     early, c_send = lax.optimization_barrier((early, c_send))
     early = turn(early)
 

time: 137 us -> 131 us (0.956)
  starting transfers between devices: 47.7 us -> 40.1 us
  waiting for transfers between devices: 61.4 us -> 64.1 us
    ppermute x9, starting transfers between devices: 30.6 us -> 16.5 us  [shift(): return lax.ppermute(value, 'ctx', [(i, (i + s) % n) for i in range(n)])]
    all_to_all x2, starting transfers between devices: 9.84 us -> 16.4 us  [turn(): return lax.all_to_all(value, 'ctx', split_axis=0, concat_axis=0, tiled=True)]
    ppermute x9, waiting for transfers between devices: 43 us -> 46.8 us  [shift(): return lax.ppermute(value, 'ctx', [(i, (i + s) % n) for i in range(n)])]
  transfers between devices with their start and end apart: 20 -> 20, of which waited for: 14 -> 15; matrix products, arithmetic and copies ran while one was open for 0% -> 0% of each run, Pallas kernels for 12% -> 11%
where the time goes in v4:
time: 131 us
  waiting for transfers between devices  64.1 us (49%)
  starting transfers between devices  40.1 us (31%)
  Pallas kernels  25.7 us (20%)
    ppermute x9, waiting for transfers between devices, shift(): return lax.ppermute(value, 'ctx', [(i, (i + s) % n) for i in range(n)])  46.8 us
    pallas_call x13, Pallas kernels, call(): pl.pallas_call(kernel, out_shape=out_shape, in_specs=in_specs, out_specs=...  25.7 us
    ppermute x9, starting transfers between devices, shift(): return lax.ppermute(value, 'ctx', [(i, (i + s) % n) for i in range(n)])  16.5 us
    all_to_all x2, starting transfers between devices, turn(): return lax.all_to_all(value, 'ctx', split_axis=0, concat_axis=0, tiled=True)  16.4 us
    ppermute x9, waiting for transfers between devices, swap(): return lax.ppermute(value, 'dp', [(i, i ^ k) for i in range(n_dp)])  11.5 us
    ppermute x9, starting transfers between devices, swap(): return lax.ppermute(value, 'dp', [(i, i ^ k) for i in range(n_dp)])  7.19 us
    all_to_all x2, waiting for transfers between devices, turn(): return lax.all_to_all(value, 'ctx', split_axis=0, concat_axis=0, tiled=True)  5.82 us
  transfers between devices with their start and end apart: 20, of which 15 were waited for; matrix products, arithmetic and copies ran while one was open for 0% of the time, Pallas kernels for 11%

profile of v4, /device:TPU:0, one launch (start us, length us, event | category | flops | bytes accessed | tf_op | source)
XLA Modules:
  0.0 130.8 jit_solution(15281960145240066913)
XLA Ops:
  0.7 0.1 concatenate.3.ids
  0.8 2.3 %pack0_1.1 = (bf16[736,256]{1,0:T(8,128)(2,1)S(1)}, bf16[736,256]{1,0:T(8,128)(2,1)S(1)}, bf16[736,256]{1,0:T(8,128)(2,1)S(1)}) custom-call(s32[18]{0:T(128)S(1)} %concatenate.3.ids, bf16[1,128,2560]{2,1,0:T(8,128)(2,1)} %k_ref.4, bf16[1,128,2560]{2,1,0:T(8,128)(2,1)} %v_ref.7, bf16[1,128,2560]{2,1,0:T(8,128)(2,1)} %q_ref.7, bf16[1,128,2560]{2,1,0:T(8,128)(2,1)} %o_ref.7, ...), custom_call_target="tpu_custom_call" | custom-call | flops 1000000 | bytes 1000000 | tf_op jit(solution)/shard_map/pack0_1/pallas_call | solution.py:40
  3.1 3.1 %collective-permute-start.3 = (bf16[736,256]{1,0:T(8,128)(2,1)S(1)}, bf16[736,256]{1,0:T(8,128)(2,1)S(1)}, u32[]{:S(2)}, u32[]{:S(2)}) collective-permute-start(bf16[736,256]{1,0:T(8,128)(2,1)S(1)} %get-tuple-element.50), channel_id=1, source_target_pairs={{0,1},{1,2},{2,3},{3,0},{4,5},{5,6},{6,7},{7,4},{8,9},{9,10},{10,1... | collective-permute-start | bytes 1130504 | tf_op jit(solution)/shard_map/ppermute | solution.py:377
  6.1 2.6 %collective-permute-start.4 = (bf16[736,256]{1,0:T(8,128)(2,1)S(1)}, bf16[736,256]{1,0:T(8,128)(2,1)S(1)}, u32[]{:S(2)}, u32[]{:S(2)}) collective-permute-start(bf16[736,256]{1,0:T(8,128)(2,1)S(1)} %get-tuple-element.51), channel_id=1, source_target_pairs={{0,2},{1,3},{2,0},{3,1},{4,6},{5,7},{6,4},{7,5},{8,10},{9,11},{10,... | collective-permute-start | bytes 1130504 | tf_op jit(solution)/shard_map/ppermute | solution.py:377
  8.7 1.3 %collective-permute-start.5 = (bf16[736,256]{1,0:T(8,128)(2,1)S(1)}, bf16[736,256]{1,0:T(8,128)(2,1)S(1)}, u32[]{:S(2)}, u32[]{:S(2)}) collective-permute-start(bf16[736,256]{1,0:T(8,128)(2,1)S(1)} %get-tuple-element.52), channel_id=1, source_target_pairs={{0,3},{1,0},{2,1},{3,2},{4,7},{5,4},{6,5},{7,6},{8,11},{9,8},{10,9... | collective-permute-start | bytes 1130504 | tf_op jit(solution)/shard_map/ppermute | solution.py:377
  10.1 2.2 %pack1_1.1 = (bf16[608,384]{1,0:T(8,128)(2,1)S(1)}, bf16[608,384]{1,0:T(8,128)(2,1)S(1)}, bf16[608,384]{1,0:T(8,128)(2,1)S(1)}) custom-call(s32[18]{0:T(128)S(1)} %concatenate.3.ids, bf16[1,128,2560]{2,1,0:T(8,128)(2,1)} %k_ref.4, bf16[1,128,2560]{2,1,0:T(8,128)(2,1)} %v_ref.7, bf16[1,128,2560]{2,1,0:T(8,128)(2,1)} %q_ref.7, bf16[1,128,2560]{2,1,0:T(8,128)(2,1)} %o_ref.7, ...), custom_call_target="tpu_custom_call" | custom-call | flops 1000000 | bytes 1000000 | tf_op jit(solution)/shard_map/pack1_1/pallas_call | solution.py:40
  12.2 0.7 collective-permute-start
  13.0 0.3 collective-permute-start.1
  13.3 4.6 %collective-permute-done.3.refs_1_ = bf16[736,256]{1,0:T(8,128)(2,1)S(1)} collective-permute-done((bf16[736,256]{1,0:T(8,128)(2,1)S(1)}, bf16[736,256]{1,0:T(8,128)(2,1)S(1)}, u32[]{:S(2)}, u32[]{:S(2)}) %collective-permute-start.3) | collective-permute-done | bytes 376864 | tf_op jit(solution)/shard_map/ppermute | solution.py:377
  17.9 2.5 %collective-permute-start.2 = (bf16[608,384]{1,0:T(8,128)(2,1)S(1)}, bf16[608,384]{1,0:T(8,128)(2,1)S(1)}, u32[]{:S(2)}, u32[]{:S(2)}) collective-permute-start(bf16[608,384]{1,0:T(8,128)(2,1)S(1)} %get-tuple-element.49), channel_id=1, source_target_pairs={{0,3},{1,0},{2,1},{3,2},{4,7},{5,4},{6,5},{7,6},{8,11},{9,8},{10,9... | collective-permute-start | bytes 1400840 | tf_op jit(solution)/shard_map/ppermute | solution.py:377
  20.4 1.7 %pack0_0.1.refs_0_ = bf16[736,256]{1,0:T(8,128)(2,1)S(1)} custom-call(s32[18]{0:T(128)S(1)} %concatenate.3.ids, bf16[1,128,2560]{2,1,0:T(8,128)(2,1)} %k_ref.4, bf16[1,128,2560]{2,1,0:T(8,128)(2,1)} %v_ref.7, bf16[1,128,2560]{2,1,0:T(8,128)(2,1)} %q_ref.7, bf16[1,128,2560]{2,1,0:T(8,128)(2,1)} %o_ref.7, f32[3,20,32,128]{3,2,1,0:T(8,128)} %s_ref.7, ...), custom_call_target="tpu_custom_call" | custom-call | flops 1000000 | bytes 1000000 | tf_op jit(solution)/shard_map/pack0_0/pallas_call | solution.py:40
  22.1 12.0 %collective-permute-done.4.refs_2_ = bf16[736,256]{1,0:T(8,128)(2,1)S(1)} collective-permute-done((bf16[736,256]{1,0:T(8,128)(2,1)S(1)}, bf16[736,256]{1,0:T(8,128)(2,1)S(1)}, u32[]{:S(2)}, u32[]{:S(2)}) %collective-permute-start.4) | collective-permute-done | bytes 376864 | tf_op jit(solution)/shard_map/ppermute | solution.py:377
  34.1 0.6 start_share.1.refs_4_
  34.7 0.1 collective-permute-start.6
  34.8 1.7 %pack1_0.1.refs_0_ = bf16[608,384]{1,0:T(8,128)(2,1)S(1)} custom-call(s32[18]{0:T(128)S(1)} %concatenate.3.ids, bf16[1,128,2560]{2,1,0:T(8,128)(2,1)} %k_ref.4, bf16[1,128,2560]{2,1,0:T(8,128)(2,1)} %v_ref.7, bf16[1,128,2560]{2,1,0:T(8,128)(2,1)} %q_ref.7, bf16[1,128,2560]{2,1,0:T(8,128)(2,1)} %o_ref.7, f32[3,20,32,128]{3,2,1,0:T(8,128)} %s_ref.7, ...), custom_call_target="tpu_custom_call" | custom-call | flops 1000000 | bytes 1000000 | tf_op jit(solution)/shard_map/pack1_0/pallas_call | solution.py:40
  36.5 4.8 %chunk0.1 = (bf16[4,256,256]{2,1,0:T(8,128)(2,1)S(1)}, bf16[6,128,128]{2,1,0:T(8,128)(2,1)S(1)}) custom-call(s32[18]{0:T(128)S(1)} %concatenate.3.ids, bf16[736,256]{1,0:T(8,128)(2,1)S(1)} %pack0_0.1.refs_0_, bf16[736,256]{1,0:T(8,128)(2,1)S(1)} %collective-permute-done.3.refs_1_, bf16[736,256]{1,0:T(8,128)(2,1)S(1)} %collective-permute-done.4.refs_2_, ...), custom_call_target="tpu_custom_call" | custom-call | flops 1280000000 | bytes 2000000 | tf_op jit(solution)/shard_map/chunk0/pallas_call | solution.py:40
  41.3 2.8 %collective-permute-done.refs_1_ = bf16[608,384]{1,0:T(8,128)(2,1)S(1)} collective-permute-done((bf16[608,384]{1,0:T(8,128)(2,1)S(1)}, bf16[608,384]{1,0:T(8,128)(2,1)S(1)}, u32[]{:S(2)}, u32[]{:S(2)}) %collective-permute-start) | collective-permute-done | bytes 466976 | tf_op jit(solution)/shard_map/ppermute | solution.py:377
  44.1 27.3 %collective-permute-done.1.refs_2_ = bf16[608,384]{1,0:T(8,128)(2,1)S(1)} collective-permute-done((bf16[608,384]{1,0:T(8,128)(2,1)S(1)}, bf16[608,384]{1,0:T(8,128)(2,1)S(1)}, u32[]{:S(2)}, u32[]{:S(2)}) %collective-permute-start.1) | collective-permute-done | bytes 466976 | tf_op jit(solution)/shard_map/ppermute | solution.py:377
  71.3 7.2 %chunk1.1 = (bf16[4,256,384]{2,1,0:T(8,128)(2,1)}, bf16[4,256,256]{2,1,0:T(8,128)(2,1)}, bf16[8,128,128]{2,1,0:T(8,128)(2,1)S(1)}, bf16[8,128,128]{2,1,0:T(8,128)(2,1)S(1)}) custom-call(s32[18]{0:T(128)S(1)} %concatenate.3.ids, bf16[608,384]{1,0:T(8,128)(2,1)S(1)} %pack1_0.1.refs_0_, bf16[608,384]{1,0:T(8,128)(2,1)S(1)} %collective-permute-done.refs_1_, ...), custom_call_target="tpu_custom_call" | custom-call | flops 1920000000 | bytes 3000000 | tf_op jit(solution)/shard_map/chunk1/pallas_call | solution.py:40
  78.5 12.8 %all-to-all-start = ((bf16[4,256,384]{2,1,0:T(8,128)(2,1)}), bf16[4,256,384]{2,1,0:T(8,128)(2,1)S(1)}, u32[]{:S(2)}, u32[]{:S(2)}) async-start(bf16[4,256,384]{2,1,0:T(8,128)(2,1)} %get-tuple-element.64), calls=%async_computation | async-start | bytes 1572864 | tf_op jit(solution)/shard_map/all_to_all | solution.py:380
  91.3 1.5 %collective-permute-done.7.got_ref = bf16[8,128,128]{2,1,0:T(8,128)(2,1)S(1)} collective-permute-done((bf16[8,128,128]{2,1,0:T(8,128)(2,1)S(1)}, bf16[8,128,128]{2,1,0:T(8,128)(2,1)S(1)}, u32[]{:S(2)}, u32[]{:S(2)}) %collective-permute-start.7) | collective-permute-done | bytes 262176 | tf_op jit(solution)/shard_map/ppermute | solution.py:372
  92.8 0.6 state_pair.1
  93.5 1.6 %collective-permute-start.8 = (bf16[2,128,128]{2,1,0:T(8,128)(2,1)S(1)}, bf16[2,128,128]{2,1,0:T(8,128)(2,1)S(1)}, u32[]{:S(2)}, u32[]{:S(2)}) collective-permute-start(bf16[2,128,128]{2,1,0:T(8,128)(2,1)S(1)} %get-tuple-element.60), channel_id=1, source_target_pairs={{0,8},{4,12},{8,0},{12,4},{16,24},{20,28},{24,16},{28,20},{1,9},{5... | collective-permute-start | bytes 196616 | tf_op jit(solution)/shard_map/ppermute | solution.py:372
  95.0 1.5 %collective-permute-start.9 = (bf16[2,128,128]{2,1,0:T(8,128)(2,1)S(1)}, bf16[2,128,128]{2,1,0:T(8,128)(2,1)S(1)}, u32[]{:S(2)}, u32[]{:S(2)}) collective-permute-start(bf16[2,128,128]{2,1,0:T(8,128)(2,1)S(1)} %get-tuple-element.61), channel_id=1, source_target_pairs={{0,16},{4,20},{8,24},{12,28},{16,0},{20,4},{24,8},{28,12},{1,17},{... | collective-permute-start | bytes 196616 | tf_op jit(solution)/shard_map/ppermute | solution.py:372
  96.6 0.5 collective-permute-start.10
  97.0 0.8 collective-permute-done.8.refs_1_
  97.8 1.5 %collective-permute-done.9.refs_2_ = bf16[2,128,128]{2,1,0:T(8,128)(2,1)S(1)} collective-permute-done((bf16[2,128,128]{2,1,0:T(8,128)(2,1)S(1)}, bf16[2,128,128]{2,1,0:T(8,128)(2,1)S(1)}, u32[]{:S(2)}, u32[]{:S(2)}) %collective-permute-start.9) | collective-permute-done | bytes 65568 | tf_op jit(solution)/shard_map/ppermute | solution.py:372
  99.3 2.4 %collective-permute-done.10.refs_3_ = bf16[2,128,128]{2,1,0:T(8,128)(2,1)S(1)} collective-permute-done((bf16[2,128,128]{2,1,0:T(8,128)(2,1)S(1)}, bf16[2,128,128]{2,1,0:T(8,128)(2,1)S(1)}, u32[]{:S(2)}, u32[]{:S(2)}) %collective-permute-start.10) | collective-permute-done | bytes 65568 | tf_op jit(solution)/shard_map/ppermute | solution.py:372
  101.7 0.6 state_sum.1
  102.3 2.1 %collective-permute-start.11 = (bf16[2,32,128]{2,1,0:T(8,128)(2,1)S(1)}, bf16[2,32,128]{2,1,0:T(8,128)(2,1)S(1)}, u32[]{:S(2)}, u32[]{:S(2)}) collective-permute-start(bf16[2,32,128]{2,1,0:T(8,128)(2,1)S(1)} %get-tuple-element.67), channel_id=1, source_target_pairs={{0,1},{1,2},{2,3},{3,0},{4,5},{5,6},{6,7},{7,4},{8,9},{9,10},{10,1... | collective-permute-start | bytes 49160 | tf_op jit(solution)/shard_map/ppermute | solution.py:377
  104.4 2.4 %collective-permute-start.12 = (bf16[2,32,128]{2,1,0:T(8,128)(2,1)S(1)}, bf16[2,32,128]{2,1,0:T(8,128)(2,1)S(1)}, u32[]{:S(2)}, u32[]{:S(2)}) collective-permute-start(bf16[2,32,128]{2,1,0:T(8,128)(2,1)S(1)} %get-tuple-element.68), channel_id=1, source_target_pairs={{0,2},{1,3},{2,0},{3,1},{4,6},{5,7},{6,4},{7,5},{8,10},{9,11},{10,... | collective-permute-start | bytes 49160 | tf_op jit(solution)/shard_map/ppermute | solution.py:377
  106.8 1.5 %collective-permute-start.13 = (bf16[2,32,128]{2,1,0:T(8,128)(2,1)S(1)}, bf16[2,32,128]{2,1,0:T(8,128)(2,1)S(1)}, u32[]{:S(2)}, u32[]{:S(2)}) collective-permute-start(bf16[2,32,128]{2,1,0:T(8,128)(2,1)S(1)} %get-tuple-element.69), channel_id=1, source_target_pairs={{0,3},{1,0},{2,1},{3,2},{4,7},{5,4},{6,5},{7,6},{8,11},{9,8},{10,9... | collective-permute-start | bytes 49160 | tf_op jit(solution)/shard_map/ppermute | solution.py:377
  108.2 3.4 %all-to-all-done.refs_0_ = bf16[4,256,384]{2,1,0:T(8,128)(2,1)S(1)} async-done(((bf16[4,256,384]{2,1,0:T(8,128)(2,1)}), bf16[4,256,384]{2,1,0:T(8,128)(2,1)S(1)}, u32[]{:S(2)}, u32[]{:S(2)}) %all-to-all-start) | async-done | bytes 786464 | tf_op jit(solution)/shard_map/all_to_all | solution.py:380
  111.6 0.2 collective-permute-done.12.refs_2_
  111.8 0.5 state_rows.1.refs_0_
  112.4 3.7 %all-to-all-start.1 = ((bf16[4,256,256]{2,1,0:T(8,128)(2,1)}), bf16[4,256,256]{2,1,0:T(8,128)(2,1)S(1)}, u32[]{:S(2)}, u32[]{:S(2)}) async-start(bf16[4,256,256]{2,1,0:T(8,128)(2,1)} %get-tuple-element.71), calls=%async_computation.1 | async-start | bytes 1048576 | tf_op jit(solution)/shard_map/all_to_all | solution.py:380
  116.0 2.4 %collective-permute-start.16 = (bf16[4,2,32,128]{3,2,1,0:T(8,128)(2,1)S(1)}, bf16[4,2,32,128]{3,2,1,0:T(8,128)(2,1)S(1)}, u32[]{:S(2)}, u32[]{:S(2)}) collective-permute-start(bf16[4,2,32,128]{3,2,1,0:T(8,128)(2,1)S(1)} %state_rows.1.refs_0_), channel_id=1, source_target_pairs={{0,24},{4,28},{8,16},{12,20},{16,8},{20,12},{24,0},{28,4},{1,25},{... | collective-permute-start | bytes 196616 | tf_op jit(solution)/shard_map/ppermute | solution.py:372
  118.5 0.5 collective-permute-start.15
  119.0 0.5 collective-permute-start.14
  119.5 2.1 %collective-permute-done.16.refs_3_ = bf16[4,2,32,128]{3,2,1,0:T(8,128)(2,1)S(1)} collective-permute-done((bf16[4,2,32,128]{3,2,1,0:T(8,128)(2,1)S(1)}, bf16[4,2,32,128]{3,2,1,0:T(8,128)(2,1)S(1)}, u32[]{:S(2)}, u32[]{:S(2)}) %collective-permute-start.16) | collective-permute-done | bytes 65568 | tf_op jit(solution)/shard_map/ppermute | solution.py:372
  121.6 1.1 collective-permute-done.15.refs_2_
  122.7 0.5 collective-permute-done.14.refs_1_
  123.2 0.6 state_rest.1.refs_0_
  123.8 0.1 collective-permute-start.17
  123.9 1.5 %collective-permute-done.17.refs_1_ = bf16[4,4,2,32,128]{4,3,2,1,0:T(8,128)(2,1)S(1)} collective-permute-done((bf16[4,4,2,32,128]{4,3,2,1,0:T(8,128)(2,1)S(1)}, bf16[4,4,2,32,128]{4,3,2,1,0:T(8,128)(2,1)S(1)}, u32[]{:S(2)}, u32[]{:S(2)}) %collective-permute-start.17) | collective-permute-done | bytes 262176 | tf_op jit(solution)/shard_map/ppermute | solution.py:372
  125.4 1.8 %state_out.1 = f32[3,20,32,128]{3,2,1,0:T(8,128)} custom-call(s32[18]{0:T(128)S(1)} %concatenate.3.ids, bf16[4,4,2,32,128]{4,3,2,1,0:T(8,128)(2,1)S(1)} %state_rest.1.refs_0_, bf16[4,4,2,32,128]{4,3,2,1,0:T(8,128)(2,1)S(1)} %collective-permute-done.17.refs_1_), custom_call_target="tpu_custom_call" | custom-call | flops 1000000 | bytes 1000000 | tf_op jit(solution)/shard_map/state_out/pallas_call | solution.py:40
  127.2 2.4 %all-to-all-done.1.refs_1_ = bf16[4,256,256]{2,1,0:T(8,128)(2,1)S(1)} async-done(((bf16[4,256,256]{2,1,0:T(8,128)(2,1)}), bf16[4,256,256]{2,1,0:T(8,128)(2,1)S(1)}, u32[]{:S(2)}, u32[]{:S(2)}) %all-to-all-start.1) | async-done | bytes 524320 | tf_op jit(solution)/shard_map/all_to_all | solution.py:380
  129.6 1.2 unpack.1
  (8 shorter events, 0.0 us)
Async XLA Ops:
  3.1 14.8 %collective-permute-start.3 = (bf16[736,256]{1,0:T(8,128)(2,1)S(1)}, bf16[736,256]{1,0:T(8,128)(2,1)S(1)}, u32[]{:S(2)}, u32[]{:S(2)}) collective-permute-start(bf16[736,256]{1,0:T(8,128)(2,1)S(1)} %get-tuple-element.50), channel_id=1, source_target_pairs={{0,1},{1,2},{2,3},{3,0},{4,5},{5,6},{6,7},{7,4},{8,9},{9,10},{10,1... | collective-permute-start | bytes 1130504 | tf_op jit(solution)/shard_map/ppermute | solution.py:377
  6.1 28.0 %collective-permute-start.4 = (bf16[736,256]{1,0:T(8,128)(2,1)S(1)}, bf16[736,256]{1,0:T(8,128)(2,1)S(1)}, u32[]{:S(2)}, u32[]{:S(2)}) collective-permute-start(bf16[736,256]{1,0:T(8,128)(2,1)S(1)} %get-tuple-element.51), channel_id=1, source_target_pairs={{0,2},{1,3},{2,0},{3,1},{4,6},{5,7},{6,4},{7,5},{8,10},{9,11},{10,... | collective-permute-start | bytes 1130504 | tf_op jit(solution)/shard_map/ppermute | solution.py:377
  8.7 25.4 %collective-permute-start.5 = (bf16[736,256]{1,0:T(8,128)(2,1)S(1)}, bf16[736,256]{1,0:T(8,128)(2,1)S(1)}, u32[]{:S(2)}, u32[]{:S(2)}) collective-permute-start(bf16[736,256]{1,0:T(8,128)(2,1)S(1)} %get-tuple-element.52), channel_id=1, source_target_pairs={{0,3},{1,0},{2,1},{3,2},{4,7},{5,4},{6,5},{7,6},{8,11},{9,8},{10,9... | collective-permute-start | bytes 1130504 | tf_op jit(solution)/shard_map/ppermute | solution.py:377
  12.2 31.8 %collective-permute-start = (bf16[608,384]{1,0:T(8,128)(2,1)S(1)}, bf16[608,384]{1,0:T(8,128)(2,1)S(1)}, u32[]{:S(2)}, u32[]{:S(2)}) collective-permute-start(bf16[608,384]{1,0:T(8,128)(2,1)S(1)} %get-tuple-element.47), channel_id=1, source_target_pairs={{0,1},{1,2},{2,3},{3,0},{4,5},{5,6},{6,7},{7,4},{8,9},{9,10},{10,1... | collective-permute-start | bytes 1400840 | tf_op jit(solution)/shard_map/ppermute | solution.py:377
  13.0 58.4 %collective-permute-start.1 = (bf16[608,384]{1,0:T(8,128)(2,1)S(1)}, bf16[608,384]{1,0:T(8,128)(2,1)S(1)}, u32[]{:S(2)}, u32[]{:S(2)}) collective-permute-start(bf16[608,384]{1,0:T(8,128)(2,1)S(1)} %get-tuple-element.48), channel_id=1, source_target_pairs={{0,2},{1,3},{2,0},{3,1},{4,6},{5,7},{6,4},{7,5},{8,10},{9,11},{10,... | collective-permute-start | bytes 1400840 | tf_op jit(solution)/shard_map/ppermute | solution.py:377
  17.9 53.5 %collective-permute-start.2 = (bf16[608,384]{1,0:T(8,128)(2,1)S(1)}, bf16[608,384]{1,0:T(8,128)(2,1)S(1)}, u32[]{:S(2)}, u32[]{:S(2)}) collective-permute-start(bf16[608,384]{1,0:T(8,128)(2,1)S(1)} %get-tuple-element.49), channel_id=1, source_target_pairs={{0,3},{1,0},{2,1},{3,2},{4,7},{5,4},{6,5},{7,6},{8,11},{9,8},{10,9... | collective-permute-start | bytes 1400840 | tf_op jit(solution)/shard_map/ppermute | solution.py:377
  34.7 1.8 %collective-permute-start.6 = (bf16[8,128,128]{2,1,0:T(8,128)(2,1)S(1)}, bf16[8,128,128]{2,1,0:T(8,128)(2,1)S(1)}, u32[]{:S(2)}, u32[]{:S(2)}) collective-permute-start(bf16[8,128,128]{2,1,0:T(8,128)(2,1)S(1)} %start_share.1.refs_4_), channel_id=1, source_target_pairs={{0,4},{4,0},{8,12},{12,8},{16,20},{20,16},{24,28},{28,24},{1,5},{5... | collective-permute-start | bytes 786440 | tf_op jit(solution)/shard_map/ppermute | solution.py:372
  78.5 33.1 %all-to-all-start = ((bf16[4,256,384]{2,1,0:T(8,128)(2,1)}), bf16[4,256,384]{2,1,0:T(8,128)(2,1)S(1)}, u32[]{:S(2)}, u32[]{:S(2)}) async-start(bf16[4,256,384]{2,1,0:T(8,128)(2,1)} %get-tuple-element.64), calls=%async_computation | async-start | bytes 1572864 | tf_op jit(solution)/shard_map/all_to_all | solution.py:380
  91.3 1.5 %collective-permute-start.7 = (bf16[8,128,128]{2,1,0:T(8,128)(2,1)S(1)}, bf16[8,128,128]{2,1,0:T(8,128)(2,1)S(1)}, u32[]{:S(2)}, u32[]{:S(2)}) collective-permute-start(bf16[8,128,128]{2,1,0:T(8,128)(2,1)S(1)} %get-tuple-element.58), channel_id=1, source_target_pairs={{0,4},{4,0},{8,12},{12,8},{16,20},{20,16},{24,28},{28,24},{1,5},{5... | collective-permute-start | bytes 786440 | tf_op jit(solution)/shard_map/ppermute | solution.py:372
  93.5 4.3 %collective-permute-start.8 = (bf16[2,128,128]{2,1,0:T(8,128)(2,1)S(1)}, bf16[2,128,128]{2,1,0:T(8,128)(2,1)S(1)}, u32[]{:S(2)}, u32[]{:S(2)}) collective-permute-start(bf16[2,128,128]{2,1,0:T(8,128)(2,1)S(1)} %get-tuple-element.60), channel_id=1, source_target_pairs={{0,8},{4,12},{8,0},{12,4},{16,24},{20,28},{24,16},{28,20},{1,9},{5... | collective-permute-start | bytes 196616 | tf_op jit(solution)/shard_map/ppermute | solution.py:372
  95.0 4.3 %collective-permute-start.9 = (bf16[2,128,128]{2,1,0:T(8,128)(2,1)S(1)}, bf16[2,128,128]{2,1,0:T(8,128)(2,1)S(1)}, u32[]{:S(2)}, u32[]{:S(2)}) collective-permute-start(bf16[2,128,128]{2,1,0:T(8,128)(2,1)S(1)} %get-tuple-element.61), channel_id=1, source_target_pairs={{0,16},{4,20},{8,24},{12,28},{16,0},{20,4},{24,8},{28,12},{1,17},{... | collective-permute-start | bytes 196616 | tf_op jit(solution)/shard_map/ppermute | solution.py:372
  96.6 5.2 %collective-permute-start.10 = (bf16[2,128,128]{2,1,0:T(8,128)(2,1)S(1)}, bf16[2,128,128]{2,1,0:T(8,128)(2,1)S(1)}, u32[]{:S(2)}, u32[]{:S(2)}) collective-permute-start(bf16[2,128,128]{2,1,0:T(8,128)(2,1)S(1)} %get-tuple-element.62), channel_id=1, source_target_pairs={{0,24},{4,28},{8,16},{12,20},{16,8},{20,12},{24,0},{28,4},{1,25},{... | collective-permute-start | bytes 196616 | tf_op jit(solution)/shard_map/ppermute | solution.py:372
  102.3 9.3 %collective-permute-start.11 = (bf16[2,32,128]{2,1,0:T(8,128)(2,1)S(1)}, bf16[2,32,128]{2,1,0:T(8,128)(2,1)S(1)}, u32[]{:S(2)}, u32[]{:S(2)}) collective-permute-start(bf16[2,32,128]{2,1,0:T(8,128)(2,1)S(1)} %get-tuple-element.67), channel_id=1, source_target_pairs={{0,1},{1,2},{2,3},{3,0},{4,5},{5,6},{6,7},{7,4},{8,9},{9,10},{10,1... | collective-permute-start | bytes 49160 | tf_op jit(solution)/shard_map/ppermute | solution.py:377
  104.4 7.4 %collective-permute-start.12 = (bf16[2,32,128]{2,1,0:T(8,128)(2,1)S(1)}, bf16[2,32,128]{2,1,0:T(8,128)(2,1)S(1)}, u32[]{:S(2)}, u32[]{:S(2)}) collective-permute-start(bf16[2,32,128]{2,1,0:T(8,128)(2,1)S(1)} %get-tuple-element.68), channel_id=1, source_target_pairs={{0,2},{1,3},{2,0},{3,1},{4,6},{5,7},{6,4},{7,5},{8,10},{9,11},{10,... | collective-permute-start | bytes 49160 | tf_op jit(solution)/shard_map/ppermute | solution.py:377
  106.8 5.0 %collective-permute-start.13 = (bf16[2,32,128]{2,1,0:T(8,128)(2,1)S(1)}, bf16[2,32,128]{2,1,0:T(8,128)(2,1)S(1)}, u32[]{:S(2)}, u32[]{:S(2)}) collective-permute-start(bf16[2,32,128]{2,1,0:T(8,128)(2,1)S(1)} %get-tuple-element.69), channel_id=1, source_target_pairs={{0,3},{1,0},{2,1},{3,2},{4,7},{5,4},{6,5},{7,6},{8,11},{9,8},{10,9... | collective-permute-start | bytes 49160 | tf_op jit(solution)/shard_map/ppermute | solution.py:377
  112.4 17.3 %all-to-all-start.1 = ((bf16[4,256,256]{2,1,0:T(8,128)(2,1)}), bf16[4,256,256]{2,1,0:T(8,128)(2,1)S(1)}, u32[]{:S(2)}, u32[]{:S(2)}) async-start(bf16[4,256,256]{2,1,0:T(8,128)(2,1)} %get-tuple-element.71), calls=%async_computation.1 | async-start | bytes 1048576 | tf_op jit(solution)/shard_map/all_to_all | solution.py:380
  116.0 5.6 %collective-permute-start.16 = (bf16[4,2,32,128]{3,2,1,0:T(8,128)(2,1)S(1)}, bf16[4,2,32,128]{3,2,1,0:T(8,128)(2,1)S(1)}, u32[]{:S(2)}, u32[]{:S(2)}) collective-permute-start(bf16[4,2,32,128]{3,2,1,0:T(8,128)(2,1)S(1)} %state_rows.1.refs_0_), channel_id=1, source_target_pairs={{0,24},{4,28},{8,16},{12,20},{16,8},{20,12},{24,0},{28,4},{1,25},{... | collective-permute-start | bytes 196616 | tf_op jit(solution)/shard_map/ppermute | solution.py:372
  118.5 4.3 %collective-permute-start.15 = (bf16[4,2,32,128]{3,2,1,0:T(8,128)(2,1)S(1)}, bf16[4,2,32,128]{3,2,1,0:T(8,128)(2,1)S(1)}, u32[]{:S(2)}, u32[]{:S(2)}) collective-permute-start(bf16[4,2,32,128]{3,2,1,0:T(8,128)(2,1)S(1)} %state_rows.1.refs_0_), channel_id=1, source_target_pairs={{0,16},{4,20},{8,24},{12,28},{16,0},{20,4},{24,8},{28,12},{1,17},{... | collective-permute-start | bytes 196616 | tf_op jit(solution)/shard_map/ppermute | solution.py:372
  119.0 4.3 %collective-permute-start.14 = (bf16[4,2,32,128]{3,2,1,0:T(8,128)(2,1)S(1)}, bf16[4,2,32,128]{3,2,1,0:T(8,128)(2,1)S(1)}, u32[]{:S(2)}, u32[]{:S(2)}) collective-permute-start(bf16[4,2,32,128]{3,2,1,0:T(8,128)(2,1)S(1)} %state_rows.1.refs_0_), channel_id=1, source_target_pairs={{0,8},{4,12},{8,0},{12,4},{16,24},{20,28},{24,16},{28,20},{1,9},{5... | collective-permute-start | bytes 196616 | tf_op jit(solution)/shard_map/ppermute | solution.py:372
  123.8 1.6 %collective-permute-start.17 = (bf16[4,4,2,32,128]{4,3,2,1,0:T(8,128)(2,1)S(1)}, bf16[4,4,2,32,128]{4,3,2,1,0:T(8,128)(2,1)S(1)}, u32[]{:S(2)}, u32[]{:S(2)}) collective-permute-start(bf16[4,4,2,32,128]{4,3,2,1,0:T(8,128)(2,1)S(1)} %state_rest.1.refs_0_), channel_id=1, source_target_pairs={{0,4},{4,0},{8,12},{12,8},{16,20},{20,16},{24,28},{28,24},{1,5},{5... | collective-permute-start | bytes 786440 | tf_op jit(solution)/shard_map/ppermute | solution.py:372

commit v5 on v4

--- a/solution.py
+++ b/solution.py
@@ -97,18 +97,27 @@
         self.mats = 3 * self.per
         least = max(1, self.per // 2)
         self.chunks = [(0, least), (least, self.per - least)]
-        self.early = (self.per + 1) // 2
         self.pair = min(2, n_dp)
         self.rest = n_dp // self.pair
         self.own = -(-self.mats // n_dp)
         self.block = -(-rows // 16) * 16
         self.share = -(-self.mats // self.pair)
         self.share_blocks = -(-self.share // least)
-        self.ids = {}
-        at = 0
-        for name, size in (("to", n), ("from", n), ("head", n), ("rest", self.rest), ("mine", 1), ("place", 1)):
-            self.ids[name] = at
-            at += size
+
+    def to(self, me, slot):
+        return lax.rem(me[0] + slot, self.n)
+
+    def source(self, me, slot):
+        return lax.rem(me[0] + (self.n - slot), self.n)
+
+    def head(self, me, slot):
+        return jnp.minimum(self.to(me, slot) * self.per, self.heads - self.per)
+
+    def mine(self, dp):
+        return lax.rem(dp[0], self.pair)
+
+    def other(self, dp, k):
+        return jnp.bitwise_xor(lax.div(dp[0], self.pair), k)
 
     def packed_rows(self, chunk):
         return 4 * self.tokens + (3 + (self.share_blocks if chunk == 0 else 0)) * self.block
@@ -117,7 +126,7 @@
         return min(c * self.per, self.heads - self.per)
 
 
-def pack_kernel(ids, k_ref, v_ref, q_ref, o_ref, s_ref, t_ref, *refs, plan, slots, chunk):
+def pack_kernel(me, dp, k_ref, v_ref, q_ref, o_ref, s_ref, t_ref, *refs, plan, slots, chunk):
     t, w = plan.tokens, plan.width
     first, count = plan.chunks[chunk]
     outs, (state, sems) = refs[:-2], refs[-2:]
@@ -125,7 +134,7 @@
     loads = []
     copies = []
     for k, slot in enumerate(slots):
-        head = ids[plan.ids["head"] + slot]
+        head = plan.head(me, slot)
         wanted = [(t_ref.at[0, :, pl.ds(head + first, count)], state.at[k, :, pl.ds(0, count)])]
         if chunk == 0:
             wanted.append((s_ref.at[:, pl.ds(head, per)], state.at[k, :, pl.ds(count, per)]))
@@ -146,7 +155,7 @@
                 top = 4 * t + m * plan.block
                 outs[k][top : top + plan.rows, j * w : (j + 1) * w] = state[k, m, j].astype(BF16)
         for q in range(plan.share if chunk == 0 else 0):
-            mat = jnp.minimum(ids[plan.ids["mine"]] * plan.share + q, plan.mats - 1)
+            mat = jnp.minimum(plan.mine(dp) * plan.share + q, plan.mats - 1)
             top = 4 * t + (3 + q // count) * plan.block
             left = (q % count) * w
             part = state[k, lax.rem(mat, 3), count + lax.div(mat, 3)]
@@ -155,11 +164,11 @@
         copy.wait()
 
 
-def start_kernel(ids, *refs, plan):
+def start_kernel(me, *refs, plan):
     in_refs, (out, whole) = refs[: plan.n], refs[plan.n :]
     count, w = plan.chunks[0][1], plan.width
     for slot in range(plan.n):
-        at = pl.ds(pl.multiple_of(ids[plan.ids["from"] + slot] * plan.rows, plan.rows), plan.rows)
+        at = pl.ds(pl.multiple_of(plan.source(me, slot) * plan.rows, plan.rows), plan.rows)
         for q in range(plan.share):
             top = 4 * plan.tokens + (3 + q // count) * plan.block
             left = (q % count) * w
@@ -190,7 +199,7 @@
     return (ab[:, :w], ab[:, w:], dot_tn(y, hidden)), (g, u, p, s), (dg, du, hidden)
 
 
-def chunk_kernel(ids, *refs, plan, chunk):
+def chunk_kernel(me, dp, *refs, plan, chunk):
     n, t, w = plan.n, plan.tokens, plan.width
     first, count = plan.chunks[chunk]
     last = chunk + 1 == len(plan.chunks)
@@ -204,22 +213,22 @@
 
     in_refs = take(n)
     shares = take(plan.pair)
-    before, held = take(2) if last else (None, None)
-    d_refs = take(2 if last else 1)
+    (before,) = take(1) if last else (None,)
+    (d_ref,) = take(1)
     c_refs = take(2 if last else 1)
     w0, w1, gsum, ssum, acts, fields = take(6)
     total = take(1)[0] if last else c_refs[0]
     base = 3 * first if last else 0
 
     for slot in range(n):
-        at = pl.ds(pl.multiple_of(ids[plan.ids["from"] + slot] * plan.rows, plan.rows), plan.rows)
+        at = pl.ds(pl.multiple_of(plan.source(me, slot) * plan.rows, plan.rows), plan.rows)
         for j in range(count):
             for m in range(3):
                 top = 4 * t + m * plan.block
                 part = in_refs[slot][top : top + plan.rows, j * w : (j + 1) * w]
                 w1[3 * j + m, at, :] = part.astype(F32)
     for k, part in enumerate(shares):
-        at = jnp.bitwise_xor(ids[plan.ids["mine"]], k) * plan.share
+        at = jnp.bitwise_xor(plan.mine(dp), k) * plan.share
         w0[pl.ds(at, plan.share)] = part[...]
 
     for j in range(count):
@@ -258,10 +267,9 @@
         dg, du, hidden = fields[j, 0], fields[j, 1], fields[j, 2]
         dx = dot_nt(jnp.concatenate([dg, du, cg, cu], axis=1), jnp.concatenate([fab, wab], axis=1))
         dy = dot_nt(jnp.concatenate([hidden, cp], axis=1), jnp.concatenate([fc, wc], axis=1))
-        d_ref, at = (d_refs[0], first + j) if first + j < plan.early else (d_refs[1], first + j - plan.early)
-        cols = slice(at * w, (at + 1) * w)
+        cols = slice(j * w, (j + 1) * w)
         for slot in range(n):
-            to = ids[plan.ids["from"] + slot]
+            to = plan.source(me, slot)
             d_ref[to, 0:t, cols] = dx[slot * t : (slot + 1) * t].astype(BF16)
             d_ref[to, t : 2 * t, cols] = dy[slot * t : (slot + 1) * t].astype(BF16)
         ab = dot_tn(x, jnp.concatenate([cg, cu], axis=1))
@@ -271,46 +279,49 @@
 
     if last:
         total[0 : before.shape[0]] = before[...]
-        d_refs[0][:, :, 0 : held.shape[2]] = held[...]
         for m in range(plan.mats, plan.n_dp * plan.own):
             total[m] = jnp.zeros((w, w), BF16)
-        mine = ids[plan.ids["mine"]]
+        mine = plan.mine(dp)
         for r in range(plan.rest):
             to = slice(r * plan.own, (r + 1) * plan.own)
             for ref, which in zip(c_refs, (mine, plan.pair - 1 - mine)):
                 ref[to] = total[pl.ds((plan.pair * r + which) * plan.own, plan.own)]
 
 
-def pair_kernel(ids, keep_ref, got_ref, *refs, plan):
+def pair_kernel(dp, keep_ref, got_ref, *refs, plan):
     outs, whole = refs[:-1], refs[-1]
     whole[...] = keep_ref[...].astype(F32) + got_ref[...].astype(F32)
     for k in range(plan.rest):
-        outs[k][...] = whole[pl.ds(ids[plan.ids["rest"] + k] * plan.own, plan.own)].astype(BF16)
-
-
-def sum_kernel(ids, *refs, plan):
+        outs[k][...] = whole[pl.ds(plan.other(dp, k) * plan.own, plan.own)].astype(BF16)
+
+
+def sum_kernel(me, *refs, plan):
     parts, outs, whole = refs[: plan.rest], refs[plan.rest : -1], refs[-1]
     added = parts[0][...].astype(F32)
     for part in parts[1:]:
         added = added + part[...].astype(F32)
     whole[...] = added / plan.n_dp
     for slot in range(plan.n):
-        at = pl.ds(pl.multiple_of(ids[plan.ids["to"] + slot] * plan.rows, plan.rows), plan.rows)
+        at = pl.ds(pl.multiple_of(plan.to(me, slot) * plan.rows, plan.rows), plan.rows)
         outs[slot][...] = whole[:, at, :].astype(BF16)
 
 
-def order_kernel(ids, *refs, plan, name):
-    parts, out = refs[:-1], refs[-1]
-    for k, part in enumerate(parts):
-        out[ids[plan.ids[name] + k]] = part[...]
-
-
-def state_kernel(ids, *refs, plan):
+def rows_kernel(me, *refs, plan):
+    for slot, part in enumerate(refs[:-1]):
+        refs[-1][plan.source(me, slot)] = part[...]
+
+
+def rest_kernel(dp, *refs, plan):
+    for k, part in enumerate(refs[:-1]):
+        refs[-1][plan.other(dp, k)] = part[...]
+
+
+def state_kernel(dp, *refs, plan):
     out = refs[-1]
     for k in range(plan.pair):
         for r in range(plan.rest):
             for i in range(plan.own):
-                mat = (plan.pair * r + jnp.bitwise_xor(ids[plan.ids["mine"]], k)) * plan.own + i
+                mat = (plan.pair * r + jnp.bitwise_xor(plan.mine(dp), k)) * plan.own + i
 
                 @pl.when(mat < plan.mats)
                 def _(mat=mat, ref=refs[k], r=r, i=i):
@@ -323,8 +334,7 @@
     t, w = plan.tokens, plan.width
     ins, (dk, dv, sems) = refs[:-3], refs[-3:]
     copies = []
-    parts = [(0, plan.early), (plan.early, plan.per - plan.early)]
-    for c, (first, count) in enumerate(parts):
+    for c, (first, count) in enumerate(plan.chunks):
         for owner in range(plan.n):
             cols = pl.ds((plan.first_head(owner) + first) * w, count * w)
             for part, dst in enumerate((dk, dv)):
@@ -351,20 +361,7 @@
     per, own, chunks = plan.per, plan.own, plan.chunks
     bind = lambda kernel, **more: functools.partial(kernel, plan=plan, **more)
 
-    me, dp = lax.axis_index("ctx"), lax.axis_index("dp")
-    places = jnp.arange(n, dtype=jnp.int32)
-    to_ids = lax.rem(me + places, n)
-    place = lax.div(dp, plan.pair)
-    ids = jnp.concatenate(
-        [
-            to_ids,
-            lax.rem(me + n - places, n),
-            jnp.minimum(to_ids * per, heads - per),
-            jnp.bitwise_xor(place, jnp.arange(plan.rest, dtype=jnp.int32)),
-            lax.rem(dp, plan.pair).reshape(1),
-            place.reshape(1),
-        ]
-    )
+    me, dp = lax.axis_index("ctx").reshape(1), lax.axis_index("dp").reshape(1)
 
     def swap(value, k):
         if k == 0:
@@ -387,8 +384,8 @@
         outs = call(
             bind(pack_kernel, slots=slots, chunk=c),
             [shape(plan.packed_rows(c), chunks[c][1] * width)] * len(slots),
-            (ids, *[pltpu.with_memory_space_constraint(arg, pltpu.HBM) for arg in args]),
-            [SMEM] + [HBM] * 6,
+            (me, dp, *[pltpu.with_memory_space_constraint(arg, pltpu.HBM) for arg in args]),
+            [SMEM] * 2 + [HBM] * 6,
             [VMEM] * len(slots),
             f"pack{c}_{slots[0]}",
             [
@@ -408,7 +405,7 @@
     start_own = call(
         bind(start_kernel),
         shape(plan.share, width, width),
-        (ids, *arrived[0]),
+        (me, *arrived[0]),
         [SMEM] + [VMEM] * n,
         VMEM,
         "start_share",
@@ -417,13 +414,14 @@
     shares = [swap(start_own, k) for k in range(plan.pair)]
 
     before = []
+    grads = []
     for c, (_, count) in enumerate(chunks):
         last = c + 1 == len(chunks)
         if last:
-            outs = [shape(n, 2 * t, size * width) for size in (plan.early, per - plan.early)]
-            outs += [shape(plan.rest * own, width, width)] * 2
+            outs = [shape(plan.rest * own, width, width)] * 2
         else:
-            outs = [shape(n, 2 * t, count * width), shape(3 * count, width, width)]
+            outs = [shape(3 * count, width, width)]
+        outs = [shape(n, 2 * t, count * width)] + outs
         scratch = [pltpu.VMEM((plan.pair * plan.share, width, width), BF16)]
         scratch += [pltpu.VMEM((3 * count, width, width), F32)] * 3 + [
             pltpu.VMEM((count, 4, n * t, width), F32),
@@ -434,8 +432,8 @@
         got = call(
             bind(chunk_kernel, chunk=c),
             outs,
-            (ids, *arrived[c], *shares, *before),
-            [SMEM] + [VMEM] * (n + plan.pair + len(before)),
+            (me, dp, *arrived[c], *shares, *before),
+            [SMEM] * 2 + [VMEM] * (n + plan.pair + len(before)),
             [VMEM] * len(outs),
             f"chunk{c}",
             scratch,
@@ -443,15 +441,17 @@
             size=count * 10**6,
             vmem=VMEM_LARGE,
         )
-        before = [got[1], got[0]]
-    early, late, c_keep, c_send = got
+        grads.append(got[0])
+        before = [got[1]]
+    late, early = grads
+    c_keep, c_send = got[1:]
     early, c_send = lax.optimization_barrier((early, c_send))
     early = turn(early)
 
     halves = call(
         bind(pair_kernel),
         [shape(own, width, width)] * plan.rest,
-        (ids, c_keep, swap(c_send, plan.pair - 1)),
+        (dp, c_keep, swap(c_send, plan.pair - 1)),
         [SMEM] + [VMEM] * 2,
         [VMEM] * plan.rest,
         "state_pair",
@@ -461,7 +461,7 @@
     by_rows = call(
         bind(sum_kernel),
         [shape(own, rows, width)] * n,
-        (ids, *halves),
+        (me, *halves),
         [SMEM] + [VMEM] * plan.rest,
         [VMEM] * n,
         "state_sum",
@@ -470,9 +470,9 @@
     by_rows = [shift(by_rows[s], s) for s in range(n)]
     by_rows[0], early = lax.optimization_barrier((by_rows[0], early))
     mine = call(
-        bind(order_kernel, name="from"),
+        bind(rows_kernel),
         shape(n, own, rows, width),
-        (ids, *by_rows),
+        (me, *by_rows),
         [SMEM] + [VMEM] * n,
         VMEM,
         "state_rows",
@@ -481,9 +481,9 @@
     late = turn(late)
     rest = [swap(mine, plan.pair * k) for k in range(plan.rest)]
     half = call(
-        bind(order_kernel, name="rest"),
+        bind(rest_kernel),
         shape(plan.rest, n, own, rows, width),
-        (ids, *rest),
+        (dp, *rest),
         [SMEM] + [VMEM] * plan.rest,
         VMEM,
         "state_rest",
@@ -492,7 +492,7 @@
     grad_state = call(
         bind(state_kernel),
         shape(*state_start.shape, dtype=F32),
-        (ids, *both),
+        (dp, *both),
         [SMEM] + [VMEM] * plan.pair,
         VMEM,
         "state_out",
@@ -500,7 +500,7 @@
     grad_keys, grad_values = call(
         bind(unpack_kernel),
         [shape(*keys_a.shape), shape(*values_a.shape)],
-        (early, late),
+        (late, early),
         [VMEM] * 2,
         [ANY] * 2,
         "unpack",

time: 131 us -> 129 us (0.985)
  Pallas kernels: 25.7 us -> 19.7 us
  waiting for transfers between devices: 64.1 us -> 68.4 us
    pallas_call x13, Pallas kernels: 25.7 us -> 19.7 us  [call(): pl.pallas_call(kernel, out_shape=out_shape, in_specs=in_specs, out_specs=...]
    all_to_all x2, waiting for transfers between devices: 5.82 us -> 8.1 us  [turn(): return lax.all_to_all(value, 'ctx', split_axis=0, concat_axis=0, tiled=True)]
    ppermute x9, waiting for transfers between devices: 46.8 us -> 48.5 us  [shift(): return lax.ppermute(value, 'ctx', [(i, (i + s) % n) for i in range(n)])]
  transfers between devices with their start and end apart: 20 -> 20, of which waited for: 15 -> 16; matrix products, arithmetic and copies ran while one was open for 0% -> 0% of each run, Pallas kernels for 11% -> 8%
where the time goes in v5:
time: 129 us
  waiting for transfers between devices  68.4 us (53%)
  starting transfers between devices  40.1 us (31%)
  Pallas kernels  19.7 us (15%)
    ppermute x9, waiting for transfers between devices, shift(): return lax.ppermute(value, 'ctx', [(i, (i + s) % n) for i in range(n)])  48.5 us
    pallas_call x13, Pallas kernels, call(): pl.pallas_call(kernel, out_shape=out_shape, in_specs=in_specs, out_specs=...  19.7 us
    ppermute x9, starting transfers between devices, shift(): return lax.ppermute(value, 'ctx', [(i, (i + s) % n) for i in range(n)])  16.5 us
    all_to_all x2, starting transfers between devices, turn(): return lax.all_to_all(value, 'ctx', split_axis=0, concat_axis=0, tiled=True)  16.4 us
    ppermute x9, waiting for transfers between devices, swap(): return lax.ppermute(value, 'dp', [(i, i ^ k) for i in range(n_dp)])  11.8 us
    all_to_all x2, waiting for transfers between devices, turn(): return lax.all_to_all(value, 'ctx', split_axis=0, concat_axis=0, tiled=True)  8.1 us
    ppermute x9, starting transfers between devices, swap(): return lax.ppermute(value, 'dp', [(i, i ^ k) for i in range(n_dp)])  7.19 us
  transfers between devices with their start and end apart: 20, of which 16 were waited for; matrix products, arithmetic and copies ran while one was open for 0% of the time, Pallas kernels for 8%

profile of v5, /device:TPU:0, one launch (start us, length us, event | category | flops | bytes accessed | tf_op | source)
XLA Modules:
  0.0 128.9 jit_solution(5528297017732075778)
XLA Ops:
  0.6 1.7 %pack0_1.1 = (bf16[736,256]{1,0:T(8,128)(2,1)S(1)}, bf16[736,256]{1,0:T(8,128)(2,1)S(1)}, bf16[736,256]{1,0:T(8,128)(2,1)S(1)}) custom-call(s32[1]{0:T(128)} %bitcast.me, s32[1]{0:T(128)} %bitcast.1.dp, bf16[1,128,2560]{2,1,0:T(8,128)(2,1)} %k_ref.4, bf16[1,128,2560]{2,1,0:T(8,128)(2,1)} %v_ref.7, bf16[1,128,2560]{2,1,0:T(8,128)(2,1)} %q_ref.7, ...), custom_call_target="tpu_custom_call" | custom-call | flops 1000000 | bytes 1000000 | tf_op jit(solution)/shard_map/pack0_1/pallas_call | solution.py:40
  2.4 3.1 %collective-permute-start.3 = (bf16[736,256]{1,0:T(8,128)(2,1)S(1)}, bf16[736,256]{1,0:T(8,128)(2,1)S(1)}, u32[]{:S(2)}, u32[]{:S(2)}) collective-permute-start(bf16[736,256]{1,0:T(8,128)(2,1)S(1)} %get-tuple-element.49), channel_id=1, source_target_pairs={{0,1},{1,2},{2,3},{3,0},{4,5},{5,6},{6,7},{7,4},{8,9},{9,10},{10,1... | collective-permute-start | bytes 1130504 | tf_op jit(solution)/shard_map/ppermute | solution.py:374
  5.4 2.6 %collective-permute-start.4 = (bf16[736,256]{1,0:T(8,128)(2,1)S(1)}, bf16[736,256]{1,0:T(8,128)(2,1)S(1)}, u32[]{:S(2)}, u32[]{:S(2)}) collective-permute-start(bf16[736,256]{1,0:T(8,128)(2,1)S(1)} %get-tuple-element.50), channel_id=1, source_target_pairs={{0,2},{1,3},{2,0},{3,1},{4,6},{5,7},{6,4},{7,5},{8,10},{9,11},{10,... | collective-permute-start | bytes 1130504 | tf_op jit(solution)/shard_map/ppermute | solution.py:374
  8.0 1.3 %collective-permute-start.5 = (bf16[736,256]{1,0:T(8,128)(2,1)S(1)}, bf16[736,256]{1,0:T(8,128)(2,1)S(1)}, u32[]{:S(2)}, u32[]{:S(2)}) collective-permute-start(bf16[736,256]{1,0:T(8,128)(2,1)S(1)} %get-tuple-element.51), channel_id=1, source_target_pairs={{0,3},{1,0},{2,1},{3,2},{4,7},{5,4},{6,5},{7,6},{8,11},{9,8},{10,9... | collective-permute-start | bytes 1130504 | tf_op jit(solution)/shard_map/ppermute | solution.py:374
  9.4 1.6 %pack1_1.1 = (bf16[608,384]{1,0:T(8,128)(2,1)S(1)}, bf16[608,384]{1,0:T(8,128)(2,1)S(1)}, bf16[608,384]{1,0:T(8,128)(2,1)S(1)}) custom-call(s32[1]{0:T(128)} %bitcast.me, s32[1]{0:T(128)} %bitcast.1.dp, bf16[1,128,2560]{2,1,0:T(8,128)(2,1)} %k_ref.4, bf16[1,128,2560]{2,1,0:T(8,128)(2,1)} %v_ref.7, bf16[1,128,2560]{2,1,0:T(8,128)(2,1)} %q_ref.7, ...), custom_call_target="tpu_custom_call" | custom-call | flops 1000000 | bytes 1000000 | tf_op jit(solution)/shard_map/pack1_1/pallas_call | solution.py:40
  11.0 0.7 collective-permute-start
  11.7 0.3 collective-permute-start.1
  12.1 5.1 %collective-permute-done.3.refs_1_ = bf16[736,256]{1,0:T(8,128)(2,1)S(1)} collective-permute-done((bf16[736,256]{1,0:T(8,128)(2,1)S(1)}, bf16[736,256]{1,0:T(8,128)(2,1)S(1)}, u32[]{:S(2)}, u32[]{:S(2)}) %collective-permute-start.3) | collective-permute-done | bytes 376864 | tf_op jit(solution)/shard_map/ppermute | solution.py:374
  17.2 2.5 %collective-permute-start.2 = (bf16[608,384]{1,0:T(8,128)(2,1)S(1)}, bf16[608,384]{1,0:T(8,128)(2,1)S(1)}, u32[]{:S(2)}, u32[]{:S(2)}) collective-permute-start(bf16[608,384]{1,0:T(8,128)(2,1)S(1)} %get-tuple-element.48), channel_id=1, source_target_pairs={{0,3},{1,0},{2,1},{3,2},{4,7},{5,4},{6,5},{7,6},{8,11},{9,8},{10,9... | collective-permute-start | bytes 1400840 | tf_op jit(solution)/shard_map/ppermute | solution.py:374
  19.7 1.2 pack0_0.1.refs_0_
  20.8 12.6 %collective-permute-done.4.refs_2_ = bf16[736,256]{1,0:T(8,128)(2,1)S(1)} collective-permute-done((bf16[736,256]{1,0:T(8,128)(2,1)S(1)}, bf16[736,256]{1,0:T(8,128)(2,1)S(1)}, u32[]{:S(2)}, u32[]{:S(2)}) %collective-permute-start.4) | collective-permute-done | bytes 376864 | tf_op jit(solution)/shard_map/ppermute | solution.py:374
  33.4 0.0 collective-permute-done.5.refs_3_
  33.4 0.1 start_share.1.refs_4_
  33.5 0.1 collective-permute-start.6
  33.5 1.2 pack1_0.1.refs_0_
  34.7 0.3 collective-permute-done.6.refs_5_
  35.1 5.0 %chunk0.1 = (bf16[4,256,256]{2,1,0:T(8,128)(2,1)}, bf16[6,128,128]{2,1,0:T(8,128)(2,1)S(1)}) custom-call(s32[1]{0:T(128)} %bitcast.me, s32[1]{0:T(128)} %bitcast.1.dp, bf16[736,256]{1,0:T(8,128)(2,1)S(1)} %pack0_0.1.refs_0_, bf16[736,256]{1,0:T(8,128)(2,1)S(1)} %collective-permute-done.3.refs_1_, bf16[736,256]{1,0:T(8,128)(2,1)S(1)} %collective-permute-done.4.refs_2_, ...), custom_call_target="tpu_custom_call" | custom-call | flops 1280000000 | bytes 2000000 | tf_op jit(solution)/shard_map/chunk0/pallas_call | solution.py:40
  40.0 3.4 %collective-permute-done.refs_1_ = bf16[608,384]{1,0:T(8,128)(2,1)S(1)} collective-permute-done((bf16[608,384]{1,0:T(8,128)(2,1)S(1)}, bf16[608,384]{1,0:T(8,128)(2,1)S(1)}, u32[]{:S(2)}, u32[]{:S(2)}) %collective-permute-start) | collective-permute-done | bytes 466976 | tf_op jit(solution)/shard_map/ppermute | solution.py:374
  43.4 27.3 %collective-permute-done.1.refs_2_ = bf16[608,384]{1,0:T(8,128)(2,1)S(1)} collective-permute-done((bf16[608,384]{1,0:T(8,128)(2,1)S(1)}, bf16[608,384]{1,0:T(8,128)(2,1)S(1)}, u32[]{:S(2)}, u32[]{:S(2)}) %collective-permute-start.1) | collective-permute-done | bytes 466976 | tf_op jit(solution)/shard_map/ppermute | solution.py:374
  70.6 0.0 collective-permute-done.2.refs_3_
  70.6 6.5 %chunk1.1 = (bf16[4,256,384]{2,1,0:T(8,128)(2,1)}, bf16[8,128,128]{2,1,0:T(8,128)(2,1)S(1)}, bf16[8,128,128]{2,1,0:T(8,128)(2,1)S(1)}) custom-call(s32[1]{0:T(128)} %bitcast.me, s32[1]{0:T(128)} %bitcast.1.dp, bf16[608,384]{1,0:T(8,128)(2,1)S(1)} %pack1_0.1.refs_0_, bf16[608,384]{1,0:T(8,128)(2,1)S(1)} %collective-permute-done.refs_1_, ...), custom_call_target="tpu_custom_call" | custom-call | flops 1920000000 | bytes 3000000 | tf_op jit(solution)/shard_map/chunk1/pallas_call | solution.py:40
  77.1 12.8 %all-to-all-start = ((bf16[4,256,384]{2,1,0:T(8,128)(2,1)}), bf16[4,256,384]{2,1,0:T(8,128)(2,1)S(1)}, u32[]{:S(2)}, u32[]{:S(2)}) async-start(bf16[4,256,384]{2,1,0:T(8,128)(2,1)} %get-tuple-element.62), calls=%async_computation | async-start | bytes 1572864 | tf_op jit(solution)/shard_map/all_to_all | solution.py:377
  89.9 1.5 %collective-permute-done.7.got_ref = bf16[8,128,128]{2,1,0:T(8,128)(2,1)S(1)} collective-permute-done((bf16[8,128,128]{2,1,0:T(8,128)(2,1)S(1)}, bf16[8,128,128]{2,1,0:T(8,128)(2,1)S(1)}, u32[]{:S(2)}, u32[]{:S(2)}) %collective-permute-start.7) | collective-permute-done | bytes 262176 | tf_op jit(solution)/shard_map/ppermute | solution.py:369
  91.4 0.1 state_pair.1
  91.5 1.6 %collective-permute-start.8 = (bf16[2,128,128]{2,1,0:T(8,128)(2,1)S(1)}, bf16[2,128,128]{2,1,0:T(8,128)(2,1)S(1)}, u32[]{:S(2)}, u32[]{:S(2)}) collective-permute-start(bf16[2,128,128]{2,1,0:T(8,128)(2,1)S(1)} %get-tuple-element.58), channel_id=1, source_target_pairs={{0,8},{4,12},{8,0},{12,4},{16,24},{20,28},{24,16},{28,20},{1,9},{5... | collective-permute-start | bytes 196616 | tf_op jit(solution)/shard_map/ppermute | solution.py:369
  93.1 1.5 %collective-permute-start.9 = (bf16[2,128,128]{2,1,0:T(8,128)(2,1)S(1)}, bf16[2,128,128]{2,1,0:T(8,128)(2,1)S(1)}, u32[]{:S(2)}, u32[]{:S(2)}) collective-permute-start(bf16[2,128,128]{2,1,0:T(8,128)(2,1)S(1)} %get-tuple-element.59), channel_id=1, source_target_pairs={{0,16},{4,20},{8,24},{12,28},{16,0},{20,4},{24,8},{28,12},{1,17},{... | collective-permute-start | bytes 196616 | tf_op jit(solution)/shard_map/ppermute | solution.py:369
  94.6 0.5 collective-permute-start.10
  95.1 0.8 collective-permute-done.8.refs_1_
  95.9 1.5 %collective-permute-done.9.refs_2_ = bf16[2,128,128]{2,1,0:T(8,128)(2,1)S(1)} collective-permute-done((bf16[2,128,128]{2,1,0:T(8,128)(2,1)S(1)}, bf16[2,128,128]{2,1,0:T(8,128)(2,1)S(1)}, u32[]{:S(2)}, u32[]{:S(2)}) %collective-permute-start.9) | collective-permute-done | bytes 65568 | tf_op jit(solution)/shard_map/ppermute | solution.py:369
  97.3 2.4 %collective-permute-done.10.refs_3_ = bf16[2,128,128]{2,1,0:T(8,128)(2,1)S(1)} collective-permute-done((bf16[2,128,128]{2,1,0:T(8,128)(2,1)S(1)}, bf16[2,128,128]{2,1,0:T(8,128)(2,1)S(1)}, u32[]{:S(2)}, u32[]{:S(2)}) %collective-permute-start.10) | collective-permute-done | bytes 65568 | tf_op jit(solution)/shard_map/ppermute | solution.py:369
  99.8 0.1 state_sum.1
  99.8 2.1 %collective-permute-start.11 = (bf16[2,32,128]{2,1,0:T(8,128)(2,1)S(1)}, bf16[2,32,128]{2,1,0:T(8,128)(2,1)S(1)}, u32[]{:S(2)}, u32[]{:S(2)}) collective-permute-start(bf16[2,32,128]{2,1,0:T(8,128)(2,1)S(1)} %get-tuple-element.64), channel_id=1, source_target_pairs={{0,1},{1,2},{2,3},{3,0},{4,5},{5,6},{6,7},{7,4},{8,9},{9,10},{10,1... | collective-permute-start | bytes 49160 | tf_op jit(solution)/shard_map/ppermute | solution.py:374
  101.9 2.4 %collective-permute-start.12 = (bf16[2,32,128]{2,1,0:T(8,128)(2,1)S(1)}, bf16[2,32,128]{2,1,0:T(8,128)(2,1)S(1)}, u32[]{:S(2)}, u32[]{:S(2)}) collective-permute-start(bf16[2,32,128]{2,1,0:T(8,128)(2,1)S(1)} %get-tuple-element.65), channel_id=1, source_target_pairs={{0,2},{1,3},{2,0},{3,1},{4,6},{5,7},{6,4},{7,5},{8,10},{9,11},{10,... | collective-permute-start | bytes 49160 | tf_op jit(solution)/shard_map/ppermute | solution.py:374
  104.3 1.5 %collective-permute-start.13 = (bf16[2,32,128]{2,1,0:T(8,128)(2,1)S(1)}, bf16[2,32,128]{2,1,0:T(8,128)(2,1)S(1)}, u32[]{:S(2)}, u32[]{:S(2)}) collective-permute-start(bf16[2,32,128]{2,1,0:T(8,128)(2,1)S(1)} %get-tuple-element.66), channel_id=1, source_target_pairs={{0,3},{1,0},{2,1},{3,2},{4,7},{5,4},{6,5},{7,6},{8,11},{9,8},{10,9... | collective-permute-start | bytes 49160 | tf_op jit(solution)/shard_map/ppermute | solution.py:374
  105.7 4.5 %all-to-all-done.refs_1_ = bf16[4,256,384]{2,1,0:T(8,128)(2,1)S(1)} async-done(((bf16[4,256,384]{2,1,0:T(8,128)(2,1)}), bf16[4,256,384]{2,1,0:T(8,128)(2,1)S(1)}, u32[]{:S(2)}, u32[]{:S(2)}) %all-to-all-start) | async-done | bytes 786464 | tf_op jit(solution)/shard_map/all_to_all | solution.py:377
  110.2 0.2 collective-permute-done.12.refs_2_
  110.4 3.7 %all-to-all-start.1 = ((bf16[4,256,256]{2,1,0:T(8,128)(2,1)}), bf16[4,256,256]{2,1,0:T(8,128)(2,1)S(1)}, u32[]{:S(2)}, u32[]{:S(2)}) async-start(bf16[4,256,256]{2,1,0:T(8,128)(2,1)} %get-tuple-element.68), calls=%async_computation.1 | async-start | bytes 1048576 | tf_op jit(solution)/shard_map/all_to_all | solution.py:377
  114.1 2.4 %collective-permute-start.16 = (bf16[4,2,32,128]{3,2,1,0:T(8,128)(2,1)S(1)}, bf16[4,2,32,128]{3,2,1,0:T(8,128)(2,1)S(1)}, u32[]{:S(2)}, u32[]{:S(2)}) collective-permute-start(bf16[4,2,32,128]{3,2,1,0:T(8,128)(2,1)S(1)} %state_rows.1.refs_0_), channel_id=1, source_target_pairs={{0,24},{4,28},{8,16},{12,20},{16,8},{20,12},{24,0},{28,4},{1,25},{... | collective-permute-start | bytes 196616 | tf_op jit(solution)/shard_map/ppermute | solution.py:369
  116.5 0.5 collective-permute-start.15
  117.0 0.5 collective-permute-start.14
  117.6 2.1 %collective-permute-done.16.refs_3_ = bf16[4,2,32,128]{3,2,1,0:T(8,128)(2,1)S(1)} collective-permute-done((bf16[4,2,32,128]{3,2,1,0:T(8,128)(2,1)S(1)}, bf16[4,2,32,128]{3,2,1,0:T(8,128)(2,1)S(1)}, u32[]{:S(2)}, u32[]{:S(2)}) %collective-permute-start.16) | collective-permute-done | bytes 65568 | tf_op jit(solution)/shard_map/ppermute | solution.py:369
  119.7 1.1 collective-permute-done.15.refs_2_
  120.8 0.5 collective-permute-done.14.refs_1_
  121.3 0.1 collective-permute-start.17
  121.4 1.5 %collective-permute-done.17.refs_1_ = bf16[4,4,2,32,128]{4,3,2,1,0:T(8,128)(2,1)S(1)} collective-permute-done((bf16[4,4,2,32,128]{4,3,2,1,0:T(8,128)(2,1)S(1)}, bf16[4,4,2,32,128]{4,3,2,1,0:T(8,128)(2,1)S(1)}, u32[]{:S(2)}, u32[]{:S(2)}) %collective-permute-start.17) | collective-permute-done | bytes 262176 | tf_op jit(solution)/shard_map/ppermute | solution.py:369
  122.9 1.2 state_out.1
  124.1 3.6 %all-to-all-done.1.refs_0_ = bf16[4,256,256]{2,1,0:T(8,128)(2,1)S(1)} async-done(((bf16[4,256,256]{2,1,0:T(8,128)(2,1)}), bf16[4,256,256]{2,1,0:T(8,128)(2,1)S(1)}, u32[]{:S(2)}, u32[]{:S(2)}) %all-to-all-start.1) | async-done | bytes 524320 | tf_op jit(solution)/shard_map/all_to_all | solution.py:377
  127.7 1.2 unpack.1
  (5 shorter events, 0.0 us)
Async XLA Ops:
  2.4 14.8 %collective-permute-start.3 = (bf16[736,256]{1,0:T(8,128)(2,1)S(1)}, bf16[736,256]{1,0:T(8,128)(2,1)S(1)}, u32[]{:S(2)}, u32[]{:S(2)}) collective-permute-start(bf16[736,256]{1,0:T(8,128)(2,1)S(1)} %get-tuple-element.49), channel_id=1, source_target_pairs={{0,1},{1,2},{2,3},{3,0},{4,5},{5,6},{6,7},{7,4},{8,9},{9,10},{10,1... | collective-permute-start | bytes 1130504 | tf_op jit(solution)/shard_map/ppermute | solution.py:374
  5.4 28.0 %collective-permute-start.4 = (bf16[736,256]{1,0:T(8,128)(2,1)S(1)}, bf16[736,256]{1,0:T(8,128)(2,1)S(1)}, u32[]{:S(2)}, u32[]{:S(2)}) collective-permute-start(bf16[736,256]{1,0:T(8,128)(2,1)S(1)} %get-tuple-element.50), channel_id=1, source_target_pairs={{0,2},{1,3},{2,0},{3,1},{4,6},{5,7},{6,4},{7,5},{8,10},{9,11},{10,... | collective-permute-start | bytes 1130504 | tf_op jit(solution)/shard_map/ppermute | solution.py:374
  8.0 25.4 %collective-permute-start.5 = (bf16[736,256]{1,0:T(8,128)(2,1)S(1)}, bf16[736,256]{1,0:T(8,128)(2,1)S(1)}, u32[]{:S(2)}, u32[]{:S(2)}) collective-permute-start(bf16[736,256]{1,0:T(8,128)(2,1)S(1)} %get-tuple-element.51), channel_id=1, source_target_pairs={{0,3},{1,0},{2,1},{3,2},{4,7},{5,4},{6,5},{7,6},{8,11},{9,8},{10,9... | collective-permute-start | bytes 1130504 | tf_op jit(solution)/shard_map/ppermute | solution.py:374
  11.0 32.4 %collective-permute-start = (bf16[608,384]{1,0:T(8,128)(2,1)S(1)}, bf16[608,384]{1,0:T(8,128)(2,1)S(1)}, u32[]{:S(2)}, u32[]{:S(2)}) collective-permute-start(bf16[608,384]{1,0:T(8,128)(2,1)S(1)} %get-tuple-element.46), channel_id=1, source_target_pairs={{0,1},{1,2},{2,3},{3,0},{4,5},{5,6},{6,7},{7,4},{8,9},{9,10},{10,1... | collective-permute-start | bytes 1400840 | tf_op jit(solution)/shard_map/ppermute | solution.py:374
  11.7 58.9 %collective-permute-start.1 = (bf16[608,384]{1,0:T(8,128)(2,1)S(1)}, bf16[608,384]{1,0:T(8,128)(2,1)S(1)}, u32[]{:S(2)}, u32[]{:S(2)}) collective-permute-start(bf16[608,384]{1,0:T(8,128)(2,1)S(1)} %get-tuple-element.47), channel_id=1, source_target_pairs={{0,2},{1,3},{2,0},{3,1},{4,6},{5,7},{6,4},{7,5},{8,10},{9,11},{10,... | collective-permute-start | bytes 1400840 | tf_op jit(solution)/shard_map/ppermute | solution.py:374
  17.2 53.5 %collective-permute-start.2 = (bf16[608,384]{1,0:T(8,128)(2,1)S(1)}, bf16[608,384]{1,0:T(8,128)(2,1)S(1)}, u32[]{:S(2)}, u32[]{:S(2)}) collective-permute-start(bf16[608,384]{1,0:T(8,128)(2,1)S(1)} %get-tuple-element.48), channel_id=1, source_target_pairs={{0,3},{1,0},{2,1},{3,2},{4,7},{5,4},{6,5},{7,6},{8,11},{9,8},{10,9... | collective-permute-start | bytes 1400840 | tf_op jit(solution)/shard_map/ppermute | solution.py:374
  33.5 1.6 %collective-permute-start.6 = (bf16[8,128,128]{2,1,0:T(8,128)(2,1)S(1)}, bf16[8,128,128]{2,1,0:T(8,128)(2,1)S(1)}, u32[]{:S(2)}, u32[]{:S(2)}) collective-permute-start(bf16[8,128,128]{2,1,0:T(8,128)(2,1)S(1)} %start_share.1.refs_4_), channel_id=1, source_target_pairs={{0,4},{4,0},{8,12},{12,8},{16,20},{20,16},{24,28},{28,24},{1,5},{5... | collective-permute-start | bytes 786440 | tf_op jit(solution)/shard_map/ppermute | solution.py:369
  77.1 33.1 %all-to-all-start = ((bf16[4,256,384]{2,1,0:T(8,128)(2,1)}), bf16[4,256,384]{2,1,0:T(8,128)(2,1)S(1)}, u32[]{:S(2)}, u32[]{:S(2)}) async-start(bf16[4,256,384]{2,1,0:T(8,128)(2,1)} %get-tuple-element.62), calls=%async_computation | async-start | bytes 1572864 | tf_op jit(solution)/shard_map/all_to_all | solution.py:377
  89.9 1.5 %collective-permute-start.7 = (bf16[8,128,128]{2,1,0:T(8,128)(2,1)S(1)}, bf16[8,128,128]{2,1,0:T(8,128)(2,1)S(1)}, u32[]{:S(2)}, u32[]{:S(2)}) collective-permute-start(bf16[8,128,128]{2,1,0:T(8,128)(2,1)S(1)} %get-tuple-element.56), channel_id=1, source_target_pairs={{0,4},{4,0},{8,12},{12,8},{16,20},{20,16},{24,28},{28,24},{1,5},{5... | collective-permute-start | bytes 786440 | tf_op jit(solution)/shard_map/ppermute | solution.py:369
  91.5 4.3 %collective-permute-start.8 = (bf16[2,128,128]{2,1,0:T(8,128)(2,1)S(1)}, bf16[2,128,128]{2,1,0:T(8,128)(2,1)S(1)}, u32[]{:S(2)}, u32[]{:S(2)}) collective-permute-start(bf16[2,128,128]{2,1,0:T(8,128)(2,1)S(1)} %get-tuple-element.58), channel_id=1, source_target_pairs={{0,8},{4,12},{8,0},{12,4},{16,24},{20,28},{24,16},{28,20},{1,9},{5... | collective-permute-start | bytes 196616 | tf_op jit(solution)/shard_map/ppermute | solution.py:369
  93.1 4.3 %collective-permute-start.9 = (bf16[2,128,128]{2,1,0:T(8,128)(2,1)S(1)}, bf16[2,128,128]{2,1,0:T(8,128)(2,1)S(1)}, u32[]{:S(2)}, u32[]{:S(2)}) collective-permute-start(bf16[2,128,128]{2,1,0:T(8,128)(2,1)S(1)} %get-tuple-element.59), channel_id=1, source_target_pairs={{0,16},{4,20},{8,24},{12,28},{16,0},{20,4},{24,8},{28,12},{1,17},{... | collective-permute-start | bytes 196616 | tf_op jit(solution)/shard_map/ppermute | solution.py:369
  94.6 5.2 %collective-permute-start.10 = (bf16[2,128,128]{2,1,0:T(8,128)(2,1)S(1)}, bf16[2,128,128]{2,1,0:T(8,128)(2,1)S(1)}, u32[]{:S(2)}, u32[]{:S(2)}) collective-permute-start(bf16[2,128,128]{2,1,0:T(8,128)(2,1)S(1)} %get-tuple-element.60), channel_id=1, source_target_pairs={{0,24},{4,28},{8,16},{12,20},{16,8},{20,12},{24,0},{28,4},{1,25},{... | collective-permute-start | bytes 196616 | tf_op jit(solution)/shard_map/ppermute | solution.py:369
  99.8 10.4 %collective-permute-start.11 = (bf16[2,32,128]{2,1,0:T(8,128)(2,1)S(1)}, bf16[2,32,128]{2,1,0:T(8,128)(2,1)S(1)}, u32[]{:S(2)}, u32[]{:S(2)}) collective-permute-start(bf16[2,32,128]{2,1,0:T(8,128)(2,1)S(1)} %get-tuple-element.64), channel_id=1, source_target_pairs={{0,1},{1,2},{2,3},{3,0},{4,5},{5,6},{6,7},{7,4},{8,9},{9,10},{10,1... | collective-permute-start | bytes 49160 | tf_op jit(solution)/shard_map/ppermute | solution.py:374
  101.9 8.5 %collective-permute-start.12 = (bf16[2,32,128]{2,1,0:T(8,128)(2,1)S(1)}, bf16[2,32,128]{2,1,0:T(8,128)(2,1)S(1)}, u32[]{:S(2)}, u32[]{:S(2)}) collective-permute-start(bf16[2,32,128]{2,1,0:T(8,128)(2,1)S(1)} %get-tuple-element.65), channel_id=1, source_target_pairs={{0,2},{1,3},{2,0},{3,1},{4,6},{5,7},{6,4},{7,5},{8,10},{9,11},{10,... | collective-permute-start | bytes 49160 | tf_op jit(solution)/shard_map/ppermute | solution.py:374
  104.3 6.2 %collective-permute-start.13 = (bf16[2,32,128]{2,1,0:T(8,128)(2,1)S(1)}, bf16[2,32,128]{2,1,0:T(8,128)(2,1)S(1)}, u32[]{:S(2)}, u32[]{:S(2)}) collective-permute-start(bf16[2,32,128]{2,1,0:T(8,128)(2,1)S(1)} %get-tuple-element.66), channel_id=1, source_target_pairs={{0,3},{1,0},{2,1},{3,2},{4,7},{5,4},{6,5},{7,6},{8,11},{9,8},{10,9... | collective-permute-start | bytes 49160 | tf_op jit(solution)/shard_map/ppermute | solution.py:374
  110.4 17.3 %all-to-all-start.1 = ((bf16[4,256,256]{2,1,0:T(8,128)(2,1)}), bf16[4,256,256]{2,1,0:T(8,128)(2,1)S(1)}, u32[]{:S(2)}, u32[]{:S(2)}) async-start(bf16[4,256,256]{2,1,0:T(8,128)(2,1)} %get-tuple-element.68), calls=%async_computation.1 | async-start | bytes 1048576 | tf_op jit(solution)/shard_map/all_to_all | solution.py:377
  114.1 5.6 %collective-permute-start.16 = (bf16[4,2,32,128]{3,2,1,0:T(8,128)(2,1)S(1)}, bf16[4,2,32,128]{3,2,1,0:T(8,128)(2,1)S(1)}, u32[]{:S(2)}, u32[]{:S(2)}) collective-permute-start(bf16[4,2,32,128]{3,2,1,0:T(8,128)(2,1)S(1)} %state_rows.1.refs_0_), channel_id=1, source_target_pairs={{0,24},{4,28},{8,16},{12,20},{16,8},{20,12},{24,0},{28,4},{1,25},{... | collective-permute-start | bytes 196616 | tf_op jit(solution)/shard_map/ppermute | solution.py:369
  116.5 4.3 %collective-permute-start.15 = (bf16[4,2,32,128]{3,2,1,0:T(8,128)(2,1)S(1)}, bf16[4,2,32,128]{3,2,1,0:T(8,128)(2,1)S(1)}, u32[]{:S(2)}, u32[]{:S(2)}) collective-permute-start(bf16[4,2,32,128]{3,2,1,0:T(8,128)(2,1)S(1)} %state_rows.1.refs_0_), channel_id=1, source_target_pairs={{0,16},{4,20},{8,24},{12,28},{16,0},{20,4},{24,8},{28,12},{1,17},{... | collective-permute-start | bytes 196616 | tf_op jit(solution)/shard_map/ppermute | solution.py:369
  117.0 4.3 %collective-permute-start.14 = (bf16[4,2,32,128]{3,2,1,0:T(8,128)(2,1)S(1)}, bf16[4,2,32,128]{3,2,1,0:T(8,128)(2,1)S(1)}, u32[]{:S(2)}, u32[]{:S(2)}) collective-permute-start(bf16[4,2,32,128]{3,2,1,0:T(8,128)(2,1)S(1)} %state_rows.1.refs_0_), channel_id=1, source_target_pairs={{0,8},{4,12},{8,0},{12,4},{16,24},{20,28},{24,16},{28,20},{1,9},{5... | collective-permute-start | bytes 196616 | tf_op jit(solution)/shard_map/ppermute | solution.py:369
  121.3 1.6 %collective-permute-start.17 = (bf16[4,4,2,32,128]{4,3,2,1,0:T(8,128)(2,1)S(1)}, bf16[4,4,2,32,128]{4,3,2,1,0:T(8,128)(2,1)S(1)}, u32[]{:S(2)}, u32[]{:S(2)}) collective-permute-start(bf16[4,4,2,32,128]{4,3,2,1,0:T(8,128)(2,1)S(1)} %state_rest.1.refs_0_), channel_id=1, source_target_pairs={{0,4},{4,0},{8,12},{12,8},{16,20},{20,16},{24,28},{28,24},{1,5},{5... | collective-permute-start | bytes 786440 | tf_op jit(solution)/shard_map/ppermute | solution.py:369

commit v6 on v5

--- a/solution.py
+++ b/solution.py
@@ -101,7 +101,8 @@
         self.rest = n_dp // self.pair
         self.own = -(-self.mats // n_dp)
         self.block = -(-rows // 16) * 16
-        self.share = -(-self.mats // self.pair)
+        self.group = min(4, n_dp)
+        self.share = -(-self.mats // self.group)
         self.share_blocks = -(-self.share // least)
 
     def to(self, me, slot):
@@ -115,6 +116,9 @@
 
     def mine(self, dp):
         return lax.rem(dp[0], self.pair)
+
+    def member(self, dp):
+        return lax.rem(dp[0], self.group)
 
     def other(self, dp, k):
         return jnp.bitwise_xor(lax.div(dp[0], self.pair), k)
@@ -155,7 +159,7 @@
                 top = 4 * t + m * plan.block
                 outs[k][top : top + plan.rows, j * w : (j + 1) * w] = state[k, m, j].astype(BF16)
         for q in range(plan.share if chunk == 0 else 0):
-            mat = jnp.minimum(plan.mine(dp) * plan.share + q, plan.mats - 1)
+            mat = jnp.minimum(plan.member(dp) * plan.share + q, plan.mats - 1)
             top = 4 * t + (3 + q // count) * plan.block
             left = (q % count) * w
             part = state[k, lax.rem(mat, 3), count + lax.div(mat, 3)]
@@ -212,7 +216,7 @@
         return got
 
     in_refs = take(n)
-    shares = take(plan.pair)
+    shares = take(plan.group)
     (before,) = take(1) if last else (None,)
     (d_ref,) = take(1)
     c_refs = take(2 if last else 1)
@@ -228,7 +232,7 @@
                 part = in_refs[slot][top : top + plan.rows, j * w : (j + 1) * w]
                 w1[3 * j + m, at, :] = part.astype(F32)
     for k, part in enumerate(shares):
-        at = jnp.bitwise_xor(plan.mine(dp), k) * plan.share
+        at = jnp.bitwise_xor(plan.member(dp), k) * plan.share
         w0[pl.ds(at, plan.share)] = part[...]
 
     for j in range(count):
@@ -411,7 +415,7 @@
         "start_share",
         [pltpu.VMEM((plan.share, width, width), F32)],
     )
-    shares = [swap(start_own, k) for k in range(plan.pair)]
+    shares = [swap(start_own, k) for k in range(plan.group)]
 
     before = []
     grads = []
@@ -422,7 +426,7 @@
         else:
             outs = [shape(3 * count, width, width)]
         outs = [shape(n, 2 * t, count * width)] + outs
-        scratch = [pltpu.VMEM((plan.pair * plan.share, width, width), BF16)]
+        scratch = [pltpu.VMEM((plan.group * plan.share, width, width), BF16)]
         scratch += [pltpu.VMEM((3 * count, width, width), F32)] * 3 + [
             pltpu.VMEM((count, 4, n * t, width), F32),
             pltpu.VMEM((count, 3, n * t, width), BF16),
@@ -433,7 +437,7 @@
             bind(chunk_kernel, chunk=c),
             outs,
             (me, dp, *arrived[c], *shares, *before),
-            [SMEM] * 2 + [VMEM] * (n + plan.pair + len(before)),
+            [SMEM] * 2 + [VMEM] * (n + plan.group + len(before)),
             [VMEM] * len(outs),
             f"chunk{c}",
             scratch,

time: 129 us -> 126 us (0.977)
  waiting for transfers between devices: 68.4 us -> 63.1 us
  starting transfers between devices: 40.1 us -> 42.6 us
    ppermute x9, waiting for transfers between devices: 48.5 us -> 38.6 us  [shift(): return lax.ppermute(value, 'ctx', [(i, (i + s) % n) for i in range(n)])]
    ppermute x9 -> x11, waiting for transfers between devices: 11.8 us -> 16.4 us  [swap(): return lax.ppermute(value, 'dp', [(i, i ^ k) for i in range(n_dp)])]
    ppermute x9 -> x11, starting transfers between devices: 7.19 us -> 9.7 us  [swap(): return lax.ppermute(value, 'dp', [(i, i ^ k) for i in range(n_dp)])]
  transfers between devices with their start and end apart: 20 -> 22, of which waited for: 16 -> 16; matrix products, arithmetic and copies ran while one was open for 0% -> 0% of each run, Pallas kernels for 8% -> 8%
where the time goes in v6:
time: 126 us
  waiting for transfers between devices  63.1 us (50%)
  starting transfers between devices  42.6 us (34%)
  Pallas kernels  19.7 us (16%)
    ppermute x9, waiting for transfers between devices, shift(): return lax.ppermute(value, 'ctx', [(i, (i + s) % n) for i in range(n)])  38.6 us
    pallas_call x13, Pallas kernels, call(): pl.pallas_call(kernel, out_shape=out_shape, in_specs=in_specs, out_specs=...  19.7 us
    ppermute x9, starting transfers between devices, shift(): return lax.ppermute(value, 'ctx', [(i, (i + s) % n) for i in range(n)])  16.5 us
    all_to_all x2, starting transfers between devices, turn(): return lax.all_to_all(value, 'ctx', split_axis=0, concat_axis=0, tiled=True)  16.4 us
    ppermute x11, waiting for transfers between devices, swap(): return lax.ppermute(value, 'dp', [(i, i ^ k) for i in range(n_dp)])  16.4 us
    ppermute x11, starting transfers between devices, swap(): return lax.ppermute(value, 'dp', [(i, i ^ k) for i in range(n_dp)])  9.7 us
    all_to_all x2, waiting for transfers between devices, turn(): return lax.all_to_all(value, 'ctx', split_axis=0, concat_axis=0, tiled=True)  8.09 us
  transfers between devices with their start and end apart: 22, of which 16 were waited for; matrix products, arithmetic and copies ran while one was open for 0% of the time, Pallas kernels for 8%

profile of v6, /device:TPU:0, one launch (start us, length us, event | category | flops | bytes accessed | tf_op | source)
XLA Modules:
  0.0 126.1 jit_solution(17500808395431592616)
XLA Ops:
  0.6 1.7 %pack0_1.1 = (bf16[672,256]{1,0:T(8,128)(2,1)S(1)}, bf16[672,256]{1,0:T(8,128)(2,1)S(1)}, bf16[672,256]{1,0:T(8,128)(2,1)S(1)}) custom-call(s32[1]{0:T(128)} %bitcast.me, s32[1]{0:T(128)} %bitcast.1.dp, bf16[1,128,2560]{2,1,0:T(8,128)(2,1)} %k_ref.4, bf16[1,128,2560]{2,1,0:T(8,128)(2,1)} %v_ref.7, bf16[1,128,2560]{2,1,0:T(8,128)(2,1)} %q_ref.7, ...), custom_call_target="tpu_custom_call" | custom-call | flops 1000000 | bytes 1000000 | tf_op jit(solution)/shard_map/pack0_1/pallas_call | solution.py:40
  2.3 3.1 %collective-permute-start.3 = (bf16[672,256]{1,0:T(8,128)(2,1)S(1)}, bf16[672,256]{1,0:T(8,128)(2,1)S(1)}, u32[]{:S(2)}, u32[]{:S(2)}) collective-permute-start(bf16[672,256]{1,0:T(8,128)(2,1)S(1)} %get-tuple-element.49), channel_id=1, source_target_pairs={{0,1},{1,2},{2,3},{3,0},{4,5},{5,6},{6,7},{7,4},{8,9},{9,10},{10,1... | collective-permute-start | bytes 1032200 | tf_op jit(solution)/shard_map/ppermute | solution.py:378
  5.4 2.6 %collective-permute-start.4 = (bf16[672,256]{1,0:T(8,128)(2,1)S(1)}, bf16[672,256]{1,0:T(8,128)(2,1)S(1)}, u32[]{:S(2)}, u32[]{:S(2)}) collective-permute-start(bf16[672,256]{1,0:T(8,128)(2,1)S(1)} %get-tuple-element.50), channel_id=1, source_target_pairs={{0,2},{1,3},{2,0},{3,1},{4,6},{5,7},{6,4},{7,5},{8,10},{9,11},{10,... | collective-permute-start | bytes 1032200 | tf_op jit(solution)/shard_map/ppermute | solution.py:378
  8.0 1.3 %collective-permute-start.5 = (bf16[672,256]{1,0:T(8,128)(2,1)S(1)}, bf16[672,256]{1,0:T(8,128)(2,1)S(1)}, u32[]{:S(2)}, u32[]{:S(2)}) collective-permute-start(bf16[672,256]{1,0:T(8,128)(2,1)S(1)} %get-tuple-element.51), channel_id=1, source_target_pairs={{0,3},{1,0},{2,1},{3,2},{4,7},{5,4},{6,5},{7,6},{8,11},{9,8},{10,9... | collective-permute-start | bytes 1032200 | tf_op jit(solution)/shard_map/ppermute | solution.py:378
  9.3 1.6 %pack1_1.1 = (bf16[608,384]{1,0:T(8,128)(2,1)S(1)}, bf16[608,384]{1,0:T(8,128)(2,1)S(1)}, bf16[608,384]{1,0:T(8,128)(2,1)S(1)}) custom-call(s32[1]{0:T(128)} %bitcast.me, s32[1]{0:T(128)} %bitcast.1.dp, bf16[1,128,2560]{2,1,0:T(8,128)(2,1)} %k_ref.4, bf16[1,128,2560]{2,1,0:T(8,128)(2,1)} %v_ref.7, bf16[1,128,2560]{2,1,0:T(8,128)(2,1)} %q_ref.7, ...), custom_call_target="tpu_custom_call" | custom-call | flops 1000000 | bytes 1000000 | tf_op jit(solution)/shard_map/pack1_1/pallas_call | solution.py:40
  11.0 0.7 collective-permute-start
  11.7 0.3 collective-permute-start.1
  12.0 4.4 %collective-permute-done.3.refs_1_ = bf16[672,256]{1,0:T(8,128)(2,1)S(1)} collective-permute-done((bf16[672,256]{1,0:T(8,128)(2,1)S(1)}, bf16[672,256]{1,0:T(8,128)(2,1)S(1)}, u32[]{:S(2)}, u32[]{:S(2)}) %collective-permute-start.3) | collective-permute-done | bytes 344096 | tf_op jit(solution)/shard_map/ppermute | solution.py:378
  16.5 2.5 %collective-permute-start.2 = (bf16[608,384]{1,0:T(8,128)(2,1)S(1)}, bf16[608,384]{1,0:T(8,128)(2,1)S(1)}, u32[]{:S(2)}, u32[]{:S(2)}) collective-permute-start(bf16[608,384]{1,0:T(8,128)(2,1)S(1)} %get-tuple-element.48), channel_id=1, source_target_pairs={{0,3},{1,0},{2,1},{3,2},{4,7},{5,4},{6,5},{7,6},{8,11},{9,8},{10,9... | collective-permute-start | bytes 1400840 | tf_op jit(solution)/shard_map/ppermute | solution.py:378
  19.0 1.2 pack0_0.1.refs_0_
  20.1 11.1 %collective-permute-done.4.refs_2_ = bf16[672,256]{1,0:T(8,128)(2,1)S(1)} collective-permute-done((bf16[672,256]{1,0:T(8,128)(2,1)S(1)}, bf16[672,256]{1,0:T(8,128)(2,1)S(1)}, u32[]{:S(2)}, u32[]{:S(2)}) %collective-permute-start.4) | collective-permute-done | bytes 344096 | tf_op jit(solution)/shard_map/ppermute | solution.py:378
  31.3 1.2 collective-permute-start.8
  32.5 0.7 collective-permute-start.7
  33.2 3.7 %collective-permute-done.8.refs_7_ = bf16[4,128,128]{2,1,0:T(8,128)(2,1)S(1)} collective-permute-done((bf16[4,128,128]{2,1,0:T(8,128)(2,1)S(1)}, bf16[4,128,128]{2,1,0:T(8,128)(2,1)S(1)}, u32[]{:S(2)}, u32[]{:S(2)}) %collective-permute-start.8) | collective-permute-done | bytes 131104 | tf_op jit(solution)/shard_map/ppermute | solution.py:373
  36.9 0.7 collective-permute-start.6
  37.6 1.2 pack1_0.1.refs_0_
  38.7 1.2 collective-permute-done.7.refs_6_
  40.0 0.0 collective-permute-done.6.refs_5_
  40.0 5.0 %chunk0.1 = (bf16[4,256,256]{2,1,0:T(8,128)(2,1)}, bf16[6,128,128]{2,1,0:T(8,128)(2,1)S(1)}) custom-call(s32[1]{0:T(128)} %bitcast.me, s32[1]{0:T(128)} %bitcast.1.dp, bf16[672,256]{1,0:T(8,128)(2,1)S(1)} %pack0_0.1.refs_0_, bf16[672,256]{1,0:T(8,128)(2,1)S(1)} %collective-permute-done.3.refs_1_, bf16[672,256]{1,0:T(8,128)(2,1)S(1)} %collective-permute-done.4.refs_2_, ...), custom_call_target="tpu_custom_call" | custom-call | flops 1280000000 | bytes 2000000 | tf_op jit(solution)/shard_map/chunk0/pallas_call | solution.py:40
  45.0 22.9 %collective-permute-done.1.refs_2_ = bf16[608,384]{1,0:T(8,128)(2,1)S(1)} collective-permute-done((bf16[608,384]{1,0:T(8,128)(2,1)S(1)}, bf16[608,384]{1,0:T(8,128)(2,1)S(1)}, u32[]{:S(2)}, u32[]{:S(2)}) %collective-permute-start.1) | collective-permute-done | bytes 466976 | tf_op jit(solution)/shard_map/ppermute | solution.py:378
  67.8 6.5 %chunk1.1 = (bf16[4,256,384]{2,1,0:T(8,128)(2,1)}, bf16[8,128,128]{2,1,0:T(8,128)(2,1)S(1)}, bf16[8,128,128]{2,1,0:T(8,128)(2,1)S(1)}) custom-call(s32[1]{0:T(128)} %bitcast.me, s32[1]{0:T(128)} %bitcast.1.dp, bf16[608,384]{1,0:T(8,128)(2,1)S(1)} %pack1_0.1.refs_0_, bf16[608,384]{1,0:T(8,128)(2,1)S(1)} %collective-permute-done.refs_1_, ...), custom_call_target="tpu_custom_call" | custom-call | flops 1920000000 | bytes 3000000 | tf_op jit(solution)/shard_map/chunk1/pallas_call | solution.py:40
  74.3 12.8 %all-to-all-start = ((bf16[4,256,384]{2,1,0:T(8,128)(2,1)}), bf16[4,256,384]{2,1,0:T(8,128)(2,1)S(1)}, u32[]{:S(2)}, u32[]{:S(2)}) async-start(bf16[4,256,384]{2,1,0:T(8,128)(2,1)} %get-tuple-element.62), calls=%async_computation | async-start | bytes 1572864 | tf_op jit(solution)/shard_map/all_to_all | solution.py:381
  87.1 1.5 %collective-permute-done.9.got_ref = bf16[8,128,128]{2,1,0:T(8,128)(2,1)S(1)} collective-permute-done((bf16[8,128,128]{2,1,0:T(8,128)(2,1)S(1)}, bf16[8,128,128]{2,1,0:T(8,128)(2,1)S(1)}, u32[]{:S(2)}, u32[]{:S(2)}) %collective-permute-start.9) | collective-permute-done | bytes 262176 | tf_op jit(solution)/shard_map/ppermute | solution.py:373
  88.6 0.1 state_pair.1
  88.7 1.6 %collective-permute-start.10 = (bf16[2,128,128]{2,1,0:T(8,128)(2,1)S(1)}, bf16[2,128,128]{2,1,0:T(8,128)(2,1)S(1)}, u32[]{:S(2)}, u32[]{:S(2)}) collective-permute-start(bf16[2,128,128]{2,1,0:T(8,128)(2,1)S(1)} %get-tuple-element.58), channel_id=1, source_target_pairs={{0,8},{4,12},{8,0},{12,4},{16,24},{20,28},{24,16},{28,20},{1,9},{5... | collective-permute-start | bytes 196616 | tf_op jit(solution)/shard_map/ppermute | solution.py:373
  90.3 1.5 %collective-permute-start.11 = (bf16[2,128,128]{2,1,0:T(8,128)(2,1)S(1)}, bf16[2,128,128]{2,1,0:T(8,128)(2,1)S(1)}, u32[]{:S(2)}, u32[]{:S(2)}) collective-permute-start(bf16[2,128,128]{2,1,0:T(8,128)(2,1)S(1)} %get-tuple-element.59), channel_id=1, source_target_pairs={{0,16},{4,20},{8,24},{12,28},{16,0},{20,4},{24,8},{28,12},{1,17},{... | collective-permute-start | bytes 196616 | tf_op jit(solution)/shard_map/ppermute | solution.py:373
  91.8 0.5 collective-permute-start.12
  92.3 0.8 collective-permute-done.10.refs_1_
  93.0 1.5 %collective-permute-done.11.refs_2_ = bf16[2,128,128]{2,1,0:T(8,128)(2,1)S(1)} collective-permute-done((bf16[2,128,128]{2,1,0:T(8,128)(2,1)S(1)}, bf16[2,128,128]{2,1,0:T(8,128)(2,1)S(1)}, u32[]{:S(2)}, u32[]{:S(2)}) %collective-permute-start.11) | collective-permute-done | bytes 65568 | tf_op jit(solution)/shard_map/ppermute | solution.py:373
  94.5 2.4 %collective-permute-done.12.refs_3_ = bf16[2,128,128]{2,1,0:T(8,128)(2,1)S(1)} collective-permute-done((bf16[2,128,128]{2,1,0:T(8,128)(2,1)S(1)}, bf16[2,128,128]{2,1,0:T(8,128)(2,1)S(1)}, u32[]{:S(2)}, u32[]{:S(2)}) %collective-permute-start.12) | collective-permute-done | bytes 65568 | tf_op jit(solution)/shard_map/ppermute | solution.py:373
  97.0 0.1 state_sum.1
  97.0 2.1 %collective-permute-start.13 = (bf16[2,32,128]{2,1,0:T(8,128)(2,1)S(1)}, bf16[2,32,128]{2,1,0:T(8,128)(2,1)S(1)}, u32[]{:S(2)}, u32[]{:S(2)}) collective-permute-start(bf16[2,32,128]{2,1,0:T(8,128)(2,1)S(1)} %get-tuple-element.64), channel_id=1, source_target_pairs={{0,1},{1,2},{2,3},{3,0},{4,5},{5,6},{6,7},{7,4},{8,9},{9,10},{10,1... | collective-permute-start | bytes 49160 | tf_op jit(solution)/shard_map/ppermute | solution.py:378
  99.1 2.4 %collective-permute-start.14 = (bf16[2,32,128]{2,1,0:T(8,128)(2,1)S(1)}, bf16[2,32,128]{2,1,0:T(8,128)(2,1)S(1)}, u32[]{:S(2)}, u32[]{:S(2)}) collective-permute-start(bf16[2,32,128]{2,1,0:T(8,128)(2,1)S(1)} %get-tuple-element.65), channel_id=1, source_target_pairs={{0,2},{1,3},{2,0},{3,1},{4,6},{5,7},{6,4},{7,5},{8,10},{9,11},{10,... | collective-permute-start | bytes 49160 | tf_op jit(solution)/shard_map/ppermute | solution.py:378
  101.5 1.5 %collective-permute-start.15 = (bf16[2,32,128]{2,1,0:T(8,128)(2,1)S(1)}, bf16[2,32,128]{2,1,0:T(8,128)(2,1)S(1)}, u32[]{:S(2)}, u32[]{:S(2)}) collective-permute-start(bf16[2,32,128]{2,1,0:T(8,128)(2,1)S(1)} %get-tuple-element.66), channel_id=1, source_target_pairs={{0,3},{1,0},{2,1},{3,2},{4,7},{5,4},{6,5},{7,6},{8,11},{9,8},{10,9... | collective-permute-start | bytes 49160 | tf_op jit(solution)/shard_map/ppermute | solution.py:378
  102.9 4.5 %all-to-all-done.refs_1_ = bf16[4,256,384]{2,1,0:T(8,128)(2,1)S(1)} async-done(((bf16[4,256,384]{2,1,0:T(8,128)(2,1)}), bf16[4,256,384]{2,1,0:T(8,128)(2,1)S(1)}, u32[]{:S(2)}, u32[]{:S(2)}) %all-to-all-start) | async-done | bytes 786464 | tf_op jit(solution)/shard_map/all_to_all | solution.py:381
  107.4 0.2 collective-permute-done.14.refs_2_
  107.6 3.7 %all-to-all-start.1 = ((bf16[4,256,256]{2,1,0:T(8,128)(2,1)}), bf16[4,256,256]{2,1,0:T(8,128)(2,1)S(1)}, u32[]{:S(2)}, u32[]{:S(2)}) async-start(bf16[4,256,256]{2,1,0:T(8,128)(2,1)} %get-tuple-element.68), calls=%async_computation.1 | async-start | bytes 1048576 | tf_op jit(solution)/shard_map/all_to_all | solution.py:381
  111.3 2.5 %collective-permute-start.18 = (bf16[4,2,32,128]{3,2,1,0:T(8,128)(2,1)S(1)}, bf16[4,2,32,128]{3,2,1,0:T(8,128)(2,1)S(1)}, u32[]{:S(2)}, u32[]{:S(2)}) collective-permute-start(bf16[4,2,32,128]{3,2,1,0:T(8,128)(2,1)S(1)} %state_rows.1.refs_0_), channel_id=1, source_target_pairs={{0,24},{4,28},{8,16},{12,20},{16,8},{20,12},{24,0},{28,4},{1,25},{... | collective-permute-start | bytes 196616 | tf_op jit(solution)/shard_map/ppermute | solution.py:373
  113.7 0.5 collective-permute-start.17
  114.2 0.5 collective-permute-start.16
  114.8 2.1 %collective-permute-done.18.refs_3_ = bf16[4,2,32,128]{3,2,1,0:T(8,128)(2,1)S(1)} collective-permute-done((bf16[4,2,32,128]{3,2,1,0:T(8,128)(2,1)S(1)}, bf16[4,2,32,128]{3,2,1,0:T(8,128)(2,1)S(1)}, u32[]{:S(2)}, u32[]{:S(2)}) %collective-permute-start.18) | collective-permute-done | bytes 65568 | tf_op jit(solution)/shard_map/ppermute | solution.py:373
  116.9 1.1 collective-permute-done.17.refs_2_
  118.0 0.5 collective-permute-done.16.refs_1_
  118.5 0.1 collective-permute-start.19
  118.6 1.5 %collective-permute-done.19.refs_1_ = bf16[4,4,2,32,128]{4,3,2,1,0:T(8,128)(2,1)S(1)} collective-permute-done((bf16[4,4,2,32,128]{4,3,2,1,0:T(8,128)(2,1)S(1)}, bf16[4,4,2,32,128]{4,3,2,1,0:T(8,128)(2,1)S(1)}, u32[]{:S(2)}, u32[]{:S(2)}) %collective-permute-start.19) | collective-permute-done | bytes 262176 | tf_op jit(solution)/shard_map/ppermute | solution.py:373
  120.1 1.2 state_out.1
  121.3 3.6 %all-to-all-done.1.refs_0_ = bf16[4,256,256]{2,1,0:T(8,128)(2,1)S(1)} async-done(((bf16[4,256,256]{2,1,0:T(8,128)(2,1)}), bf16[4,256,256]{2,1,0:T(8,128)(2,1)S(1)}, u32[]{:S(2)}, u32[]{:S(2)}) %all-to-all-start.1) | async-done | bytes 524320 | tf_op jit(solution)/shard_map/all_to_all | solution.py:381
  124.9 1.2 unpack.1
  (9 shorter events, 0.1 us)
Async XLA Ops:
  2.3 14.1 %collective-permute-start.3 = (bf16[672,256]{1,0:T(8,128)(2,1)S(1)}, bf16[672,256]{1,0:T(8,128)(2,1)S(1)}, u32[]{:S(2)}, u32[]{:S(2)}) collective-permute-start(bf16[672,256]{1,0:T(8,128)(2,1)S(1)} %get-tuple-element.49), channel_id=1, source_target_pairs={{0,1},{1,2},{2,3},{3,0},{4,5},{5,6},{6,7},{7,4},{8,9},{9,10},{10,1... | collective-permute-start | bytes 1032200 | tf_op jit(solution)/shard_map/ppermute | solution.py:378
  5.4 25.9 %collective-permute-start.4 = (bf16[672,256]{1,0:T(8,128)(2,1)S(1)}, bf16[672,256]{1,0:T(8,128)(2,1)S(1)}, u32[]{:S(2)}, u32[]{:S(2)}) collective-permute-start(bf16[672,256]{1,0:T(8,128)(2,1)S(1)} %get-tuple-element.50), channel_id=1, source_target_pairs={{0,2},{1,3},{2,0},{3,1},{4,6},{5,7},{6,4},{7,5},{8,10},{9,11},{10,... | collective-permute-start | bytes 1032200 | tf_op jit(solution)/shard_map/ppermute | solution.py:378
  8.0 23.3 %collective-permute-start.5 = (bf16[672,256]{1,0:T(8,128)(2,1)S(1)}, bf16[672,256]{1,0:T(8,128)(2,1)S(1)}, u32[]{:S(2)}, u32[]{:S(2)}) collective-permute-start(bf16[672,256]{1,0:T(8,128)(2,1)S(1)} %get-tuple-element.51), channel_id=1, source_target_pairs={{0,3},{1,0},{2,1},{3,2},{4,7},{5,4},{6,5},{7,6},{8,11},{9,8},{10,9... | collective-permute-start | bytes 1032200 | tf_op jit(solution)/shard_map/ppermute | solution.py:378
  11.0 34.0 %collective-permute-start = (bf16[608,384]{1,0:T(8,128)(2,1)S(1)}, bf16[608,384]{1,0:T(8,128)(2,1)S(1)}, u32[]{:S(2)}, u32[]{:S(2)}) collective-permute-start(bf16[608,384]{1,0:T(8,128)(2,1)S(1)} %get-tuple-element.46), channel_id=1, source_target_pairs={{0,1},{1,2},{2,3},{3,0},{4,5},{5,6},{6,7},{7,4},{8,9},{9,10},{10,1... | collective-permute-start | bytes 1400840 | tf_op jit(solution)/shard_map/ppermute | solution.py:378
  11.7 56.1 %collective-permute-start.1 = (bf16[608,384]{1,0:T(8,128)(2,1)S(1)}, bf16[608,384]{1,0:T(8,128)(2,1)S(1)}, u32[]{:S(2)}, u32[]{:S(2)}) collective-permute-start(bf16[608,384]{1,0:T(8,128)(2,1)S(1)} %get-tuple-element.47), channel_id=1, source_target_pairs={{0,2},{1,3},{2,0},{3,1},{4,6},{5,7},{6,4},{7,5},{8,10},{9,11},{10,... | collective-permute-start | bytes 1400840 | tf_op jit(solution)/shard_map/ppermute | solution.py:378
  16.5 51.4 %collective-permute-start.2 = (bf16[608,384]{1,0:T(8,128)(2,1)S(1)}, bf16[608,384]{1,0:T(8,128)(2,1)S(1)}, u32[]{:S(2)}, u32[]{:S(2)}) collective-permute-start(bf16[608,384]{1,0:T(8,128)(2,1)S(1)} %get-tuple-element.48), channel_id=1, source_target_pairs={{0,3},{1,0},{2,1},{3,2},{4,7},{5,4},{6,5},{7,6},{8,11},{9,8},{10,9... | collective-permute-start | bytes 1400840 | tf_op jit(solution)/shard_map/ppermute | solution.py:378
  31.3 5.6 %collective-permute-start.8 = (bf16[4,128,128]{2,1,0:T(8,128)(2,1)S(1)}, bf16[4,128,128]{2,1,0:T(8,128)(2,1)S(1)}, u32[]{:S(2)}, u32[]{:S(2)}) collective-permute-start(bf16[4,128,128]{2,1,0:T(8,128)(2,1)S(1)} %start_share.1.refs_4_), channel_id=1, source_target_pairs={{0,12},{4,8},{8,4},{12,0},{16,28},{20,24},{24,20},{28,16},{1,13},{... | collective-permute-start | bytes 393224 | tf_op jit(solution)/shard_map/ppermute | solution.py:373
  32.5 7.5 %collective-permute-start.7 = (bf16[4,128,128]{2,1,0:T(8,128)(2,1)S(1)}, bf16[4,128,128]{2,1,0:T(8,128)(2,1)S(1)}, u32[]{:S(2)}, u32[]{:S(2)}) collective-permute-start(bf16[4,128,128]{2,1,0:T(8,128)(2,1)S(1)} %start_share.1.refs_4_), channel_id=1, source_target_pairs={{0,8},{4,12},{8,0},{12,4},{16,24},{20,28},{24,16},{28,20},{1,9},{5... | collective-permute-start | bytes 393224 | tf_op jit(solution)/shard_map/ppermute | solution.py:373
  36.9 3.1 %collective-permute-start.6 = (bf16[4,128,128]{2,1,0:T(8,128)(2,1)S(1)}, bf16[4,128,128]{2,1,0:T(8,128)(2,1)S(1)}, u32[]{:S(2)}, u32[]{:S(2)}) collective-permute-start(bf16[4,128,128]{2,1,0:T(8,128)(2,1)S(1)} %start_share.1.refs_4_), channel_id=1, source_target_pairs={{0,4},{4,0},{8,12},{12,8},{16,20},{20,16},{24,28},{28,24},{1,5},{5... | collective-permute-start | bytes 393224 | tf_op jit(solution)/shard_map/ppermute | solution.py:373
  74.3 33.1 %all-to-all-start = ((bf16[4,256,384]{2,1,0:T(8,128)(2,1)}), bf16[4,256,384]{2,1,0:T(8,128)(2,1)S(1)}, u32[]{:S(2)}, u32[]{:S(2)}) async-start(bf16[4,256,384]{2,1,0:T(8,128)(2,1)} %get-tuple-element.62), calls=%async_computation | async-start | bytes 1572864 | tf_op jit(solution)/shard_map/all_to_all | solution.py:381
  87.1 1.5 %collective-permute-start.9 = (bf16[8,128,128]{2,1,0:T(8,128)(2,1)S(1)}, bf16[8,128,128]{2,1,0:T(8,128)(2,1)S(1)}, u32[]{:S(2)}, u32[]{:S(2)}) collective-permute-start(bf16[8,128,128]{2,1,0:T(8,128)(2,1)S(1)} %get-tuple-element.56), channel_id=1, source_target_pairs={{0,4},{4,0},{8,12},{12,8},{16,20},{20,16},{24,28},{28,24},{1,5},{5... | collective-permute-start | bytes 786440 | tf_op jit(solution)/shard_map/ppermute | solution.py:373
  88.7 4.3 %collective-permute-start.10 = (bf16[2,128,128]{2,1,0:T(8,128)(2,1)S(1)}, bf16[2,128,128]{2,1,0:T(8,128)(2,1)S(1)}, u32[]{:S(2)}, u32[]{:S(2)}) collective-permute-start(bf16[2,128,128]{2,1,0:T(8,128)(2,1)S(1)} %get-tuple-element.58), channel_id=1, source_target_pairs={{0,8},{4,12},{8,0},{12,4},{16,24},{20,28},{24,16},{28,20},{1,9},{5... | collective-permute-start | bytes 196616 | tf_op jit(solution)/shard_map/ppermute | solution.py:373
  90.3 4.3 %collective-permute-start.11 = (bf16[2,128,128]{2,1,0:T(8,128)(2,1)S(1)}, bf16[2,128,128]{2,1,0:T(8,128)(2,1)S(1)}, u32[]{:S(2)}, u32[]{:S(2)}) collective-permute-start(bf16[2,128,128]{2,1,0:T(8,128)(2,1)S(1)} %get-tuple-element.59), channel_id=1, source_target_pairs={{0,16},{4,20},{8,24},{12,28},{16,0},{20,4},{24,8},{28,12},{1,17},{... | collective-permute-start | bytes 196616 | tf_op jit(solution)/shard_map/ppermute | solution.py:373
  91.8 5.2 %collective-permute-start.12 = (bf16[2,128,128]{2,1,0:T(8,128)(2,1)S(1)}, bf16[2,128,128]{2,1,0:T(8,128)(2,1)S(1)}, u32[]{:S(2)}, u32[]{:S(2)}) collective-permute-start(bf16[2,128,128]{2,1,0:T(8,128)(2,1)S(1)} %get-tuple-element.60), channel_id=1, source_target_pairs={{0,24},{4,28},{8,16},{12,20},{16,8},{20,12},{24,0},{28,4},{1,25},{... | collective-permute-start | bytes 196616 | tf_op jit(solution)/shard_map/ppermute | solution.py:373
  97.0 10.4 %collective-permute-start.13 = (bf16[2,32,128]{2,1,0:T(8,128)(2,1)S(1)}, bf16[2,32,128]{2,1,0:T(8,128)(2,1)S(1)}, u32[]{:S(2)}, u32[]{:S(2)}) collective-permute-start(bf16[2,32,128]{2,1,0:T(8,128)(2,1)S(1)} %get-tuple-element.64), channel_id=1, source_target_pairs={{0,1},{1,2},{2,3},{3,0},{4,5},{5,6},{6,7},{7,4},{8,9},{9,10},{10,1... | collective-permute-start | bytes 49160 | tf_op jit(solution)/shard_map/ppermute | solution.py:378
  99.1 8.5 %collective-permute-start.14 = (bf16[2,32,128]{2,1,0:T(8,128)(2,1)S(1)}, bf16[2,32,128]{2,1,0:T(8,128)(2,1)S(1)}, u32[]{:S(2)}, u32[]{:S(2)}) collective-permute-start(bf16[2,32,128]{2,1,0:T(8,128)(2,1)S(1)} %get-tuple-element.65), channel_id=1, source_target_pairs={{0,2},{1,3},{2,0},{3,1},{4,6},{5,7},{6,4},{7,5},{8,10},{9,11},{10,... | collective-permute-start | bytes 49160 | tf_op jit(solution)/shard_map/ppermute | solution.py:378
  101.5 6.1 %collective-permute-start.15 = (bf16[2,32,128]{2,1,0:T(8,128)(2,1)S(1)}, bf16[2,32,128]{2,1,0:T(8,128)(2,1)S(1)}, u32[]{:S(2)}, u32[]{:S(2)}) collective-permute-start(bf16[2,32,128]{2,1,0:T(8,128)(2,1)S(1)} %get-tuple-element.66), channel_id=1, source_target_pairs={{0,3},{1,0},{2,1},{3,2},{4,7},{5,4},{6,5},{7,6},{8,11},{9,8},{10,9... | collective-permute-start | bytes 49160 | tf_op jit(solution)/shard_map/ppermute | solution.py:378
  107.6 17.3 %all-to-all-start.1 = ((bf16[4,256,256]{2,1,0:T(8,128)(2,1)}), bf16[4,256,256]{2,1,0:T(8,128)(2,1)S(1)}, u32[]{:S(2)}, u32[]{:S(2)}) async-start(bf16[4,256,256]{2,1,0:T(8,128)(2,1)} %get-tuple-element.68), calls=%async_computation.1 | async-start | bytes 1048576 | tf_op jit(solution)/shard_map/all_to_all | solution.py:381
  111.3 5.6 %collective-permute-start.18 = (bf16[4,2,32,128]{3,2,1,0:T(8,128)(2,1)S(1)}, bf16[4,2,32,128]{3,2,1,0:T(8,128)(2,1)S(1)}, u32[]{:S(2)}, u32[]{:S(2)}) collective-permute-start(bf16[4,2,32,128]{3,2,1,0:T(8,128)(2,1)S(1)} %state_rows.1.refs_0_), channel_id=1, source_target_pairs={{0,24},{4,28},{8,16},{12,20},{16,8},{20,12},{24,0},{28,4},{1,25},{... | collective-permute-start | bytes 196616 | tf_op jit(solution)/shard_map/ppermute | solution.py:373
  113.7 4.3 %collective-permute-start.17 = (bf16[4,2,32,128]{3,2,1,0:T(8,128)(2,1)S(1)}, bf16[4,2,32,128]{3,2,1,0:T(8,128)(2,1)S(1)}, u32[]{:S(2)}, u32[]{:S(2)}) collective-permute-start(bf16[4,2,32,128]{3,2,1,0:T(8,128)(2,1)S(1)} %state_rows.1.refs_0_), channel_id=1, source_target_pairs={{0,16},{4,20},{8,24},{12,28},{16,0},{20,4},{24,8},{28,12},{1,17},{... | collective-permute-start | bytes 196616 | tf_op jit(solution)/shard_map/ppermute | solution.py:373
  114.2 4.3 %collective-permute-start.16 = (bf16[4,2,32,128]{3,2,1,0:T(8,128)(2,1)S(1)}, bf16[4,2,32,128]{3,2,1,0:T(8,128)(2,1)S(1)}, u32[]{:S(2)}, u32[]{:S(2)}) collective-permute-start(bf16[4,2,32,128]{3,2,1,0:T(8,128)(2,1)S(1)} %state_rows.1.refs_0_), channel_id=1, source_target_pairs={{0,8},{4,12},{8,0},{12,4},{16,24},{20,28},{24,16},{28,20},{1,9},{5... | collective-permute-start | bytes 196616 | tf_op jit(solution)/shard_map/ppermute | solution.py:373
  118.5 1.6 %collective-permute-start.19 = (bf16[4,4,2,32,128]{4,3,2,1,0:T(8,128)(2,1)S(1)}, bf16[4,4,2,32,128]{4,3,2,1,0:T(8,128)(2,1)S(1)}, u32[]{:S(2)}, u32[]{:S(2)}) collective-permute-start(bf16[4,4,2,32,128]{4,3,2,1,0:T(8,128)(2,1)S(1)} %state_rest.1.refs_0_), channel_id=1, source_target_pairs={{0,4},{4,0},{8,12},{12,8},{16,20},{20,16},{24,28},{28,24},{1,5},{5... | collective-permute-start | bytes 786440 | tf_op jit(solution)/shard_map/ppermute | solution.py:373

commit v7 on v6

--- a/solution.py
+++ b/solution.py
@@ -28,10 +28,6 @@
 
 def dot_nt(a, b):
     return lax.dot_general(a, b, (((1,), (1,)), ((), ())), preferred_element_type=F32)
-
-
-def dot_tn(a, b):
-    return lax.dot_general(a, b, (((0,), (0,)), ((), ())), preferred_element_type=F32)
 
 
 def call(
@@ -73,10 +69,10 @@
     d = updates
     for step in reversed(range(STEPS)):
         x, gram, poly = xs[step], grams[step], polys[step]
-        dp = [dot_nt(d[m], x[m]) for m in each]
-        sym = [dp[m] + dp[m].T for m in each]
-        turned = [dot_nn(sym[m].astype(BF16), gram[m]) for m in each]
-        da = [(CB * sym[m] + CC * (turned[m] + turned[m].T)).astype(BF16) for m in each]
+        sym = [dot_nt(d[m], x[m]) + dot_nt(x[m], d[m]) for m in each]
+        low = [sym[m].astype(BF16) for m in each]
+        turned = [dot_nn(low[m], gram[m]) + dot_nn(gram[m], low[m]) for m in each]
+        da = [(CB * sym[m] + CC * turned[m]).astype(BF16) for m in each]
         d = [
             (CA * d[m].astype(F32) + dot_nn(poly[m], d[m]) + dot_nn(da[m], x[m])).astype(BF16)
             for m in each
@@ -189,7 +185,7 @@
     return x, y
 
 
-def forward(x, y, wa, wb, wc):
+def forward(x, y, x_turned, y_turned, wa, wb, wc):
     w = wa.shape[1]
     gu = dot_nn(x, jnp.concatenate([wa, wb], axis=1))
     g, u = gu[:, :w], gu[:, w:]
@@ -199,8 +195,8 @@
     hidden = (sw * u).astype(BF16)
     dg = (p * u * slope).astype(BF16)
     du = (p * sw).astype(BF16)
-    ab = dot_tn(x, jnp.concatenate([dg, du], axis=1))
-    return (ab[:, :w], ab[:, w:], dot_tn(y, hidden)), (g, u, p, s), (dg, du, hidden)
+    ab = dot_nn(x_turned, jnp.concatenate([dg, du], axis=1))
+    return (ab[:, :w], ab[:, w:], dot_nn(y_turned, hidden)), (g, u, p, s), (dg, du, hidden)
 
 
 def chunk_kernel(me, dp, *refs, plan, chunk):
@@ -220,7 +216,7 @@
     (before,) = take(1) if last else (None,)
     (d_ref,) = take(1)
     c_refs = take(2 if last else 1)
-    w0, w1, gsum, ssum, acts, fields = take(6)
+    w0, w1, gsum, ssum, acts, fields, flips = take(7)
     total = take(1)[0] if last else c_refs[0]
     base = 3 * first if last else 0
 
@@ -237,14 +233,15 @@
 
     for j in range(count):
         x, y = tokens_of(in_refs, j, 0, plan)
-        sums, act, field = forward(x, y, *[w0[3 * (first + j) + m] for m in range(3)])
+        flips[j, 0], flips[j, 1] = x.T, y.T
+        sums, act, field = forward(x, y, flips[j, 0], flips[j, 1], *[w0[3 * (first + j) + m] for m in range(3)])
         for m in range(3):
             gsum[3 * j + m] = sums[m]
             fields[j, m] = field[m]
         for i, val in enumerate(act):
             acts[j, i] = val
         x, y = tokens_of(in_refs, j, 1, plan)
-        sums, _, _ = forward(x, y, *[w1[3 * j + m].astype(BF16) for m in range(3)])
+        sums, _, _ = forward(x, y, x.T, y.T, *[w1[3 * j + m].astype(BF16) for m in range(3)])
         for m in range(3):
             ssum[3 * j + m] = sums[m]
 
@@ -276,8 +273,8 @@
             to = plan.source(me, slot)
             d_ref[to, 0:t, cols] = dx[slot * t : (slot + 1) * t].astype(BF16)
             d_ref[to, t : 2 * t, cols] = dy[slot * t : (slot + 1) * t].astype(BF16)
-        ab = dot_tn(x, jnp.concatenate([cg, cu], axis=1))
-        grown = (ab[:, :w], ab[:, w:], dot_tn(y, cp))
+        ab = dot_nn(flips[j, 0], jnp.concatenate([cg, cu], axis=1))
+        grown = (ab[:, :w], ab[:, w:], dot_nn(flips[j, 1], cp))
         for m in range(3):
             total[base + 3 * j + m] = (ssum[3 * j + m] + grown[m]).astype(BF16)
 
@@ -430,6 +427,7 @@
         scratch += [pltpu.VMEM((3 * count, width, width), F32)] * 3 + [
             pltpu.VMEM((count, 4, n * t, width), F32),
             pltpu.VMEM((count, 3, n * t, width), BF16),
+            pltpu.VMEM((count, 2, width, n * t), BF16),
         ]
         if last:
             scratch.append(pltpu.VMEM((n_dp * own, width, width), BF16))

time: 126 us -> 126 us (level)
  no operation moved by 1% of the time
where the time goes in v7:
time: 126 us
  waiting for transfers between devices  63.1 us (50%)
  starting transfers between devices  42.6 us (34%)
  Pallas kernels  19.6 us (16%)
    ppermute x9, waiting for transfers between devices, shift(): return lax.ppermute(value, 'ctx', [(i, (i + s) % n) for i in range(n)])  38.7 us
    pallas_call x13, Pallas kernels, call(): pl.pallas_call(kernel, out_shape=out_shape, in_specs=in_specs, out_specs=...  19.6 us
    ppermute x9, starting transfers between devices, shift(): return lax.ppermute(value, 'ctx', [(i, (i + s) % n) for i in range(n)])  16.5 us
    all_to_all x2, starting transfers between devices, turn(): return lax.all_to_all(value, 'ctx', split_axis=0, concat_axis=0, tiled=True)  16.4 us
    ppermute x11, waiting for transfers between devices, swap(): return lax.ppermute(value, 'dp', [(i, i ^ k) for i in range(n_dp)])  16.4 us
    ppermute x11, starting transfers between devices, swap(): return lax.ppermute(value, 'dp', [(i, i ^ k) for i in range(n_dp)])  9.7 us
    all_to_all x2, waiting for transfers between devices, turn(): return lax.all_to_all(value, 'ctx', split_axis=0, concat_axis=0, tiled=True)  8.11 us
  transfers between devices with their start and end apart: 22, of which 16 were waited for; matrix products, arithmetic and copies ran while one was open for 0% of the time, Pallas kernels for 8%

profile of v7, /device:TPU:0, one launch (start us, length us, event | category | flops | bytes accessed | tf_op | source)
XLA Modules:
  0.0 126.1 jit_solution(1273218424133985878)
XLA Ops:
  0.6 1.7 %pack0_1.1 = (bf16[672,256]{1,0:T(8,128)(2,1)S(1)}, bf16[672,256]{1,0:T(8,128)(2,1)S(1)}, bf16[672,256]{1,0:T(8,128)(2,1)S(1)}) custom-call(s32[1]{0:T(128)} %bitcast.me, s32[1]{0:T(128)} %bitcast.1.dp, bf16[1,128,2560]{2,1,0:T(8,128)(2,1)} %k_ref.4, bf16[1,128,2560]{2,1,0:T(8,128)(2,1)} %v_ref.7, bf16[1,128,2560]{2,1,0:T(8,128)(2,1)} %q_ref.7, ...), custom_call_target="tpu_custom_call" | custom-call | flops 1000000 | bytes 1000000 | tf_op jit(solution)/shard_map/pack0_1/pallas_call | solution.py:36
  2.3 3.1 %collective-permute-start.3 = (bf16[672,256]{1,0:T(8,128)(2,1)S(1)}, bf16[672,256]{1,0:T(8,128)(2,1)S(1)}, u32[]{:S(2)}, u32[]{:S(2)}) collective-permute-start(bf16[672,256]{1,0:T(8,128)(2,1)S(1)} %get-tuple-element.49), channel_id=1, source_target_pairs={{0,1},{1,2},{2,3},{3,0},{4,5},{5,6},{6,7},{7,4},{8,9},{9,10},{10,1... | collective-permute-start | bytes 1032200 | tf_op jit(solution)/shard_map/ppermute | solution.py:375
  5.4 2.6 %collective-permute-start.4 = (bf16[672,256]{1,0:T(8,128)(2,1)S(1)}, bf16[672,256]{1,0:T(8,128)(2,1)S(1)}, u32[]{:S(2)}, u32[]{:S(2)}) collective-permute-start(bf16[672,256]{1,0:T(8,128)(2,1)S(1)} %get-tuple-element.50), channel_id=1, source_target_pairs={{0,2},{1,3},{2,0},{3,1},{4,6},{5,7},{6,4},{7,5},{8,10},{9,11},{10,... | collective-permute-start | bytes 1032200 | tf_op jit(solution)/shard_map/ppermute | solution.py:375
  8.0 1.3 %collective-permute-start.5 = (bf16[672,256]{1,0:T(8,128)(2,1)S(1)}, bf16[672,256]{1,0:T(8,128)(2,1)S(1)}, u32[]{:S(2)}, u32[]{:S(2)}) collective-permute-start(bf16[672,256]{1,0:T(8,128)(2,1)S(1)} %get-tuple-element.51), channel_id=1, source_target_pairs={{0,3},{1,0},{2,1},{3,2},{4,7},{5,4},{6,5},{7,6},{8,11},{9,8},{10,9... | collective-permute-start | bytes 1032200 | tf_op jit(solution)/shard_map/ppermute | solution.py:375
  9.3 1.6 %pack1_1.1 = (bf16[608,384]{1,0:T(8,128)(2,1)S(1)}, bf16[608,384]{1,0:T(8,128)(2,1)S(1)}, bf16[608,384]{1,0:T(8,128)(2,1)S(1)}) custom-call(s32[1]{0:T(128)} %bitcast.me, s32[1]{0:T(128)} %bitcast.1.dp, bf16[1,128,2560]{2,1,0:T(8,128)(2,1)} %k_ref.4, bf16[1,128,2560]{2,1,0:T(8,128)(2,1)} %v_ref.7, bf16[1,128,2560]{2,1,0:T(8,128)(2,1)} %q_ref.7, ...), custom_call_target="tpu_custom_call" | custom-call | flops 1000000 | bytes 1000000 | tf_op jit(solution)/shard_map/pack1_1/pallas_call | solution.py:36
  11.0 0.7 collective-permute-start
  11.7 0.3 collective-permute-start.1
  12.0 4.4 %collective-permute-done.3.refs_1_ = bf16[672,256]{1,0:T(8,128)(2,1)S(1)} collective-permute-done((bf16[672,256]{1,0:T(8,128)(2,1)S(1)}, bf16[672,256]{1,0:T(8,128)(2,1)S(1)}, u32[]{:S(2)}, u32[]{:S(2)}) %collective-permute-start.3) | collective-permute-done | bytes 344096 | tf_op jit(solution)/shard_map/ppermute | solution.py:375
  16.5 2.5 %collective-permute-start.2 = (bf16[608,384]{1,0:T(8,128)(2,1)S(1)}, bf16[608,384]{1,0:T(8,128)(2,1)S(1)}, u32[]{:S(2)}, u32[]{:S(2)}) collective-permute-start(bf16[608,384]{1,0:T(8,128)(2,1)S(1)} %get-tuple-element.48), channel_id=1, source_target_pairs={{0,3},{1,0},{2,1},{3,2},{4,7},{5,4},{6,5},{7,6},{8,11},{9,8},{10,9... | collective-permute-start | bytes 1400840 | tf_op jit(solution)/shard_map/ppermute | solution.py:375
  19.0 1.2 pack0_0.1.refs_0_
  20.1 11.1 %collective-permute-done.4.refs_2_ = bf16[672,256]{1,0:T(8,128)(2,1)S(1)} collective-permute-done((bf16[672,256]{1,0:T(8,128)(2,1)S(1)}, bf16[672,256]{1,0:T(8,128)(2,1)S(1)}, u32[]{:S(2)}, u32[]{:S(2)}) %collective-permute-start.4) | collective-permute-done | bytes 344096 | tf_op jit(solution)/shard_map/ppermute | solution.py:375
  31.3 1.2 collective-permute-start.8
  32.5 0.7 collective-permute-start.7
  33.2 3.7 %collective-permute-done.8.refs_7_ = bf16[4,128,128]{2,1,0:T(8,128)(2,1)S(1)} collective-permute-done((bf16[4,128,128]{2,1,0:T(8,128)(2,1)S(1)}, bf16[4,128,128]{2,1,0:T(8,128)(2,1)S(1)}, u32[]{:S(2)}, u32[]{:S(2)}) %collective-permute-start.8) | collective-permute-done | bytes 131104 | tf_op jit(solution)/shard_map/ppermute | solution.py:370
  36.9 0.7 collective-permute-start.6
  37.6 1.2 pack1_0.1.refs_0_
  38.7 1.2 collective-permute-done.7.refs_6_
  40.0 4.9 %chunk0.1 = (bf16[4,256,256]{2,1,0:T(8,128)(2,1)}, bf16[6,128,128]{2,1,0:T(8,128)(2,1)S(1)}) custom-call(s32[1]{0:T(128)} %bitcast.me, s32[1]{0:T(128)} %bitcast.1.dp, bf16[672,256]{1,0:T(8,128)(2,1)S(1)} %pack0_0.1.refs_0_, bf16[672,256]{1,0:T(8,128)(2,1)S(1)} %collective-permute-done.3.refs_1_, bf16[672,256]{1,0:T(8,128)(2,1)S(1)} %collective-permute-done.4.refs_2_, ...), custom_call_target="tpu_custom_call" | custom-call | flops 1280000000 | bytes 2000000 | tf_op jit(solution)/shard_map/chunk0/pallas_call | solution.py:36
  44.9 22.9 %collective-permute-done.1.refs_2_ = bf16[608,384]{1,0:T(8,128)(2,1)S(1)} collective-permute-done((bf16[608,384]{1,0:T(8,128)(2,1)S(1)}, bf16[608,384]{1,0:T(8,128)(2,1)S(1)}, u32[]{:S(2)}, u32[]{:S(2)}) %collective-permute-start.1) | collective-permute-done | bytes 466976 | tf_op jit(solution)/shard_map/ppermute | solution.py:375
  67.8 0.0 collective-permute-done.2.refs_3_
  67.8 6.5 %chunk1.1 = (bf16[4,256,384]{2,1,0:T(8,128)(2,1)}, bf16[8,128,128]{2,1,0:T(8,128)(2,1)S(1)}, bf16[8,128,128]{2,1,0:T(8,128)(2,1)S(1)}) custom-call(s32[1]{0:T(128)} %bitcast.me, s32[1]{0:T(128)} %bitcast.1.dp, bf16[608,384]{1,0:T(8,128)(2,1)S(1)} %pack1_0.1.refs_0_, bf16[608,384]{1,0:T(8,128)(2,1)S(1)} %collective-permute-done.refs_1_, ...), custom_call_target="tpu_custom_call" | custom-call | flops 1920000000 | bytes 3000000 | tf_op jit(solution)/shard_map/chunk1/pallas_call | solution.py:36
  74.3 12.8 %all-to-all-start = ((bf16[4,256,384]{2,1,0:T(8,128)(2,1)}), bf16[4,256,384]{2,1,0:T(8,128)(2,1)S(1)}, u32[]{:S(2)}, u32[]{:S(2)}) async-start(bf16[4,256,384]{2,1,0:T(8,128)(2,1)} %get-tuple-element.62), calls=%async_computation | async-start | bytes 1572864 | tf_op jit(solution)/shard_map/all_to_all | solution.py:378
  87.1 1.5 %collective-permute-done.9.got_ref = bf16[8,128,128]{2,1,0:T(8,128)(2,1)S(1)} collective-permute-done((bf16[8,128,128]{2,1,0:T(8,128)(2,1)S(1)}, bf16[8,128,128]{2,1,0:T(8,128)(2,1)S(1)}, u32[]{:S(2)}, u32[]{:S(2)}) %collective-permute-start.9) | collective-permute-done | bytes 262176 | tf_op jit(solution)/shard_map/ppermute | solution.py:370
  88.6 0.1 state_pair.1
  88.7 1.6 %collective-permute-start.10 = (bf16[2,128,128]{2,1,0:T(8,128)(2,1)S(1)}, bf16[2,128,128]{2,1,0:T(8,128)(2,1)S(1)}, u32[]{:S(2)}, u32[]{:S(2)}) collective-permute-start(bf16[2,128,128]{2,1,0:T(8,128)(2,1)S(1)} %get-tuple-element.58), channel_id=1, source_target_pairs={{0,8},{4,12},{8,0},{12,4},{16,24},{20,28},{24,16},{28,20},{1,9},{5... | collective-permute-start | bytes 196616 | tf_op jit(solution)/shard_map/ppermute | solution.py:370
  90.3 1.5 %collective-permute-start.11 = (bf16[2,128,128]{2,1,0:T(8,128)(2,1)S(1)}, bf16[2,128,128]{2,1,0:T(8,128)(2,1)S(1)}, u32[]{:S(2)}, u32[]{:S(2)}) collective-permute-start(bf16[2,128,128]{2,1,0:T(8,128)(2,1)S(1)} %get-tuple-element.59), channel_id=1, source_target_pairs={{0,16},{4,20},{8,24},{12,28},{16,0},{20,4},{24,8},{28,12},{1,17},{... | collective-permute-start | bytes 196616 | tf_op jit(solution)/shard_map/ppermute | solution.py:370
  91.8 0.5 collective-permute-start.12
  92.3 0.8 collective-permute-done.10.refs_1_
  93.0 1.5 %collective-permute-done.11.refs_2_ = bf16[2,128,128]{2,1,0:T(8,128)(2,1)S(1)} collective-permute-done((bf16[2,128,128]{2,1,0:T(8,128)(2,1)S(1)}, bf16[2,128,128]{2,1,0:T(8,128)(2,1)S(1)}, u32[]{:S(2)}, u32[]{:S(2)}) %collective-permute-start.11) | collective-permute-done | bytes 65568 | tf_op jit(solution)/shard_map/ppermute | solution.py:370
  94.5 2.4 %collective-permute-done.12.refs_3_ = bf16[2,128,128]{2,1,0:T(8,128)(2,1)S(1)} collective-permute-done((bf16[2,128,128]{2,1,0:T(8,128)(2,1)S(1)}, bf16[2,128,128]{2,1,0:T(8,128)(2,1)S(1)}, u32[]{:S(2)}, u32[]{:S(2)}) %collective-permute-start.12) | collective-permute-done | bytes 65568 | tf_op jit(solution)/shard_map/ppermute | solution.py:370
  97.0 0.1 state_sum.1
  97.0 2.1 %collective-permute-start.13 = (bf16[2,32,128]{2,1,0:T(8,128)(2,1)S(1)}, bf16[2,32,128]{2,1,0:T(8,128)(2,1)S(1)}, u32[]{:S(2)}, u32[]{:S(2)}) collective-permute-start(bf16[2,32,128]{2,1,0:T(8,128)(2,1)S(1)} %get-tuple-element.64), channel_id=1, source_target_pairs={{0,1},{1,2},{2,3},{3,0},{4,5},{5,6},{6,7},{7,4},{8,9},{9,10},{10,1... | collective-permute-start | bytes 49160 | tf_op jit(solution)/shard_map/ppermute | solution.py:375
  99.1 2.4 %collective-permute-start.14 = (bf16[2,32,128]{2,1,0:T(8,128)(2,1)S(1)}, bf16[2,32,128]{2,1,0:T(8,128)(2,1)S(1)}, u32[]{:S(2)}, u32[]{:S(2)}) collective-permute-start(bf16[2,32,128]{2,1,0:T(8,128)(2,1)S(1)} %get-tuple-element.65), channel_id=1, source_target_pairs={{0,2},{1,3},{2,0},{3,1},{4,6},{5,7},{6,4},{7,5},{8,10},{9,11},{10,... | collective-permute-start | bytes 49160 | tf_op jit(solution)/shard_map/ppermute | solution.py:375
  101.5 1.5 %collective-permute-start.15 = (bf16[2,32,128]{2,1,0:T(8,128)(2,1)S(1)}, bf16[2,32,128]{2,1,0:T(8,128)(2,1)S(1)}, u32[]{:S(2)}, u32[]{:S(2)}) collective-permute-start(bf16[2,32,128]{2,1,0:T(8,128)(2,1)S(1)} %get-tuple-element.66), channel_id=1, source_target_pairs={{0,3},{1,0},{2,1},{3,2},{4,7},{5,4},{6,5},{7,6},{8,11},{9,8},{10,9... | collective-permute-start | bytes 49160 | tf_op jit(solution)/shard_map/ppermute | solution.py:375
  102.9 4.5 %all-to-all-done.refs_1_ = bf16[4,256,384]{2,1,0:T(8,128)(2,1)S(1)} async-done(((bf16[4,256,384]{2,1,0:T(8,128)(2,1)}), bf16[4,256,384]{2,1,0:T(8,128)(2,1)S(1)}, u32[]{:S(2)}, u32[]{:S(2)}) %all-to-all-start) | async-done | bytes 786464 | tf_op jit(solution)/shard_map/all_to_all | solution.py:378
  107.4 0.2 collective-permute-done.14.refs_2_
  107.6 3.7 %all-to-all-start.1 = ((bf16[4,256,256]{2,1,0:T(8,128)(2,1)}), bf16[4,256,256]{2,1,0:T(8,128)(2,1)S(1)}, u32[]{:S(2)}, u32[]{:S(2)}) async-start(bf16[4,256,256]{2,1,0:T(8,128)(2,1)} %get-tuple-element.68), calls=%async_computation.1 | async-start | bytes 1048576 | tf_op jit(solution)/shard_map/all_to_all | solution.py:378
  111.3 2.4 %collective-permute-start.18 = (bf16[4,2,32,128]{3,2,1,0:T(8,128)(2,1)S(1)}, bf16[4,2,32,128]{3,2,1,0:T(8,128)(2,1)S(1)}, u32[]{:S(2)}, u32[]{:S(2)}) collective-permute-start(bf16[4,2,32,128]{3,2,1,0:T(8,128)(2,1)S(1)} %state_rows.1.refs_0_), channel_id=1, source_target_pairs={{0,24},{4,28},{8,16},{12,20},{16,8},{20,12},{24,0},{28,4},{1,25},{... | collective-permute-start | bytes 196616 | tf_op jit(solution)/shard_map/ppermute | solution.py:370
  113.7 0.5 collective-permute-start.17
  114.2 0.5 collective-permute-start.16
  114.8 2.1 %collective-permute-done.18.refs_3_ = bf16[4,2,32,128]{3,2,1,0:T(8,128)(2,1)S(1)} collective-permute-done((bf16[4,2,32,128]{3,2,1,0:T(8,128)(2,1)S(1)}, bf16[4,2,32,128]{3,2,1,0:T(8,128)(2,1)S(1)}, u32[]{:S(2)}, u32[]{:S(2)}) %collective-permute-start.18) | collective-permute-done | bytes 65568 | tf_op jit(solution)/shard_map/ppermute | solution.py:370
  116.9 1.1 collective-permute-done.17.refs_2_
  118.0 0.5 collective-permute-done.16.refs_1_
  118.5 0.1 collective-permute-start.19
  118.6 1.5 %collective-permute-done.19.refs_1_ = bf16[4,4,2,32,128]{4,3,2,1,0:T(8,128)(2,1)S(1)} collective-permute-done((bf16[4,4,2,32,128]{4,3,2,1,0:T(8,128)(2,1)S(1)}, bf16[4,4,2,32,128]{4,3,2,1,0:T(8,128)(2,1)S(1)}, u32[]{:S(2)}, u32[]{:S(2)}) %collective-permute-start.19) | collective-permute-done | bytes 262176 | tf_op jit(solution)/shard_map/ppermute | solution.py:370
  120.1 1.2 state_out.1
  121.3 3.6 %all-to-all-done.1.refs_0_ = bf16[4,256,256]{2,1,0:T(8,128)(2,1)S(1)} async-done(((bf16[4,256,256]{2,1,0:T(8,128)(2,1)}), bf16[4,256,256]{2,1,0:T(8,128)(2,1)S(1)}, u32[]{:S(2)}, u32[]{:S(2)}) %all-to-all-start.1) | async-done | bytes 524320 | tf_op jit(solution)/shard_map/all_to_all | solution.py:378
  124.9 1.2 unpack.1
  (9 shorter events, 0.1 us)
Async XLA Ops:
  2.3 14.1 %collective-permute-start.3 = (bf16[672,256]{1,0:T(8,128)(2,1)S(1)}, bf16[672,256]{1,0:T(8,128)(2,1)S(1)}, u32[]{:S(2)}, u32[]{:S(2)}) collective-permute-start(bf16[672,256]{1,0:T(8,128)(2,1)S(1)} %get-tuple-element.49), channel_id=1, source_target_pairs={{0,1},{1,2},{2,3},{3,0},{4,5},{5,6},{6,7},{7,4},{8,9},{9,10},{10,1... | collective-permute-start | bytes 1032200 | tf_op jit(solution)/shard_map/ppermute | solution.py:375
  5.4 25.9 %collective-permute-start.4 = (bf16[672,256]{1,0:T(8,128)(2,1)S(1)}, bf16[672,256]{1,0:T(8,128)(2,1)S(1)}, u32[]{:S(2)}, u32[]{:S(2)}) collective-permute-start(bf16[672,256]{1,0:T(8,128)(2,1)S(1)} %get-tuple-element.50), channel_id=1, source_target_pairs={{0,2},{1,3},{2,0},{3,1},{4,6},{5,7},{6,4},{7,5},{8,10},{9,11},{10,... | collective-permute-start | bytes 1032200 | tf_op jit(solution)/shard_map/ppermute | solution.py:375
  8.0 23.3 %collective-permute-start.5 = (bf16[672,256]{1,0:T(8,128)(2,1)S(1)}, bf16[672,256]{1,0:T(8,128)(2,1)S(1)}, u32[]{:S(2)}, u32[]{:S(2)}) collective-permute-start(bf16[672,256]{1,0:T(8,128)(2,1)S(1)} %get-tuple-element.51), channel_id=1, source_target_pairs={{0,3},{1,0},{2,1},{3,2},{4,7},{5,4},{6,5},{7,6},{8,11},{9,8},{10,9... | collective-permute-start | bytes 1032200 | tf_op jit(solution)/shard_map/ppermute | solution.py:375
  11.0 33.9 %collective-permute-start = (bf16[608,384]{1,0:T(8,128)(2,1)S(1)}, bf16[608,384]{1,0:T(8,128)(2,1)S(1)}, u32[]{:S(2)}, u32[]{:S(2)}) collective-permute-start(bf16[608,384]{1,0:T(8,128)(2,1)S(1)} %get-tuple-element.46), channel_id=1, source_target_pairs={{0,1},{1,2},{2,3},{3,0},{4,5},{5,6},{6,7},{7,4},{8,9},{9,10},{10,1... | collective-permute-start | bytes 1400840 | tf_op jit(solution)/shard_map/ppermute | solution.py:375
  11.7 56.1 %collective-permute-start.1 = (bf16[608,384]{1,0:T(8,128)(2,1)S(1)}, bf16[608,384]{1,0:T(8,128)(2,1)S(1)}, u32[]{:S(2)}, u32[]{:S(2)}) collective-permute-start(bf16[608,384]{1,0:T(8,128)(2,1)S(1)} %get-tuple-element.47), channel_id=1, source_target_pairs={{0,2},{1,3},{2,0},{3,1},{4,6},{5,7},{6,4},{7,5},{8,10},{9,11},{10,... | collective-permute-start | bytes 1400840 | tf_op jit(solution)/shard_map/ppermute | solution.py:375
  16.5 51.4 %collective-permute-start.2 = (bf16[608,384]{1,0:T(8,128)(2,1)S(1)}, bf16[608,384]{1,0:T(8,128)(2,1)S(1)}, u32[]{:S(2)}, u32[]{:S(2)}) collective-permute-start(bf16[608,384]{1,0:T(8,128)(2,1)S(1)} %get-tuple-element.48), channel_id=1, source_target_pairs={{0,3},{1,0},{2,1},{3,2},{4,7},{5,4},{6,5},{7,6},{8,11},{9,8},{10,9... | collective-permute-start | bytes 1400840 | tf_op jit(solution)/shard_map/ppermute | solution.py:375
  31.3 5.6 %collective-permute-start.8 = (bf16[4,128,128]{2,1,0:T(8,128)(2,1)S(1)}, bf16[4,128,128]{2,1,0:T(8,128)(2,1)S(1)}, u32[]{:S(2)}, u32[]{:S(2)}) collective-permute-start(bf16[4,128,128]{2,1,0:T(8,128)(2,1)S(1)} %start_share.1.refs_4_), channel_id=1, source_target_pairs={{0,12},{4,8},{8,4},{12,0},{16,28},{20,24},{24,20},{28,16},{1,13},{... | collective-permute-start | bytes 393224 | tf_op jit(solution)/shard_map/ppermute | solution.py:370
  32.5 7.5 %collective-permute-start.7 = (bf16[4,128,128]{2,1,0:T(8,128)(2,1)S(1)}, bf16[4,128,128]{2,1,0:T(8,128)(2,1)S(1)}, u32[]{:S(2)}, u32[]{:S(2)}) collective-permute-start(bf16[4,128,128]{2,1,0:T(8,128)(2,1)S(1)} %start_share.1.refs_4_), channel_id=1, source_target_pairs={{0,8},{4,12},{8,0},{12,4},{16,24},{20,28},{24,16},{28,20},{1,9},{5... | collective-permute-start | bytes 393224 | tf_op jit(solution)/shard_map/ppermute | solution.py:370
  36.9 3.1 %collective-permute-start.6 = (bf16[4,128,128]{2,1,0:T(8,128)(2,1)S(1)}, bf16[4,128,128]{2,1,0:T(8,128)(2,1)S(1)}, u32[]{:S(2)}, u32[]{:S(2)}) collective-permute-start(bf16[4,128,128]{2,1,0:T(8,128)(2,1)S(1)} %start_share.1.refs_4_), channel_id=1, source_target_pairs={{0,4},{4,0},{8,12},{12,8},{16,20},{20,16},{24,28},{28,24},{1,5},{5... | collective-permute-start | bytes 393224 | tf_op jit(solution)/shard_map/ppermute | solution.py:370
  74.3 33.1 %all-to-all-start = ((bf16[4,256,384]{2,1,0:T(8,128)(2,1)}), bf16[4,256,384]{2,1,0:T(8,128)(2,1)S(1)}, u32[]{:S(2)}, u32[]{:S(2)}) async-start(bf16[4,256,384]{2,1,0:T(8,128)(2,1)} %get-tuple-element.62), calls=%async_computation | async-start | bytes 1572864 | tf_op jit(solution)/shard_map/all_to_all | solution.py:378
  87.1 1.5 %collective-permute-start.9 = (bf16[8,128,128]{2,1,0:T(8,128)(2,1)S(1)}, bf16[8,128,128]{2,1,0:T(8,128)(2,1)S(1)}, u32[]{:S(2)}, u32[]{:S(2)}) collective-permute-start(bf16[8,128,128]{2,1,0:T(8,128)(2,1)S(1)} %get-tuple-element.56), channel_id=1, source_target_pairs={{0,4},{4,0},{8,12},{12,8},{16,20},{20,16},{24,28},{28,24},{1,5},{5... | collective-permute-start | bytes 786440 | tf_op jit(solution)/shard_map/ppermute | solution.py:370
  88.7 4.3 %collective-permute-start.10 = (bf16[2,128,128]{2,1,0:T(8,128)(2,1)S(1)}, bf16[2,128,128]{2,1,0:T(8,128)(2,1)S(1)}, u32[]{:S(2)}, u32[]{:S(2)}) collective-permute-start(bf16[2,128,128]{2,1,0:T(8,128)(2,1)S(1)} %get-tuple-element.58), channel_id=1, source_target_pairs={{0,8},{4,12},{8,0},{12,4},{16,24},{20,28},{24,16},{28,20},{1,9},{5... | collective-permute-start | bytes 196616 | tf_op jit(solution)/shard_map/ppermute | solution.py:370
  90.3 4.3 %collective-permute-start.11 = (bf16[2,128,128]{2,1,0:T(8,128)(2,1)S(1)}, bf16[2,128,128]{2,1,0:T(8,128)(2,1)S(1)}, u32[]{:S(2)}, u32[]{:S(2)}) collective-permute-start(bf16[2,128,128]{2,1,0:T(8,128)(2,1)S(1)} %get-tuple-element.59), channel_id=1, source_target_pairs={{0,16},{4,20},{8,24},{12,28},{16,0},{20,4},{24,8},{28,12},{1,17},{... | collective-permute-start | bytes 196616 | tf_op jit(solution)/shard_map/ppermute | solution.py:370
  91.8 5.2 %collective-permute-start.12 = (bf16[2,128,128]{2,1,0:T(8,128)(2,1)S(1)}, bf16[2,128,128]{2,1,0:T(8,128)(2,1)S(1)}, u32[]{:S(2)}, u32[]{:S(2)}) collective-permute-start(bf16[2,128,128]{2,1,0:T(8,128)(2,1)S(1)} %get-tuple-element.60), channel_id=1, source_target_pairs={{0,24},{4,28},{8,16},{12,20},{16,8},{20,12},{24,0},{28,4},{1,25},{... | collective-permute-start | bytes 196616 | tf_op jit(solution)/shard_map/ppermute | solution.py:370
  97.0 10.4 %collective-permute-start.13 = (bf16[2,32,128]{2,1,0:T(8,128)(2,1)S(1)}, bf16[2,32,128]{2,1,0:T(8,128)(2,1)S(1)}, u32[]{:S(2)}, u32[]{:S(2)}) collective-permute-start(bf16[2,32,128]{2,1,0:T(8,128)(2,1)S(1)} %get-tuple-element.64), channel_id=1, source_target_pairs={{0,1},{1,2},{2,3},{3,0},{4,5},{5,6},{6,7},{7,4},{8,9},{9,10},{10,1... | collective-permute-start | bytes 49160 | tf_op jit(solution)/shard_map/ppermute | solution.py:375
  99.1 8.5 %collective-permute-start.14 = (bf16[2,32,128]{2,1,0:T(8,128)(2,1)S(1)}, bf16[2,32,128]{2,1,0:T(8,128)(2,1)S(1)}, u32[]{:S(2)}, u32[]{:S(2)}) collective-permute-start(bf16[2,32,128]{2,1,0:T(8,128)(2,1)S(1)} %get-tuple-element.65), channel_id=1, source_target_pairs={{0,2},{1,3},{2,0},{3,1},{4,6},{5,7},{6,4},{7,5},{8,10},{9,11},{10,... | collective-permute-start | bytes 49160 | tf_op jit(solution)/shard_map/ppermute | solution.py:375
  101.5 6.2 %collective-permute-start.15 = (bf16[2,32,128]{2,1,0:T(8,128)(2,1)S(1)}, bf16[2,32,128]{2,1,0:T(8,128)(2,1)S(1)}, u32[]{:S(2)}, u32[]{:S(2)}) collective-permute-start(bf16[2,32,128]{2,1,0:T(8,128)(2,1)S(1)} %get-tuple-element.66), channel_id=1, source_target_pairs={{0,3},{1,0},{2,1},{3,2},{4,7},{5,4},{6,5},{7,6},{8,11},{9,8},{10,9... | collective-permute-start | bytes 49160 | tf_op jit(solution)/shard_map/ppermute | solution.py:375
  107.6 17.3 %all-to-all-start.1 = ((bf16[4,256,256]{2,1,0:T(8,128)(2,1)}), bf16[4,256,256]{2,1,0:T(8,128)(2,1)S(1)}, u32[]{:S(2)}, u32[]{:S(2)}) async-start(bf16[4,256,256]{2,1,0:T(8,128)(2,1)} %get-tuple-element.68), calls=%async_computation.1 | async-start | bytes 1048576 | tf_op jit(solution)/shard_map/all_to_all | solution.py:378
  111.3 5.6 %collective-permute-start.18 = (bf16[4,2,32,128]{3,2,1,0:T(8,128)(2,1)S(1)}, bf16[4,2,32,128]{3,2,1,0:T(8,128)(2,1)S(1)}, u32[]{:S(2)}, u32[]{:S(2)}) collective-permute-start(bf16[4,2,32,128]{3,2,1,0:T(8,128)(2,1)S(1)} %state_rows.1.refs_0_), channel_id=1, source_target_pairs={{0,24},{4,28},{8,16},{12,20},{16,8},{20,12},{24,0},{28,4},{1,25},{... | collective-permute-start | bytes 196616 | tf_op jit(solution)/shard_map/ppermute | solution.py:370
  113.7 4.3 %collective-permute-start.17 = (bf16[4,2,32,128]{3,2,1,0:T(8,128)(2,1)S(1)}, bf16[4,2,32,128]{3,2,1,0:T(8,128)(2,1)S(1)}, u32[]{:S(2)}, u32[]{:S(2)}) collective-permute-start(bf16[4,2,32,128]{3,2,1,0:T(8,128)(2,1)S(1)} %state_rows.1.refs_0_), channel_id=1, source_target_pairs={{0,16},{4,20},{8,24},{12,28},{16,0},{20,4},{24,8},{28,12},{1,17},{... | collective-permute-start | bytes 196616 | tf_op jit(solution)/shard_map/ppermute | solution.py:370
  114.2 4.3 %collective-permute-start.16 = (bf16[4,2,32,128]{3,2,1,0:T(8,128)(2,1)S(1)}, bf16[4,2,32,128]{3,2,1,0:T(8,128)(2,1)S(1)}, u32[]{:S(2)}, u32[]{:S(2)}) collective-permute-start(bf16[4,2,32,128]{3,2,1,0:T(8,128)(2,1)S(1)} %state_rows.1.refs_0_), channel_id=1, source_target_pairs={{0,8},{4,12},{8,0},{12,4},{16,24},{20,28},{24,16},{28,20},{1,9},{5... | collective-permute-start | bytes 196616 | tf_op jit(solution)/shard_map/ppermute | solution.py:370
  118.5 1.6 %collective-permute-start.19 = (bf16[4,4,2,32,128]{4,3,2,1,0:T(8,128)(2,1)S(1)}, bf16[4,4,2,32,128]{4,3,2,1,0:T(8,128)(2,1)S(1)}, u32[]{:S(2)}, u32[]{:S(2)}) collective-permute-start(bf16[4,4,2,32,128]{4,3,2,1,0:T(8,128)(2,1)S(1)} %state_rest.1.refs_0_), channel_id=1, source_target_pairs={{0,4},{4,0},{8,12},{12,8},{16,20},{20,16},{24,28},{28,24},{1,5},{5... | collective-permute-start | bytes 786440 | tf_op jit(solution)/shard_map/ppermute | solution.py:370

commit v8 on v7

--- a/solution.py
+++ b/solution.py
@@ -52,23 +52,26 @@
     return g * s, s + bent, 2.0 * both + bent * (rest - s)
 
 
-def newton_pullback(grads, updates):
+def newton_forward(grads, kept):
     each = range(len(grads))
     inv = [lax.rsqrt(jnp.sum(g * g, keepdims=True) + 1e-06) for g in grads]
-    xs = [[(grads[m] * inv[m]).astype(BF16) for m in each]]
-    grams = []
-    polys = []
+    x = [(grads[m] * inv[m]).astype(BF16) for m in each]
     for step in range(STEPS):
-        x = xs[-1]
         gram = [dot_nt(x[m], x[m]).astype(BF16) for m in each]
+        yield
         poly = [(CB * gram[m].astype(F32) + CC * dot_nn(gram[m], gram[m])).astype(BF16) for m in each]
-        grams.append(gram)
-        polys.append(poly)
+        kept.append((x, gram, poly))
         if step + 1 < STEPS:
-            xs.append([(CA * x[m].astype(F32) + dot_nn(poly[m], x[m])).astype(BF16) for m in each])
+            yield
+            x = [(CA * x[m].astype(F32) + dot_nn(poly[m], x[m])).astype(BF16) for m in each]
+            yield
+
+
+def newton_pullback(grads, kept, updates):
+    each = range(len(grads))
+    inv = [lax.rsqrt(jnp.sum(g * g, keepdims=True) + 1e-06) for g in grads]
     d = updates
-    for step in reversed(range(STEPS)):
-        x, gram, poly = xs[step], grams[step], polys[step]
+    for x, gram, poly in reversed(kept):
         sym = [dot_nt(d[m], x[m]) + dot_nt(x[m], d[m]) for m in each]
         low = [sym[m].astype(BF16) for m in each]
         turned = [dot_nn(low[m], gram[m]) + dot_nn(gram[m], low[m]) for m in each]
@@ -240,14 +243,22 @@
             fields[j, m] = field[m]
         for i, val in enumerate(act):
             acts[j, i] = val
+
+    grads = [gsum[m] for m in range(mats)]
+    kept = []
+    steps = newton_forward(grads, kept)
+    for j in range(count):
+        next(steps, None)
         x, y = tokens_of(in_refs, j, 1, plan)
         sums, _, _ = forward(x, y, x.T, y.T, *[w1[3 * j + m].astype(BF16) for m in range(3)])
+        next(steps, None)
         for m in range(3):
             ssum[3 * j + m] = sums[m]
-
-    grads = [gsum[m] for m in range(mats)]
+    for _ in steps:
+        pass
+
     updates = [(RATE * ssum[m]).astype(BF16) for m in range(mats)]
-    for m, val in enumerate(newton_pullback(grads, updates)):
+    for m, val in enumerate(newton_pullback(grads, kept, updates)):
         gsum[m] = val
 
     for j in range(count):

time: 126 us -> 127 us (level)
  no operation moved by 1% of the time
where the time goes in v8:
time: 127 us; the launch traced here: 126 us
  waiting for transfers between devices  62.9 us (50%)
  starting transfers between devices  42.6 us (34%)
  Pallas kernels  20 us (16%)
    ppermute x9, waiting for transfers between devices, shift(): return lax.ppermute(value, 'ctx', [(i, (i + s) % n) for i in range(n)])  38.5 us
    pallas_call x13, Pallas kernels, call(): pl.pallas_call(kernel, out_shape=out_shape, in_specs=in_specs, out_specs=...  20 us
    ppermute x9, starting transfers between devices, shift(): return lax.ppermute(value, 'ctx', [(i, (i + s) % n) for i in range(n)])  16.5 us
    all_to_all x2, starting transfers between devices, turn(): return lax.all_to_all(value, 'ctx', split_axis=0, concat_axis=0, tiled=True)  16.4 us
    ppermute x11, waiting for transfers between devices, swap(): return lax.ppermute(value, 'dp', [(i, i ^ k) for i in range(n_dp)])  16.4 us
    ppermute x11, starting transfers between devices, swap(): return lax.ppermute(value, 'dp', [(i, i ^ k) for i in range(n_dp)])  9.7 us
    all_to_all x2, waiting for transfers between devices, turn(): return lax.all_to_all(value, 'ctx', split_axis=0, concat_axis=0, tiled=True)  8.08 us
  transfers between devices with their start and end apart: 22, of which 16 were waited for; matrix products, arithmetic and copies ran while one was open for 0% of the time, Pallas kernels for 8%

profile of v8, /device:TPU:0, one launch (start us, length us, event | category | flops | bytes accessed | tf_op | source)
XLA Modules:
  0.0 126.2 jit_solution(17854065241882059237)
XLA Ops:
  0.6 1.7 %pack0_1.1 = (bf16[672,256]{1,0:T(8,128)(2,1)S(1)}, bf16[672,256]{1,0:T(8,128)(2,1)S(1)}, bf16[672,256]{1,0:T(8,128)(2,1)S(1)}) custom-call(s32[1]{0:T(128)} %bitcast.me, s32[1]{0:T(128)} %bitcast.1.dp, bf16[1,128,2560]{2,1,0:T(8,128)(2,1)} %k_ref.4, bf16[1,128,2560]{2,1,0:T(8,128)(2,1)} %v_ref.7, bf16[1,128,2560]{2,1,0:T(8,128)(2,1)} %q_ref.7, ...), custom_call_target="tpu_custom_call" | custom-call | flops 1000000 | bytes 1000000 | tf_op jit(solution)/shard_map/pack0_1/pallas_call | solution.py:36
  2.3 3.1 %collective-permute-start.3 = (bf16[672,256]{1,0:T(8,128)(2,1)S(1)}, bf16[672,256]{1,0:T(8,128)(2,1)S(1)}, u32[]{:S(2)}, u32[]{:S(2)}) collective-permute-start(bf16[672,256]{1,0:T(8,128)(2,1)S(1)} %get-tuple-element.49), channel_id=1, source_target_pairs={{0,1},{1,2},{2,3},{3,0},{4,5},{5,6},{6,7},{7,4},{8,9},{9,10},{10,1... | collective-permute-start | bytes 1032200 | tf_op jit(solution)/shard_map/ppermute | solution.py:386
  5.4 2.6 %collective-permute-start.4 = (bf16[672,256]{1,0:T(8,128)(2,1)S(1)}, bf16[672,256]{1,0:T(8,128)(2,1)S(1)}, u32[]{:S(2)}, u32[]{:S(2)}) collective-permute-start(bf16[672,256]{1,0:T(8,128)(2,1)S(1)} %get-tuple-element.50), channel_id=1, source_target_pairs={{0,2},{1,3},{2,0},{3,1},{4,6},{5,7},{6,4},{7,5},{8,10},{9,11},{10,... | collective-permute-start | bytes 1032200 | tf_op jit(solution)/shard_map/ppermute | solution.py:386
  8.0 1.3 %collective-permute-start.5 = (bf16[672,256]{1,0:T(8,128)(2,1)S(1)}, bf16[672,256]{1,0:T(8,128)(2,1)S(1)}, u32[]{:S(2)}, u32[]{:S(2)}) collective-permute-start(bf16[672,256]{1,0:T(8,128)(2,1)S(1)} %get-tuple-element.51), channel_id=1, source_target_pairs={{0,3},{1,0},{2,1},{3,2},{4,7},{5,4},{6,5},{7,6},{8,11},{9,8},{10,9... | collective-permute-start | bytes 1032200 | tf_op jit(solution)/shard_map/ppermute | solution.py:386
  9.3 1.6 %pack1_1.1 = (bf16[608,384]{1,0:T(8,128)(2,1)S(1)}, bf16[608,384]{1,0:T(8,128)(2,1)S(1)}, bf16[608,384]{1,0:T(8,128)(2,1)S(1)}) custom-call(s32[1]{0:T(128)} %bitcast.me, s32[1]{0:T(128)} %bitcast.1.dp, bf16[1,128,2560]{2,1,0:T(8,128)(2,1)} %k_ref.4, bf16[1,128,2560]{2,1,0:T(8,128)(2,1)} %v_ref.7, bf16[1,128,2560]{2,1,0:T(8,128)(2,1)} %q_ref.7, ...), custom_call_target="tpu_custom_call" | custom-call | flops 1000000 | bytes 1000000 | tf_op jit(solution)/shard_map/pack1_1/pallas_call | solution.py:36
  11.0 0.7 collective-permute-start
  11.7 0.3 collective-permute-start.1
  12.0 4.4 %collective-permute-done.3.refs_1_ = bf16[672,256]{1,0:T(8,128)(2,1)S(1)} collective-permute-done((bf16[672,256]{1,0:T(8,128)(2,1)S(1)}, bf16[672,256]{1,0:T(8,128)(2,1)S(1)}, u32[]{:S(2)}, u32[]{:S(2)}) %collective-permute-start.3) | collective-permute-done | bytes 344096 | tf_op jit(solution)/shard_map/ppermute | solution.py:386
  16.5 2.5 %collective-permute-start.2 = (bf16[608,384]{1,0:T(8,128)(2,1)S(1)}, bf16[608,384]{1,0:T(8,128)(2,1)S(1)}, u32[]{:S(2)}, u32[]{:S(2)}) collective-permute-start(bf16[608,384]{1,0:T(8,128)(2,1)S(1)} %get-tuple-element.48), channel_id=1, source_target_pairs={{0,3},{1,0},{2,1},{3,2},{4,7},{5,4},{6,5},{7,6},{8,11},{9,8},{10,9... | collective-permute-start | bytes 1400840 | tf_op jit(solution)/shard_map/ppermute | solution.py:386
  19.0 1.2 pack0_0.1.refs_0_
  20.1 11.1 %collective-permute-done.4.refs_2_ = bf16[672,256]{1,0:T(8,128)(2,1)S(1)} collective-permute-done((bf16[672,256]{1,0:T(8,128)(2,1)S(1)}, bf16[672,256]{1,0:T(8,128)(2,1)S(1)}, u32[]{:S(2)}, u32[]{:S(2)}) %collective-permute-start.4) | collective-permute-done | bytes 344096 | tf_op jit(solution)/shard_map/ppermute | solution.py:386
  31.3 0.0 collective-permute-done.5.refs_3_
  31.3 1.2 collective-permute-start.8
  32.5 0.7 collective-permute-start.7
  33.2 3.7 %collective-permute-done.8.refs_7_ = bf16[4,128,128]{2,1,0:T(8,128)(2,1)S(1)} collective-permute-done((bf16[4,128,128]{2,1,0:T(8,128)(2,1)S(1)}, bf16[4,128,128]{2,1,0:T(8,128)(2,1)S(1)}, u32[]{:S(2)}, u32[]{:S(2)}) %collective-permute-start.8) | collective-permute-done | bytes 131104 | tf_op jit(solution)/shard_map/ppermute | solution.py:381
  36.9 0.7 collective-permute-start.6
  37.6 1.2 pack1_0.1.refs_0_
  38.7 1.2 collective-permute-done.7.refs_6_
  40.0 5.1 %chunk0.1 = (bf16[4,256,256]{2,1,0:T(8,128)(2,1)}, bf16[6,128,128]{2,1,0:T(8,128)(2,1)S(1)}) custom-call(s32[1]{0:T(128)} %bitcast.me, s32[1]{0:T(128)} %bitcast.1.dp, bf16[672,256]{1,0:T(8,128)(2,1)S(1)} %pack0_0.1.refs_0_, bf16[672,256]{1,0:T(8,128)(2,1)S(1)} %collective-permute-done.3.refs_1_, bf16[672,256]{1,0:T(8,128)(2,1)S(1)} %collective-permute-done.4.refs_2_, ...), custom_call_target="tpu_custom_call" | custom-call | flops 1280000000 | bytes 2000000 | tf_op jit(solution)/shard_map/chunk0/pallas_call | solution.py:36
  45.1 22.7 %collective-permute-done.1.refs_2_ = bf16[608,384]{1,0:T(8,128)(2,1)S(1)} collective-permute-done((bf16[608,384]{1,0:T(8,128)(2,1)S(1)}, bf16[608,384]{1,0:T(8,128)(2,1)S(1)}, u32[]{:S(2)}, u32[]{:S(2)}) %collective-permute-start.1) | collective-permute-done | bytes 466976 | tf_op jit(solution)/shard_map/ppermute | solution.py:386
  67.8 6.6 %chunk1.1 = (bf16[4,256,384]{2,1,0:T(8,128)(2,1)}, bf16[8,128,128]{2,1,0:T(8,128)(2,1)S(1)}, bf16[8,128,128]{2,1,0:T(8,128)(2,1)S(1)}) custom-call(s32[1]{0:T(128)} %bitcast.me, s32[1]{0:T(128)} %bitcast.1.dp, bf16[608,384]{1,0:T(8,128)(2,1)S(1)} %pack1_0.1.refs_0_, bf16[608,384]{1,0:T(8,128)(2,1)S(1)} %collective-permute-done.refs_1_, ...), custom_call_target="tpu_custom_call" | custom-call | flops 1920000000 | bytes 3000000 | tf_op jit(solution)/shard_map/chunk1/pallas_call | solution.py:36
  74.5 12.8 %all-to-all-start = ((bf16[4,256,384]{2,1,0:T(8,128)(2,1)}), bf16[4,256,384]{2,1,0:T(8,128)(2,1)S(1)}, u32[]{:S(2)}, u32[]{:S(2)}) async-start(bf16[4,256,384]{2,1,0:T(8,128)(2,1)} %get-tuple-element.62), calls=%async_computation | async-start | bytes 1572864 | tf_op jit(solution)/shard_map/all_to_all | solution.py:389
  87.2 1.5 %collective-permute-done.9.got_ref = bf16[8,128,128]{2,1,0:T(8,128)(2,1)S(1)} collective-permute-done((bf16[8,128,128]{2,1,0:T(8,128)(2,1)S(1)}, bf16[8,128,128]{2,1,0:T(8,128)(2,1)S(1)}, u32[]{:S(2)}, u32[]{:S(2)}) %collective-permute-start.9) | collective-permute-done | bytes 262176 | tf_op jit(solution)/shard_map/ppermute | solution.py:381
  88.8 0.1 state_pair.1
  88.9 1.6 %collective-permute-start.10 = (bf16[2,128,128]{2,1,0:T(8,128)(2,1)S(1)}, bf16[2,128,128]{2,1,0:T(8,128)(2,1)S(1)}, u32[]{:S(2)}, u32[]{:S(2)}) collective-permute-start(bf16[2,128,128]{2,1,0:T(8,128)(2,1)S(1)} %get-tuple-element.58), channel_id=1, source_target_pairs={{0,8},{4,12},{8,0},{12,4},{16,24},{20,28},{24,16},{28,20},{1,9},{5... | collective-permute-start | bytes 196616 | tf_op jit(solution)/shard_map/ppermute | solution.py:381
  90.4 1.5 %collective-permute-start.11 = (bf16[2,128,128]{2,1,0:T(8,128)(2,1)S(1)}, bf16[2,128,128]{2,1,0:T(8,128)(2,1)S(1)}, u32[]{:S(2)}, u32[]{:S(2)}) collective-permute-start(bf16[2,128,128]{2,1,0:T(8,128)(2,1)S(1)} %get-tuple-element.59), channel_id=1, source_target_pairs={{0,16},{4,20},{8,24},{12,28},{16,0},{20,4},{24,8},{28,12},{1,17},{... | collective-permute-start | bytes 196616 | tf_op jit(solution)/shard_map/ppermute | solution.py:381
  92.0 0.5 collective-permute-start.12
  92.4 0.8 collective-permute-done.10.refs_1_
  93.2 1.5 %collective-permute-done.11.refs_2_ = bf16[2,128,128]{2,1,0:T(8,128)(2,1)S(1)} collective-permute-done((bf16[2,128,128]{2,1,0:T(8,128)(2,1)S(1)}, bf16[2,128,128]{2,1,0:T(8,128)(2,1)S(1)}, u32[]{:S(2)}, u32[]{:S(2)}) %collective-permute-start.11) | collective-permute-done | bytes 65568 | tf_op jit(solution)/shard_map/ppermute | solution.py:381
  94.7 2.4 %collective-permute-done.12.refs_3_ = bf16[2,128,128]{2,1,0:T(8,128)(2,1)S(1)} collective-permute-done((bf16[2,128,128]{2,1,0:T(8,128)(2,1)S(1)}, bf16[2,128,128]{2,1,0:T(8,128)(2,1)S(1)}, u32[]{:S(2)}, u32[]{:S(2)}) %collective-permute-start.12) | collective-permute-done | bytes 65568 | tf_op jit(solution)/shard_map/ppermute | solution.py:381
  97.1 0.1 state_sum.1
  97.2 2.1 %collective-permute-start.13 = (bf16[2,32,128]{2,1,0:T(8,128)(2,1)S(1)}, bf16[2,32,128]{2,1,0:T(8,128)(2,1)S(1)}, u32[]{:S(2)}, u32[]{:S(2)}) collective-permute-start(bf16[2,32,128]{2,1,0:T(8,128)(2,1)S(1)} %get-tuple-element.64), channel_id=1, source_target_pairs={{0,1},{1,2},{2,3},{3,0},{4,5},{5,6},{6,7},{7,4},{8,9},{9,10},{10,1... | collective-permute-start | bytes 49160 | tf_op jit(solution)/shard_map/ppermute | solution.py:386
  99.2 2.4 %collective-permute-start.14 = (bf16[2,32,128]{2,1,0:T(8,128)(2,1)S(1)}, bf16[2,32,128]{2,1,0:T(8,128)(2,1)S(1)}, u32[]{:S(2)}, u32[]{:S(2)}) collective-permute-start(bf16[2,32,128]{2,1,0:T(8,128)(2,1)S(1)} %get-tuple-element.65), channel_id=1, source_target_pairs={{0,2},{1,3},{2,0},{3,1},{4,6},{5,7},{6,4},{7,5},{8,10},{9,11},{10,... | collective-permute-start | bytes 49160 | tf_op jit(solution)/shard_map/ppermute | solution.py:386
  101.6 1.5 %collective-permute-start.15 = (bf16[2,32,128]{2,1,0:T(8,128)(2,1)S(1)}, bf16[2,32,128]{2,1,0:T(8,128)(2,1)S(1)}, u32[]{:S(2)}, u32[]{:S(2)}) collective-permute-start(bf16[2,32,128]{2,1,0:T(8,128)(2,1)S(1)} %get-tuple-element.66), channel_id=1, source_target_pairs={{0,3},{1,0},{2,1},{3,2},{4,7},{5,4},{6,5},{7,6},{8,11},{9,8},{10,9... | collective-permute-start | bytes 49160 | tf_op jit(solution)/shard_map/ppermute | solution.py:386
  103.1 4.5 %all-to-all-done.refs_1_ = bf16[4,256,384]{2,1,0:T(8,128)(2,1)S(1)} async-done(((bf16[4,256,384]{2,1,0:T(8,128)(2,1)}), bf16[4,256,384]{2,1,0:T(8,128)(2,1)S(1)}, u32[]{:S(2)}, u32[]{:S(2)}) %all-to-all-start) | async-done | bytes 786464 | tf_op jit(solution)/shard_map/all_to_all | solution.py:389
  107.6 0.2 collective-permute-done.14.refs_2_
  107.8 3.7 %all-to-all-start.1 = ((bf16[4,256,256]{2,1,0:T(8,128)(2,1)}), bf16[4,256,256]{2,1,0:T(8,128)(2,1)S(1)}, u32[]{:S(2)}, u32[]{:S(2)}) async-start(bf16[4,256,256]{2,1,0:T(8,128)(2,1)} %get-tuple-element.68), calls=%async_computation.1 | async-start | bytes 1048576 | tf_op jit(solution)/shard_map/all_to_all | solution.py:389
  111.4 2.5 %collective-permute-start.18 = (bf16[4,2,32,128]{3,2,1,0:T(8,128)(2,1)S(1)}, bf16[4,2,32,128]{3,2,1,0:T(8,128)(2,1)S(1)}, u32[]{:S(2)}, u32[]{:S(2)}) collective-permute-start(bf16[4,2,32,128]{3,2,1,0:T(8,128)(2,1)S(1)} %state_rows.1.refs_0_), channel_id=1, source_target_pairs={{0,24},{4,28},{8,16},{12,20},{16,8},{20,12},{24,0},{28,4},{1,25},{... | collective-permute-start | bytes 196616 | tf_op jit(solution)/shard_map/ppermute | solution.py:381
  113.9 0.5 collective-permute-start.17
  114.4 0.5 collective-permute-start.16
  114.9 2.1 %collective-permute-done.18.refs_3_ = bf16[4,2,32,128]{3,2,1,0:T(8,128)(2,1)S(1)} collective-permute-done((bf16[4,2,32,128]{3,2,1,0:T(8,128)(2,1)S(1)}, bf16[4,2,32,128]{3,2,1,0:T(8,128)(2,1)S(1)}, u32[]{:S(2)}, u32[]{:S(2)}) %collective-permute-start.18) | collective-permute-done | bytes 65568 | tf_op jit(solution)/shard_map/ppermute | solution.py:381
  117.0 1.1 collective-permute-done.17.refs_2_
  118.1 0.5 collective-permute-done.16.refs_1_
  118.7 0.1 collective-permute-start.19
  118.8 1.5 %collective-permute-done.19.refs_1_ = bf16[4,4,2,32,128]{4,3,2,1,0:T(8,128)(2,1)S(1)} collective-permute-done((bf16[4,4,2,32,128]{4,3,2,1,0:T(8,128)(2,1)S(1)}, bf16[4,4,2,32,128]{4,3,2,1,0:T(8,128)(2,1)S(1)}, u32[]{:S(2)}, u32[]{:S(2)}) %collective-permute-start.19) | collective-permute-done | bytes 262176 | tf_op jit(solution)/shard_map/ppermute | solution.py:381
  120.3 1.2 state_out.1
  121.5 3.6 %all-to-all-done.1.refs_0_ = bf16[4,256,256]{2,1,0:T(8,128)(2,1)S(1)} async-done(((bf16[4,256,256]{2,1,0:T(8,128)(2,1)}), bf16[4,256,256]{2,1,0:T(8,128)(2,1)S(1)}, u32[]{:S(2)}, u32[]{:S(2)}) %all-to-all-start.1) | async-done | bytes 524320 | tf_op jit(solution)/shard_map/all_to_all | solution.py:389
  125.0 1.2 unpack.1
  (9 shorter events, 0.1 us)
Async XLA Ops:
  2.3 14.1 %collective-permute-start.3 = (bf16[672,256]{1,0:T(8,128)(2,1)S(1)}, bf16[672,256]{1,0:T(8,128)(2,1)S(1)}, u32[]{:S(2)}, u32[]{:S(2)}) collective-permute-start(bf16[672,256]{1,0:T(8,128)(2,1)S(1)} %get-tuple-element.49), channel_id=1, source_target_pairs={{0,1},{1,2},{2,3},{3,0},{4,5},{5,6},{6,7},{7,4},{8,9},{9,10},{10,1... | collective-permute-start | bytes 1032200 | tf_op jit(solution)/shard_map/ppermute | solution.py:386
  5.4 25.9 %collective-permute-start.4 = (bf16[672,256]{1,0:T(8,128)(2,1)S(1)}, bf16[672,256]{1,0:T(8,128)(2,1)S(1)}, u32[]{:S(2)}, u32[]{:S(2)}) collective-permute-start(bf16[672,256]{1,0:T(8,128)(2,1)S(1)} %get-tuple-element.50), channel_id=1, source_target_pairs={{0,2},{1,3},{2,0},{3,1},{4,6},{5,7},{6,4},{7,5},{8,10},{9,11},{10,... | collective-permute-start | bytes 1032200 | tf_op jit(solution)/shard_map/ppermute | solution.py:386
  8.0 23.3 %collective-permute-start.5 = (bf16[672,256]{1,0:T(8,128)(2,1)S(1)}, bf16[672,256]{1,0:T(8,128)(2,1)S(1)}, u32[]{:S(2)}, u32[]{:S(2)}) collective-permute-start(bf16[672,256]{1,0:T(8,128)(2,1)S(1)} %get-tuple-element.51), channel_id=1, source_target_pairs={{0,3},{1,0},{2,1},{3,2},{4,7},{5,4},{6,5},{7,6},{8,11},{9,8},{10,9... | collective-permute-start | bytes 1032200 | tf_op jit(solution)/shard_map/ppermute | solution.py:386
  11.0 34.1 %collective-permute-start = (bf16[608,384]{1,0:T(8,128)(2,1)S(1)}, bf16[608,384]{1,0:T(8,128)(2,1)S(1)}, u32[]{:S(2)}, u32[]{:S(2)}) collective-permute-start(bf16[608,384]{1,0:T(8,128)(2,1)S(1)} %get-tuple-element.46), channel_id=1, source_target_pairs={{0,1},{1,2},{2,3},{3,0},{4,5},{5,6},{6,7},{7,4},{8,9},{9,10},{10,1... | collective-permute-start | bytes 1400840 | tf_op jit(solution)/shard_map/ppermute | solution.py:386
  11.7 56.1 %collective-permute-start.1 = (bf16[608,384]{1,0:T(8,128)(2,1)S(1)}, bf16[608,384]{1,0:T(8,128)(2,1)S(1)}, u32[]{:S(2)}, u32[]{:S(2)}) collective-permute-start(bf16[608,384]{1,0:T(8,128)(2,1)S(1)} %get-tuple-element.47), channel_id=1, source_target_pairs={{0,2},{1,3},{2,0},{3,1},{4,6},{5,7},{6,4},{7,5},{8,10},{9,11},{10,... | collective-permute-start | bytes 1400840 | tf_op jit(solution)/shard_map/ppermute | solution.py:386
  16.5 51.4 %collective-permute-start.2 = (bf16[608,384]{1,0:T(8,128)(2,1)S(1)}, bf16[608,384]{1,0:T(8,128)(2,1)S(1)}, u32[]{:S(2)}, u32[]{:S(2)}) collective-permute-start(bf16[608,384]{1,0:T(8,128)(2,1)S(1)} %get-tuple-element.48), channel_id=1, source_target_pairs={{0,3},{1,0},{2,1},{3,2},{4,7},{5,4},{6,5},{7,6},{8,11},{9,8},{10,9... | collective-permute-start | bytes 1400840 | tf_op jit(solution)/shard_map/ppermute | solution.py:386
  31.3 5.6 %collective-permute-start.8 = (bf16[4,128,128]{2,1,0:T(8,128)(2,1)S(1)}, bf16[4,128,128]{2,1,0:T(8,128)(2,1)S(1)}, u32[]{:S(2)}, u32[]{:S(2)}) collective-permute-start(bf16[4,128,128]{2,1,0:T(8,128)(2,1)S(1)} %start_share.1.refs_4_), channel_id=1, source_target_pairs={{0,12},{4,8},{8,4},{12,0},{16,28},{20,24},{24,20},{28,16},{1,13},{... | collective-permute-start | bytes 393224 | tf_op jit(solution)/shard_map/ppermute | solution.py:381
  32.5 7.5 %collective-permute-start.7 = (bf16[4,128,128]{2,1,0:T(8,128)(2,1)S(1)}, bf16[4,128,128]{2,1,0:T(8,128)(2,1)S(1)}, u32[]{:S(2)}, u32[]{:S(2)}) collective-permute-start(bf16[4,128,128]{2,1,0:T(8,128)(2,1)S(1)} %start_share.1.refs_4_), channel_id=1, source_target_pairs={{0,8},{4,12},{8,0},{12,4},{16,24},{20,28},{24,16},{28,20},{1,9},{5... | collective-permute-start | bytes 393224 | tf_op jit(solution)/shard_map/ppermute | solution.py:381
  36.9 3.1 %collective-permute-start.6 = (bf16[4,128,128]{2,1,0:T(8,128)(2,1)S(1)}, bf16[4,128,128]{2,1,0:T(8,128)(2,1)S(1)}, u32[]{:S(2)}, u32[]{:S(2)}) collective-permute-start(bf16[4,128,128]{2,1,0:T(8,128)(2,1)S(1)} %start_share.1.refs_4_), channel_id=1, source_target_pairs={{0,4},{4,0},{8,12},{12,8},{16,20},{20,16},{24,28},{28,24},{1,5},{5... | collective-permute-start | bytes 393224 | tf_op jit(solution)/shard_map/ppermute | solution.py:381
  74.5 33.1 %all-to-all-start = ((bf16[4,256,384]{2,1,0:T(8,128)(2,1)}), bf16[4,256,384]{2,1,0:T(8,128)(2,1)S(1)}, u32[]{:S(2)}, u32[]{:S(2)}) async-start(bf16[4,256,384]{2,1,0:T(8,128)(2,1)} %get-tuple-element.62), calls=%async_computation | async-start | bytes 1572864 | tf_op jit(solution)/shard_map/all_to_all | solution.py:389
  87.2 1.5 %collective-permute-start.9 = (bf16[8,128,128]{2,1,0:T(8,128)(2,1)S(1)}, bf16[8,128,128]{2,1,0:T(8,128)(2,1)S(1)}, u32[]{:S(2)}, u32[]{:S(2)}) collective-permute-start(bf16[8,128,128]{2,1,0:T(8,128)(2,1)S(1)} %get-tuple-element.56), channel_id=1, source_target_pairs={{0,4},{4,0},{8,12},{12,8},{16,20},{20,16},{24,28},{28,24},{1,5},{5... | collective-permute-start | bytes 786440 | tf_op jit(solution)/shard_map/ppermute | solution.py:381
  88.9 4.3 %collective-permute-start.10 = (bf16[2,128,128]{2,1,0:T(8,128)(2,1)S(1)}, bf16[2,128,128]{2,1,0:T(8,128)(2,1)S(1)}, u32[]{:S(2)}, u32[]{:S(2)}) collective-permute-start(bf16[2,128,128]{2,1,0:T(8,128)(2,1)S(1)} %get-tuple-element.58), channel_id=1, source_target_pairs={{0,8},{4,12},{8,0},{12,4},{16,24},{20,28},{24,16},{28,20},{1,9},{5... | collective-permute-start | bytes 196616 | tf_op jit(solution)/shard_map/ppermute | solution.py:381
  90.4 4.3 %collective-permute-start.11 = (bf16[2,128,128]{2,1,0:T(8,128)(2,1)S(1)}, bf16[2,128,128]{2,1,0:T(8,128)(2,1)S(1)}, u32[]{:S(2)}, u32[]{:S(2)}) collective-permute-start(bf16[2,128,128]{2,1,0:T(8,128)(2,1)S(1)} %get-tuple-element.59), channel_id=1, source_target_pairs={{0,16},{4,20},{8,24},{12,28},{16,0},{20,4},{24,8},{28,12},{1,17},{... | collective-permute-start | bytes 196616 | tf_op jit(solution)/shard_map/ppermute | solution.py:381
  92.0 5.2 %collective-permute-start.12 = (bf16[2,128,128]{2,1,0:T(8,128)(2,1)S(1)}, bf16[2,128,128]{2,1,0:T(8,128)(2,1)S(1)}, u32[]{:S(2)}, u32[]{:S(2)}) collective-permute-start(bf16[2,128,128]{2,1,0:T(8,128)(2,1)S(1)} %get-tuple-element.60), channel_id=1, source_target_pairs={{0,24},{4,28},{8,16},{12,20},{16,8},{20,12},{24,0},{28,4},{1,25},{... | collective-permute-start | bytes 196616 | tf_op jit(solution)/shard_map/ppermute | solution.py:381
  97.2 10.4 %collective-permute-start.13 = (bf16[2,32,128]{2,1,0:T(8,128)(2,1)S(1)}, bf16[2,32,128]{2,1,0:T(8,128)(2,1)S(1)}, u32[]{:S(2)}, u32[]{:S(2)}) collective-permute-start(bf16[2,32,128]{2,1,0:T(8,128)(2,1)S(1)} %get-tuple-element.64), channel_id=1, source_target_pairs={{0,1},{1,2},{2,3},{3,0},{4,5},{5,6},{6,7},{7,4},{8,9},{9,10},{10,1... | collective-permute-start | bytes 49160 | tf_op jit(solution)/shard_map/ppermute | solution.py:386
  99.2 8.5 %collective-permute-start.14 = (bf16[2,32,128]{2,1,0:T(8,128)(2,1)S(1)}, bf16[2,32,128]{2,1,0:T(8,128)(2,1)S(1)}, u32[]{:S(2)}, u32[]{:S(2)}) collective-permute-start(bf16[2,32,128]{2,1,0:T(8,128)(2,1)S(1)} %get-tuple-element.65), channel_id=1, source_target_pairs={{0,2},{1,3},{2,0},{3,1},{4,6},{5,7},{6,4},{7,5},{8,10},{9,11},{10,... | collective-permute-start | bytes 49160 | tf_op jit(solution)/shard_map/ppermute | solution.py:386
  101.6 6.1 %collective-permute-start.15 = (bf16[2,32,128]{2,1,0:T(8,128)(2,1)S(1)}, bf16[2,32,128]{2,1,0:T(8,128)(2,1)S(1)}, u32[]{:S(2)}, u32[]{:S(2)}) collective-permute-start(bf16[2,32,128]{2,1,0:T(8,128)(2,1)S(1)} %get-tuple-element.66), channel_id=1, source_target_pairs={{0,3},{1,0},{2,1},{3,2},{4,7},{5,4},{6,5},{7,6},{8,11},{9,8},{10,9... | collective-permute-start | bytes 49160 | tf_op jit(solution)/shard_map/ppermute | solution.py:386
  107.8 17.3 %all-to-all-start.1 = ((bf16[4,256,256]{2,1,0:T(8,128)(2,1)}), bf16[4,256,256]{2,1,0:T(8,128)(2,1)S(1)}, u32[]{:S(2)}, u32[]{:S(2)}) async-start(bf16[4,256,256]{2,1,0:T(8,128)(2,1)} %get-tuple-element.68), calls=%async_computation.1 | async-start | bytes 1048576 | tf_op jit(solution)/shard_map/all_to_all | solution.py:389
  111.4 5.6 %collective-permute-start.18 = (bf16[4,2,32,128]{3,2,1,0:T(8,128)(2,1)S(1)}, bf16[4,2,32,128]{3,2,1,0:T(8,128)(2,1)S(1)}, u32[]{:S(2)}, u32[]{:S(2)}) collective-permute-start(bf16[4,2,32,128]{3,2,1,0:T(8,128)(2,1)S(1)} %state_rows.1.refs_0_), channel_id=1, source_target_pairs={{0,24},{4,28},{8,16},{12,20},{16,8},{20,12},{24,0},{28,4},{1,25},{... | collective-permute-start | bytes 196616 | tf_op jit(solution)/shard_map/ppermute | solution.py:381
  113.9 4.3 %collective-permute-start.17 = (bf16[4,2,32,128]{3,2,1,0:T(8,128)(2,1)S(1)}, bf16[4,2,32,128]{3,2,1,0:T(8,128)(2,1)S(1)}, u32[]{:S(2)}, u32[]{:S(2)}) collective-permute-start(bf16[4,2,32,128]{3,2,1,0:T(8,128)(2,1)S(1)} %state_rows.1.refs_0_), channel_id=1, source_target_pairs={{0,16},{4,20},{8,24},{12,28},{16,0},{20,4},{24,8},{28,12},{1,17},{... | collective-permute-start | bytes 196616 | tf_op jit(solution)/shard_map/ppermute | solution.py:381
  114.4 4.3 %collective-permute-start.16 = (bf16[4,2,32,128]{3,2,1,0:T(8,128)(2,1)S(1)}, bf16[4,2,32,128]{3,2,1,0:T(8,128)(2,1)S(1)}, u32[]{:S(2)}, u32[]{:S(2)}) collective-permute-start(bf16[4,2,32,128]{3,2,1,0:T(8,128)(2,1)S(1)} %state_rows.1.refs_0_), channel_id=1, source_target_pairs={{0,8},{4,12},{8,0},{12,4},{16,24},{20,28},{24,16},{28,20},{1,9},{5... | collective-permute-start | bytes 196616 | tf_op jit(solution)/shard_map/ppermute | solution.py:381
  118.7 1.6 %collective-permute-start.19 = (bf16[4,4,2,32,128]{4,3,2,1,0:T(8,128)(2,1)S(1)}, bf16[4,4,2,32,128]{4,3,2,1,0:T(8,128)(2,1)S(1)}, u32[]{:S(2)}, u32[]{:S(2)}) collective-permute-start(bf16[4,4,2,32,128]{4,3,2,1,0:T(8,128)(2,1)S(1)} %state_rest.1.refs_0_), channel_id=1, source_target_pairs={{0,4},{4,0},{8,12},{12,8},{16,20},{20,16},{24,28},{28,24},{1,5},{5... | collective-permute-start | bytes 786440 | tf_op jit(solution)/shard_map/ppermute | solution.py:381

commit v9 on v6

--- a/solution.py
+++ b/solution.py
@@ -101,7 +101,7 @@
         self.rest = n_dp // self.pair
         self.own = -(-self.mats // n_dp)
         self.block = -(-rows // 16) * 16
-        self.group = min(4, n_dp)
+        self.group = min(8, n_dp)
         self.share = -(-self.mats // self.group)
         self.share_blocks = -(-self.share // least)
 

time: 126 us -> 125 us (level)
  waiting for transfers between devices: 63.1 us -> 56 us
  starting transfers between devices: 42.6 us -> 48.7 us
    ppermute x9, waiting for transfers between devices: 38.6 us -> 29.6 us  [shift(): return lax.ppermute(value, 'ctx', [(i, (i + s) % n) for i in range(n)])]
    ppermute x11 -> x15, starting transfers between devices: 9.7 us -> 15.7 us  [swap(): return lax.ppermute(value, 'dp', [(i, i ^ k) for i in range(n_dp)])]
    ppermute x11 -> x15, waiting for transfers between devices: 16.4 us -> 18.1 us  [swap(): return lax.ppermute(value, 'dp', [(i, i ^ k) for i in range(n_dp)])]
  transfers between devices with their start and end apart: 22 -> 26, of which waited for: 16 -> 20; matrix products, arithmetic and copies ran while one was open for 0% -> 0% of each run, Pallas kernels for 8% -> 8%
where the time goes in v9:
time: 125 us
  waiting for transfers between devices  56 us (45%)
  starting transfers between devices  48.7 us (39%)
  Pallas kernels  19.6 us (16%)
    ppermute x9, waiting for transfers between devices, shift(): return lax.ppermute(value, 'ctx', [(i, (i + s) % n) for i in range(n)])  29.6 us
    pallas_call x13, Pallas kernels, call(): pl.pallas_call(kernel, out_shape=out_shape, in_specs=in_specs, out_specs=...  19.6 us
    ppermute x15, waiting for transfers between devices, swap(): return lax.ppermute(value, 'dp', [(i, i ^ k) for i in range(n_dp)])  18.1 us
    all_to_all x2, starting transfers between devices, turn(): return lax.all_to_all(value, 'ctx', split_axis=0, concat_axis=0, tiled=True)  16.5 us
    ppermute x9, starting transfers between devices, shift(): return lax.ppermute(value, 'ctx', [(i, (i + s) % n) for i in range(n)])  16.5 us
    ppermute x15, starting transfers between devices, swap(): return lax.ppermute(value, 'dp', [(i, i ^ k) for i in range(n_dp)])  15.7 us
    all_to_all x2, waiting for transfers between devices, turn(): return lax.all_to_all(value, 'ctx', split_axis=0, concat_axis=0, tiled=True)  8.35 us
  transfers between devices with their start and end apart: 26, of which 20 were waited for; matrix products, arithmetic and copies ran while one was open for 0% of the time, Pallas kernels for 8%

profile of v9, /device:TPU:0, one launch (start us, length us, event | category | flops | bytes accessed | tf_op | source)
XLA Modules:
  0.0 125.1 jit_solution(8546580054017256943)
XLA Ops:
  0.6 1.7 %pack0_1.1 = (bf16[640,256]{1,0:T(8,128)(2,1)S(1)}, bf16[640,256]{1,0:T(8,128)(2,1)S(1)}, bf16[640,256]{1,0:T(8,128)(2,1)S(1)}) custom-call(s32[1]{0:T(128)} %bitcast.me, s32[1]{0:T(128)} %bitcast.1.dp, bf16[1,128,2560]{2,1,0:T(8,128)(2,1)} %k_ref.4, bf16[1,128,2560]{2,1,0:T(8,128)(2,1)} %v_ref.7, bf16[1,128,2560]{2,1,0:T(8,128)(2,1)} %q_ref.7, ...), custom_call_target="tpu_custom_call" | custom-call | flops 1000000 | bytes 1000000 | tf_op jit(solution)/shard_map/pack0_1/pallas_call | solution.py:40
  2.3 3.1 %collective-permute-start.3 = (bf16[640,256]{1,0:T(8,128)(2,1)S(1)}, bf16[640,256]{1,0:T(8,128)(2,1)S(1)}, u32[]{:S(2)}, u32[]{:S(2)}) collective-permute-start(bf16[640,256]{1,0:T(8,128)(2,1)S(1)} %get-tuple-element.49), channel_id=1, source_target_pairs={{0,1},{1,2},{2,3},{3,0},{4,5},{5,6},{6,7},{7,4},{8,9},{9,10},{10,1... | collective-permute-start | bytes 983048 | tf_op jit(solution)/shard_map/ppermute | solution.py:378
  5.4 2.6 %collective-permute-start.4 = (bf16[640,256]{1,0:T(8,128)(2,1)S(1)}, bf16[640,256]{1,0:T(8,128)(2,1)S(1)}, u32[]{:S(2)}, u32[]{:S(2)}) collective-permute-start(bf16[640,256]{1,0:T(8,128)(2,1)S(1)} %get-tuple-element.50), channel_id=1, source_target_pairs={{0,2},{1,3},{2,0},{3,1},{4,6},{5,7},{6,4},{7,5},{8,10},{9,11},{10,... | collective-permute-start | bytes 983048 | tf_op jit(solution)/shard_map/ppermute | solution.py:378
  8.0 1.3 %collective-permute-start.5 = (bf16[640,256]{1,0:T(8,128)(2,1)S(1)}, bf16[640,256]{1,0:T(8,128)(2,1)S(1)}, u32[]{:S(2)}, u32[]{:S(2)}) collective-permute-start(bf16[640,256]{1,0:T(8,128)(2,1)S(1)} %get-tuple-element.51), channel_id=1, source_target_pairs={{0,3},{1,0},{2,1},{3,2},{4,7},{5,4},{6,5},{7,6},{8,11},{9,8},{10,9... | collective-permute-start | bytes 983048 | tf_op jit(solution)/shard_map/ppermute | solution.py:378
  9.3 1.6 %pack1_1.1 = (bf16[608,384]{1,0:T(8,128)(2,1)S(1)}, bf16[608,384]{1,0:T(8,128)(2,1)S(1)}, bf16[608,384]{1,0:T(8,128)(2,1)S(1)}) custom-call(s32[1]{0:T(128)} %bitcast.me, s32[1]{0:T(128)} %bitcast.1.dp, bf16[1,128,2560]{2,1,0:T(8,128)(2,1)} %k_ref.4, bf16[1,128,2560]{2,1,0:T(8,128)(2,1)} %v_ref.7, bf16[1,128,2560]{2,1,0:T(8,128)(2,1)} %q_ref.7, ...), custom_call_target="tpu_custom_call" | custom-call | flops 1000000 | bytes 1000000 | tf_op jit(solution)/shard_map/pack1_1/pallas_call | solution.py:40
  11.0 0.7 collective-permute-start
  12.0 4.1 %collective-permute-done.3.refs_1_ = bf16[640,256]{1,0:T(8,128)(2,1)S(1)} collective-permute-done((bf16[640,256]{1,0:T(8,128)(2,1)S(1)}, bf16[640,256]{1,0:T(8,128)(2,1)S(1)}, u32[]{:S(2)}, u32[]{:S(2)}) %collective-permute-start.3) | collective-permute-done | bytes 327712 | tf_op jit(solution)/shard_map/ppermute | solution.py:378
  16.1 2.5 %collective-permute-start.2 = (bf16[608,384]{1,0:T(8,128)(2,1)S(1)}, bf16[608,384]{1,0:T(8,128)(2,1)S(1)}, u32[]{:S(2)}, u32[]{:S(2)}) collective-permute-start(bf16[608,384]{1,0:T(8,128)(2,1)S(1)} %get-tuple-element.48), channel_id=1, source_target_pairs={{0,3},{1,0},{2,1},{3,2},{4,7},{5,4},{6,5},{7,6},{8,11},{9,8},{10,9... | collective-permute-start | bytes 1400840 | tf_op jit(solution)/shard_map/ppermute | solution.py:378
  18.6 1.2 pack0_0.1.refs_0_
  19.8 10.4 %collective-permute-done.4.refs_2_ = bf16[640,256]{1,0:T(8,128)(2,1)S(1)} collective-permute-done((bf16[640,256]{1,0:T(8,128)(2,1)S(1)}, bf16[640,256]{1,0:T(8,128)(2,1)S(1)}, u32[]{:S(2)}, u32[]{:S(2)}) %collective-permute-start.4) | collective-permute-done | bytes 327712 | tf_op jit(solution)/shard_map/ppermute | solution.py:378
  30.2 2.2 %collective-permute-start.12 = (bf16[2,128,128]{2,1,0:T(8,128)(2,1)S(1)}, bf16[2,128,128]{2,1,0:T(8,128)(2,1)S(1)}, u32[]{:S(2)}, u32[]{:S(2)}) collective-permute-start(bf16[2,128,128]{2,1,0:T(8,128)(2,1)S(1)} %start_share.1.refs_4_), channel_id=1, source_target_pairs={{0,28},{4,24},{8,20},{12,16},{16,12},{20,8},{24,4},{28,0},{1,29},{... | collective-permute-start | bytes 196616 | tf_op jit(solution)/shard_map/ppermute | solution.py:373
  32.4 0.7 collective-permute-start.11
  33.1 2.3 %collective-permute-done.12.refs_11_ = bf16[2,128,128]{2,1,0:T(8,128)(2,1)S(1)} collective-permute-done((bf16[2,128,128]{2,1,0:T(8,128)(2,1)S(1)}, bf16[2,128,128]{2,1,0:T(8,128)(2,1)S(1)}, u32[]{:S(2)}, u32[]{:S(2)}) %collective-permute-start.12) | collective-permute-done | bytes 65568 | tf_op jit(solution)/shard_map/ppermute | solution.py:373
  35.3 1.7 %collective-permute-start.10 = (bf16[2,128,128]{2,1,0:T(8,128)(2,1)S(1)}, bf16[2,128,128]{2,1,0:T(8,128)(2,1)S(1)}, u32[]{:S(2)}, u32[]{:S(2)}) collective-permute-start(bf16[2,128,128]{2,1,0:T(8,128)(2,1)S(1)} %start_share.1.refs_4_), channel_id=1, source_target_pairs={{0,20},{4,16},{8,28},{12,24},{16,4},{20,0},{24,12},{28,8},{1,21},{... | collective-permute-start | bytes 196616 | tf_op jit(solution)/shard_map/ppermute | solution.py:373
  37.1 0.9 collective-permute-done.11.refs_10_
  38.0 0.7 collective-permute-start.9
  38.7 0.8 collective-permute-done.10.refs_9_
  39.5 2.1 %collective-permute-start.8 = (bf16[2,128,128]{2,1,0:T(8,128)(2,1)S(1)}, bf16[2,128,128]{2,1,0:T(8,128)(2,1)S(1)}, u32[]{:S(2)}, u32[]{:S(2)}) collective-permute-start(bf16[2,128,128]{2,1,0:T(8,128)(2,1)S(1)} %start_share.1.refs_4_), channel_id=1, source_target_pairs={{0,12},{4,8},{8,4},{12,0},{16,28},{20,24},{24,20},{28,16},{1,13},{... | collective-permute-start | bytes 196616 | tf_op jit(solution)/shard_map/ppermute | solution.py:373
  41.6 0.7 collective-permute-done.9.refs_8_
  42.3 0.8 collective-permute-start.7
  43.1 0.9 collective-permute-done.8.refs_7_
  44.1 0.4 collective-permute-start.6
  44.4 1.2 pack1_0.1.refs_0_
  45.6 0.9 collective-permute-done.7.refs_6_
  46.5 5.0 %chunk0.1 = (bf16[4,256,256]{2,1,0:T(8,128)(2,1)}, bf16[6,128,128]{2,1,0:T(8,128)(2,1)S(1)}) custom-call(s32[1]{0:T(128)} %bitcast.me, s32[1]{0:T(128)} %bitcast.1.dp, bf16[640,256]{1,0:T(8,128)(2,1)S(1)} %pack0_0.1.refs_0_, bf16[640,256]{1,0:T(8,128)(2,1)S(1)} %collective-permute-done.3.refs_1_, bf16[640,256]{1,0:T(8,128)(2,1)S(1)} %collective-permute-done.4.refs_2_, ...), custom_call_target="tpu_custom_call" | custom-call | flops 1280000000 | bytes 2000000 | tf_op jit(solution)/shard_map/chunk0/pallas_call | solution.py:40
  51.5 14.9 %collective-permute-done.1.refs_2_ = bf16[608,384]{1,0:T(8,128)(2,1)S(1)} collective-permute-done((bf16[608,384]{1,0:T(8,128)(2,1)S(1)}, bf16[608,384]{1,0:T(8,128)(2,1)S(1)}, u32[]{:S(2)}, u32[]{:S(2)}) %collective-permute-start.1) | collective-permute-done | bytes 466976 | tf_op jit(solution)/shard_map/ppermute | solution.py:378
  66.4 6.5 %chunk1.1 = (bf16[4,256,384]{2,1,0:T(8,128)(2,1)}, bf16[8,128,128]{2,1,0:T(8,128)(2,1)S(1)}, bf16[8,128,128]{2,1,0:T(8,128)(2,1)S(1)}) custom-call(s32[1]{0:T(128)} %bitcast.me, s32[1]{0:T(128)} %bitcast.1.dp, bf16[608,384]{1,0:T(8,128)(2,1)S(1)} %pack1_0.1.refs_0_, bf16[608,384]{1,0:T(8,128)(2,1)S(1)} %collective-permute-done.refs_1_, ...), custom_call_target="tpu_custom_call" | custom-call | flops 1920000000 | bytes 3000000 | tf_op jit(solution)/shard_map/chunk1/pallas_call | solution.py:40
  72.9 12.9 %all-to-all-start = ((bf16[4,256,384]{2,1,0:T(8,128)(2,1)}), bf16[4,256,384]{2,1,0:T(8,128)(2,1)S(1)}, u32[]{:S(2)}, u32[]{:S(2)}) async-start(bf16[4,256,384]{2,1,0:T(8,128)(2,1)} %get-tuple-element.62), calls=%async_computation | async-start | bytes 1572864 | tf_op jit(solution)/shard_map/all_to_all | solution.py:381
  85.8 1.5 %collective-permute-done.13.got_ref = bf16[8,128,128]{2,1,0:T(8,128)(2,1)S(1)} collective-permute-done((bf16[8,128,128]{2,1,0:T(8,128)(2,1)S(1)}, bf16[8,128,128]{2,1,0:T(8,128)(2,1)S(1)}, u32[]{:S(2)}, u32[]{:S(2)}) %collective-permute-start.13) | collective-permute-done | bytes 262176 | tf_op jit(solution)/shard_map/ppermute | solution.py:373
  87.4 1.4 %collective-permute-start.14 = (bf16[2,128,128]{2,1,0:T(8,128)(2,1)S(1)}, bf16[2,128,128]{2,1,0:T(8,128)(2,1)S(1)}, u32[]{:S(2)}, u32[]{:S(2)}) collective-permute-start(bf16[2,128,128]{2,1,0:T(8,128)(2,1)S(1)} %get-tuple-element.58), channel_id=1, source_target_pairs={{0,8},{4,12},{8,0},{12,4},{16,24},{20,28},{24,16},{28,20},{1,9},{5... | collective-permute-start | bytes 196616 | tf_op jit(solution)/shard_map/ppermute | solution.py:373
  88.9 1.5 %collective-permute-start.15 = (bf16[2,128,128]{2,1,0:T(8,128)(2,1)S(1)}, bf16[2,128,128]{2,1,0:T(8,128)(2,1)S(1)}, u32[]{:S(2)}, u32[]{:S(2)}) collective-permute-start(bf16[2,128,128]{2,1,0:T(8,128)(2,1)S(1)} %get-tuple-element.59), channel_id=1, source_target_pairs={{0,16},{4,20},{8,24},{12,28},{16,0},{20,4},{24,8},{28,12},{1,17},{... | collective-permute-start | bytes 196616 | tf_op jit(solution)/shard_map/ppermute | solution.py:373
  90.4 0.6 collective-permute-start.16
  91.0 0.8 collective-permute-done.14.refs_1_
  91.8 1.4 %collective-permute-done.15.refs_2_ = bf16[2,128,128]{2,1,0:T(8,128)(2,1)S(1)} collective-permute-done((bf16[2,128,128]{2,1,0:T(8,128)(2,1)S(1)}, bf16[2,128,128]{2,1,0:T(8,128)(2,1)S(1)}, u32[]{:S(2)}, u32[]{:S(2)}) %collective-permute-start.15) | collective-permute-done | bytes 65568 | tf_op jit(solution)/shard_map/ppermute | solution.py:373
  93.1 2.4 %collective-permute-done.16.refs_3_ = bf16[2,128,128]{2,1,0:T(8,128)(2,1)S(1)} collective-permute-done((bf16[2,128,128]{2,1,0:T(8,128)(2,1)S(1)}, bf16[2,128,128]{2,1,0:T(8,128)(2,1)S(1)}, u32[]{:S(2)}, u32[]{:S(2)}) %collective-permute-start.16) | collective-permute-done | bytes 65568 | tf_op jit(solution)/shard_map/ppermute | solution.py:373
  95.6 2.1 %collective-permute-start.17 = (bf16[2,32,128]{2,1,0:T(8,128)(2,1)S(1)}, bf16[2,32,128]{2,1,0:T(8,128)(2,1)S(1)}, u32[]{:S(2)}, u32[]{:S(2)}) collective-permute-start(bf16[2,32,128]{2,1,0:T(8,128)(2,1)S(1)} %get-tuple-element.64), channel_id=1, source_target_pairs={{0,1},{1,2},{2,3},{3,0},{4,5},{5,6},{6,7},{7,4},{8,9},{9,10},{10,1... | collective-permute-start | bytes 49160 | tf_op jit(solution)/shard_map/ppermute | solution.py:378
  97.7 2.4 %collective-permute-start.18 = (bf16[2,32,128]{2,1,0:T(8,128)(2,1)S(1)}, bf16[2,32,128]{2,1,0:T(8,128)(2,1)S(1)}, u32[]{:S(2)}, u32[]{:S(2)}) collective-permute-start(bf16[2,32,128]{2,1,0:T(8,128)(2,1)S(1)} %get-tuple-element.65), channel_id=1, source_target_pairs={{0,2},{1,3},{2,0},{3,1},{4,6},{5,7},{6,4},{7,5},{8,10},{9,11},{10,... | collective-permute-start | bytes 49160 | tf_op jit(solution)/shard_map/ppermute | solution.py:378
  100.0 1.5 %collective-permute-start.19 = (bf16[2,32,128]{2,1,0:T(8,128)(2,1)S(1)}, bf16[2,32,128]{2,1,0:T(8,128)(2,1)S(1)}, u32[]{:S(2)}, u32[]{:S(2)}) collective-permute-start(bf16[2,32,128]{2,1,0:T(8,128)(2,1)S(1)} %get-tuple-element.66), channel_id=1, source_target_pairs={{0,3},{1,0},{2,1},{3,2},{4,7},{5,4},{6,5},{7,6},{8,11},{9,8},{10,9... | collective-permute-start | bytes 49160 | tf_op jit(solution)/shard_map/ppermute | solution.py:378
  101.5 4.9 %all-to-all-done.refs_1_ = bf16[4,256,384]{2,1,0:T(8,128)(2,1)S(1)} async-done(((bf16[4,256,384]{2,1,0:T(8,128)(2,1)}), bf16[4,256,384]{2,1,0:T(8,128)(2,1)S(1)}, u32[]{:S(2)}, u32[]{:S(2)}) %all-to-all-start) | async-done | bytes 786464 | tf_op jit(solution)/shard_map/all_to_all | solution.py:381
  106.6 3.6 %all-to-all-start.1 = ((bf16[4,256,256]{2,1,0:T(8,128)(2,1)}), bf16[4,256,256]{2,1,0:T(8,128)(2,1)S(1)}, u32[]{:S(2)}, u32[]{:S(2)}) async-start(bf16[4,256,256]{2,1,0:T(8,128)(2,1)} %get-tuple-element.68), calls=%async_computation.1 | async-start | bytes 1048576 | tf_op jit(solution)/shard_map/all_to_all | solution.py:381
  110.2 2.8 %collective-permute-start.22 = (bf16[4,2,32,128]{3,2,1,0:T(8,128)(2,1)S(1)}, bf16[4,2,32,128]{3,2,1,0:T(8,128)(2,1)S(1)}, u32[]{:S(2)}, u32[]{:S(2)}) collective-permute-start(bf16[4,2,32,128]{3,2,1,0:T(8,128)(2,1)S(1)} %state_rows.1.refs_0_), channel_id=1, source_target_pairs={{0,24},{4,28},{8,16},{12,20},{16,8},{20,12},{24,0},{28,4},{1,25},{... | collective-permute-start | bytes 196616 | tf_op jit(solution)/shard_map/ppermute | solution.py:373
  113.4 0.3 collective-permute-start.20
  113.7 1.8 %collective-permute-done.22.refs_3_ = bf16[4,2,32,128]{3,2,1,0:T(8,128)(2,1)S(1)} collective-permute-done((bf16[4,2,32,128]{3,2,1,0:T(8,128)(2,1)S(1)}, bf16[4,2,32,128]{3,2,1,0:T(8,128)(2,1)S(1)}, u32[]{:S(2)}, u32[]{:S(2)}) %collective-permute-start.22) | collective-permute-done | bytes 65568 | tf_op jit(solution)/shard_map/ppermute | solution.py:373
  115.5 1.8 %collective-permute-done.21.refs_2_ = bf16[4,2,32,128]{3,2,1,0:T(8,128)(2,1)S(1)} collective-permute-done((bf16[4,2,32,128]{3,2,1,0:T(8,128)(2,1)S(1)}, bf16[4,2,32,128]{3,2,1,0:T(8,128)(2,1)S(1)}, u32[]{:S(2)}, u32[]{:S(2)}) %collective-permute-start.21) | collective-permute-done | bytes 65568 | tf_op jit(solution)/shard_map/ppermute | solution.py:373
  117.8 1.5 %collective-permute-done.23.refs_1_ = bf16[4,4,2,32,128]{4,3,2,1,0:T(8,128)(2,1)S(1)} collective-permute-done((bf16[4,4,2,32,128]{4,3,2,1,0:T(8,128)(2,1)S(1)}, bf16[4,4,2,32,128]{4,3,2,1,0:T(8,128)(2,1)S(1)}, u32[]{:S(2)}, u32[]{:S(2)}) %collective-permute-start.23) | collective-permute-done | bytes 262176 | tf_op jit(solution)/shard_map/ppermute | solution.py:373
  119.3 1.2 state_out.1
  120.5 3.4 %all-to-all-done.1.refs_0_ = bf16[4,256,256]{2,1,0:T(8,128)(2,1)S(1)} async-done(((bf16[4,256,256]{2,1,0:T(8,128)(2,1)}), bf16[4,256,256]{2,1,0:T(8,128)(2,1)S(1)}, u32[]{:S(2)}, u32[]{:S(2)}) %all-to-all-start.1) | async-done | bytes 524320 | tf_op jit(solution)/shard_map/all_to_all | solution.py:381
  123.9 1.2 unpack.1
  (17 shorter events, 1.5 us)
Async XLA Ops:
  2.3 13.8 %collective-permute-start.3 = (bf16[640,256]{1,0:T(8,128)(2,1)S(1)}, bf16[640,256]{1,0:T(8,128)(2,1)S(1)}, u32[]{:S(2)}, u32[]{:S(2)}) collective-permute-start(bf16[640,256]{1,0:T(8,128)(2,1)S(1)} %get-tuple-element.49), channel_id=1, source_target_pairs={{0,1},{1,2},{2,3},{3,0},{4,5},{5,6},{6,7},{7,4},{8,9},{9,10},{10,1... | collective-permute-start | bytes 983048 | tf_op jit(solution)/shard_map/ppermute | solution.py:378
  5.4 24.8 %collective-permute-start.4 = (bf16[640,256]{1,0:T(8,128)(2,1)S(1)}, bf16[640,256]{1,0:T(8,128)(2,1)S(1)}, u32[]{:S(2)}, u32[]{:S(2)}) collective-permute-start(bf16[640,256]{1,0:T(8,128)(2,1)S(1)} %get-tuple-element.50), channel_id=1, source_target_pairs={{0,2},{1,3},{2,0},{3,1},{4,6},{5,7},{6,4},{7,5},{8,10},{9,11},{10,... | collective-permute-start | bytes 983048 | tf_op jit(solution)/shard_map/ppermute | solution.py:378
  8.0 22.2 %collective-permute-start.5 = (bf16[640,256]{1,0:T(8,128)(2,1)S(1)}, bf16[640,256]{1,0:T(8,128)(2,1)S(1)}, u32[]{:S(2)}, u32[]{:S(2)}) collective-permute-start(bf16[640,256]{1,0:T(8,128)(2,1)S(1)} %get-tuple-element.51), channel_id=1, source_target_pairs={{0,3},{1,0},{2,1},{3,2},{4,7},{5,4},{6,5},{7,6},{8,11},{9,8},{10,9... | collective-permute-start | bytes 983048 | tf_op jit(solution)/shard_map/ppermute | solution.py:378
  11.0 40.5 %collective-permute-start = (bf16[608,384]{1,0:T(8,128)(2,1)S(1)}, bf16[608,384]{1,0:T(8,128)(2,1)S(1)}, u32[]{:S(2)}, u32[]{:S(2)}) collective-permute-start(bf16[608,384]{1,0:T(8,128)(2,1)S(1)} %get-tuple-element.46), channel_id=1, source_target_pairs={{0,1},{1,2},{2,3},{3,0},{4,5},{5,6},{6,7},{7,4},{8,9},{9,10},{10,1... | collective-permute-start | bytes 1400840 | tf_op jit(solution)/shard_map/ppermute | solution.py:378
  11.7 54.7 %collective-permute-start.1 = (bf16[608,384]{1,0:T(8,128)(2,1)S(1)}, bf16[608,384]{1,0:T(8,128)(2,1)S(1)}, u32[]{:S(2)}, u32[]{:S(2)}) collective-permute-start(bf16[608,384]{1,0:T(8,128)(2,1)S(1)} %get-tuple-element.47), channel_id=1, source_target_pairs={{0,2},{1,3},{2,0},{3,1},{4,6},{5,7},{6,4},{7,5},{8,10},{9,11},{10,... | collective-permute-start | bytes 1400840 | tf_op jit(solution)/shard_map/ppermute | solution.py:378
  16.1 50.3 %collective-permute-start.2 = (bf16[608,384]{1,0:T(8,128)(2,1)S(1)}, bf16[608,384]{1,0:T(8,128)(2,1)S(1)}, u32[]{:S(2)}, u32[]{:S(2)}) collective-permute-start(bf16[608,384]{1,0:T(8,128)(2,1)S(1)} %get-tuple-element.48), channel_id=1, source_target_pairs={{0,3},{1,0},{2,1},{3,2},{4,7},{5,4},{6,5},{7,6},{8,11},{9,8},{10,9... | collective-permute-start | bytes 1400840 | tf_op jit(solution)/shard_map/ppermute | solution.py:378
  30.2 5.1 %collective-permute-start.12 = (bf16[2,128,128]{2,1,0:T(8,128)(2,1)S(1)}, bf16[2,128,128]{2,1,0:T(8,128)(2,1)S(1)}, u32[]{:S(2)}, u32[]{:S(2)}) collective-permute-start(bf16[2,128,128]{2,1,0:T(8,128)(2,1)S(1)} %start_share.1.refs_4_), channel_id=1, source_target_pairs={{0,28},{4,24},{8,20},{12,16},{16,12},{20,8},{24,4},{28,0},{1,29},{... | collective-permute-start | bytes 196616 | tf_op jit(solution)/shard_map/ppermute | solution.py:373
  32.4 5.6 %collective-permute-start.11 = (bf16[2,128,128]{2,1,0:T(8,128)(2,1)S(1)}, bf16[2,128,128]{2,1,0:T(8,128)(2,1)S(1)}, u32[]{:S(2)}, u32[]{:S(2)}) collective-permute-start(bf16[2,128,128]{2,1,0:T(8,128)(2,1)S(1)} %start_share.1.refs_4_), channel_id=1, source_target_pairs={{0,24},{4,28},{8,16},{12,20},{16,8},{20,12},{24,0},{28,4},{1,25},{... | collective-permute-start | bytes 196616 | tf_op jit(solution)/shard_map/ppermute | solution.py:373
  35.3 4.2 %collective-permute-start.10 = (bf16[2,128,128]{2,1,0:T(8,128)(2,1)S(1)}, bf16[2,128,128]{2,1,0:T(8,128)(2,1)S(1)}, u32[]{:S(2)}, u32[]{:S(2)}) collective-permute-start(bf16[2,128,128]{2,1,0:T(8,128)(2,1)S(1)} %start_share.1.refs_4_), channel_id=1, source_target_pairs={{0,20},{4,16},{8,28},{12,24},{16,4},{20,0},{24,12},{28,8},{1,21},{... | collective-permute-start | bytes 196616 | tf_op jit(solution)/shard_map/ppermute | solution.py:373
  38.0 4.3 %collective-permute-start.9 = (bf16[2,128,128]{2,1,0:T(8,128)(2,1)S(1)}, bf16[2,128,128]{2,1,0:T(8,128)(2,1)S(1)}, u32[]{:S(2)}, u32[]{:S(2)}) collective-permute-start(bf16[2,128,128]{2,1,0:T(8,128)(2,1)S(1)} %start_share.1.refs_4_), channel_id=1, source_target_pairs={{0,16},{4,20},{8,24},{12,28},{16,0},{20,4},{24,8},{28,12},{1,17},{... | collective-permute-start | bytes 196616 | tf_op jit(solution)/shard_map/ppermute | solution.py:373
  39.5 4.5 %collective-permute-start.8 = (bf16[2,128,128]{2,1,0:T(8,128)(2,1)S(1)}, bf16[2,128,128]{2,1,0:T(8,128)(2,1)S(1)}, u32[]{:S(2)}, u32[]{:S(2)}) collective-permute-start(bf16[2,128,128]{2,1,0:T(8,128)(2,1)S(1)} %start_share.1.refs_4_), channel_id=1, source_target_pairs={{0,12},{4,8},{8,4},{12,0},{16,28},{20,24},{24,20},{28,16},{1,13},{... | collective-permute-start | bytes 196616 | tf_op jit(solution)/shard_map/ppermute | solution.py:373
  42.3 4.3 %collective-permute-start.7 = (bf16[2,128,128]{2,1,0:T(8,128)(2,1)S(1)}, bf16[2,128,128]{2,1,0:T(8,128)(2,1)S(1)}, u32[]{:S(2)}, u32[]{:S(2)}) collective-permute-start(bf16[2,128,128]{2,1,0:T(8,128)(2,1)S(1)} %start_share.1.refs_4_), channel_id=1, source_target_pairs={{0,8},{4,12},{8,0},{12,4},{16,24},{20,28},{24,16},{28,20},{1,9},{5... | collective-permute-start | bytes 196616 | tf_op jit(solution)/shard_map/ppermute | solution.py:373
  44.1 2.5 %collective-permute-start.6 = (bf16[2,128,128]{2,1,0:T(8,128)(2,1)S(1)}, bf16[2,128,128]{2,1,0:T(8,128)(2,1)S(1)}, u32[]{:S(2)}, u32[]{:S(2)}) collective-permute-start(bf16[2,128,128]{2,1,0:T(8,128)(2,1)S(1)} %start_share.1.refs_4_), channel_id=1, source_target_pairs={{0,4},{4,0},{8,12},{12,8},{16,20},{20,16},{24,28},{28,24},{1,5},{5... | collective-permute-start | bytes 196616 | tf_op jit(solution)/shard_map/ppermute | solution.py:373
  72.9 33.5 %all-to-all-start = ((bf16[4,256,384]{2,1,0:T(8,128)(2,1)}), bf16[4,256,384]{2,1,0:T(8,128)(2,1)S(1)}, u32[]{:S(2)}, u32[]{:S(2)}) async-start(bf16[4,256,384]{2,1,0:T(8,128)(2,1)} %get-tuple-element.62), calls=%async_computation | async-start | bytes 1572864 | tf_op jit(solution)/shard_map/all_to_all | solution.py:381
  85.8 1.5 %collective-permute-start.13 = (bf16[8,128,128]{2,1,0:T(8,128)(2,1)S(1)}, bf16[8,128,128]{2,1,0:T(8,128)(2,1)S(1)}, u32[]{:S(2)}, u32[]{:S(2)}) collective-permute-start(bf16[8,128,128]{2,1,0:T(8,128)(2,1)S(1)} %get-tuple-element.56), channel_id=1, source_target_pairs={{0,4},{4,0},{8,12},{12,8},{16,20},{20,16},{24,28},{28,24},{1,5},{5... | collective-permute-start | bytes 786440 | tf_op jit(solution)/shard_map/ppermute | solution.py:373
  87.4 4.3 %collective-permute-start.14 = (bf16[2,128,128]{2,1,0:T(8,128)(2,1)S(1)}, bf16[2,128,128]{2,1,0:T(8,128)(2,1)S(1)}, u32[]{:S(2)}, u32[]{:S(2)}) collective-permute-start(bf16[2,128,128]{2,1,0:T(8,128)(2,1)S(1)} %get-tuple-element.58), channel_id=1, source_target_pairs={{0,8},{4,12},{8,0},{12,4},{16,24},{20,28},{24,16},{28,20},{1,9},{5... | collective-permute-start | bytes 196616 | tf_op jit(solution)/shard_map/ppermute | solution.py:373
  88.9 4.3 %collective-permute-start.15 = (bf16[2,128,128]{2,1,0:T(8,128)(2,1)S(1)}, bf16[2,128,128]{2,1,0:T(8,128)(2,1)S(1)}, u32[]{:S(2)}, u32[]{:S(2)}) collective-permute-start(bf16[2,128,128]{2,1,0:T(8,128)(2,1)S(1)} %get-tuple-element.59), channel_id=1, source_target_pairs={{0,16},{4,20},{8,24},{12,28},{16,0},{20,4},{24,8},{28,12},{1,17},{... | collective-permute-start | bytes 196616 | tf_op jit(solution)/shard_map/ppermute | solution.py:373
  90.4 5.2 %collective-permute-start.16 = (bf16[2,128,128]{2,1,0:T(8,128)(2,1)S(1)}, bf16[2,128,128]{2,1,0:T(8,128)(2,1)S(1)}, u32[]{:S(2)}, u32[]{:S(2)}) collective-permute-start(bf16[2,128,128]{2,1,0:T(8,128)(2,1)S(1)} %get-tuple-element.60), channel_id=1, source_target_pairs={{0,24},{4,28},{8,16},{12,20},{16,8},{20,12},{24,0},{28,4},{1,25},{... | collective-permute-start | bytes 196616 | tf_op jit(solution)/shard_map/ppermute | solution.py:373
  95.6 10.8 %collective-permute-start.17 = (bf16[2,32,128]{2,1,0:T(8,128)(2,1)S(1)}, bf16[2,32,128]{2,1,0:T(8,128)(2,1)S(1)}, u32[]{:S(2)}, u32[]{:S(2)}) collective-permute-start(bf16[2,32,128]{2,1,0:T(8,128)(2,1)S(1)} %get-tuple-element.64), channel_id=1, source_target_pairs={{0,1},{1,2},{2,3},{3,0},{4,5},{5,6},{6,7},{7,4},{8,9},{9,10},{10,1... | collective-permute-start | bytes 49160 | tf_op jit(solution)/shard_map/ppermute | solution.py:378
  97.7 8.9 %collective-permute-start.18 = (bf16[2,32,128]{2,1,0:T(8,128)(2,1)S(1)}, bf16[2,32,128]{2,1,0:T(8,128)(2,1)S(1)}, u32[]{:S(2)}, u32[]{:S(2)}) collective-permute-start(bf16[2,32,128]{2,1,0:T(8,128)(2,1)S(1)} %get-tuple-element.65), channel_id=1, source_target_pairs={{0,2},{1,3},{2,0},{3,1},{4,6},{5,7},{6,4},{7,5},{8,10},{9,11},{10,... | collective-permute-start | bytes 49160 | tf_op jit(solution)/shard_map/ppermute | solution.py:378
  100.0 6.6 %collective-permute-start.19 = (bf16[2,32,128]{2,1,0:T(8,128)(2,1)S(1)}, bf16[2,32,128]{2,1,0:T(8,128)(2,1)S(1)}, u32[]{:S(2)}, u32[]{:S(2)}) collective-permute-start(bf16[2,32,128]{2,1,0:T(8,128)(2,1)S(1)} %get-tuple-element.66), channel_id=1, source_target_pairs={{0,3},{1,0},{2,1},{3,2},{4,7},{5,4},{6,5},{7,6},{8,11},{9,8},{10,9... | collective-permute-start | bytes 49160 | tf_op jit(solution)/shard_map/ppermute | solution.py:378
  106.6 17.3 %all-to-all-start.1 = ((bf16[4,256,256]{2,1,0:T(8,128)(2,1)}), bf16[4,256,256]{2,1,0:T(8,128)(2,1)S(1)}, u32[]{:S(2)}, u32[]{:S(2)}) async-start(bf16[4,256,256]{2,1,0:T(8,128)(2,1)} %get-tuple-element.68), calls=%async_computation.1 | async-start | bytes 1048576 | tf_op jit(solution)/shard_map/all_to_all | solution.py:381
  110.2 5.3 %collective-permute-start.22 = (bf16[4,2,32,128]{3,2,1,0:T(8,128)(2,1)S(1)}, bf16[4,2,32,128]{3,2,1,0:T(8,128)(2,1)S(1)}, u32[]{:S(2)}, u32[]{:S(2)}) collective-permute-start(bf16[4,2,32,128]{3,2,1,0:T(8,128)(2,1)S(1)} %state_rows.1.refs_0_), channel_id=1, source_target_pairs={{0,24},{4,28},{8,16},{12,20},{16,8},{20,12},{24,0},{28,4},{1,25},{... | collective-permute-start | bytes 196616 | tf_op jit(solution)/shard_map/ppermute | solution.py:373
  113.1 4.3 %collective-permute-start.21 = (bf16[4,2,32,128]{3,2,1,0:T(8,128)(2,1)S(1)}, bf16[4,2,32,128]{3,2,1,0:T(8,128)(2,1)S(1)}, u32[]{:S(2)}, u32[]{:S(2)}) collective-permute-start(bf16[4,2,32,128]{3,2,1,0:T(8,128)(2,1)S(1)} %state_rows.1.refs_0_), channel_id=1, source_target_pairs={{0,16},{4,20},{8,24},{12,28},{16,0},{20,4},{24,8},{28,12},{1,17},{... | collective-permute-start | bytes 196616 | tf_op jit(solution)/shard_map/ppermute | solution.py:373
  113.4 4.3 %collective-permute-start.20 = (bf16[4,2,32,128]{3,2,1,0:T(8,128)(2,1)S(1)}, bf16[4,2,32,128]{3,2,1,0:T(8,128)(2,1)S(1)}, u32[]{:S(2)}, u32[]{:S(2)}) collective-permute-start(bf16[4,2,32,128]{3,2,1,0:T(8,128)(2,1)S(1)} %state_rows.1.refs_0_), channel_id=1, source_target_pairs={{0,8},{4,12},{8,0},{12,4},{16,24},{20,28},{24,16},{28,20},{1,9},{5... | collective-permute-start | bytes 196616 | tf_op jit(solution)/shard_map/ppermute | solution.py:373
  117.7 1.6 %collective-permute-start.23 = (bf16[4,4,2,32,128]{4,3,2,1,0:T(8,128)(2,1)S(1)}, bf16[4,4,2,32,128]{4,3,2,1,0:T(8,128)(2,1)S(1)}, u32[]{:S(2)}, u32[]{:S(2)}) collective-permute-start(bf16[4,4,2,32,128]{4,3,2,1,0:T(8,128)(2,1)S(1)} %state_rest.1.refs_0_), channel_id=1, source_target_pairs={{0,4},{4,0},{8,12},{12,8},{16,20},{20,16},{24,28},{28,24},{1,5},{5... | collective-permute-start | bytes 786440 | tf_op jit(solution)/shard_map/ppermute | solution.py:373
